TPU v7x, 32 devices: a whole 2x2x4 slice. The times are simulated.
32 devices in a mesh: dp: 8 (over z, x), tensor: 4 (over y, core).
Axes of the slice: x: 2, y: 2, z: 4, core: 2. Of those that a mesh axis runs over, the one named last changes fastest.
Arguments:
- byte_ids: int32 [32, 512], P(('dp', 'tensor')), may hold values from 0 to 255
- targets: int32 [32, 512], P(('dp', 'tensor')), may hold values from 0 to 255
- boundaries: int32 [32, 512], P(('dp', 'tensor')), may hold values from 0 to 1, as said below
- lengths: int32 [32], P(('dp', 'tensor')), may hold values from 1 to 512, as said below
- tables: float32 [2, 256, 1024], P(None, ('dp', 'tensor'))
- tables_first: float32 [2, 256, 1024], P(None, ('dp', 'tensor')), may hold values from -9.536743e-07 to 9.536743e-07
- tables_second: float32 [2, 256, 1024], P(None, ('dp', 'tensor')), may hold values from 5.753581e-14 to 9.294246e-13
- mamba_in: float32 [2, 1024, 4384], P(None, ('dp', 'tensor')), may hold values from -0.1875 to 0.1875
- mamba_in_first: float32 [2, 1024, 4384], P(None, ('dp', 'tensor')), may hold values from -9.536743e-07 to 9.536743e-07
- mamba_in_second: float32 [2, 1024, 4384], P(None, ('dp', 'tensor')), may hold values from 5.753581e-14 to 9.294246e-13
- mamba_out: float32 [2, 2048, 1024], P(None, ('dp', 'tensor')), may hold values from -0.125 to 0.125
- mamba_out_first: float32 [2, 2048, 1024], P(None, ('dp', 'tensor')), may hold values from -9.536743e-07 to 9.536743e-07
- mamba_out_second: float32 [2, 2048, 1024], P(None, ('dp', 'tensor')), may hold values from 5.753581e-14 to 9.294246e-13
- route_proj: float32 [1024, 3072], P(('dp', 'tensor'))
- route_proj_first: float32 [1024, 3072], P(('dp', 'tensor')), may hold values from -9.536743e-07 to 9.536743e-07
- route_proj_second: float32 [1024, 3072], P(('dp', 'tensor')), may hold values from 5.753581e-14 to 9.294246e-13
- small_params: float32 [34944], P(('dp', 'tensor'))
- small_params_first: float32 [34944], P(('dp', 'tensor')), may hold values from -3.8146973e-06 to 3.8146973e-06
- small_params_second: float32 [34944], P(('dp', 'tensor')), may hold values from 9.294246e-13 to 1.4826536e-11
- heed_triple_matrix: float32 [1536, 3, 1536], P('dp', None, 'tensor'), may hold values from -0.15625 to 0.15625
- attn_qkv_first: float32 [1536, 3, 1536], P('dp', None, 'tensor'), may hold values from -9.536743e-07 to 9.536743e-07
- attn_qkv_second: float32 [1536, 3, 1536], P('dp', None, 'tensor'), may hold values from 5.753581e-14 to 9.294246e-13
- heed_exit_matrix: float32 [1536, 1536], P('tensor', 'dp'), may hold values from -0.625 to 0.625
- attn_out_first: float32 [1536, 1536], P('tensor', 'dp'), may hold values from -9.536743e-07 to 9.536743e-07
- attn_out_second: float32 [1536, 1536], P('tensor', 'dp'), may hold values from 5.753581e-14 to 9.294246e-13
- lifting_matrix: float32 [1536, 2, 4096], P('dp', None, 'tensor'), may hold values from -0.15625 to 0.15625
- mlp_gate_up_first: float32 [1536, 2, 4096], P('dp', None, 'tensor'), may hold values from -9.536743e-07 to 9.536743e-07
- mlp_gate_up_second: float32 [1536, 2, 4096], P('dp', None, 'tensor'), may hold values from 5.753581e-14 to 9.294246e-13
- lowering_matrix: float32 [4096, 1536], P('tensor', 'dp'), may hold values from -0.09375 to 0.09375
- mlp_down_first: float32 [4096, 1536], P('tensor', 'dp'), may hold values from -9.536743e-07 to 9.536743e-07
- mlp_down_second: float32 [4096, 1536], P('tensor', 'dp'), may hold values from 5.753581e-14 to 9.294246e-13
Outputs:
- loss_sum: float32 [], replicated
- byte_count: float32 [], replicated
- grad_norm: float32 [], replicated
- tables_first_new: float32 [2, 256, 1024], P(None, ('dp', 'tensor'))
- tables_second_new: float32 [2, 256, 1024], P(None, ('dp', 'tensor'))
- tables_new: float32 [2, 256, 1024], P(None, ('dp', 'tensor'))
- mamba_in_first_new: float32 [2, 1024, 4384], P(None, ('dp', 'tensor'))
- mamba_in_second_new: float32 [2, 1024, 4384], P(None, ('dp', 'tensor'))
- mamba_in_new: float32 [2, 1024, 4384], P(None, ('dp', 'tensor'))
- mamba_out_first_new: float32 [2, 2048, 1024], P(None, ('dp', 'tensor'))
- mamba_out_second_new: float32 [2, 2048, 1024], P(None, ('dp', 'tensor'))
- mamba_out_new: float32 [2, 2048, 1024], P(None, ('dp', 'tensor'))
- route_proj_first_new: float32 [1024, 3072], P(('dp', 'tensor'))
- route_proj_second_new: float32 [1024, 3072], P(('dp', 'tensor'))
- route_proj_new: float32 [1024, 3072], P(('dp', 'tensor'))
- small_params_first_new: float32 [34944], P(('dp', 'tensor'))
- small_params_second_new: float32 [34944], P(('dp', 'tensor'))
- small_params_new: float32 [34944], P(('dp', 'tensor'))
- attn_qkv_first_new: float32 [1536, 3, 1536], P('dp', None, 'tensor')
- attn_qkv_second_new: float32 [1536, 3, 1536], P('dp', None, 'tensor')
- attn_qkv_new: float32 [1536, 3, 1536], P('dp', None, 'tensor')
- attn_out_first_new: float32 [1536, 1536], P('tensor', 'dp')
- attn_out_second_new: float32 [1536, 1536], P('tensor', 'dp')
- attn_out_new: float32 [1536, 1536], P('tensor', 'dp')
- mlp_gate_up_first_new: float32 [1536, 2, 4096], P('dp', None, 'tensor')
- mlp_gate_up_second_new: float32 [1536, 2, 4096], P('dp', None, 'tensor')
- mlp_gate_up_new: float32 [1536, 2, 4096], P('dp', None, 'tensor')
- mlp_down_first_new: float32 [4096, 1536], P('tensor', 'dp')
- mlp_down_second_new: float32 [4096, 1536], P('tensor', 'dp')
- mlp_down_new: float32 [4096, 1536], P('tensor', 'dp')
Inputs may be any that keep to these rules, and one draw needn't show every extreme that they name: `boundaries`: in every sequence the first byte opens a span, and between 64 and 128 bytes do; some sequence has exactly 128 spans. `lengths`: the last sequence counts all its 512 bytes.
All inputs are finite; a program needn't handle non-finite values.
Results may differ from a plain program's by a relative error of at most 0.017.
The roundings to bfloat16 on the way count: a program that leaves them out, or rounds other values in their place, can miss the bound.
Values may be sent and summed in bfloat16 or wider, within the bound.
A program may use at most 384 MiB of HBM per device.

v0:
```python
from functools import partial

import jax
import jax.numpy as jnp
from jax import lax
from jax.sharding import PartitionSpec as P

BYTE_WIDTH = 1024
CORE_WIDTH = 1536
VOCAB = 256
STATE = 128
HEADDIM = 64
STEP = 10
INNER = 2048
MHEADS = 32
HD = 96
MAX_PIECES = 128


deepest_tier = lax.Precision.HIGHEST
norm_eps = 1e-05
ssd_block = 128
beta_one = 0.9
beta_two = 0.95
adam_eps = 1e-08
weight_decay = 0.1
max_norm = 0.01
rate_byte = 0.06
rate_main = 0.05
rate_small = 0.5


def root_mean_rescale(value_entries, gain_vec):
    return (
        value_entries
        * lax.rsqrt(jnp.mean(value_entries * value_entries, axis=-1, keepdims=True) + norm_eps)
        * gain_vec
    )


def softplus(value_entries):
    return jnp.log1p(jnp.exp(value_entries))


def unpack_small(vector):
    extents = [
        2 * BYTE_WIDTH,
        2 * INNER,
        3 * CORE_WIDTH,
        BYTE_WIDTH,
        CORE_WIDTH - BYTE_WIDTH,
        8 * (INNER + 2 * STATE),
        2 * INNER,
        2 * MHEADS,
        2 * MHEADS,
    ]
    pieces = []
    offset = 0
    for extent in extents:
        pieces.append(vector[offset : offset + extent])
        offset += extent
    return (
        pieces[0].reshape(2, BYTE_WIDTH),
        pieces[1].reshape(2, INNER),
        pieces[2].reshape(3, CORE_WIDTH),
        pieces[3],
        pieces[4],
        pieces[5].reshape(2, 4, INNER + 2 * STATE),
        pieces[6].reshape(2, INNER),
        pieces[7].reshape(2, MHEADS),
        pieces[8].reshape(2, MHEADS),
    )


def ssd_scan(inputs, steps, rates, in_map, out_map):
    blocks = inputs.shape[0] // ssd_block
    cumulative = jnp.cumsum((steps * rates).reshape(blocks, ssd_block, MHEADS), axis=1)
    weighted = (inputs * steps[:, :, None]).reshape(blocks, ssd_block, MHEADS, HEADDIM)
    in_blocks = in_map.reshape(blocks, ssd_block, STATE)
    out_blocks = out_map.reshape(blocks, ssd_block, STATE)
    causal = jnp.tril(jnp.ones((ssd_block, ssd_block), dtype=bool))
    log_gaps = jnp.where(
        causal[None, :, :, None], cumulative[:, :, None, :] - cumulative[:, None, :, :], -jnp.inf
    )
    affinity = jnp.einsum("bin,bjn->bij", out_blocks, in_blocks, precision=deepest_tier)
    within = jnp.einsum(
        "bij,bijh,bjhp->bihp", affinity, jnp.exp(log_gaps), weighted, precision=deepest_tier
    )
    to_end = jnp.exp(cumulative[:, -1:, :] - cumulative)
    states = jnp.einsum("bjn,bjh,bjhp->bhpn", in_blocks, to_end, weighted, precision=deepest_tier)

    def advance(running, scanned):
        total_decay, block_state = scanned
        return (jnp.exp(total_decay)[:, None, None] * running + block_state, running)

    _, starts = lax.scan(
        advance, jnp.zeros((MHEADS, HEADDIM, STATE), jnp.float32), (cumulative[:, -1, :], states)
    )
    across = jnp.einsum(
        "bin,bih,bhpn->bihp", out_blocks, jnp.exp(cumulative), starts, precision=deepest_tier
    )
    return (within + across).reshape(-1, MHEADS * HEADDIM)


def mixer_middle(projected, conv_taps, skip_gain, a_log, dt_bias, gated_gain):
    span_extent_size = projected.shape[0]
    gate_part = projected[:, :INNER]
    streams = projected[:, INNER : 2 * INNER + 2 * STATE]
    raw_steps = projected[:, 2 * INNER + 2 * STATE :]
    padded = jnp.concatenate([jnp.zeros((3, streams.shape[1]), jnp.float32), streams], axis=0)
    convolved = conv_taps[0] * padded[0:span_extent_size]
    for tap_index in range(1, 4):
        convolved = (
            convolved + conv_taps[tap_index] * padded[tap_index : tap_index + span_extent_size]
        )
    active = jax.nn.silu(convolved)
    inputs = active[:, :INNER]
    steps = softplus(raw_steps + dt_bias)
    outcome = ssd_scan(
        inputs.reshape(span_extent_size, MHEADS, HEADDIM),
        steps,
        -jnp.exp(a_log),
        active[:, INNER : INNER + STATE],
        active[:, INNER + STATE :],
    )
    outcome = outcome + inputs * skip_gain
    return root_mean_rescale(outcome * jax.nn.silu(gate_part), gated_gain)


def route_prob(queries, key_rows):
    unit_query = queries * lax.rsqrt(jnp.sum(queries * queries, axis=-1, keepdims=True) + 1e-06)
    unit_key = key_rows * lax.rsqrt(jnp.sum(key_rows * key_rows, axis=-1, keepdims=True) + 1e-06)
    cosine = jnp.sum(unit_query[1:] * unit_key[:-1], axis=-1)
    return jnp.concatenate([jnp.ones((1,), jnp.float32), 0.5 * (1.0 - cosine)])


def span_maps(cut_marks):
    owner_slot = jnp.cumsum(cut_marks) - 1
    position_labels = jnp.arange(MAX_PIECES, dtype=jnp.int32)
    broadcast_back = (owner_slot[:, None] == position_labels[None, :]).astype(jnp.float32)
    select_items = broadcast_back.T * cut_marks[None, :].astype(jnp.float32)
    return (select_items, broadcast_back)


def merge_into_pieces(select_items, value_entries, blank_row):
    spans = jnp.dot(select_items, value_entries, precision=deepest_tier)
    return jnp.concatenate(
        [spans, jnp.broadcast_to(blank_row, (MAX_PIECES, CORE_WIDTH - BYTE_WIDTH))], axis=1
    )


def smooth_spans(piece_output, confidence):

    def update(running, scanned):
        span_row, weight = scanned
        updated = weight * span_row + (1.0 - weight) * running
        return (updated, updated)

    _, smoothed = lax.scan(
        update, jnp.zeros((piece_output.shape[1],), jnp.float32), (piece_output, confidence)
    )
    return smoothed


def link_layers(
    select_items,
    broadcast_back,
    cut_marks,
    latent_holder,
    closing_scale,
    cut_likelihood,
    shortcut_sum,
):
    piece_output = root_mean_rescale(latent_holder, closing_scale)[:, :BYTE_WIDTH]
    smoothed = smooth_spans(
        piece_output, jnp.dot(select_items, cut_likelihood, precision=deepest_tier)
    )
    confidence = jnp.where(cut_marks == 1, cut_likelihood, 1.0 - cut_likelihood)
    return shortcut_sum + confidence[:, None] * jnp.dot(
        broadcast_back, smoothed, precision=deepest_tier
    )


def adam_step(weight, grad, first, second, rate, decay):
    first_new = beta_one * first + (1.0 - beta_one) * grad
    second_new = beta_two * second + (1.0 - beta_two) * grad * grad
    ratio = (
        first_new
        / (1.0 - beta_one**STEP)
        / (jnp.sqrt(second_new / (1.0 - beta_two**STEP)) + adam_eps)
    )
    return (first_new, second_new, weight - rate * (ratio + decay * weight))


def to_low(value_entries):
    return value_entries.astype(jnp.bfloat16)


def matmul_apply(left, right):
    return jnp.dot(left, right, preferred_element_type=jnp.float32)


def product_tn(left, right):
    return lax.dot_general(
        left, right, (((0,), (0,)), ((), ())), preferred_element_type=jnp.float32
    )


def product_nt(left, right):
    return lax.dot_general(
        left, right, (((1,), (1,)), ((), ())), preferred_element_type=jnp.float32
    )


def gather_rows(value_entries):
    return lax.all_gather(value_entries, "tensor", axis=0, tiled=True)


def total_lines(value_entries):
    return lax.psum_scatter(
        value_entries.astype(jnp.bfloat16), "tensor", scatter_dimension=0, tiled=True
    ).astype(jnp.float32)


def gather_grads(value_entries):
    return lax.all_gather(value_entries, "tensor", axis=0, tiled=True)


def sum_grads(value_entries):
    return lax.psum_scatter(
        value_entries.astype(jnp.bfloat16), "tensor", scatter_dimension=0, tiled=True
    ).astype(jnp.float32)


def mixer_forward(value_entries, w_in, exit_matrix, block_gain, smalls):
    rescaled_rows, rescale_grad = jax.vjp(root_mean_rescale, value_entries, block_gain)
    normed_low = to_low(rescaled_rows)
    projected = matmul_apply(normed_low, w_in)
    middle, middle_pull = jax.vjp(mixer_middle, projected, *smalls)
    middle_low = to_low(middle)
    return (
        value_entries + matmul_apply(middle_low, exit_matrix),
        (rescale_grad, normed_low, middle_pull, middle_low),
    )


def mixer_backward(slope_emitted, kept, w_in, exit_matrix):
    rescale_grad, normed_low, middle_pull, middle_low = kept
    grad_low = to_low(slope_emitted)
    slope_exit_matrix = product_tn(middle_low, grad_low)
    pulled = middle_pull(product_nt(grad_low, exit_matrix))
    grad_proj = to_low(pulled[0])
    grad_w_in = product_tn(normed_low, grad_proj)
    grad_values, slope_scale = rescale_grad(product_nt(grad_proj, w_in))
    return (grad_values + slope_emitted, grad_w_in, slope_exit_matrix, slope_scale, pulled[1:])


def causal_scores(queries, key_rows):
    scores = jnp.einsum(
        "gqhd,gkhd->ghqk", queries, key_rows, preferred_element_type=jnp.float32
    ) * HD ** (-0.5)
    causal = jnp.tril(jnp.ones((MAX_PIECES, MAX_PIECES), dtype=bool))
    return jnp.where(causal[None, None], scores, -jnp.inf)


def apply_heads(latent_holder, heed_scale, triple_matrix, exit_matrix):
    rescaled_rows, rescale_grad = jax.vjp(root_mean_rescale, latent_holder, heed_scale)
    rows_low = gather_rows(to_low(rescaled_rows))
    triple = to_low(
        jnp.einsum("td,dsh->tsh", rows_low, triple_matrix, preferred_element_type=jnp.float32)
    )
    groups = rows_low.shape[0] // MAX_PIECES
    heads_here = triple_matrix.shape[2] // HD
    split_heads = triple.reshape(groups, MAX_PIECES, 3, heads_here, HD)
    queries, key_rows, value_rows = (
        split_heads[:, :, 0],
        split_heads[:, :, 1],
        split_heads[:, :, 2],
    )
    scores = causal_scores(queries, key_rows)
    maxima = jnp.max(scores, axis=-1, keepdims=True)
    log_total = maxima + jnp.log(jnp.sum(jnp.exp(scores - maxima), axis=-1, keepdims=True))
    weights_soft = to_low(jnp.exp(scores - log_total))
    heads_output = to_low(
        jnp.einsum("ghqk,gkhd->gqhd", weights_soft, value_rows, preferred_element_type=jnp.float32)
    )
    heads_output = heads_output.reshape(rows_low.shape[0], heads_here * HD)
    outcome = latent_holder + total_lines(matmul_apply(heads_output, exit_matrix))
    return (
        outcome,
        (rescale_grad, rows_low, queries, key_rows, value_rows, log_total, heads_output),
    )


def apply_heads_grad(slope_emitted, kept, triple_matrix, exit_matrix):
    rescale_grad, rows_low, queries, key_rows, value_rows, log_total, heads_output = kept
    grad_rows = gather_grads(to_low(slope_emitted))
    slope_exit_matrix = product_tn(heads_output, grad_rows)
    grad_attended = to_low(product_nt(grad_rows, exit_matrix)).reshape(queries.shape)
    weights_soft = jnp.exp(causal_scores(queries, key_rows) - log_total)
    grad_values = jnp.einsum(
        "ghqk,gqhd->gkhd", to_low(weights_soft), grad_attended, preferred_element_type=jnp.float32
    )
    grad_weights = jnp.einsum(
        "gqhd,gkhd->ghqk", grad_attended, value_rows, preferred_element_type=jnp.float32
    )
    grad_scores = to_low(
        weights_soft * (grad_weights - jnp.sum(weights_soft * grad_weights, axis=-1, keepdims=True))
    )
    grad_queries = jnp.einsum(
        "ghqk,gkhd->gqhd", grad_scores, key_rows, preferred_element_type=jnp.float32
    ) * HD ** (-0.5)
    grad_keys = jnp.einsum(
        "ghqk,gqhd->gkhd", grad_scores, queries, preferred_element_type=jnp.float32
    ) * HD ** (-0.5)
    grad_triple = to_low(
        jnp.stack([grad_queries, grad_keys, grad_values], axis=2).reshape(rows_low.shape[0], 3, -1)
    )
    slope_triple_matrix = jnp.einsum(
        "td,tsh->dsh", rows_low, grad_triple, preferred_element_type=jnp.float32
    )
    slope_rescaled = sum_grads(
        jnp.einsum("tsh,dsh->td", grad_triple, triple_matrix, preferred_element_type=jnp.float32)
    )
    gradient_holder, slope_scale = rescale_grad(slope_rescaled)
    return (gradient_holder + slope_emitted, slope_triple_matrix, slope_exit_matrix, slope_scale)


def swiglu(both):
    return jax.nn.silu(both[:, 0]) * both[:, 1]


def perceptron_apply(latent_holder, perceptron_scale, lift_matrix, lower_matrix):
    rescaled_rows, rescale_grad = jax.vjp(root_mean_rescale, latent_holder, perceptron_scale)
    rows_low = gather_rows(to_low(rescaled_rows))
    latent_state, act_pull = jax.vjp(
        swiglu, jnp.einsum("td,dsf->tsf", rows_low, lift_matrix, preferred_element_type=jnp.float32)
    )
    latent_merged = to_low(latent_state)
    outcome = latent_holder + total_lines(matmul_apply(latent_merged, lower_matrix))
    return (outcome, (rescale_grad, rows_low, act_pull, latent_merged))


def perceptron_grad(slope_emitted, kept, lift_matrix, lower_matrix):
    rescale_grad, rows_low, act_pull, latent_merged = kept
    grad_rows = gather_grads(to_low(slope_emitted))
    slope_lower_matrix = product_tn(latent_merged, grad_rows)
    (grad_both,) = act_pull(product_nt(grad_rows, lower_matrix))
    grad_both = to_low(grad_both)
    slope_lift_matrix = jnp.einsum(
        "td,tsf->dsf", rows_low, grad_both, preferred_element_type=jnp.float32
    )
    slope_rescaled = sum_grads(
        jnp.einsum("tsf,dsf->td", grad_both, lift_matrix, preferred_element_type=jnp.float32)
    )
    gradient_holder, slope_scale = rescale_grad(slope_rescaled)
    return (gradient_holder + slope_emitted, slope_lift_matrix, slope_lower_matrix, slope_scale)


def body(
    byte_ids,
    targets,
    boundaries,
    lengths,
    tables,
    tables_first,
    tables_second,
    mamba_in,
    mamba_in_first,
    mamba_in_second,
    mamba_out,
    mamba_out_first,
    mamba_out_second,
    route_proj,
    route_proj_first,
    route_proj_second,
    small_params,
    small_params_first,
    small_params_second,
    heed_triple_matrix,
    attn_qkv_first,
    attn_qkv_second,
    heed_exit_matrix,
    attn_out_first,
    attn_out_second,
    lifting_matrix,
    mlp_gate_up_first,
    mlp_gate_up_second,
    lowering_matrix,
    mlp_down_first,
    mlp_down_second,
):
    full_tables, full_in, full_out, full_route, full_small = (
        lax.all_gather(to_low(tables), ("dp", "tensor"), axis=1, tiled=True),
        lax.all_gather(to_low(mamba_in), ("dp", "tensor"), axis=1, tiled=True),
        lax.all_gather(to_low(mamba_out), ("dp", "tensor"), axis=1, tiled=True),
        lax.all_gather(to_low(route_proj), ("dp", "tensor"), axis=0, tiled=True),
        lax.all_gather(to_low(small_params), ("dp", "tensor"), axis=0, tiled=True),
    )
    triple_whole, heed_exit_whole, lift_matrix_whole, lower_matrix_whole = (
        lax.all_gather(to_low(heed_triple_matrix), "dp", axis=0, tiled=True),
        lax.all_gather(to_low(heed_exit_matrix), "dp", axis=1, tiled=True),
        lax.all_gather(to_low(lifting_matrix), "dp", axis=0, tiled=True),
        lax.all_gather(to_low(lowering_matrix), "dp", axis=1, tiled=True),
    )
    byte_count = lax.psum(jnp.sum(lengths.astype(jnp.float32)), ("dp", "tensor"))
    (
        block_gains,
        gated_gains,
        core_scales,
        head_gain,
        blank_row,
        conv_taps,
        skip_gains,
        a_logs,
        dt_biases,
    ) = unpack_small(full_small.astype(jnp.float32))
    layer_smalls = [
        (
            conv_taps[layer_index],
            skip_gains[layer_index],
            a_logs[layer_index],
            dt_biases[layer_index],
            gated_gains[layer_index],
        )
        for layer_index in range(2)
    ]
    cut_marks = boundaries[0]
    seq_len = byte_ids.shape[1]
    vocab_ids = jnp.arange(VOCAB, dtype=jnp.int32)
    onehot_in = (byte_ids[0][:, None] == vocab_ids[None, :]).astype(jnp.bfloat16)
    embedded = matmul_apply(onehot_in, full_tables[0])
    packer_output, kept_enc = mixer_forward(
        embedded, full_in[0], full_out[0], block_gains[0], layer_smalls[0]
    )
    encoded_low = to_low(packer_output)
    directed_rows = matmul_apply(encoded_low, full_route)
    cut_likelihood, prob_pull = jax.vjp(
        route_prob, directed_rows[:, :BYTE_WIDTH], directed_rows[:, BYTE_WIDTH : 2 * BYTE_WIDTH]
    )
    select_items, broadcast_back = span_maps(cut_marks)
    latent_holder, merge_transpose = jax.vjp(
        partial(merge_into_pieces, select_items), packer_output, blank_row
    )
    latent_holder, saved_heeding = apply_heads(
        latent_holder, core_scales[0], triple_whole, heed_exit_whole
    )
    latent_holder, saved_perceptron = perceptron_apply(
        latent_holder, core_scales[1], lift_matrix_whole, lower_matrix_whole
    )
    unpacked_bytes, link_layers_grad = jax.vjp(
        partial(link_layers, select_items, broadcast_back, cut_marks),
        latent_holder,
        core_scales[2],
        cut_likelihood,
        directed_rows[:, 2 * BYTE_WIDTH :],
    )
    final_out, kept_dec = mixer_forward(
        unpacked_bytes, full_in[1], full_out[1], block_gains[1], layer_smalls[1]
    )
    head_in, head_pull = jax.vjp(root_mean_rescale, final_out, head_gain)
    head_low = to_low(head_in)
    logits = product_nt(head_low, full_tables[1])
    maxima = jnp.max(logits, axis=-1, keepdims=True)
    log_total = maxima + jnp.log(jnp.sum(jnp.exp(logits - maxima), axis=-1, keepdims=True))
    onehot_out = (targets[0][:, None] == vocab_ids[None, :]).astype(jnp.float32)
    counted = (jnp.arange(seq_len, dtype=jnp.int32) < lengths[0]).astype(jnp.float32)[:, None]
    loss_local = jnp.sum((log_total - logits) * onehot_out * counted)
    grad_logits = to_low((jnp.exp(logits - log_total) - onehot_out) * counted / byte_count)
    grad_table_out = product_tn(grad_logits, head_low)
    grad_final, grad_head_gain = head_pull(matmul_apply(grad_logits, full_tables[1]))
    slope_unpacked, grad_in_dec, grad_out_dec, grad_block_dec, grad_small_dec = mixer_backward(
        grad_final, kept_dec, full_in[1], full_out[1]
    )
    gradient_holder, slope_closing_scale, slope_likelihood, slope_shortcut = link_layers_grad(
        slope_unpacked
    )
    gradient_holder, slope_lifting, slope_lowering, slope_perceptron_scale = perceptron_grad(
        gradient_holder, saved_perceptron, lift_matrix_whole, lower_matrix_whole
    )
    gradient_holder, slope_triple, slope_heed_exit, slope_heed_scale = apply_heads_grad(
        gradient_holder, saved_heeding, triple_whole, heed_exit_whole
    )
    gradient_merged, gradient_blank = merge_transpose(gradient_holder)
    grad_query, grad_key = prob_pull(slope_likelihood)
    grad_routed = to_low(jnp.concatenate([grad_query, grad_key, slope_shortcut], axis=1))
    grad_route = product_tn(encoded_low, grad_routed)
    grad_embedded, grad_in_enc, grad_out_enc, grad_block_enc, grad_small_enc = mixer_backward(
        gradient_merged + product_nt(grad_routed, full_route), kept_enc, full_in[0], full_out[0]
    )
    grad_table_in = jnp.dot(onehot_in.astype(jnp.float32).T, grad_embedded, precision=deepest_tier)
    grad_small = jnp.concatenate(
        [
            piece.reshape(-1)
            for piece in (
                jnp.stack([grad_block_enc, grad_block_dec]),
                jnp.stack([grad_small_enc[4], grad_small_dec[4]]),
                jnp.stack([slope_heed_scale, slope_perceptron_scale, slope_closing_scale]),
                grad_head_gain,
                gradient_blank,
                jnp.stack([grad_small_enc[0], grad_small_dec[0]]),
                jnp.stack([grad_small_enc[1], grad_small_dec[1]]),
                jnp.stack([grad_small_enc[2], grad_small_dec[2]]),
                jnp.stack([grad_small_enc[3], grad_small_dec[3]]),
            )
        ]
    )
    grad_tables = jnp.stack([grad_table_in, grad_table_out])
    grad_mixer_in = jnp.stack([grad_in_enc, grad_in_dec])
    grad_mixer_out = jnp.stack([grad_out_enc, grad_out_dec])
    reduced_tables, reduced_in, reduced_out, reduced_route, reduced_small = (
        lax.psum_scatter(grad_tables, ("dp", "tensor"), scatter_dimension=1, tiled=True),
        lax.psum_scatter(grad_mixer_in, ("dp", "tensor"), scatter_dimension=1, tiled=True),
        lax.psum_scatter(grad_mixer_out, ("dp", "tensor"), scatter_dimension=1, tiled=True),
        lax.psum_scatter(grad_route, ("dp", "tensor"), scatter_dimension=0, tiled=True),
        lax.psum_scatter(grad_small, ("dp", "tensor"), scatter_dimension=0, tiled=True),
    )
    reduced_qkv, reduced_wo, reduced_gate_up, reduced_down = (
        lax.psum_scatter(
            slope_triple.astype(jnp.bfloat16), "dp", scatter_dimension=0, tiled=True
        ).astype(jnp.float32),
        lax.psum_scatter(
            slope_heed_exit.astype(jnp.bfloat16), "dp", scatter_dimension=1, tiled=True
        ).astype(jnp.float32),
        lax.psum_scatter(
            slope_lifting.astype(jnp.bfloat16), "dp", scatter_dimension=0, tiled=True
        ).astype(jnp.float32),
        lax.psum_scatter(
            slope_lowering.astype(jnp.bfloat16), "dp", scatter_dimension=1, tiled=True
        ).astype(jnp.float32),
    )
    reduced = (
        reduced_tables,
        reduced_in,
        reduced_out,
        reduced_route,
        reduced_small,
        reduced_qkv,
        reduced_wo,
        reduced_gate_up,
        reduced_down,
    )
    squares = sum((jnp.sum(grad * grad) for grad in reduced))
    square_total, loss_sum = lax.psum((squares, loss_local), ("dp", "tensor"))
    grad_norm = jnp.sqrt(square_total)
    clip_factor = jnp.minimum(1.0, max_norm / (grad_norm + 1e-06))
    masters = (
        tables,
        mamba_in,
        mamba_out,
        route_proj,
        small_params,
        heed_triple_matrix,
        heed_exit_matrix,
        lifting_matrix,
        lowering_matrix,
    )
    firsts = (
        tables_first,
        mamba_in_first,
        mamba_out_first,
        route_proj_first,
        small_params_first,
        attn_qkv_first,
        attn_out_first,
        mlp_gate_up_first,
        mlp_down_first,
    )
    seconds = (
        tables_second,
        mamba_in_second,
        mamba_out_second,
        route_proj_second,
        small_params_second,
        attn_qkv_second,
        attn_out_second,
        mlp_gate_up_second,
        mlp_down_second,
    )
    rate_list = (
        rate_byte,
        rate_byte,
        rate_byte,
        rate_byte,
        rate_small,
        rate_main,
        rate_main,
        rate_main,
        rate_main,
    )
    decay_list = (
        weight_decay,
        weight_decay,
        weight_decay,
        weight_decay,
        0.0,
        weight_decay,
        weight_decay,
        weight_decay,
        weight_decay,
    )
    updated = [
        adam_step(
            masters[position],
            clip_factor * reduced[position],
            firsts[position],
            seconds[position],
            rate_list[position],
            decay_list[position],
        )
        for position in range(9)
    ]
    return (loss_sum, byte_count, grad_norm) + tuple(
        (member for triple_out in updated for member in triple_out)
    )


def solution(mesh):
    return jax.shard_map(
        body,
        mesh=mesh,
        in_specs=(
            P(("dp", "tensor"), None),
            P(("dp", "tensor"), None),
            P(("dp", "tensor"), None),
            P(("dp", "tensor")),
            P(None, ("dp", "tensor"), None),
            P(None, ("dp", "tensor"), None),
            P(None, ("dp", "tensor"), None),
            P(None, ("dp", "tensor"), None),
            P(None, ("dp", "tensor"), None),
            P(None, ("dp", "tensor"), None),
            P(None, ("dp", "tensor"), None),
            P(None, ("dp", "tensor"), None),
            P(None, ("dp", "tensor"), None),
            P(("dp", "tensor"), None),
            P(("dp", "tensor"), None),
            P(("dp", "tensor"), None),
            P(("dp", "tensor")),
            P(("dp", "tensor")),
            P(("dp", "tensor")),
            P("dp", None, "tensor"),
            P("dp", None, "tensor"),
            P("dp", None, "tensor"),
            P("tensor", "dp"),
            P("tensor", "dp"),
            P("tensor", "dp"),
            P("dp", None, "tensor"),
            P("dp", None, "tensor"),
            P("dp", None, "tensor"),
            P("tensor", "dp"),
            P("tensor", "dp"),
            P("tensor", "dp"),
        ),
        out_specs=(
            P(),
            P(),
            P(),
            P(None, ("dp", "tensor"), None),
            P(None, ("dp", "tensor"), None),
            P(None, ("dp", "tensor"), None),
            P(None, ("dp", "tensor"), None),
            P(None, ("dp", "tensor"), None),
            P(None, ("dp", "tensor"), None),
            P(None, ("dp", "tensor"), None),
            P(None, ("dp", "tensor"), None),
            P(None, ("dp", "tensor"), None),
            P(("dp", "tensor"), None),
            P(("dp", "tensor"), None),
            P(("dp", "tensor"), None),
            P(("dp", "tensor")),
            P(("dp", "tensor")),
            P(("dp", "tensor")),
            P("dp", None, "tensor"),
            P("dp", None, "tensor"),
            P("dp", None, "tensor"),
            P("tensor", "dp"),
            P("tensor", "dp"),
            P("tensor", "dp"),
            P("dp", None, "tensor"),
            P("dp", None, "tensor"),
            P("dp", None, "tensor"),
            P("tensor", "dp"),
            P("tensor", "dp"),
            P("tensor", "dp"),
        ),
        check_vma=False,
    )
```

profile of v0, /device:TPU:0, one launch (start us, length us, event | category | flops | bytes accessed | tf_op | source)
XLA Modules:
  0.0 4323.2 jit_solution(9680605007730146472)
XLA Ops:
  18.1 117.0 %all-reduce.47.cloned.1.call-done = bf16[34944]{0:T(1024)(128)(2,1)} async-done(((bf16[34944]{0:T(1024)(128)(2,1)}), bf16[34944]{0:T(1024)(128)(2,1)}) %all-reduce.47.cloned.1.call-update) | async-done | bytes 69904
  143.6 50.7 %all-gather.13.cloned.1.call-done = bf16[2,256,1024]{2,1,0:T(8,128)(2,1)} async-done(((bf16[2,8,1024]{2,1,0:T(8,128)(2,1)}), bf16[2,256,1024]{2,1,0:T(8,128)(2,1)}) %all-gather.13.cloned.1.call-update) | async-done | bytes 1048592 | tf_op jit(solution)/shard_map/all_gather | solution.py:394
  195.9 123.0 %all-gather.15.cloned.1.call-done = bf16[2,1024,4384]{2,1,0:T(8,128)(2,1)} async-done(((bf16[2,32,4384]{2,1,0:T(8,128)(2,1)}), bf16[2,1024,4384]{2,1,0:T(8,128)(2,1)}) %all-gather.15.cloned.1.call-update) | async-done | bytes 17956880 | tf_op jit(solution)/shard_map/all_gather | solution.py:395
  318.9 8.0 fusion.25
  327.6 7.4 fusion.37
  362.1 7.0 fusion.96
  372.8 19.7 while.108
  398.4 18.3 fusion.62
  437.5 26.9 all-gather.23.cloned.1.call-done
  464.4 20.2 all-gather.21.cloned.1.call-done
  501.6 26.8 all-gather.25.cloned.1.call-done
  533.5 25.6 reduce-scatter.12.cloned.1.call-done
  564.0 97.2 %all-gather.29.cloned.1.call-done = bf16[1536,2,1024]{2,0,1:T(8,128)(2,1)} async-done(((bf16[192,2,1024]{2,0,1:T(8,128)(2,1)}), bf16[1536,2,1024]{2,0,1:T(8,128)(2,1)}) %all-gather.29.cloned.1.call-update) | async-done | bytes 6291472 | tf_op jit(solution)/shard_map/all_gather | solution.py:403
  661.3 19.9 all-gather.27.cloned.1.call-done
  689.8 54.9 %all-gather.31.cloned.1.call-done = bf16[1024,1536]{0,1:T(8,128)(2,1)} async-done(((bf16[1024,192]{0,1:T(8,128)(2,1)}), bf16[1024,1536]{0,1:T(8,128)(2,1)}) %all-gather.31.cloned.1.call-update) | async-done | bytes 3145744 | tf_op jit(solution)/shard_map/all_gather | solution.py:404
  750.3 40.5 psum.22
  791.4 25.4 all-gather.19.cloned.1.call-done
  816.9 6.2 fusion.239
  828.0 18.8 reduce-scatter.14.cloned.1.call-done
  851.2 448.7 %while.109 = (s32[]{:T(128)}, f32[1024]{0:T(1024)S(1)}, f32[128,1024]{1,0:T(8,128)S(1)}, f32[128,1024]{1,0:T(8,128)}, f32[128]{0:T(128)S(1)}, /*index=5*/f32[128...) while((s32[]{:T(128)}, f32[1024]{0:T(1024)S(1)}, ...), condition=%wide.region_18.19_spmd.clone, body=%wide.region_17.18_spmd.clone.sunk | while | flops 4100 | bytes 41127 | solution.py:159
  1304.4 8.8 fusion.27
  1314.1 7.3 fusion.36
  1335.1 7.3 fusion.92
  1344.9 10.2 while.110
  1362.8 19.6 fusion.60
  1399.9 8.5 multiply_reduce_fusion.14
  1408.4 7.6 multiply_reduce_fusion.12
  1431.8 19.4 fusion.29
  1451.2 7.6 fusion.186
  1461.9 21.9 while.111
  1483.8 8.2 multiply_reduce_fusion.11
  1492.0 7.8 fusion.195
  1499.8 9.7 bitcast_add_fusion.7
  1537.4 9.5 multiply_reduce_fusion.4
  1555.9 13.5 multiply_reduce_fusion.21
  1576.2 1017.5 %while.112 = (s32[]{:T(128)}, f32[1024]{0:T(1024)}, f32[128,1024]{1,0:T(8,128)S(1)}, f32[128]{0:T(128)S(1)}, f32[128]{0:T(128)}, /*index=5*/f32[128,1024]{1,0:T(...) while((s32[]{:T(128)}, f32[1024]{0:T(1024)}, ...), condition=%wide.region_44.45_spmd.clone, body=%wide.region_41.44_spmd.clone.sunk | while | flops 8196 | bytes 65759 | solution.py:159
  2595.7 19.8 all-gather.33.cloned.1.call-done
  2623.5 7.3 fusion.111
  2631.1 28.1 reduce-scatter.16.cloned.1.call-done
  2663.6 19.8 all-gather.35.cloned.1.call-done
  2731.6 6.7 multiply_reduce_fusion.15
  2738.3 7.4 multiply_reduce_fusion.13
  2761.3 19.3 fusion.31
  2780.5 7.6 fusion.189
  2790.7 17.0 while.113
  2807.7 8.0 multiply_reduce_fusion.10
  2815.8 7.8 fusion.192
  2823.6 9.9 bitcast_add_fusion.6
  2859.2 9.9 multiply_reduce_fusion.8
  2878.9 12.8 multiply_reduce_fusion.22
  2898.6 8.8 convolution_convert_fusion
  2916.5 10.5 fusion.178
  2927.9 15.4 convolution_bitcast_fusion
  2943.3 13.5 convolution_bitcast_fusion.1
  2956.8 27.6 pad_maximum_fusion
  2984.4 53.0 %copy.409 = f32[2,1024,4384]{2,0,1:T(2,128)} copy(f32[2,1024,4384]{1,2,0:T(8,128)} %pad_maximum_fusion) | data formatting | bytes 71827456 | tf_op jit(solution)/shard_map/stack | solution.py:509
  3046.2 6.6 pad_maximum_fusion.1
  3058.4 39.6 reduce-scatter.26.cloned.1.call-done
  3099.8 119.3 %reduce-scatter.30.cloned.1.call-done = bf16[192,2,1024]{2,0,1:T(8,128)(2,1)} async-done(((bf16[1536,2,1024]{2,0,1:T(8,128)(2,1)}), bf16[192,2,1024]{2,0,1:T(8,128)(2,1)}) %reduce-scatter.30.cloned.1.call-update) | async-done | bytes 786448 | tf_op jit(solution)/shard_map/reduce_scatter | solution.py:525
  3221.3 136.0 %reduce-scatter.20.cloned.1.call-done = f32[2,8,1024]{2,1,0:T(8,128)} async-done(((f32[2,256,1024]{2,1,0:T(8,128)}), f32[2,8,1024]{2,1,0:T(8,128)}) %reduce-scatter.20.cloned.1.call-update) | async-done | bytes 65552 | tf_op jit(solution)/shard_map/reduce_scatter | solution.py:512
  3358.8 156.7 %reduce-scatter.24.cloned.1.call-done = f32[32,3072]{1,0:T(8,128)} async-done(((f32[1024,3072]{1,0:T(8,128)}), f32[32,3072]{1,0:T(8,128)}) %reduce-scatter.24.cloned.1.call-update) | async-done | bytes 393232 | tf_op jit(solution)/shard_map/reduce_scatter | solution.py:515
  3517.2 540.3 %all-reduce.49.cloned.1.call-done = f32[2,1024,4384]{2,0,1:T(2,128)} async-done(((f32[2,1024,4384]{2,0,1:T(2,128)}), f32[2,1024,4384]{2,0,1:T(2,128)}) %all-reduce.49.cloned.1.call-update) | async-done | bytes 35913744
  4061.8 180.7 %reduce-scatter.22.cloned.1.call-done = f32[2,64,1024]{2,1,0:T(8,128)} async-done(((f32[2,2048,1024]{2,1,0:T(8,128)}), f32[2,64,1024]{2,1,0:T(8,128)}) %reduce-scatter.22.cloned.1.call-update) | async-done | bytes 524304 | tf_op jit(solution)/shard_map/reduce_scatter | solution.py:514
  4248.9 41.7 all-reduce.42
  (2866 shorter events, 1697.8 us)
Async XLA Ops:
  7.2 187.0 %copy-start.246 = (s32[1,512]{1,0:T(1,128)S(1)}, s32[1,512]{1,0:T(1,128)}, u32[]{:S(2)}) copy-start(s32[1,512]{1,0:T(1,128)} %param.43) | copy-start | bytes 6148
  7.2 127.9 %all-reduce.47.cloned.1.call-start = ((), (), s32[]{:S(2)}) async-start(), calls=%async_computation.34 | async-start | bytes 143360
  9.0 185.2 %all-gather.13.cloned.1.call-start = ((), (), s32[]{:S(2)}) async-start(), calls=%async_computation.11 | async-start | bytes 1081344 | tf_op jit(solution)/shard_map/all_gather | solution.py:394
  10.6 308.4 %all-gather.15.cloned.1.call-start = ((), (), s32[]{:S(2)}) async-start(), calls=%async_computation.12 | async-start | bytes 18923520 | tf_op jit(solution)/shard_map/all_gather | solution.py:395
  12.8 413.6 %all-gather.17.cloned.1.call-start = ((), (), s32[]{:S(2)}) async-start(), calls=%async_computation.13 | async-start | bytes 8650752 | tf_op jit(solution)/shard_map/all_gather | solution.py:396
  14.6 449.8 %all-gather.23.cloned.1.call-start = ((), (), s32[]{:S(2)}) async-start(), calls=%async_computation.16 | async-start | bytes 3981312 | tf_op jit(solution)/shard_map/all_gather | solution.py:401
  15.5 469.1 %all-gather.21.cloned.1.call-start = ((), (), s32[]{:S(2)}) async-start(), calls=%async_computation.15 | async-start | bytes 1966080 | tf_op jit(solution)/shard_map/all_gather | solution.py:216
  15.6 120.2 %copy-start.150 = (pred[128,128]{0,1:T(8,128)(4,1)}, pred[128,128]{0,1:T(8,128)(4,1)S(1)}, u32[]{:S(2)}) copy-start(pred[128,128]{0,1:T(8,128)(4,1)S(1)} %iota_compare_fusion.12) | copy-start | bytes 49156
  135.8 712.3 %copy-start.102 = (f32[1536]{0:T(1024)}, f32[1536]{0:T(1024)S(1)}, u32[]{:S(2)}) copy-start(f32[1536]{0:T(1024)S(1)} %pad.175.clone) | copy-start | bytes 18436
  137.1 189.8 %copy-start.236 = (f32[1024]{0:T(1024)}, f32[1024]{0:T(1024)S(1)}, u32[]{:S(2)}) copy-start(f32[1024]{0:T(1024)S(1)} %get-tuple-element.1179) | copy-start | bytes 12292
  138.0 56.3 %copy-start.149 = (f32[34944]{0:T(1024)}, f32[34944]{0:T(1024)S(1)}, u32[]{:S(2)}) copy-start(f32[34944]{0:T(1024)S(1)} %convert_element_type.172) | copy-start | bytes 419332
  139.5 188.0 %copy-start.163 = (f32[2304]{0:T(1024)}, f32[2304]{0:T(1024)S(1)}, u32[]{:S(2)}) copy-start(f32[2304]{0:T(1024)S(1)} %get-tuple-element.1190) | copy-start | bytes 27652
  139.5 188.0 %copy-start.165 = (f32[2304]{0:T(1024)}, f32[2304]{0:T(1024)S(1)}, u32[]{:S(2)}) copy-start(f32[2304]{0:T(1024)S(1)} %get-tuple-element.1191) | copy-start | bytes 27652
  139.5 188.0 %copy-start.167 = (f32[2304]{0:T(1024)}, f32[2304]{0:T(1024)S(1)}, u32[]{:S(2)}) copy-start(f32[2304]{0:T(1024)S(1)} %get-tuple-element.1192) | copy-start | bytes 27652
  139.5 188.0 %copy-start.169 = (f32[2304]{0:T(1024)}, f32[2304]{0:T(1024)S(1)}, u32[]{:S(2)}) copy-start(f32[2304]{0:T(1024)S(1)} %get-tuple-element.1193) | copy-start | bytes 27652
  140.9 286.0 %copy-start.132 = (f32[2048]{0:T(1024)}, f32[2048]{0:T(1024)S(1)}, u32[]{:S(2)}) copy-start(f32[2048]{0:T(1024)S(1)} %get-tuple-element.1182) | copy-start | bytes 24580
  143.6 195.8 %copy-start.267 = (f32[32]{0:T(128)}, f32[32]{0:T(128)S(1)}, u32[]{:S(2)}) copy-start(f32[32]{0:T(128)S(1)} %get-tuple-element.1172) | copy-start | bytes 388
  143.6 195.8 %copy-start.268 = (f32[32]{0:T(128)}, f32[32]{0:T(128)S(1)}, u32[]{:S(2)}) copy-start(f32[32]{0:T(128)S(1)} %get-tuple-element.1220) | copy-start | bytes 388
  195.9 131.1 %copy-start.222 = (f32[512]{0:T(512)}, f32[512]{0:T(512)S(1)}, u32[]{:S(2)}) copy-start(f32[512]{0:T(512)S(1)} %get-tuple-element.1200) | copy-start | bytes 6148
  195.9 231.0 %copy-start.33 = (f32[512,1024]{1,0:T(8,128)}, f32[512,1024]{1,0:T(8,128)S(1)}, u32[]{:S(2)}) copy-start(f32[512,1024]{1,0:T(8,128)S(1)} %get-tuple-element.1201) | copy-start | bytes 6291460
  195.9 131.1 %copy-start.253 = (f32[512]{0:T(512)}, f32[512]{0:T(512)S(1)}, u32[]{:S(2)}) copy-start(f32[512]{0:T(512)S(1)} %fusion.294) | copy-start | bytes 6148
  353.2 45.2 %copy-start.104 = (f32[4,128,32]{1,2,0:T(8,128)}, f32[4,128,32]{1,2,0:T(8,128)S(1)}, u32[]{:S(2)}) copy-start(f32[4,128,32]{1,2,0:T(8,128)S(1)} %copy_bitcast_fusion.1) | copy-start | bytes 196612
  359.7 38.7 copy-start.120
  435.6 412.5 %copy-start.2 = (f32[128,1024]{1,0:T(8,128)}, f32[128,1024]{1,0:T(8,128)S(1)}, u32[]{:S(2)}) copy-start(f32[128,1024]{1,0:T(8,128)S(1)} %fusion.244) | copy-start | bytes 1572868
  435.7 54.5 %copy-start.282 = (f32[128]{0:T(128)}, f32[128]{0:T(128)S(1)}, u32[]{:S(2)}) copy-start(f32[128]{0:T(128)S(1)} %fusion.230) | copy-start | bytes 1540
  435.8 54.5 %copy-start.265 = (f32[128]{0:T(128)}, f32[128]{0:T(128)S(1)}, u32[]{:S(2)}) copy-start(f32[128]{0:T(128)S(1)} %fusion.300) | copy-start | bytes 1540
  436.7 91.7 %all-gather.25.cloned.1.call-start = ((), (), s32[]{:S(2)}) async-start(), calls=%async_computation.17 | async-start | bytes 1327104 | tf_op jit(solution)/shard_map/all_gather | solution.py:402
  437.5 121.7 %reduce-scatter.12.cloned.1.call-start = ((), (), s32[]{:S(2)}) async-start(), calls=%async_computation.18 | async-start | bytes 1966080 | tf_op jit(solution)/shard_map/reduce_scatter | solution.py:220
  532.1 129.2 %all-gather.29.cloned.1.call-start = ((), (), s32[]{:S(2)}) async-start(), calls=%async_computation.20 | async-start | bytes 7077888 | tf_op jit(solution)/shard_map/all_gather | solution.py:403
  533.5 147.7 %all-gather.27.cloned.1.call-start = ((), (), s32[]{:S(2)}) async-start(), calls=%async_computation.19 | async-start | bytes 1966080 | tf_op jit(solution)/shard_map/all_gather | solution.py:216
  560.4 120.8 %copy-start.284 = (f32[128]{0:T(128)}, f32[128]{0:T(128)S(1)}, u32[]{:S(2)}) copy-start(f32[128]{0:T(128)S(1)} %multiply_reduce_fusion.38) | copy-start | bytes 1540
  560.4 120.8 %copy-start.263 = (f32[128]{0:T(128)}, f32[128]{0:T(128)S(1)}, u32[]{:S(2)}) copy-start(f32[128]{0:T(128)S(1)} %fusion.301) | copy-start | bytes 1540
  562.3 182.4 %all-gather.31.cloned.1.call-start = ((), (), s32[]{:S(2)}) async-start(), calls=%async_computation.21 | async-start | bytes 3538944 | tf_op jit(solution)/shard_map/all_gather | solution.py:404
  563.2 253.6 %all-gather.19.cloned.1.call-start = ((), (), s32[]{:S(2)}) async-start(), calls=%async_computation.14 | async-start | bytes 6488064 | tf_op jit(solution)/shard_map/all_gather | solution.py:397
  564.0 282.9 %reduce-scatter.14.cloned.1.call-start = ((), (), s32[]{:S(2)}) async-start(), calls=%async_computation.22 | async-start | bytes 1966080 | tf_op jit(solution)/shard_map/reduce_scatter | solution.py:220
  689.8 59.8 %copy-start.112 = (bf16[512,1024]{1,0:T(8,128)(2,1)}, bf16[512,1024]{1,0:T(8,128)(2,1)S(1)}, u32[]{:S(2)}) copy-start(bf16[512,1024]{1,0:T(8,128)(2,1)S(1)} %multiply_convert_fusion.4) | copy-start | bytes 3145732
  689.8 101.6 %copy-start.231 = (s32[1,512]{1,0:T(1,128)S(1)}, s32[1,512]{1,0:T(1,128)}, u32[]{:S(2)}) copy-start(s32[1,512]{1,0:T(1,128)} %param.45) | copy-start | bytes 6148
  749.6 1865.9 %all-gather.33.cloned.1.call-start = ((), (), s32[]{:S(2)}) async-start(), calls=%async_computation.23 | async-start | bytes 1966080 | tf_op jit(solution)/shard_map/all_gather | solution.py:226
  791.4 36.2 copy-start.273
  827.7 476.6 %copy-start.213 = (f32[512]{0:T(512)}, f32[512]{0:T(512)S(1)}, u32[]{:S(2)}) copy-start(f32[512]{0:T(512)S(1)} %get-tuple-element.1198) | copy-start | bytes 6148
  850.3 454.1 %copy-start.238 = (f32[1024]{0:T(1024)S(1)}, f32[1024]{0:T(1024)}, u32[]{:S(2)}) copy-start(f32[1024]{0:T(1024)} %get-tuple-element.1177) | copy-start | bytes 12292
  1569.4 1024.3 %copy-start.31 = (bf16[128,1536]{1,0:T(8,128)(2,1)S(1)}, bf16[128,1536]{1,0:T(8,128)(2,1)}, u32[]{:S(2)}) copy-start(bf16[128,1536]{1,0:T(8,128)(2,1)} %reduce-scatter.12.cloned.1.call-done) | copy-start | bytes 1179652
  1569.4 1024.3 %copy-start.44 = (bf16[128,1536]{1,0:T(8,128)(2,1)S(1)}, bf16[128,1536]{1,0:T(8,128)(2,1)}, u32[]{:S(2)}) copy-start(bf16[128,1536]{1,0:T(8,128)(2,1)} %reduce-scatter.14.cloned.1.call-done) | copy-start | bytes 1179652
  1569.4 1024.2 %copy-start.103 = (f32[1536]{0:T(1024)S(1)}, f32[1536]{0:T(1024)}, u32[]{:S(2)}) copy-start(f32[1536]{0:T(1024)} %copy-done.102) | copy-start | bytes 18436
  1569.5 1024.2 %copy-start.155 = (f32[1536]{0:T(1024)S(1)}, f32[1536]{0:T(1024)}, u32[]{:S(2)}) copy-start(f32[1536]{0:T(1024)} %get-tuple-element.1173) | copy-start | bytes 18436
  1573.7 1020.0 %copy-start.3 = (f32[128,1024]{1,0:T(8,128)S(1)}, f32[128,1024]{1,0:T(8,128)}, u32[]{:S(2)}) copy-start(f32[128,1024]{1,0:T(8,128)} %copy-done.2) | copy-start | bytes 1572868
  1573.7 1020.0 %copy-start.53 = (f32[128,1536]{1,0:T(8,128)S(1)}, f32[128,1536]{1,0:T(8,128)}, u32[]{:S(2)}) copy-start(f32[128,1536]{1,0:T(8,128)} %copy-done.52) | copy-start | bytes 2359300
  1573.7 1020.9 %copy-start.287 = (f32[128]{0:T(128)S(1)}, f32[128]{0:T(128)}, u32[]{:S(2)}) copy-start(f32[128]{0:T(128)} %copy-done.286) | copy-start | bytes 1540
  1573.7 1020.9 %copy-start.276 = (f32[128]{0:T(128)S(1)}, f32[128]{0:T(128)}, u32[]{:S(2)}) copy-start(f32[128]{0:T(128)} %copy-done.275) | copy-start | bytes 1540
  2595.7 63.5 %reduce-scatter.16.cloned.1.call-start = ((), (), s32[]{:S(2)}) async-start(), calls=%async_computation.24 | async-start | bytes 1966080 | tf_op jit(solution)/shard_map/reduce_scatter | solution.py:230
  2623.5 37.6 copy-start.285
  2630.8 52.6 %all-gather.35.cloned.1.call-start = ((), (), s32[]{:S(2)}) async-start(), calls=%async_computation.25 | async-start | bytes 1966080 | tf_op jit(solution)/shard_map/all_gather | solution.py:226
  2663.6 61.6 %reduce-scatter.18.cloned.1.call-start = ((), (), s32[]{:S(2)}) async-start(), calls=%async_computation.26 | async-start | bytes 1966080 | tf_op jit(solution)/shard_map/reduce_scatter | solution.py:230
  2696.9 356.7 %reduce-scatter.32.cloned.1.call-start = ((), (), s32[]{:S(2)}) async-start(), calls=%async_computation.33 | async-start | bytes 3538944 | tf_op jit(solution)/shard_map/reduce_scatter | solution.py:528
  2702.0 353.4 %reduce-scatter.28.cloned.1.call-start = ((), (), s32[]{:S(2)}) async-start(), calls=%async_computation.31 | async-start | bytes 1327104 | tf_op jit(solution)/shard_map/reduce_scatter | solution.py:522
  2720.5 336.5 %all-reduce.51.cloned.1.call-start = ((), (), s32[]{:S(2)}) async-start(), calls=%async_computation.36 | async-start | bytes 286720
  2892.7 205.3 %reduce-scatter.26.cloned.1.call-start = ((), (), s32[]{:S(2)}) async-start(), calls=%async_computation.30 | async-start | bytes 3981312 | tf_op jit(solution)/shard_map/reduce_scatter | solution.py:519
  2898.5 320.6 %reduce-scatter.30.cloned.1.call-start = ((), (), s32[]{:S(2)}) async-start(), calls=%async_computation.32 | async-start | bytes 7077888 | tf_op jit(solution)/shard_map/reduce_scatter | solution.py:525
  2907.5 449.8 %reduce-scatter.20.cloned.1.call-start = ((), (), s32[]{:S(2)}) async-start(), calls=%async_computation.27 | async-start | bytes 2162688 | tf_op jit(solution)/shard_map/reduce_scatter | solution.py:512
  2916.5 599.0 %reduce-scatter.24.cloned.1.call-start = ((), (), s32[]{:S(2)}) async-start(), calls=%async_computation.29 | async-start | bytes 12976128 | tf_op jit(solution)/shard_map/reduce_scatter | solution.py:515
  2927.1 1130.4 %all-reduce.49.cloned.1.call-start = ((), (), s32[]{:S(2)}) async-start(), calls=%async_computation.35 | async-start | bytes 73400320
  3037.4 1205.2 %reduce-scatter.22.cloned.1.call-start = ((), (), s32[]{:S(2)}) async-start(), calls=%async_computation.28 | async-start | bytes 17301504 | tf_op jit(solution)/shard_map/reduce_scatter | solution.py:514
  3052.8 1238.5 %copy-start.51 = (f32[192,2,1024]{2,1,0:T(2,128)S(1)}, f32[192,2,1024]{2,1,0:T(2,128)}, u32[]{:S(2)}) copy-start(f32[192,2,1024]{2,1,0:T(2,128)} %param.68) | copy-start | bytes 4718596
  3219.1 1072.3 %copy-start.78 = (bf16[192,2,1024]{2,0,1:T(8,128)(2,1)S(1)}, bf16[192,2,1024]{2,0,1:T(8,128)(2,1)}, u32[]{:S(2)}) copy-start(bf16[192,2,1024]{2,0,1:T(8,128)(2,1)} %reduce-scatter.30.cloned.1.call-done) | copy-start | bytes 2359300
  (283 other events, 2339.7 us)
Sparse Core Ops, SparseCore 0:
  14.2 120.8 all-reduce.46
  138.6 55.5 all-gather.12
  197.7 121.1 all-gather.14
  322.3 75.7 all-gather.16
  400.6 63.7 all-gather.22
  466.4 18.1 all-gather.20
  487.3 41.0 all-gather.24
  532.2 26.9 reduce-scatter.11
  562.2 99.0 all-gather.28
  663.3 17.8 all-gather.26
  684.2 60.4 all-gather.30
  748.4 68.4 all-gather.18
  820.1 26.6 reduce-scatter.13
  2595.8 19.6 all-gather.32
  2631.0 28.1 reduce-scatter.15
  2663.7 19.6 all-gather.34
  2697.0 28.1 reduce-scatter.17
  2728.6 74.4 reduce-scatter.31
  2807.1 63.1 reduce-scatter.27
  2892.8 120.4 all-reduce.50
  3016.9 81.0 reduce-scatter.25
  3101.6 117.4 reduce-scatter.29
  3221.3 135.9 reduce-scatter.19
  3364.2 151.2 reduce-scatter.23
  3521.9 535.5 all-reduce.48
  4059.6 182.8 reduce-scatter.21
where the time goes:
time: 4370 us; the launch traced here: 4320 us
  waiting for transfers between devices  1850 us (42%)
  local copies, waits for them, and re-layouts  930 us (21%)
  other arithmetic  772 us (18%)
  matrix products  403 us (9%)
  loops' own time  256 us (6%)
  blocking collectives  82.2 us (2%)
    unnamed x29, waiting for transfers between devices  658 us
    dynamic_slice x640, local copies, waits for them, and re-layouts, smooth_spans(): lax.scan(update, jnp.zeros((piece_output.shape[1],), jnp.float32), (piece...  494 us
    mul x256, other arithmetic, update(): updated = weight * span_row + (1.0 - weight) * running  324 us
    another operation x2, loops' own time, smooth_spans(): lax.scan(update, jnp.zeros((piece_output.shape[1],), jnp.float32), (piece...  256 us
    dynamic_update_slice x640, local copies, waits for them, and re-layouts, smooth_spans(): lax.scan(update, jnp.zeros((piece_output.shape[1],), jnp.float32), (piece...  226 us
    reduce_scatter x1, waiting for transfers between devices, body(): lax.psum_scatter(grad_mixer_out, ('dp', 'tensor'), scatter_dimension=1, t...  181 us
    reduce_sum x128, other arithmetic, update(): updated = weight * span_row + (1.0 - weight) * running  166 us
    reduce_scatter x1, waiting for transfers between devices, body(): lax.psum_scatter(grad_route, ('dp', 'tensor'), scatter_dimension=0, tiled...  157 us
  transfers between devices with their start and end apart: 26, of which 22 were waited for; matrix products, arithmetic and copies ran while one was open for 12% of the time, Pallas kernels for 0%

commit v1 on v0

--- a/solution.py
+++ b/solution.py
@@ -3,6 +3,8 @@
 import jax
 import jax.numpy as jnp
 from jax import lax
+from jax.experimental import pallas as pl
+from jax.experimental.pallas import tpu as pltpu
 from jax.sharding import PartitionSpec as P
 
 BYTE_WIDTH = 1024
@@ -89,13 +91,13 @@
     to_end = jnp.exp(cumulative[:, -1:, :] - cumulative)
     states = jnp.einsum("bjn,bjh,bjhp->bhpn", in_blocks, to_end, weighted, precision=deepest_tier)
 
-    def advance(running, scanned):
-        total_decay, block_state = scanned
-        return (jnp.exp(total_decay)[:, None, None] * running + block_state, running)
-
-    _, starts = lax.scan(
-        advance, jnp.zeros((MHEADS, HEADDIM, STATE), jnp.float32), (cumulative[:, -1, :], states)
-    )
+    running = jnp.zeros((MHEADS, HEADDIM, STATE), jnp.float32)
+    starts = []
+    for block in range(blocks):
+        starts.append(running)
+        if block + 1 < blocks:
+            running = jnp.exp(cumulative[block, -1, :])[:, None, None] * running + states[block]
+    starts = jnp.stack(starts)
     across = jnp.einsum(
         "bin,bih,bhpn->bihp", out_blocks, jnp.exp(cumulative), starts, precision=deepest_tier
     )
@@ -149,17 +151,42 @@
     )
 
 
+def decay_products(confidence):
+    rows = lax.broadcasted_iota(jnp.int32, (MAX_PIECES, MAX_PIECES), 0)
+    columns = lax.broadcasted_iota(jnp.int32, (MAX_PIECES, MAX_PIECES), 1)
+    products = jnp.where(rows > columns, 1.0 - confidence[:, None], 1.0)
+    reach = 1
+    while reach < MAX_PIECES:
+        shifted = jnp.concatenate(
+            [jnp.ones((reach, MAX_PIECES), jnp.float32), products[:-reach]], axis=0
+        )
+        products = products * shifted
+        reach *= 2
+    return jnp.where(rows >= columns, products, 0.0)
+
+
+@jax.custom_vjp
 def smooth_spans(piece_output, confidence):
-
-    def update(running, scanned):
-        span_row, weight = scanned
-        updated = weight * span_row + (1.0 - weight) * running
-        return (updated, updated)
-
-    _, smoothed = lax.scan(
-        update, jnp.zeros((piece_output.shape[1],), jnp.float32), (piece_output, confidence)
-    )
-    return smoothed
+    products = decay_products(confidence)
+    return jnp.dot(products, confidence[:, None] * piece_output, precision=deepest_tier)
+
+
+def smooth_keep(piece_output, confidence):
+    products = decay_products(confidence)
+    smoothed = jnp.dot(products, confidence[:, None] * piece_output, precision=deepest_tier)
+    return smoothed, (piece_output, confidence, products, smoothed)
+
+
+def smooth_pull(kept, slope):
+    piece_output, confidence, products, smoothed = kept
+    spread = lax.dot_general(
+        products, slope, (((0,), (0,)), ((), ())), precision=deepest_tier
+    )
+    before = jnp.concatenate([jnp.zeros((1, smoothed.shape[1]), jnp.float32), smoothed[:-1]], axis=0)
+    return (confidence[:, None] * spread, jnp.sum(spread * (piece_output - before), axis=-1))
+
+
+smooth_spans.defvjp(smooth_keep, smooth_pull)
 
 
 def link_layers(
@@ -212,24 +239,151 @@
     )
 
 
+def swap(value_entries, axis, mask):
+    size = lax.axis_size(axis)
+    return lax.ppermute(value_entries, axis, [(place, place ^ mask) for place in range(size)])
+
+
+def bit_masks(size):
+    masks = []
+    mask = size // 2
+    while mask >= 1:
+        masks.append(mask)
+        mask //= 2
+    return masks
+
+
+def spread_dp(shard):
+    size = lax.axis_size("dp")
+    pieces = [shard] + [swap(shard, "dp", mask) for mask in range(2, size, 2)]
+    group = jnp.stack(pieces)
+    return [(0, 0, group), (1, 0, swap(group, "dp", 1))]
+
+
+def spread_all(shard):
+    groups = spread_dp(shard)
+    for mask in bit_masks(lax.axis_size("tensor")):
+        groups = groups + [
+            (dp_mask, tensor_mask | mask, swap(group, "tensor", mask))
+            for dp_mask, tensor_mask, group in groups
+        ]
+    return groups
+
+
+def place_kernel(marks, over_tensor, *refs):
+    groups, whole, sems = refs[: len(marks)], refs[len(marks)], refs[len(marks) + 1]
+    dp_place = lax.axis_index("dp")
+    tensor_place = lax.axis_index("tensor")
+    copies = []
+    for (dp_mask, tensor_mask), group in zip(marks, groups):
+        for position in range(group.shape[0]):
+            source = dp_place ^ (2 * position + dp_mask)
+            if over_tensor:
+                source = source * lax.axis_size("tensor") + (tensor_place ^ tensor_mask)
+            copies.append(
+                pltpu.make_async_copy(group.at[position], whole.at[source], sems.at[len(copies)])
+            )
+    for copy in copies:
+        copy.start()
+    for copy in copies:
+        copy.wait()
+
+
+def place(groups, over_tensor):
+    marks = [(dp_mask, tensor_mask) for dp_mask, tensor_mask, _ in groups]
+    arrays = [group for _, _, group in groups]
+    count = sum(array.shape[0] for array in arrays)
+    return pl.pallas_call(
+        partial(place_kernel, marks, over_tensor),
+        out_shape=jax.ShapeDtypeStruct((count,) + arrays[0].shape[1:], arrays[0].dtype),
+        in_specs=[pl.BlockSpec(memory_space=pl.ANY)] * len(arrays),
+        out_specs=pl.BlockSpec(memory_space=pl.ANY),
+        scratch_shapes=[pltpu.SemaphoreType.DMA((count,))],
+        cost_estimate=pl.CostEstimate(
+            flops=0, transcendentals=0, bytes_accessed=4 * count * arrays[0][0].size
+        ),
+    )(*arrays)
+
+
+def gather_all(shard):
+    return place(spread_all(shard), True)
+
+
+def gather_dp(shard):
+    return place(spread_dp(shard), False)
+
+
+def take(value_entries, axis, index):
+    return lax.dynamic_index_in_dim(value_entries, index, axis, keepdims=False)
+
+
+def total(addends):
+    result = addends[0].astype(jnp.float32)
+    for addend in addends[1:]:
+        result = result + addend.astype(jnp.float32)
+    return result
+
+
+def reduce_dp(addends):
+    size = lax.axis_size("dp")
+    place_dp = lax.axis_index("dp")
+    split = [a.reshape((size // 2, 2) + a.shape[1:]) for a in addends]
+    low = place_dp % 2
+    sent = to_low(total([take(a, 1, 1 - low) for a in split]))
+    addends = [take(a, 1, low) for a in split] + [swap(sent, "dp", 1)]
+    high = place_dp // 2
+    received = [
+        swap(to_low(total([take(a, 0, high ^ mask) for a in addends])), "dp", 2 * mask)
+        for mask in range(1, size // 2)
+    ]
+    return total([take(a, 0, high) for a in addends] + received)
+
+
+def reduce_all(grad):
+    tensor_size = lax.axis_size("tensor")
+    place_tensor = lax.axis_index("tensor")
+    grad = grad.reshape((lax.axis_size("dp"), tensor_size) + grad.shape[1:])
+    addends = [grad]
+    for mask in reversed(bit_masks(tensor_size)):
+        split = [
+            a.reshape((a.shape[0], a.shape[1] // 2, 2) + a.shape[2:]) for a in addends
+        ]
+        low = (place_tensor // mask) % 2
+        sent = to_low(total([take(a, 2, 1 - low) for a in split]))
+        addends = [take(a, 2, low) for a in split] + [swap(sent, "tensor", mask)]
+    return reduce_dp([a[:, 0] for a in addends])
+
+
+def add_everywhere(value_entries):
+    for axis in ("tensor", "dp"):
+        for mask in bit_masks(lax.axis_size(axis)):
+            value_entries = value_entries + swap(value_entries, axis, mask)
+    return value_entries
+
+
 def gather_rows(value_entries):
-    return lax.all_gather(value_entries, "tensor", axis=0, tiled=True)
+    pieces = [value_entries]
+    for mask in bit_masks(lax.axis_size("tensor")):
+        pieces = pieces + [swap(piece, "tensor", mask) for piece in pieces]
+    return jnp.concatenate(pieces, axis=0)
 
 
 def total_lines(value_entries):
-    return lax.psum_scatter(
-        value_entries.astype(jnp.bfloat16), "tensor", scatter_dimension=0, tiled=True
-    ).astype(jnp.float32)
-
-
-def gather_grads(value_entries):
-    return lax.all_gather(value_entries, "tensor", axis=0, tiled=True)
-
-
-def sum_grads(value_entries):
-    return lax.psum_scatter(
-        value_entries.astype(jnp.bfloat16), "tensor", scatter_dimension=0, tiled=True
-    ).astype(jnp.float32)
+    size = lax.axis_size("tensor")
+    rows = value_entries.shape[0] // size
+    pieces = [to_low(value_entries[i * rows : (i + 1) * rows]) for i in range(size)]
+    for mask in reversed(bit_masks(size)):
+        half = len(pieces) // 2
+        pieces = [
+            pieces[i].astype(jnp.float32)
+            + swap(to_low(pieces[half + i]), "tensor", mask).astype(jnp.float32)
+            for i in range(half)
+        ]
+    return pieces[0]
+
+
+gather_grads = gather_rows
+sum_grads = total_lines
 
 
 def mixer_forward(value_entries, w_in, exit_matrix, block_gain, smalls):
@@ -285,7 +439,7 @@
         jnp.einsum("ghqk,gkhd->gqhd", weights_soft, value_rows, preferred_element_type=jnp.float32)
     )
     heads_output = heads_output.reshape(rows_low.shape[0], heads_here * HD)
-    outcome = latent_holder + total_lines(matmul_apply(heads_output, exit_matrix))
+    outcome = latent_holder + total_lines(product_nt(heads_output, exit_matrix))
     return (
         outcome,
         (rescale_grad, rows_low, queries, key_rows, value_rows, log_total, heads_output),
@@ -295,8 +449,8 @@
 def apply_heads_grad(slope_emitted, kept, triple_matrix, exit_matrix):
     rescale_grad, rows_low, queries, key_rows, value_rows, log_total, heads_output = kept
     grad_rows = gather_grads(to_low(slope_emitted))
-    slope_exit_matrix = product_tn(heads_output, grad_rows)
-    grad_attended = to_low(product_nt(grad_rows, exit_matrix)).reshape(queries.shape)
+    slope_exit_matrix = product_tn(grad_rows, heads_output)
+    grad_attended = to_low(matmul_apply(grad_rows, exit_matrix)).reshape(queries.shape)
     weights_soft = jnp.exp(causal_scores(queries, key_rows) - log_total)
     grad_values = jnp.einsum(
         "ghqk,gqhd->gkhd", to_low(weights_soft), grad_attended, preferred_element_type=jnp.float32
@@ -337,15 +491,15 @@
         swiglu, jnp.einsum("td,dsf->tsf", rows_low, lift_matrix, preferred_element_type=jnp.float32)
     )
     latent_merged = to_low(latent_state)
-    outcome = latent_holder + total_lines(matmul_apply(latent_merged, lower_matrix))
+    outcome = latent_holder + total_lines(product_nt(latent_merged, lower_matrix))
     return (outcome, (rescale_grad, rows_low, act_pull, latent_merged))
 
 
 def perceptron_grad(slope_emitted, kept, lift_matrix, lower_matrix):
     rescale_grad, rows_low, act_pull, latent_merged = kept
     grad_rows = gather_grads(to_low(slope_emitted))
-    slope_lower_matrix = product_tn(latent_merged, grad_rows)
-    (grad_both,) = act_pull(product_nt(grad_rows, lower_matrix))
+    slope_lower_matrix = product_tn(grad_rows, latent_merged)
+    (grad_both,) = act_pull(matmul_apply(grad_rows, lower_matrix))
     grad_both = to_low(grad_both)
     slope_lift_matrix = jnp.einsum(
         "td,tsf->dsf", rows_low, grad_both, preferred_element_type=jnp.float32
@@ -390,20 +544,44 @@
     mlp_down_first,
     mlp_down_second,
 ):
-    full_tables, full_in, full_out, full_route, full_small = (
-        lax.all_gather(to_low(tables), ("dp", "tensor"), axis=1, tiled=True),
-        lax.all_gather(to_low(mamba_in), ("dp", "tensor"), axis=1, tiled=True),
-        lax.all_gather(to_low(mamba_out), ("dp", "tensor"), axis=1, tiled=True),
-        lax.all_gather(to_low(route_proj), ("dp", "tensor"), axis=0, tiled=True),
-        lax.all_gather(to_low(small_params), ("dp", "tensor"), axis=0, tiled=True),
-    )
-    triple_whole, heed_exit_whole, lift_matrix_whole, lower_matrix_whole = (
-        lax.all_gather(to_low(heed_triple_matrix), "dp", axis=0, tiled=True),
-        lax.all_gather(to_low(heed_exit_matrix), "dp", axis=1, tiled=True),
-        lax.all_gather(to_low(lifting_matrix), "dp", axis=0, tiled=True),
-        lax.all_gather(to_low(lowering_matrix), "dp", axis=1, tiled=True),
-    )
-    byte_count = lax.psum(jnp.sum(lengths.astype(jnp.float32)), ("dp", "tensor"))
+    devices = lax.axis_size("dp") * lax.axis_size("tensor")
+    table_rows = tables.shape[1]
+    small_here = small_params.shape[0]
+    mixed_rows = 2 * table_rows + 16
+    length_pair = jnp.stack([lengths[0] // 16, lengths[0] % 16]).astype(jnp.bfloat16)
+    tail = jnp.concatenate([to_low(small_params), length_pair])
+    mixed = jnp.concatenate(
+        [
+            to_low(tables).reshape(2 * table_rows, BYTE_WIDTH),
+            jnp.pad(tail, (0, 16 * BYTE_WIDTH - tail.shape[0])).reshape(16, BYTE_WIDTH),
+        ]
+    )
+    mixed_whole = gather_all(mixed)
+    full_tables = (
+        mixed_whole[:, : 2 * table_rows]
+        .reshape(devices, 2, table_rows, BYTE_WIDTH)
+        .transpose(1, 0, 2, 3)
+        .reshape(2, VOCAB, BYTE_WIDTH)
+    )
+    tails = mixed_whole[:, 2 * table_rows :].reshape(devices, -1)
+    full_small = tails[:, :small_here].reshape(-1)
+    pairs = tails[:, small_here : small_here + 2].astype(jnp.float32)
+    byte_count = jnp.sum(pairs[:, 0] * 16.0 + pairs[:, 1])
+    full_in = [None, None]
+    full_out = [None, None]
+    full_in[0] = gather_all(to_low(mamba_in[0])).reshape(BYTE_WIDTH, -1)
+    full_out[0] = gather_all(to_low(mamba_out[0])).reshape(INNER, BYTE_WIDTH)
+    full_route = gather_all(to_low(route_proj)).reshape(BYTE_WIDTH, -1)
+    triple_whole = gather_dp(to_low(heed_triple_matrix)).reshape(
+        (CORE_WIDTH,) + heed_triple_matrix.shape[1:]
+    )
+    heed_exit_whole = gather_dp(to_low(heed_exit_matrix).T).reshape(CORE_WIDTH, -1)
+    lift_matrix_whole = gather_dp(to_low(lifting_matrix)).reshape(
+        (CORE_WIDTH,) + lifting_matrix.shape[1:]
+    )
+    lower_matrix_whole = gather_dp(to_low(lowering_matrix).T).reshape(CORE_WIDTH, -1)
+    full_in[1] = gather_all(to_low(mamba_in[1])).reshape(BYTE_WIDTH, -1)
+    full_out[1] = gather_all(to_low(mamba_out[1])).reshape(INNER, BYTE_WIDTH)
     (
         block_gains,
         gated_gains,
@@ -505,30 +683,38 @@
             )
         ]
     )
-    grad_tables = jnp.stack([grad_table_in, grad_table_out])
-    grad_mixer_in = jnp.stack([grad_in_enc, grad_in_dec])
-    grad_mixer_out = jnp.stack([grad_out_enc, grad_out_dec])
-    reduced_tables, reduced_in, reduced_out, reduced_route, reduced_small = (
-        lax.psum_scatter(grad_tables, ("dp", "tensor"), scatter_dimension=1, tiled=True),
-        lax.psum_scatter(grad_mixer_in, ("dp", "tensor"), scatter_dimension=1, tiled=True),
-        lax.psum_scatter(grad_mixer_out, ("dp", "tensor"), scatter_dimension=1, tiled=True),
-        lax.psum_scatter(grad_route, ("dp", "tensor"), scatter_dimension=0, tiled=True),
-        lax.psum_scatter(grad_small, ("dp", "tensor"), scatter_dimension=0, tiled=True),
-    )
-    reduced_qkv, reduced_wo, reduced_gate_up, reduced_down = (
-        lax.psum_scatter(
-            slope_triple.astype(jnp.bfloat16), "dp", scatter_dimension=0, tiled=True
-        ).astype(jnp.float32),
-        lax.psum_scatter(
-            slope_heed_exit.astype(jnp.bfloat16), "dp", scatter_dimension=1, tiled=True
-        ).astype(jnp.float32),
-        lax.psum_scatter(
-            slope_lifting.astype(jnp.bfloat16), "dp", scatter_dimension=0, tiled=True
-        ).astype(jnp.float32),
-        lax.psum_scatter(
-            slope_lowering.astype(jnp.bfloat16), "dp", scatter_dimension=1, tiled=True
-        ).astype(jnp.float32),
-    )
+    def by_device(grad):
+        return to_low(grad).reshape((devices, grad.shape[0] // devices) + grad.shape[1:])
+
+    def by_dp(grad):
+        size = lax.axis_size("dp")
+        return to_low(grad).reshape((size, grad.shape[0] // size) + grad.shape[1:])
+
+    reduced_in_dec = reduce_all(by_device(grad_in_dec))
+    reduced_out_dec = reduce_all(by_device(grad_out_dec))
+    reduced_gate_up = reduce_dp([by_dp(slope_lifting)])
+    reduced_down = reduce_dp([by_dp(slope_lowering)]).T
+    reduced_qkv = reduce_dp([by_dp(slope_triple)])
+    reduced_wo = reduce_dp([by_dp(slope_heed_exit)]).T
+    reduced_route = reduce_all(by_device(grad_route))
+    reduced_in_enc = reduce_all(by_device(grad_in_enc))
+    reduced_out_enc = reduce_all(by_device(grad_out_enc))
+    grad_mixed = jnp.concatenate(
+        [
+            to_low(grad_table_in).reshape(devices, table_rows, BYTE_WIDTH),
+            to_low(grad_table_out).reshape(devices, table_rows, BYTE_WIDTH),
+            jnp.pad(
+                to_low(grad_small).reshape(devices, small_here),
+                ((0, 0), (0, 16 * BYTE_WIDTH - small_here)),
+            ).reshape(devices, 16, BYTE_WIDTH),
+        ],
+        axis=1,
+    )
+    reduced_mixed = reduce_all(grad_mixed)
+    reduced_tables = reduced_mixed[: 2 * table_rows].reshape(2, table_rows, BYTE_WIDTH)
+    reduced_small = reduced_mixed[2 * table_rows :].reshape(-1)[:small_here]
+    reduced_in = jnp.stack([reduced_in_enc, reduced_in_dec])
+    reduced_out = jnp.stack([reduced_out_enc, reduced_out_dec])
     reduced = (
         reduced_tables,
         reduced_in,
@@ -541,7 +727,8 @@
         reduced_down,
     )
     squares = sum((jnp.sum(grad * grad) for grad in reduced))
-    square_total, loss_sum = lax.psum((squares, loss_local), ("dp", "tensor"))
+    totals = add_everywhere(jnp.stack([squares, loss_local]).reshape(1, 2))
+    square_total, loss_sum = (totals[0, 0], totals[0, 1])
     grad_norm = jnp.sqrt(square_total)
     clip_factor = jnp.minimum(1.0, max_norm / (grad_norm + 1e-06))
     masters = (

time: 4370 us -> 3070 us (0.70)
  Pallas kernels: 0 us -> 1540 us
  waiting for transfers between devices: 1850 us -> 513 us
  local copies, waits for them, and re-layouts: 930 us -> 196 us
  other arithmetic: 772 us -> 261 us
  loops' own time: 256 us -> 0 us
  starting transfers between devices: 2.04 us -> 190 us
  blocking collectives: 82.2 us -> 0 us
  matrix products: 403 us -> 346 us
    pallas_call x0 -> x10, Pallas kernels: none -> 1540 us  [place(): pl.pallas_call(partial(place_kernel, marks, over_tensor), out_shape=jax.S...]
    reduce_scatter x11 -> x0, waiting for transfers between devices: 710 us -> none  [the longest x1 181 us: body(): lax.psum_scatter(grad_mixer_out, ('dp', 'tensor'), scatter_dimension=1, t...]
    unnamed x29 -> x0, waiting for transfers between devices: 658 us -> none
    ppermute x0 -> x157, waiting for transfers between devices: none -> 513 us  [swap(): lax.ppermute(value_entries, axis, [(place, place ^ mask) for place in ran...]
    all_gather x12 -> x0, waiting for transfers between devices: 485 us -> none  [the longest x1 123 us: body(): lax.all_gather(to_low(mamba_in), ('dp', 'tensor'), axis=1, tiled=True)]
    dynamic_slice x640 -> x9, local copies, waits for them, and re-layouts: 494 us -> 13 us  [take(): return lax.dynamic_index_in_dim(value_entries, index, axis, keepdims=False)]
    mul x265 -> x10, other arithmetic: 329 us -> 1.85 us  [the longest x4 1.34 us: ssd_scan(): jnp.exp(cumulative[block, -1, :])[:, None, None] * running + states[block]]
    another operation x6 -> x0, loops' own time: 256 us -> none  [the longest x2 256 us: smooth_spans(): lax.scan(update, jnp.zeros((piece_output.shape[1],), jnp.float32), (piece...]
  transfers between devices with their start and end apart: 26 -> 157, of which waited for: 22 -> 55; matrix products, arithmetic and copies ran while one was open for 12% -> 16% of each run, Pallas kernels for 0% -> 50%
where the time goes in v1:
time: 3070 us; the launch traced here: 3060 us
  Pallas kernels  1540 us (50%)
  waiting for transfers between devices  513 us (17%)
  matrix products  346 us (11%)
  other arithmetic  261 us (9%)
  local copies, waits for them, and re-layouts  196 us (6%)
  starting transfers between devices  190 us (6%)
    pallas_call x10, Pallas kernels, place(): pl.pallas_call(partial(place_kernel, marks, over_tensor), out_shape=jax.S...  1540 us
    ppermute x157, waiting for transfers between devices, swap(): lax.ppermute(value_entries, axis, [(place, place ^ mask) for place in ran...  513 us
    ppermute x157, starting transfers between devices, swap(): lax.ppermute(value_entries, axis, [(place, place ^ mask) for place in ran...  190 us
    dot_general x6, matrix products, ssd_scan(): jnp.einsum('bij,bijh,bjhp->bihp', affinity, jnp.exp(log_gaps), weighted,...  93.5 us
  transfers between devices with their start and end apart: 157, of which 55 were waited for; matrix products, arithmetic and copies ran while one was open for 16% of the time, Pallas kernels for 50%

profile of v1, /device:TPU:0, one launch (start us, length us, event | category | flops | bytes accessed | tf_op | source)
XLA Modules:
  0.0 3064.3 jit_solution(5221316397209661553)
XLA Ops:
  20.6 8.9 collective-permute-start.78
  41.9 11.8 collective-permute-start.51
  57.6 8.8 collective-permute-done.39
  66.3 14.2 collective-permute-start.11
  87.7 7.6 collective-permute-done.11
  102.6 24.1 collective-permute-done.69
  135.8 18.1 collective-permute-done.62
  155.5 14.7 collective-permute-done.63
  171.3 10.1 collective-permute-done.34
  189.0 11.5 collective-permute-done.5.refs_3_
  200.5 9.7 collective-permute-start.48
  229.6 7.8 collective-permute-done.23.refs_1_
  249.4 15.4 collective-permute-done.49
  273.0 31.2 %collective-permute-done.83.refs_3_ = bf16[4,64,1024]{2,1,0:T(8,128)(2,1)S(1)} collective-permute-done((bf16[4,64,1024]{2,1,0:T(8,128)(2,1)}, bf16[4,64,1024]{2,1,0:T(8,128)(2,1)S(1)}, u32[]{:S(2)}, u32[]{:S(2)}) %collective-permute-start.83) | collective-permute-done | bytes 524320 | tf_op jit(solution)/shard_map/ppermute | solution.py:244
  313.0 36.9 %shard_map.530 = bf16[8,192,384]{2,1,0:T(8,128)(2,1)} custom-call(bf16[4,192,384]{2,1,0:T(8,128)(2,1)} %copy-done.114, bf16[4,192,384]{2,1,0:T(8,128)(2,1)} %collective-permute-done.40.refs_1_), custom_call_target="tpu_custom_call" | custom-call | bytes 2359296 | tf_op jit(solution)/shard_map/pallas_call | solution.py:296
  353.5 8.3 pad_maximum_fusion.6.refs_0_
  361.9 64.9 %shard_map.526 = bf16[32,32,1024]{2,1,0:T(8,128)(2,1)} custom-call(bf16[4,32,1024]{2,1,0:T(8,128)(2,1)} %copy-done.150, bf16[4,32,1024]{2,1,0:T(8,128)(2,1)} %collective-permute-done.3.refs_1_, bf16[4,32,1024]{2,1,0:T(8,128)(2,1)} %copy-done.206, bf16[4,32,1024]{2,1,0:T(8,128)(2,1)} %copy-done.208, bf16[4,32,1024]{2,1,0:T(8,128)(2,1)} %copy-done.205, ...), custom_call_target="tpu_custom_call" | custom-call | bytes 4194304 | tf_op jit(solution)/shard_map/pallas_call | solution.py:296
  436.1 27.6 collective-permute-done.64.refs_1_
  467.3 128.4 %shard_map.535 = bf16[32,64,1024]{2,1,0:T(8,128)(2,1)} custom-call(bf16[4,64,1024]{2,1,0:T(8,128)(2,1)} %copy-done.118, bf16[4,64,1024]{2,1,0:T(8,128)(2,1)} %collective-permute-done.81.refs_1_, bf16[4,64,1024]{2,1,0:T(8,128)(2,1)} %collective-permute-done.82.refs_2_, bf16[4,64,1024]{2,1,0:T(8,128)(2,1)} %copy-done.165, ...), custom_call_target="tpu_custom_call" | custom-call | bytes 8388608 | tf_op jit(solution)/shard_map/pallas_call | solution.py:296
  595.8 128.5 %shard_map.528 = bf16[32,64,1024]{2,1,0:T(8,128)(2,1)} custom-call(bf16[4,64,1024]{2,1,0:T(8,128)(2,1)} %copy-done.119, bf16[4,64,1024]{2,1,0:T(8,128)(2,1)} %collective-permute-done.23.refs_1_, bf16[4,64,1024]{2,1,0:T(8,128)(2,1)} %collective-permute-done.24.refs_2_, bf16[4,64,1024]{2,1,0:T(8,128)(2,1)} %collective-permute-done.25.refs_3_, ...), custom_call_target="tpu_custom_call" | custom-call | bytes 8388608 | tf_op jit(solution)/shard_map/pallas_call | solution.py:296
  724.3 96.5 %shard_map.533 = bf16[8,192,1024]{2,1,0:T(8,128)(2,1)} custom-call(bf16[4,192,1024]{2,1,0:T(8,128)(2,1)} %pad_maximum_fusion.10.refs_0_, bf16[4,192,1024]{2,1,0:T(8,128)(2,1)} %collective-permute-done.64.refs_1_), custom_call_target="tpu_custom_call" | custom-call | bytes 6291456 | tf_op jit(solution)/shard_map/pallas_call | solution.py:296
  825.2 144.1 %shard_map.529 = bf16[8,192,3,384]{3,2,1,0:T(4,128)(2,1)} custom-call(bf16[4,192,3,384]{3,2,1,0:T(4,128)(2,1)} %copy-done.21, bf16[4,192,3,384]{3,2,1,0:T(4,128)(2,1)} %copy.379.refs_1_), custom_call_target="tpu_custom_call" | custom-call | bytes 7077888 | tf_op jit(solution)/shard_map/pallas_call | solution.py:296
  969.3 192.0 %shard_map.532 = bf16[32,32,3072]{2,1,0:T(8,128)(2,1)} custom-call(bf16[4,32,3072]{2,1,0:T(8,128)(2,1)} %copy-done.90, bf16[4,32,3072]{2,1,0:T(8,128)(2,1)} %collective-permute-done.54.refs_1_, bf16[4,32,3072]{2,1,0:T(8,128)(2,1)} %copy-done.156, bf16[4,32,3072]{2,1,0:T(8,128)(2,1)} %collective-permute-done.56.refs_3_, bf16[4,32,3072]{2,1,0:T(8,128)(2,1)} %copy-done.155, ...), custom_call_target="tpu_custom_call" | custom-call | bytes 12582912 | tf_op jit(solution)/shard_map/pallas_call | solution.py:296
  1163.9 279.3 %shard_map.527 = bf16[32,32,4384]{2,1,0:T(8,128)(2,1)} custom-call(bf16[4,32,4384]{2,1,0:T(8,128)(2,1)} %copy-done.49, bf16[4,32,4384]{2,1,0:T(8,128)(2,1)} %collective-permute-done.13.refs_1_, bf16[4,32,4384]{2,1,0:T(8,128)(2,1)} %collective-permute-done.14.refs_2_, bf16[4,32,4384]{2,1,0:T(8,128)(2,1)} %collective-permute-done.15.refs_3_, ...), custom_call_target="tpu_custom_call" | custom-call | bytes 17956864 | tf_op jit(solution)/shard_map/pallas_call | solution.py:296
  1443.2 8.2 fusion.425
  1493.3 17.2 fusion.56
  1527.7 7.4 collective-permute-done.30
  1554.7 279.3 %shard_map.534 = bf16[32,32,4384]{2,1,0:T(8,128)(2,1)} custom-call(bf16[4,32,4384]{2,1,0:T(8,128)(2,1)} %pad_maximum_fusion.20.refs_0_, bf16[4,32,4384]{2,1,0:T(8,128)(2,1)} %collective-permute-done.71.refs_1_, bf16[4,32,4384]{2,1,0:T(8,128)(2,1)} %collective-permute-done.72.refs_2_, bf16[4,32,4384]{2,1,0:T(8,128)(2,1)} %collective-permute-done.73.refs_3_, ...), custom_call_target="tpu_custom_call" | custom-call | bytes 17956864 | tf_op jit(solution)/shard_map/pallas_call | solution.py:296
  1838.7 10.0 collective-permute-done.43
  1850.2 9.5 collective-permute-done.44
  1859.9 191.8 %shard_map.531 = bf16[8,192,2,1024]{3,2,1,0:T(2,128)(2,1)} custom-call(bf16[4,192,2,1024]{3,2,1,0:T(2,128)(2,1)} %pad_maximum_fusion.6.refs_0_, bf16[4,192,2,1024]{3,2,1,0:T(2,128)(2,1)} %collective-permute-done.50.refs_1_), custom_call_target="tpu_custom_call" | custom-call | bytes 12582912 | tf_op jit(solution)/shard_map/pallas_call | solution.py:296
  2063.5 10.7 collective-permute-done.67
  2080.8 8.0 fusion.426
  2134.2 18.2 fusion.54
  2165.1 8.5 multiply_reduce_fusion.12
  2178.0 7.5 multiply_reduce_fusion.10
  2196.5 7.7 fusion.191
  2204.2 19.4 fusion.21
  2230.3 7.8 fusion.200
  2243.0 9.9 bitcast_add_fusion.3
  2284.5 13.3 multiply_reduce_fusion.2
  2306.6 12.7 multiply_reduce_fusion.25
  2319.3 12.0 convolution_convert_fusion
  2344.1 12.0 copy.451
  2425.3 12.0 collective-permute-done.148
  2440.4 14.3 collective-permute-start.149
  2483.1 7.3 collective-permute-done.150
  2566.2 18.9 fusion.23
  2591.3 7.8 fusion.197
  2603.4 9.8 bitcast_add_fusion.2
  2635.2 13.6 multiply_reduce_fusion.6
  2657.1 12.7 multiply_reduce_fusion.21
  2669.9 12.0 convolution_convert_fusion.1
  2683.1 12.3 copy.449
  2732.2 8.9 fusion.174
  2756.2 27.0 collective-permute-done.138
  2793.9 24.7 collective-permute-done.145
  2823.5 30.2 collective-permute-done.146
  2878.8 16.9 collective-permute-done.119
  2898.6 42.4 %collective-permute-done.107 = bf16[8,1,32,4384]{3,2,0,1:T(8,128)(2,1)S(1)} collective-permute-done((bf16[8,1,32,4384]{3,2,0,1:T(8,128)(2,1)S(1)}, bf16[8,1,32,4384]{3,2,0,1:T(8,128)(2,1)S(1)}, u32[]{:S(2)}, u32[]{:S(2)}) %collective-permute-start.107) | collective-permute-done | bytes 2244640 | tf_op jit(solution)/shard_map/ppermute | solution.py:244
  2956.1 13.2 collective-permute-done.114
  2973.3 15.8 collective-permute-done.108
  3004.6 9.0 collective-permute-done.110
  3055.7 7.2 multiply_subtract_fusion
  (1521 shorter events, 760.7 us)
Async XLA Ops:
  36.3 47.7 %collective-permute-start.12 = (bf16[32,4384]{1,0:T(8,128)(2,1)S(1)}, bf16[32,4384]{1,0:T(8,128)(2,1)S(1)}, u32[]{:S(2)}, u32[]{:S(2)}) collective-permute-start(bf16[32,4384]{1,0:T(8,128)(2,1)S(1)} %bitcast.1090), channel_id=1, source_target_pairs={{0,24},{4,28},{8,16},{12,20},{16,8},{20,12},{24,0},{28,4},{1,25},{... | collective-permute-start | bytes 841736 | tf_op jit(solution)/shard_map/ppermute | solution.py:244
  41.9 38.6 %collective-permute-start.52 = (bf16[32,3072]{1,0:T(8,128)(2,1)S(1)}, bf16[32,3072]{1,0:T(8,128)(2,1)S(1)}, u32[]{:S(2)}, u32[]{:S(2)}) collective-permute-start(bf16[32,3072]{1,0:T(8,128)(2,1)S(1)} %convert_element_type.1386), channel_id=1, source_target_pairs={{0,16},{4,20},{8,24},{12,28},{16,0},{20,4},{24,8},{28,12},{1,17},{... | collective-permute-start | bytes 589832 | tf_op jit(solution)/shard_map/ppermute | solution.py:244
  41.9 38.6 %collective-permute-start.51 = (bf16[32,3072]{1,0:T(8,128)(2,1)S(1)}, bf16[32,3072]{1,0:T(8,128)(2,1)S(1)}, u32[]{:S(2)}, u32[]{:S(2)}) collective-permute-start(bf16[32,3072]{1,0:T(8,128)(2,1)S(1)} %convert_element_type.1386), channel_id=1, source_target_pairs={{0,8},{4,12},{8,0},{12,4},{16,24},{20,28},{24,16},{28,20},{1,9},{5... | collective-permute-start | bytes 589832 | tf_op jit(solution)/shard_map/ppermute | solution.py:244
  82.1 44.6 %collective-permute-start.69 = (bf16[32,4384]{1,0:T(8,128)(2,1)S(1)}, bf16[32,4384]{1,0:T(8,128)(2,1)S(1)}, u32[]{:S(2)}, u32[]{:S(2)}) collective-permute-start(bf16[32,4384]{1,0:T(8,128)(2,1)S(1)} %bitcast.1088), channel_id=1, source_target_pairs={{0,16},{4,20},{8,24},{12,28},{16,0},{20,4},{24,8},{28,12},{1,17},{... | collective-permute-start | bytes 841736 | tf_op jit(solution)/shard_map/ppermute | solution.py:244
  84.7 43.4 %collective-permute-start.68 = (bf16[32,4384]{1,0:T(8,128)(2,1)S(1)}, bf16[32,4384]{1,0:T(8,128)(2,1)S(1)}, u32[]{:S(2)}, u32[]{:S(2)}) collective-permute-start(bf16[32,4384]{1,0:T(8,128)(2,1)S(1)} %bitcast.1089), channel_id=1, source_target_pairs={{0,8},{4,12},{8,0},{12,4},{16,24},{20,28},{24,16},{28,20},{1,9},{5... | collective-permute-start | bytes 841736 | tf_op jit(solution)/shard_map/ppermute | solution.py:244
  96.0 57.8 %collective-permute-start.62 = (bf16[192,1024]{1,0:T(8,128)(2,1)S(1)}, bf16[192,1024]{1,0:T(8,128)(2,1)S(1)}, u32[]{:S(2)}, u32[]{:S(2)}) collective-permute-start(bf16[192,1024]{1,0:T(8,128)(2,1)S(1)} %get-tuple-element.221), channel_id=1, source_target_pairs={{0,16},{4,20},{8,24},{12,28},{16,0},{20,4},{24,8},{28,12},{1,17},{... | collective-permute-start | bytes 1179656 | tf_op jit(solution)/shard_map/ppermute | solution.py:244
  102.4 53.1 %collective-permute-start.61 = (bf16[192,1024]{1,0:T(8,128)(2,1)S(1)}, bf16[192,1024]{1,0:T(8,128)(2,1)S(1)}, u32[]{:S(2)}, u32[]{:S(2)}) collective-permute-start(bf16[192,1024]{1,0:T(8,128)(2,1)S(1)} %get-tuple-element.221), channel_id=1, source_target_pairs={{0,8},{4,12},{8,0},{12,4},{16,24},{20,28},{24,16},{28,20},{1,9},{5... | collective-permute-start | bytes 1179656 | tf_op jit(solution)/shard_map/ppermute | solution.py:244
  129.7 41.4 %collective-permute-start.35 = (bf16[192,3,384]{2,0,1:T(8,128)(2,1)S(1)}, bf16[192,3,384]{2,0,1:T(8,128)(2,1)S(1)}, u32[]{:S(2)}, u32[]{:S(2)}) collective-permute-start(bf16[192,3,384]{2,0,1:T(8,128)(2,1)S(1)} %convert_element_type.1371), channel_id=1, source_target_pairs={{0,24},{4,28},{8,16},{12,20},{16,8},{20,12},{24,0},{28,4},{1,25},{... | collective-permute-start | bytes 1327112 | tf_op jit(solution)/shard_map/ppermute | solution.py:244
  134.4 47.0 %collective-permute-start.34 = (bf16[192,3,384]{2,0,1:T(8,128)(2,1)S(1)}, bf16[192,3,384]{2,0,1:T(8,128)(2,1)S(1)}, u32[]{:S(2)}, u32[]{:S(2)}) collective-permute-start(bf16[192,3,384]{2,0,1:T(8,128)(2,1)S(1)} %convert_element_type.1371), channel_id=1, source_target_pairs={{0,16},{4,20},{8,24},{12,28},{16,0},{20,4},{24,8},{28,12},{1,17},{... | collective-permute-start | bytes 1327112 | tf_op jit(solution)/shard_map/ppermute | solution.py:244
  135.8 47.2 %collective-permute-start.33 = (bf16[192,3,384]{2,0,1:T(8,128)(2,1)S(1)}, bf16[192,3,384]{2,0,1:T(8,128)(2,1)S(1)}, u32[]{:S(2)}, u32[]{:S(2)}) collective-permute-start(bf16[192,3,384]{2,0,1:T(8,128)(2,1)S(1)} %convert_element_type.1371), channel_id=1, source_target_pairs={{0,8},{4,12},{8,0},{12,4},{16,24},{20,28},{24,16},{28,20},{1,9},{5... | collective-permute-start | bytes 1327112 | tf_op jit(solution)/shard_map/ppermute | solution.py:244
  171.1 40.2 %collective-permute-start.84 = (bf16[4,64,1024]{2,1,0:T(8,128)(2,1)S(1)}, bf16[4,64,1024]{2,1,0:T(8,128)(2,1)}, u32[]{:S(2)}, u32[]{:S(2)}) collective-permute-start(bf16[4,64,1024]{2,1,0:T(8,128)(2,1)S(1)} %pad_maximum_fusion.26.refs_0_), channel_id=1, source_target_pairs={{0,1},{1,0},{2,3},{3,2},{4,5},{5,4},{6,7},{7,6},{8,9},{9,8},{10,11... | collective-permute-start | bytes 1572872 | tf_op jit(solution)/shard_map/ppermute | solution.py:244
  200.5 45.3 %collective-permute-start.48 = (bf16[192,2,1024]{2,1,0:T(2,128)(2,1)}, bf16[192,2,1024]{2,1,0:T(2,128)(2,1)}, u32[]{:S(2)}, u32[]{:S(2)}) collective-permute-start(bf16[192,2,1024]{2,1,0:T(2,128)(2,1)} %convert_element_type.1384), channel_id=1, source_target_pairs={{0,16},{4,20},{8,24},{12,28},{16,0},{20,4},{24,8},{28,12},{1,17},{... | collective-permute-start | bytes 2359304 | tf_op jit(solution)/shard_map/ppermute | solution.py:244
  227.2 37.6 %collective-permute-start.49 = (bf16[192,2,1024]{2,1,0:T(2,128)(2,1)}, bf16[192,2,1024]{2,1,0:T(2,128)(2,1)S(1)}, u32[]{:S(2)}, u32[]{:S(2)}) collective-permute-start(bf16[192,2,1024]{2,1,0:T(2,128)(2,1)} %convert_element_type.1384), channel_id=1, source_target_pairs={{0,24},{4,28},{8,16},{12,20},{16,8},{20,12},{24,0},{28,4},{1,25},{... | collective-permute-start | bytes 2359304 | tf_op jit(solution)/shard_map/ppermute | solution.py:244
  264.8 88.3 %collective-permute-start.14 = (bf16[4,32,4384]{2,1,0:T(8,128)(2,1)S(1)}, bf16[4,32,4384]{2,1,0:T(8,128)(2,1)}, u32[]{:S(2)}, u32[]{:S(2)}) collective-permute-start(bf16[4,32,4384]{2,1,0:T(8,128)(2,1)S(1)} %pad_maximum_fusion.19.refs_0_), channel_id=1, source_target_pairs={{0,2},{1,3},{2,0},{3,1},{4,6},{5,7},{6,4},{7,5},{8,10},{9,11},{10,... | collective-permute-start | bytes 3366920 | tf_op jit(solution)/shard_map/ppermute | solution.py:244
  266.3 86.9 %collective-permute-start.13 = (bf16[4,32,4384]{2,1,0:T(8,128)(2,1)S(1)}, bf16[4,32,4384]{2,1,0:T(8,128)(2,1)}, u32[]{:S(2)}, u32[]{:S(2)}) collective-permute-start(bf16[4,32,4384]{2,1,0:T(8,128)(2,1)S(1)} %pad_maximum_fusion.19.refs_0_), channel_id=1, source_target_pairs={{0,4},{4,0},{8,12},{12,8},{16,20},{20,16},{24,28},{28,24},{1,5},{5... | collective-permute-start | bytes 3366920 | tf_op jit(solution)/shard_map/ppermute | solution.py:244
  267.9 36.3 %collective-permute-start.83 = (bf16[4,64,1024]{2,1,0:T(8,128)(2,1)}, bf16[4,64,1024]{2,1,0:T(8,128)(2,1)S(1)}, u32[]{:S(2)}, u32[]{:S(2)}) collective-permute-start(bf16[4,64,1024]{2,1,0:T(8,128)(2,1)} %collective-permute-done.81.refs_1_), channel_id=1, source_target_pairs={{0,2},{1,3},{2,0},{3,1},{4,6},{5,7},{6,4},{7,5},{8,10},{9,11},{10,... | collective-permute-start | bytes 1572872 | tf_op jit(solution)/shard_map/ppermute | solution.py:244
  271.3 80.2 %collective-permute-start.27 = (bf16[4,64,1024]{2,1,0:T(8,128)(2,1)}, bf16[4,64,1024]{2,1,0:T(8,128)(2,1)}, u32[]{:S(2)}, u32[]{:S(2)}) collective-permute-start(bf16[4,64,1024]{2,1,0:T(8,128)(2,1)} %collective-permute-done.23.refs_1_), channel_id=1, source_target_pairs={{0,1},{1,0},{2,3},{3,2},{4,5},{5,4},{6,7},{7,6},{8,9},{9,8},{10,11... | collective-permute-start | bytes 1572872 | tf_op jit(solution)/shard_map/ppermute | solution.py:244
  271.7 79.7 %collective-permute-start.25 = (bf16[4,64,1024]{2,1,0:T(8,128)(2,1)}, bf16[4,64,1024]{2,1,0:T(8,128)(2,1)}, u32[]{:S(2)}, u32[]{:S(2)}) collective-permute-start(bf16[4,64,1024]{2,1,0:T(8,128)(2,1)} %collective-permute-done.23.refs_1_), channel_id=1, source_target_pairs={{0,2},{1,3},{2,0},{3,1},{4,6},{5,7},{6,4},{7,5},{8,10},{9,11},{10,... | collective-permute-start | bytes 1572872 | tf_op jit(solution)/shard_map/ppermute | solution.py:244
  304.2 45.7 %collective-permute-start.28 = (bf16[4,64,1024]{2,1,0:T(8,128)(2,1)}, bf16[4,64,1024]{2,1,0:T(8,128)(2,1)}, u32[]{:S(2)}, u32[]{:S(2)}) collective-permute-start(bf16[4,64,1024]{2,1,0:T(8,128)(2,1)} %collective-permute-done.24.refs_2_), channel_id=1, source_target_pairs={{0,1},{1,0},{2,3},{3,2},{4,5},{5,4},{6,7},{7,6},{8,9},{9,8},{10,11... | collective-permute-start | bytes 1572872 | tf_op jit(solution)/shard_map/ppermute | solution.py:244
  349.9 114.3 %collective-permute-start.36 = (bf16[4,192,3,384]{3,1,2,0:T(8,128)(2,1)}, bf16[4,192,3,384]{3,1,2,0:T(8,128)(2,1)}, u32[]{:S(2)}, u32[]{:S(2)}) collective-permute-start(bf16[4,192,3,384]{3,1,2,0:T(8,128)(2,1)} %copy.378), channel_id=1, source_target_pairs={{0,4},{4,0},{8,12},{12,8},{16,20},{20,16},{24,28},{28,24},{1,5},{5... | collective-permute-start | bytes 5308424 | tf_op jit(solution)/shard_map/ppermute | solution.py:244
  351.4 80.1 %collective-permute-start.59 = (bf16[4,32,3072]{2,1,0:T(8,128)(2,1)}, bf16[4,32,3072]{2,1,0:T(8,128)(2,1)}, u32[]{:S(2)}, u32[]{:S(2)}) collective-permute-start(bf16[4,32,3072]{2,1,0:T(8,128)(2,1)} %copy-done.156), channel_id=1, source_target_pairs={{0,1},{1,0},{2,3},{3,2},{4,5},{5,4},{6,7},{7,6},{8,9},{9,8},{10,11... | collective-permute-start | bytes 2359304 | tf_op jit(solution)/shard_map/ppermute | solution.py:244
  351.4 80.2 %collective-permute-start.56 = (bf16[4,32,3072]{2,1,0:T(8,128)(2,1)}, bf16[4,32,3072]{2,1,0:T(8,128)(2,1)}, u32[]{:S(2)}, u32[]{:S(2)}) collective-permute-start(bf16[4,32,3072]{2,1,0:T(8,128)(2,1)} %collective-permute-done.54.refs_1_), channel_id=1, source_target_pairs={{0,2},{1,3},{2,0},{3,1},{4,6},{5,7},{6,4},{7,5},{8,10},{9,11},{10,... | collective-permute-start | bytes 2359304 | tf_op jit(solution)/shard_map/ppermute | solution.py:244
  353.0 73.8 %collective-permute-start.87 = (bf16[4,64,1024]{2,1,0:T(8,128)(2,1)}, bf16[4,64,1024]{2,1,0:T(8,128)(2,1)}, u32[]{:S(2)}, u32[]{:S(2)}) collective-permute-start(bf16[4,64,1024]{2,1,0:T(8,128)(2,1)} %copy-done.165), channel_id=1, source_target_pairs={{0,1},{1,0},{2,3},{3,2},{4,5},{5,4},{6,7},{7,6},{8,9},{9,8},{10,11... | collective-permute-start | bytes 1572872 | tf_op jit(solution)/shard_map/ppermute | solution.py:244
  353.2 77.6 %collective-permute-start.29 = (bf16[4,64,1024]{2,1,0:T(8,128)(2,1)}, bf16[4,64,1024]{2,1,0:T(8,128)(2,1)}, u32[]{:S(2)}, u32[]{:S(2)}) collective-permute-start(bf16[4,64,1024]{2,1,0:T(8,128)(2,1)} %collective-permute-done.25.refs_3_), channel_id=1, source_target_pairs={{0,1},{1,0},{2,3},{3,2},{4,5},{5,4},{6,7},{7,6},{8,9},{9,8},{10,11... | collective-permute-start | bytes 1572872 | tf_op jit(solution)/shard_map/ppermute | solution.py:244
  426.8 36.8 %collective-permute-start.64 = (bf16[4,192,1024]{2,1,0:T(8,128)(2,1)}, bf16[4,192,1024]{2,1,0:T(8,128)(2,1)}, u32[]{:S(2)}, u32[]{:S(2)}) collective-permute-start(bf16[4,192,1024]{2,1,0:T(8,128)(2,1)} %pad_maximum_fusion.10.refs_0_), channel_id=1, source_target_pairs={{0,4},{4,0},{8,12},{12,8},{16,20},{20,16},{24,28},{28,24},{1,5},{5... | collective-permute-start | bytes 4718600 | tf_op jit(solution)/shard_map/ppermute | solution.py:244
  435.1 726.7 %collective-permute-start.16 = (bf16[4,32,4384]{2,1,0:T(8,128)(2,1)S(1)}, bf16[4,32,4384]{2,1,0:T(8,128)(2,1)}, u32[]{:S(2)}, u32[]{:S(2)}) collective-permute-start(bf16[4,32,4384]{2,1,0:T(8,128)(2,1)S(1)} %pad_maximum_fusion.19.refs_0_), channel_id=1, source_target_pairs={{0,1},{1,0},{2,3},{3,2},{4,5},{5,4},{6,7},{7,6},{8,9},{9,8},{10,11... | collective-permute-start | bytes 3366920 | tf_op jit(solution)/shard_map/ppermute | solution.py:244
  463.7 697.6 %collective-permute-start.71 = (bf16[4,32,4384]{2,1,0:T(8,128)(2,1)}, bf16[4,32,4384]{2,1,0:T(8,128)(2,1)}, u32[]{:S(2)}, u32[]{:S(2)}) collective-permute-start(bf16[4,32,4384]{2,1,0:T(8,128)(2,1)} %pad_maximum_fusion.20.refs_0_), channel_id=1, source_target_pairs={{0,4},{4,0},{8,12},{12,8},{16,20},{20,16},{24,28},{28,24},{1,5},{5... | collective-permute-start | bytes 3366920 | tf_op jit(solution)/shard_map/ppermute | solution.py:244
  464.2 699.7 %collective-permute-start.17 = (bf16[4,32,4384]{2,1,0:T(8,128)(2,1)}, bf16[4,32,4384]{2,1,0:T(8,128)(2,1)}, u32[]{:S(2)}, u32[]{:S(2)}) collective-permute-start(bf16[4,32,4384]{2,1,0:T(8,128)(2,1)} %collective-permute-done.13.refs_1_), channel_id=1, source_target_pairs={{0,1},{1,0},{2,3},{3,2},{4,5},{5,4},{6,7},{7,6},{8,9},{9,8},{10,11... | collective-permute-start | bytes 3366920 | tf_op jit(solution)/shard_map/ppermute | solution.py:244
  464.2 698.1 %collective-permute-start.18 = (bf16[4,32,4384]{2,1,0:T(8,128)(2,1)}, bf16[4,32,4384]{2,1,0:T(8,128)(2,1)}, u32[]{:S(2)}, u32[]{:S(2)}) collective-permute-start(bf16[4,32,4384]{2,1,0:T(8,128)(2,1)} %collective-permute-done.14.refs_2_), channel_id=1, source_target_pairs={{0,1},{1,0},{2,3},{3,2},{4,5},{5,4},{6,7},{7,6},{8,9},{9,8},{10,11... | collective-permute-start | bytes 3366920 | tf_op jit(solution)/shard_map/ppermute | solution.py:244
  464.7 699.1 %collective-permute-start.19 = (bf16[4,32,4384]{2,1,0:T(8,128)(2,1)}, bf16[4,32,4384]{2,1,0:T(8,128)(2,1)}, u32[]{:S(2)}, u32[]{:S(2)}) collective-permute-start(bf16[4,32,4384]{2,1,0:T(8,128)(2,1)} %collective-permute-done.15.refs_3_), channel_id=1, source_target_pairs={{0,1},{1,0},{2,3},{3,2},{4,5},{5,4},{6,7},{7,6},{8,9},{9,8},{10,11... | collective-permute-start | bytes 3366920 | tf_op jit(solution)/shard_map/ppermute | solution.py:244
  1161.3 392.9 %collective-permute-start.74 = (bf16[4,32,4384]{2,1,0:T(8,128)(2,1)}, bf16[4,32,4384]{2,1,0:T(8,128)(2,1)}, u32[]{:S(2)}, u32[]{:S(2)}) collective-permute-start(bf16[4,32,4384]{2,1,0:T(8,128)(2,1)} %pad_maximum_fusion.20.refs_0_), channel_id=1, source_target_pairs={{0,1},{1,0},{2,3},{3,2},{4,5},{5,4},{6,7},{7,6},{8,9},{9,8},{10,11... | collective-permute-start | bytes 3366920 | tf_op jit(solution)/shard_map/ppermute | solution.py:244
  1161.8 375.8 %collective-permute-start.72 = (bf16[4,32,4384]{2,1,0:T(8,128)(2,1)}, bf16[4,32,4384]{2,1,0:T(8,128)(2,1)}, u32[]{:S(2)}, u32[]{:S(2)}) collective-permute-start(bf16[4,32,4384]{2,1,0:T(8,128)(2,1)} %pad_maximum_fusion.20.refs_0_), channel_id=1, source_target_pairs={{0,2},{1,3},{2,0},{3,1},{4,6},{5,7},{6,4},{7,5},{8,10},{9,11},{10,... | collective-permute-start | bytes 3366920 | tf_op jit(solution)/shard_map/ppermute | solution.py:244
  1162.3 376.8 %collective-permute-start.73 = (bf16[4,32,4384]{2,1,0:T(8,128)(2,1)}, bf16[4,32,4384]{2,1,0:T(8,128)(2,1)}, u32[]{:S(2)}, u32[]{:S(2)}) collective-permute-start(bf16[4,32,4384]{2,1,0:T(8,128)(2,1)} %collective-permute-done.71.refs_1_), channel_id=1, source_target_pairs={{0,2},{1,3},{2,0},{3,1},{4,6},{5,7},{6,4},{7,5},{8,10},{9,11},{10,... | collective-permute-start | bytes 3366920 | tf_op jit(solution)/shard_map/ppermute | solution.py:244
  1537.6 322.3 %collective-permute-start.50 = (bf16[4,192,2,1024]{3,2,1,0:T(2,128)(2,1)}, bf16[4,192,2,1024]{3,2,1,0:T(2,128)(2,1)}, u32[]{:S(2)}, u32[]{:S(2)}) collective-permute-start(bf16[4,192,2,1024]{3,2,1,0:T(2,128)(2,1)} %pad_maximum_fusion.6.refs_0_), channel_id=1, source_target_pairs={{0,4},{4,0},{8,12},{12,8},{16,20},{20,16},{24,28},{28,24},{1,5},{5... | collective-permute-start | bytes 9437192 | tf_op jit(solution)/shard_map/ppermute | solution.py:244
  1554.3 283.0 %collective-permute-start.42 = (bf16[128,1536]{1,0:T(8,128)(2,1)}, bf16[128,1536]{1,0:T(8,128)(2,1)S(1)}, u32[]{:S(2)}, u32[]{:S(2)}) collective-permute-start(bf16[128,1536]{1,0:T(8,128)(2,1)} %get-tuple-element.214), channel_id=1, source_target_pairs={{0,1},{1,0},{2,3},{3,2},{4,5},{5,4},{6,7},{7,6},{8,9},{9,8},{10,11... | collective-permute-start | bytes 1179656 | tf_op jit(solution)/shard_map/ppermute | solution.py:244
  1850.1 201.6 %collective-permute-start.45 = (bf16[128,1536]{1,0:T(8,128)(2,1)S(1)}, bf16[128,1536]{1,0:T(8,128)(2,1)S(1)}, u32[]{:S(2)}, u32[]{:S(2)}) collective-permute-start(bf16[128,1536]{1,0:T(8,128)(2,1)S(1)} %multiply_convert_fusion.8), channel_id=1, source_target_pairs={{0,1},{1,0},{2,3},{3,2},{4,5},{5,4},{6,7},{7,6},{8,9},{9,8},{10,11... | collective-permute-start | bytes 1179656 | tf_op jit(solution)/shard_map/ppermute | solution.py:244
  1859.7 192.0 %collective-permute-start.46 = (bf16[128,1536]{1,0:T(8,128)(2,1)S(1)}, bf16[128,1536]{1,0:T(8,128)(2,1)S(1)}, u32[]{:S(2)}, u32[]{:S(2)}) collective-permute-start(bf16[128,1536]{1,0:T(8,128)(2,1)S(1)} %collective-permute-done.44), channel_id=1, source_target_pairs={{0,1},{1,0},{2,3},{3,2},{4,5},{5,4},{6,7},{7,6},{8,9},{9,8},{10,11... | collective-permute-start | bytes 1179656 | tf_op jit(solution)/shard_map/ppermute | solution.py:244
  2340.6 39.6 %collective-permute-start.89 = (bf16[128,1536]{1,0:T(8,128)(2,1)}, bf16[128,1536]{1,0:T(8,128)(2,1)}, u32[]{:S(2)}, u32[]{:S(2)}) collective-permute-start(bf16[128,1536]{1,0:T(8,128)(2,1)} %fusion.361), channel_id=1, source_target_pairs={{0,1},{1,0},{2,3},{3,2},{4,5},{5,4},{6,7},{7,6},{8,9},{9,8},{10,11... | collective-permute-start | bytes 1179656 | tf_op jit(solution)/shard_map/ppermute | solution.py:244
  2343.2 78.1 %collective-permute-start.124 = (bf16[8,2,64,1024]{3,2,0,1:T(8,128)(2,1)}, bf16[8,2,64,1024]{3,2,0,1:T(8,128)(2,1)}, u32[]{:S(2)}, u32[]{:S(2)}) collective-permute-start(bf16[8,2,64,1024]{3,2,0,1:T(8,128)(2,1)} %copy_bitcast_fusion.4), channel_id=1, source_target_pairs={{0,1},{1,0},{2,3},{3,2},{4,5},{5,4},{6,7},{7,6},{8,9},{9,8},{10,11... | collective-permute-start | bytes 6291464 | tf_op jit(solution)/shard_map/ppermute | solution.py:244
  2370.6 139.7 %collective-permute-start.130 = (bf16[8,2,32,3072]{3,2,0,1:T(8,128)(2,1)}, bf16[8,2,32,3072]{3,2,0,1:T(8,128)(2,1)}, u32[]{:S(2)}, u32[]{:S(2)}) collective-permute-start(bf16[8,2,32,3072]{3,2,0,1:T(8,128)(2,1)} %copy_bitcast_fusion.3), channel_id=1, source_target_pairs={{0,1},{1,0},{2,3},{3,2},{4,5},{5,4},{6,7},{7,6},{8,9},{9,8},{10,11... | collective-permute-start | bytes 9437192 | tf_op jit(solution)/shard_map/ppermute | solution.py:244
  2400.7 36.5 %collective-permute-start.148 = (bf16[4,192,1024]{2,1,0:T(8,128)(2,1)}, bf16[4,192,1024]{2,1,0:T(8,128)(2,1)S(1)}, u32[]{:S(2)}, u32[]{:S(2)}) collective-permute-start(bf16[4,192,1024]{2,1,0:T(8,128)(2,1)} %dynamic-slice_bitcast_fusion), channel_id=1, source_target_pairs={{0,4},{4,0},{8,12},{12,8},{16,20},{20,16},{24,28},{28,24},{1,5},{5... | collective-permute-start | bytes 4718600 | tf_op jit(solution)/shard_map/ppermute | solution.py:244
  2420.2 37.7 %collective-permute-start.95 = (bf16[128,1536]{1,0:T(8,128)(2,1)}, bf16[128,1536]{1,0:T(8,128)(2,1)S(1)}, u32[]{:S(2)}, u32[]{:S(2)}) collective-permute-start(bf16[128,1536]{1,0:T(8,128)(2,1)} %get-tuple-element.121), channel_id=1, source_target_pairs={{0,1},{1,0},{2,3},{3,2},{4,5},{5,4},{6,7},{7,6},{8,9},{9,8},{10,11... | collective-permute-start | bytes 1179656 | tf_op jit(solution)/shard_map/ppermute | solution.py:244
  2420.8 37.2 %collective-permute-start.96 = (bf16[128,1536]{1,0:T(8,128)(2,1)S(1)}, bf16[128,1536]{1,0:T(8,128)(2,1)S(1)}, u32[]{:S(2)}, u32[]{:S(2)}) collective-permute-start(bf16[128,1536]{1,0:T(8,128)(2,1)S(1)} %collective-permute-done.94), channel_id=1, source_target_pairs={{0,1},{1,0},{2,3},{3,2},{4,5},{5,4},{6,7},{7,6},{8,9},{9,8},{10,11... | collective-permute-start | bytes 1179656 | tf_op jit(solution)/shard_map/ppermute | solution.py:244
  2440.4 42.2 %collective-permute-start.149 = (bf16[192,1024]{1,0:T(8,128)(2,1)}, bf16[192,1024]{1,0:T(8,128)(2,1)}, u32[]{:S(2)}, u32[]{:S(2)}) collective-permute-start(bf16[192,1024]{1,0:T(8,128)(2,1)} %get-tuple-element.173), channel_id=1, source_target_pairs={{0,8},{4,12},{8,0},{12,4},{16,24},{20,28},{24,16},{28,20},{1,9},{5... | collective-permute-start | bytes 1179656 | tf_op jit(solution)/shard_map/ppermute | solution.py:244
  2500.8 243.0 %collective-permute-start.112 = (bf16[8,2,32,4384]{3,2,0,1:T(8,128)(2,1)}, bf16[8,2,32,4384]{3,2,0,1:T(8,128)(2,1)}, u32[]{:S(2)}, u32[]{:S(2)}) collective-permute-start(bf16[8,2,32,4384]{3,2,0,1:T(8,128)(2,1)} %copy_bitcast_fusion), channel_id=1, source_target_pairs={{0,1},{1,0},{2,3},{3,2},{4,5},{5,4},{6,7},{7,6},{8,9},{9,8},{10,11... | collective-permute-start | bytes 13467656 | tf_op jit(solution)/shard_map/ppermute | solution.py:244
  2503.6 228.6 %collective-permute-start.144 = (bf16[4,192,2,1024]{3,2,1,0:T(2,128)(2,1)}, bf16[4,192,2,1024]{3,2,1,0:T(2,128)(2,1)}, u32[]{:S(2)}, u32[]{:S(2)}) collective-permute-start(bf16[4,192,2,1024]{3,2,1,0:T(2,128)(2,1)} %bitcast.924), channel_id=1, source_target_pairs={{0,4},{4,0},{8,12},{12,8},{16,20},{20,16},{24,28},{28,24},{1,5},{5... | collective-permute-start | bytes 9437192 | tf_op jit(solution)/shard_map/ppermute | solution.py:244
  2510.3 219.7 %collective-permute-start.136 = (bf16[4,192,3,384]{3,1,2,0:T(8,128)(2,1)}, bf16[4,192,3,384]{3,1,2,0:T(8,128)(2,1)}, u32[]{:S(2)}, u32[]{:S(2)}) collective-permute-start(bf16[4,192,3,384]{3,1,2,0:T(8,128)(2,1)} %copy_bitcast_fusion.6), channel_id=1, source_target_pairs={{0,4},{4,0},{8,12},{12,8},{16,20},{20,16},{24,28},{28,24},{1,5},{5... | collective-permute-start | bytes 5308424 | tf_op jit(solution)/shard_map/ppermute | solution.py:244
  2519.2 191.5 %collective-permute-start.126 = (bf16[4,64,1024]{2,1,0:T(8,128)(2,1)}, bf16[4,64,1024]{2,1,0:T(8,128)(2,1)}, u32[]{:S(2)}, u32[]{:S(2)}) collective-permute-start(bf16[4,64,1024]{2,1,0:T(8,128)(2,1)} %fusion.267), channel_id=1, source_target_pairs={{0,4},{4,0},{8,12},{12,8},{16,20},{20,16},{24,28},{28,24},{1,5},{5... | collective-permute-start | bytes 1572872 | tf_op jit(solution)/shard_map/ppermute | solution.py:244
  2718.7 147.6 %collective-permute-start.106 = (bf16[8,2,32,4384]{3,2,0,1:T(8,128)(2,1)S(1)}, bf16[8,2,32,4384]{3,2,0,1:T(8,128)(2,1)S(1)}, u32[]{:S(2)}, u32[]{:S(2)}) collective-permute-start(bf16[8,2,32,4384]{3,2,0,1:T(8,128)(2,1)S(1)} %bitcast.1020), channel_id=1, source_target_pairs={{0,1},{1,0},{2,3},{3,2},{4,5},{5,4},{6,7},{7,6},{8,9},{9,8},{10,11... | collective-permute-start | bytes 13467656 | tf_op jit(solution)/shard_map/ppermute | solution.py:244
  2729.9 53.2 %collective-permute-start.131 = (bf16[8,1,32,3072]{3,2,0,1:T(8,128)(2,1)S(1)}, bf16[8,1,32,3072]{3,2,0,1:T(8,128)(2,1)S(1)}, u32[]{:S(2)}, u32[]{:S(2)}) collective-permute-start(bf16[8,1,32,3072]{3,2,0,1:T(8,128)(2,1)S(1)} %copy-done.128), channel_id=1, source_target_pairs={{0,2},{1,3},{2,0},{3,1},{4,6},{5,7},{6,4},{7,5},{8,10},{9,11},{10,... | collective-permute-start | bytes 4718600 | tf_op jit(solution)/shard_map/ppermute | solution.py:244
  2743.8 39.3 %collective-permute-start.138 = (bf16[192,3,384]{2,0,1:T(8,128)(2,1)S(1)}, bf16[192,3,384]{2,0,1:T(8,128)(2,1)}, u32[]{:S(2)}, u32[]{:S(2)}) collective-permute-start(bf16[192,3,384]{2,0,1:T(8,128)(2,1)S(1)} %get-tuple-element.172), channel_id=1, source_target_pairs={{0,16},{4,20},{8,24},{12,28},{16,0},{20,4},{24,8},{28,12},{1,17},{... | collective-permute-start | bytes 1327112 | tf_op jit(solution)/shard_map/ppermute | solution.py:244
  2745.7 39.9 %collective-permute-start.101 = (bf16[8,1,32,1024]{3,2,0,1:T(8,128)(2,1)S(1)}, bf16[8,1,32,1024]{3,2,0,1:T(8,128)(2,1)S(1)}, u32[]{:S(2)}, u32[]{:S(2)}) collective-permute-start(bf16[8,1,32,1024]{3,2,0,1:T(8,128)(2,1)S(1)} %fusion.207), channel_id=1, source_target_pairs={{0,2},{1,3},{2,0},{3,1},{4,6},{5,7},{6,4},{7,5},{8,10},{9,11},{10,... | collective-permute-start | bytes 1572872 | tf_op jit(solution)/shard_map/ppermute | solution.py:244
  2756.2 107.1 %collective-permute-start.118 = (bf16[8,2,64,1024]{3,2,0,1:T(8,128)(2,1)S(1)}, bf16[8,2,64,1024]{3,2,0,1:T(8,128)(2,1)S(1)}, u32[]{:S(2)}, u32[]{:S(2)}) collective-permute-start(bf16[8,2,64,1024]{3,2,0,1:T(8,128)(2,1)S(1)} %copy_bitcast_fusion.5), channel_id=1, source_target_pairs={{0,1},{1,0},{2,3},{3,2},{4,5},{5,4},{6,7},{7,6},{8,9},{9,8},{10,11... | collective-permute-start | bytes 6291464 | tf_op jit(solution)/shard_map/ppermute | solution.py:244
  2783.1 35.5 %collective-permute-start.145 = (bf16[192,2,1024]{2,1,0:T(2,128)(2,1)}, bf16[192,2,1024]{2,1,0:T(2,128)(2,1)S(1)}, u32[]{:S(2)}, u32[]{:S(2)}) collective-permute-start(bf16[192,2,1024]{2,1,0:T(2,128)(2,1)} %get-tuple-element.196), channel_id=1, source_target_pairs={{0,8},{4,12},{8,0},{12,4},{16,24},{20,28},{24,16},{28,20},{1,9},{5... | collective-permute-start | bytes 2359304 | tf_op jit(solution)/shard_map/ppermute | solution.py:244
  2783.1 38.0 %collective-permute-start.147 = (bf16[192,2,1024]{2,1,0:T(2,128)(2,1)S(1)}, bf16[192,2,1024]{2,1,0:T(2,128)(2,1)S(1)}, u32[]{:S(2)}, u32[]{:S(2)}) collective-permute-start(bf16[192,2,1024]{2,1,0:T(2,128)(2,1)S(1)} %get-tuple-element.197), channel_id=1, source_target_pairs={{0,24},{4,28},{8,16},{12,20},{16,8},{20,12},{24,0},{28,4},{1,25},{... | collective-permute-start | bytes 2359304 | tf_op jit(solution)/shard_map/ppermute | solution.py:244
  2786.4 67.3 %collective-permute-start.146 = (bf16[192,2,1024]{2,1,0:T(2,128)(2,1)S(1)}, bf16[192,2,1024]{2,1,0:T(2,128)(2,1)S(1)}, u32[]{:S(2)}, u32[]{:S(2)}) collective-permute-start(bf16[192,2,1024]{2,1,0:T(2,128)(2,1)S(1)} %get-tuple-element.198), channel_id=1, source_target_pairs={{0,16},{4,20},{8,24},{12,28},{16,0},{20,4},{24,8},{28,12},{1,17},{... | collective-permute-start | bytes 2359304 | tf_op jit(solution)/shard_map/ppermute | solution.py:244
  2818.6 79.2 %collective-permute-start.113 = (bf16[8,1,32,4384]{3,2,0,1:T(8,128)(2,1)S(1)}, bf16[8,1,32,4384]{3,2,0,1:T(8,128)(2,1)S(1)}, u32[]{:S(2)}, u32[]{:S(2)}) collective-permute-start(bf16[8,1,32,4384]{3,2,0,1:T(8,128)(2,1)S(1)} %fusion.30), channel_id=1, source_target_pairs={{0,2},{1,3},{2,0},{3,1},{4,6},{5,7},{6,4},{7,5},{8,10},{9,11},{10,... | collective-permute-start | bytes 6733832 | tf_op jit(solution)/shard_map/ppermute | solution.py:244
  2821.2 53.2 %collective-permute-start.132 = (bf16[4,32,3072]{2,1,0:T(8,128)(2,1)}, bf16[4,32,3072]{2,1,0:T(8,128)(2,1)}, u32[]{:S(2)}, u32[]{:S(2)}) collective-permute-start(bf16[4,32,3072]{2,1,0:T(8,128)(2,1)} %fusion.236), channel_id=1, source_target_pairs={{0,4},{4,0},{8,12},{12,8},{16,20},{20,16},{24,28},{28,24},{1,5},{5... | collective-permute-start | bytes 2359304 | tf_op jit(solution)/shard_map/ppermute | solution.py:244
  2871.1 69.9 %collective-permute-start.107 = (bf16[8,1,32,4384]{3,2,0,1:T(8,128)(2,1)S(1)}, bf16[8,1,32,4384]{3,2,0,1:T(8,128)(2,1)S(1)}, u32[]{:S(2)}, u32[]{:S(2)}) collective-permute-start(bf16[8,1,32,4384]{3,2,0,1:T(8,128)(2,1)S(1)} %fusion.31), channel_id=1, source_target_pairs={{0,2},{1,3},{2,0},{3,1},{4,6},{5,7},{6,4},{7,5},{8,10},{9,11},{10,... | collective-permute-start | bytes 6733832 | tf_op jit(solution)/shard_map/ppermute | solution.py:244
  2875.9 68.0 %collective-permute-start.133 = (bf16[32,3072]{1,0:T(8,128)(2,1)S(1)}, bf16[32,3072]{1,0:T(8,128)(2,1)S(1)}, u32[]{:S(2)}, u32[]{:S(2)}) collective-permute-start(bf16[32,3072]{1,0:T(8,128)(2,1)S(1)} %get-tuple-element.167), channel_id=1, source_target_pairs={{0,8},{4,12},{8,0},{12,4},{16,24},{20,28},{24,16},{28,20},{1,9},{5... | collective-permute-start | bytes 589832 | tf_op jit(solution)/shard_map/ppermute | solution.py:244
  2876.4 68.8 %collective-permute-start.135 = (bf16[32,3072]{1,0:T(8,128)(2,1)S(1)}, bf16[32,3072]{1,0:T(8,128)(2,1)S(1)}, u32[]{:S(2)}, u32[]{:S(2)}) collective-permute-start(bf16[32,3072]{1,0:T(8,128)(2,1)S(1)} %get-tuple-element.168), channel_id=1, source_target_pairs={{0,24},{4,28},{8,16},{12,20},{16,8},{20,12},{24,0},{28,4},{1,25},{... | collective-permute-start | bytes 589832 | tf_op jit(solution)/shard_map/ppermute | solution.py:244
  2895.6 51.7 %collective-permute-start.134 = (bf16[32,3072]{1,0:T(8,128)(2,1)S(1)}, bf16[32,3072]{1,0:T(8,128)(2,1)S(1)}, u32[]{:S(2)}, u32[]{:S(2)}) collective-permute-start(bf16[32,3072]{1,0:T(8,128)(2,1)S(1)} %get-tuple-element.169), channel_id=1, source_target_pairs={{0,16},{4,20},{8,24},{12,28},{16,0},{20,4},{24,8},{28,12},{1,17},{... | collective-permute-start | bytes 589832 | tf_op jit(solution)/shard_map/ppermute | solution.py:244
  2897.9 43.9 %collective-permute-start.120 = (bf16[4,64,1024]{2,1,0:T(8,128)(2,1)S(1)}, bf16[4,64,1024]{2,1,0:T(8,128)(2,1)S(1)}, u32[]{:S(2)}, u32[]{:S(2)}) collective-permute-start(bf16[4,64,1024]{2,1,0:T(8,128)(2,1)S(1)} %fusion.266), channel_id=1, source_target_pairs={{0,4},{4,0},{8,12},{12,8},{16,20},{20,16},{24,28},{28,24},{1,5},{5... | collective-permute-start | bytes 1572872 | tf_op jit(solution)/shard_map/ppermute | solution.py:244
  2941.8 47.3 %collective-permute-start.108 = (bf16[4,32,4384]{2,1,0:T(8,128)(2,1)S(1)}, bf16[4,32,4384]{2,1,0:T(8,128)(2,1)S(1)}, u32[]{:S(2)}, u32[]{:S(2)}) collective-permute-start(bf16[4,32,4384]{2,1,0:T(8,128)(2,1)S(1)} %fusion.204), channel_id=1, source_target_pairs={{0,4},{4,0},{8,12},{12,8},{16,20},{20,16},{24,28},{28,24},{1,5},{5... | collective-permute-start | bytes 3366920 | tf_op jit(solution)/shard_map/ppermute | solution.py:244
  (507 other events, 18729.0 us)

commit v2 on v1

--- a/solution.py
+++ b/solution.py
@@ -74,61 +74,6 @@
     )
 
 
-def ssd_scan(inputs, steps, rates, in_map, out_map):
-    blocks = inputs.shape[0] // ssd_block
-    cumulative = jnp.cumsum((steps * rates).reshape(blocks, ssd_block, MHEADS), axis=1)
-    weighted = (inputs * steps[:, :, None]).reshape(blocks, ssd_block, MHEADS, HEADDIM)
-    in_blocks = in_map.reshape(blocks, ssd_block, STATE)
-    out_blocks = out_map.reshape(blocks, ssd_block, STATE)
-    causal = jnp.tril(jnp.ones((ssd_block, ssd_block), dtype=bool))
-    log_gaps = jnp.where(
-        causal[None, :, :, None], cumulative[:, :, None, :] - cumulative[:, None, :, :], -jnp.inf
-    )
-    affinity = jnp.einsum("bin,bjn->bij", out_blocks, in_blocks, precision=deepest_tier)
-    within = jnp.einsum(
-        "bij,bijh,bjhp->bihp", affinity, jnp.exp(log_gaps), weighted, precision=deepest_tier
-    )
-    to_end = jnp.exp(cumulative[:, -1:, :] - cumulative)
-    states = jnp.einsum("bjn,bjh,bjhp->bhpn", in_blocks, to_end, weighted, precision=deepest_tier)
-
-    running = jnp.zeros((MHEADS, HEADDIM, STATE), jnp.float32)
-    starts = []
-    for block in range(blocks):
-        starts.append(running)
-        if block + 1 < blocks:
-            running = jnp.exp(cumulative[block, -1, :])[:, None, None] * running + states[block]
-    starts = jnp.stack(starts)
-    across = jnp.einsum(
-        "bin,bih,bhpn->bihp", out_blocks, jnp.exp(cumulative), starts, precision=deepest_tier
-    )
-    return (within + across).reshape(-1, MHEADS * HEADDIM)
-
-
-def mixer_middle(projected, conv_taps, skip_gain, a_log, dt_bias, gated_gain):
-    span_extent_size = projected.shape[0]
-    gate_part = projected[:, :INNER]
-    streams = projected[:, INNER : 2 * INNER + 2 * STATE]
-    raw_steps = projected[:, 2 * INNER + 2 * STATE :]
-    padded = jnp.concatenate([jnp.zeros((3, streams.shape[1]), jnp.float32), streams], axis=0)
-    convolved = conv_taps[0] * padded[0:span_extent_size]
-    for tap_index in range(1, 4):
-        convolved = (
-            convolved + conv_taps[tap_index] * padded[tap_index : tap_index + span_extent_size]
-        )
-    active = jax.nn.silu(convolved)
-    inputs = active[:, :INNER]
-    steps = softplus(raw_steps + dt_bias)
-    outcome = ssd_scan(
-        inputs.reshape(span_extent_size, MHEADS, HEADDIM),
-        steps,
-        -jnp.exp(a_log),
-        active[:, INNER : INNER + STATE],
-        active[:, INNER + STATE :],
-    )
-    outcome = outcome + inputs * skip_gain
-    return root_mean_rescale(outcome * jax.nn.silu(gate_part), gated_gain)
-
-
 def route_prob(queries, key_rows):
     unit_query = queries * lax.rsqrt(jnp.sum(queries * queries, axis=-1, keepdims=True) + 1e-06)
     unit_key = key_rows * lax.rsqrt(jnp.sum(key_rows * key_rows, axis=-1, keepdims=True) + 1e-06)
@@ -246,71 +191,618 @@
 
 def bit_masks(size):
     masks = []
-    mask = size // 2
-    while mask >= 1:
+    mask = 1
+    while mask < size:
         masks.append(mask)
-        mask //= 2
+        mask *= 2
     return masks
 
 
-def spread_dp(shard):
-    size = lax.axis_size("dp")
-    pieces = [shard] + [swap(shard, "dp", mask) for mask in range(2, size, 2)]
-    group = jnp.stack(pieces)
-    return [(0, 0, group), (1, 0, swap(group, "dp", 1))]
-
-
-def spread_all(shard):
-    groups = spread_dp(shard)
-    for mask in bit_masks(lax.axis_size("tensor")):
-        groups = groups + [
-            (dp_mask, tensor_mask | mask, swap(group, "tensor", mask))
-            for dp_mask, tensor_mask, group in groups
+def after(value_entries, earlier):
+    if not earlier:
+        return value_entries
+    return lax.optimization_barrier((value_entries,) + tuple(earlier))[0]
+
+
+def spread_masks(over_tensor):
+    dp_masks = bit_masks(lax.axis_size("dp"))
+    masks = [("dp", mask) for mask in dp_masks[1:] + dp_masks[:1]]
+    if over_tensor:
+        masks += [("tensor", mask) for mask in reversed(bit_masks(lax.axis_size("tensor")))]
+    return masks
+
+
+class Summing:
+    def __init__(self, grad, over_tensor):
+        self.masks = list(reversed(spread_masks(over_tensor)))
+        names = [("dp", mask) for mask in reversed(bit_masks(lax.axis_size("dp")))]
+        if over_tensor:
+            names += [("tensor", mask) for mask in reversed(bit_masks(lax.axis_size("tensor")))]
+        self.names = names
+        rows = grad.shape[0] // 2 ** len(names)
+        self.addends = [grad.reshape((2,) * len(names) + (rows,) + grad.shape[1:])]
+        self.pending = None
+
+    def operand(self):
+        axis, mask = self.masks[0]
+        position = self.names.index((axis, mask))
+        own = (lax.axis_index(axis) // mask) % 2
+        return to_low(total([take(addend, position, 1 - own) for addend in self.addends]))
+
+    def accept(self):
+        axis, mask = self.masks.pop(0)
+        position = self.names.index((axis, mask))
+        own = (lax.axis_index(axis) // mask) % 2
+        self.addends = [take(addend, position, own) for addend in self.addends] + [self.pending]
+        self.pending = None
+        self.names.pop(position)
+
+    def begun_last(self):
+        left = [mask for axis, mask in self.masks if axis == "dp" and mask > 1]
+        return 0 < len(left) == len(self.masks) < len(bit_masks(lax.axis_size("dp"))) - 1
+
+    def rest(self):
+        kind = []
+        for axis, mask in self.masks:
+            name = ("core", "y")[mask - 1] if axis == "tensor" else ("x" if mask == 1 else "z")
+            if name not in kind:
+                kind.append(name)
+        value_entries = to_low(total(self.addends)) if len(self.addends) > 1 else self.addends[0]
+        return value_entries.reshape(-1, value_entries.shape[-1]), tuple(kind)
+
+    def result(self):
+        return total(self.addends)
+
+
+def sum_slowly(job):
+    while job.masks:
+        axis, mask = job.masks[0]
+        job.pending = swap(job.operand(), axis, mask)
+        job.accept()
+    return job.result()
+
+
+class Conductor:
+    def __init__(self):
+        self.clock = 0.0
+        self.jobs = []
+        self.flights = []
+
+    def add(self, job):
+        self.jobs.append(job)
+        return job
+
+    def lane(self, job):
+        axis, mask = job.masks[0]
+        return (axis, mask if axis == "tensor" else min(mask, 2))
+
+    def launch(self, limit, banned, value_entries):
+        for job in self.jobs:
+            if len(self.flights) >= limit:
+                return
+            if job.pending is not None or not job.masks:
+                continue
+            lane = self.lane(job)
+            depth = 2 if lane in (("dp", 1), ("tensor", 1)) else 1
+            if lane in banned or sum(flight[1] == lane for flight in self.flights) >= depth:
+                continue
+            axis, mask = job.masks[0]
+            operand = job.operand()
+            rate = 3.4 if (axis, mask) == ("tensor", 1) else 24.0
+            if axis == "dp" and mask > 2:
+                rate = 48.0
+            job.pending = swap(after(operand, [value_entries]), axis, mask)
+            start = max([self.clock] + [flight[0] - 8.0 for flight in self.flights if flight[1] == lane])
+            self.flights.append((start + 8.0 + 1.2 * rate * operand.size * 2e-6, lane, job))
+
+    def tick(self, value_entries, elapsed, banned=(), limit=5):
+        self.clock += elapsed
+        ended = [flight for flight in self.flights if flight[0] <= self.clock]
+        if ended:
+            value_entries = after(value_entries, [flight[2].pending for flight in ended])
+            self.flights = [flight for flight in self.flights if flight[0] > self.clock]
+            for flight in ended:
+                flight[2].accept()
+        self.launch(limit, banned, value_entries)
+        return value_entries
+
+    def close(self):
+        for _, _, job in sorted(self.flights, key=lambda flight: flight[0]):
+            job.accept()
+        self.flights = []
+        for job in self.jobs:
+            while job.begun_last():
+                axis, mask = job.masks[0]
+                job.pending = swap(job.operand(), axis, mask)
+                job.accept()
+
+
+def flip(place, mask):
+    result = place
+    bit = 1
+    while bit <= mask:
+        if mask & bit:
+            result = result + bit * (1 - 2 * ((place // bit) % 2))
+        bit *= 2
+    return result
+
+
+def order_steps(jobs, depth=2):
+    free, busy, flights, plan = {}, {}, [], []
+    waiting = [0] * len(jobs)
+    clock = 0.0
+    while True:
+        for job, steps in enumerate(jobs):
+            step = waiting[job]
+            if step < 0 or step >= len(steps):
+                continue
+            lane, cost = steps[step]
+            if busy.get(lane, 0) >= depth:
+                continue
+            busy[lane] = busy.get(lane, 0) + 1
+            free[lane] = max(free.get(lane, 0.0), clock) + cost
+            flights.append((free[lane] + 1.5, job, step, lane))
+            plan.append(("start", job, step))
+            waiting[job] = -1 - step
+        if not flights:
+            return plan
+        flight = min(flights)
+        flights.remove(flight)
+        clock, job, step, lane = flight
+        busy[lane] -= 1
+        plan.append(("wait", job, step))
+        waiting[job] = step + 1
+
+
+def link_cost(lane, elements):
+    return elements * 2e-6 * {"core": 3.4, "y": 23.0, "x": 23.0, "z": 46.0}[lane]
+
+
+def here():
+    dp_place, tensor_place = lax.axis_index("dp"), lax.axis_index("tensor")
+    return dp_place // 2, dp_place % 2, tensor_place // 2, tensor_place % 2
+
+
+def partner(lane, mask, coordinates):
+    z, x, y, core = coordinates
+    if lane == "z":
+        z = flip(z, mask)
+    if lane == "x":
+        x = 1 - x
+    if lane == "y":
+        y = 1 - y
+    if lane == "core":
+        core = 1 - core
+    return (z * 2 + x, y * 2 + core)
+
+
+def greet(line, depth_z, coordinates):
+    z = coordinates[0]
+    barrier = pltpu.get_barrier_semaphore()
+
+    def tell(device):
+        pl.semaphore_signal(
+            barrier, inc=1, device_id=device, device_id_type=pl.DeviceIdType.MESH
+        )
+
+    for lane in ("x", "y", "core"):
+        tell(partner(lane, 1, coordinates))
+    if not line:
+        for mask in range(1, depth_z):
+            tell(partner("z", mask, coordinates))
+        pl.semaphore_wait(barrier, depth_z + 2)
+        return
+
+    @pl.when(z > 0)
+    def _():
+        tell(beside(-1, coordinates))
+
+    @pl.when(z < depth_z - 1)
+    def _():
+        tell(beside(1, coordinates))
+
+    ends = (z == 0).astype(jnp.int32) + (z == depth_z - 1).astype(jnp.int32)
+    pl.semaphore_wait(barrier, 5 - ends)
+
+
+def beside(way, coordinates):
+    z, x, y, core = coordinates
+    return ((z + way) * 2 + x, y * 2 + core)
+
+
+def spread_kernel(plan, jobs, depth_z, *refs):
+    count = (len(refs) - 3) // 2
+    shards, wholes = refs[:count], refs[count : 2 * count]
+    send_sems, receive_sems, own_sems = refs[2 * count :]
+    coordinates = here()
+    z = coordinates[0]
+    greet(True, depth_z, coordinates)
+
+    def spot(job, free, z_place):
+        array, kind, first, size = jobs[job]
+        index = [
+            slice(None) if name in free else (z_place if name == "z" else place)
+            for name, place in zip(("z", "x", "y", "core"), coordinates)
+            if name in kind
         ]
-    return groups
-
-
-def place_kernel(marks, over_tensor, *refs):
-    groups, whole, sems = refs[: len(marks)], refs[len(marks)], refs[len(marks) + 1]
-    dp_place = lax.axis_index("dp")
-    tensor_place = lax.axis_index("tensor")
-    copies = []
-    for (dp_mask, tensor_mask), group in zip(marks, groups):
-        for position in range(group.shape[0]):
-            source = dp_place ^ (2 * position + dp_mask)
-            if over_tensor:
-                source = source * lax.axis_size("tensor") + (tensor_place ^ tensor_mask)
-            copies.append(
-                pltpu.make_async_copy(group.at[position], whole.at[source], sems.at[len(copies)])
+        return wholes[array].at[tuple(index) + (slice(None), pl.ds(first, size))]
+
+    def shard(job):
+        array, _, first, size = jobs[job]
+        return shards[array].at[:, pl.ds(first, size)]
+
+    own = []
+    for job in range(len(jobs)):
+        own.append(pltpu.make_async_copy(shard(job), spot(job, (), z), own_sems.at[job]))
+        own[-1].start()
+
+    def copies(job, step, receiving):
+        steps = lanes_of(jobs[job][1], depth_z)
+        lane, reach = steps[step]
+        free = [name for name, _ in steps[:step] if name != lane]
+        base = job * (2 * depth_z + 1)
+        pairs = []
+        if lane == "z":
+            for side, way in enumerate((1, -1)):
+                number = base + 2 * (reach - 1) + side
+                if receiving:
+                    block = z - way * reach
+                    condition = (block >= 0) & (block < depth_z)
+                    target = spot(job, free, z if step == 0 else block)
+                    source = target
+                else:
+                    block = z - way * (reach - 1)
+                    condition = (block >= 0) & (block < depth_z)
+                    condition &= (z + way >= 0) & (z + way < depth_z)
+                    target = spot(job, free, block)
+                    source = shard(job) if step == 0 else target
+                copy = pltpu.make_async_remote_copy(
+                    src_ref=source,
+                    dst_ref=target,
+                    send_sem=send_sems.at[number],
+                    recv_sem=receive_sems.at[number],
+                    device_id=beside(way, coordinates),
+                    device_id_type=pl.DeviceIdType.MESH,
+                )
+                pairs.append((condition, copy))
+            return pairs
+        number = base + 2 * (depth_z - 1) + ("x", "y", "core").index(lane)
+        target = spot(job, free, z)
+        copy = pltpu.make_async_remote_copy(
+            src_ref=shard(job) if step == 0 else target,
+            dst_ref=target,
+            send_sem=send_sems.at[number],
+            recv_sem=receive_sems.at[number],
+            device_id=partner(lane, 1, coordinates),
+            device_id_type=pl.DeviceIdType.MESH,
+        )
+        return [(None, copy)]
+
+    def perform(pairs, action):
+        for condition, copy in pairs:
+            if condition is None:
+                getattr(copy, action)()
+            else:
+                pl.when(condition)(getattr(copy, action))
+
+    copied = set()
+    for action, job, step in plan:
+        steps = lanes_of(jobs[job][1], depth_z)
+        if action == "start":
+            if steps[step][0] != steps[0][0] and job not in copied:
+                own[job].wait()
+                copied.add(job)
+            perform(copies(job, step, False), "start")
+        else:
+            perform(copies(job, step, True), "wait_recv")
+    for action, job, step in plan:
+        if action == "start":
+            perform(copies(job, step, False), "wait_send")
+
+
+def lanes_of(kind, depth_z):
+    steps = []
+    for name in kind:
+        steps += [(name, reach) for reach in range(1, depth_z if name == "z" else 2)]
+    return steps
+
+
+def spread_whole(shards, jobs, collective_id):
+    depth_z = lax.axis_size("dp") // 2
+    costs = []
+    for array, kind, first, size in jobs:
+        held, steps = shards[array].shape[0] * size, []
+        for lane in kind:
+            cost = 23.0 if lane != "core" else 3.4
+            steps += [(lane, held * 2e-6 * cost)] * (depth_z - 1 if lane == "z" else 1)
+            held *= depth_z if lane == "z" else 2
+        costs.append(steps)
+    plan = order_steps(costs)
+    sizes = {"z": depth_z, "x": 2, "y": 2, "core": 2}
+    kinds = {array: kind for array, kind, _, _ in jobs}
+    shapes = [
+        tuple(sizes[name] for name in ("z", "x", "y", "core") if name in kinds[array])
+        + shard.shape
+        for array, shard in enumerate(shards)
+    ]
+    numbers = len(jobs) * (2 * depth_z + 1)
+    wholes = pl.pallas_call(
+        partial(spread_kernel, plan, jobs, depth_z),
+        out_shape=tuple(jax.ShapeDtypeStruct(shape, jnp.bfloat16) for shape in shapes),
+        in_specs=[pl.BlockSpec(memory_space=pltpu.VMEM)] * len(shards),
+        out_specs=(pl.BlockSpec(memory_space=pl.ANY),) * len(shards),
+        scratch_shapes=[
+            pltpu.SemaphoreType.DMA((numbers,)),
+            pltpu.SemaphoreType.DMA((numbers,)),
+            pltpu.SemaphoreType.DMA((len(jobs),)),
+        ],
+        compiler_params=pltpu.CompilerParams(
+            collective_id=collective_id, has_side_effects=True, vmem_limit_bytes=24 * 2**20
+        ),
+    )(*shards)
+    return [whole.reshape(-1, whole.shape[-1]) for whole in wholes]
+
+
+BYTE_LANES = ("z", "x", "y", "core")
+MAIN_LANES = ("z", "x")
+
+
+def sum_kernel(plan, kinds, depth_z, *refs):
+    count = len(kinds)
+    grads, extra = refs[:count], refs[count]
+    outputs, totals = refs[count + 1 : 2 * count + 1], refs[2 * count + 1]
+    rest = list(refs[2 * count + 2 :])
+    coordinates = here()
+    places = dict(zip(BYTE_LANES, coordinates))
+    z = coordinates[0]
+    mirrored = depth_z - 1 - z
+    held, received, held_names = [], [], []
+    for kind in kinds:
+        held.append(rest.pop(0))
+        received.append({lane: rest.pop(0) for lane in kind})
+        held_names.append(names_held(kind))
+    squares, arrivals, send_sems, receive_sems, own_sems, tile_sems = rest
+    loads = []
+    for job, kind in enumerate(kinds):
+        spot = tuple(
+            slice(None) if name in held_names[job] else places[name]
+            for name in BYTE_LANES
+            if name in kind
+        )
+        loads.append(pltpu.make_async_copy(grads[job].at[spot], held[job], own_sems.at[job]))
+        loads[-1].start()
+    squares[...] = jnp.zeros_like(squares)
+    greet(False, depth_z, coordinates)
+
+    def chosen(job, step, lane_place):
+        steps = lanes_of(kinds[job], depth_z)
+        lane = steps[step][0]
+        done = [name for name, _ in steps[:step] if name != lane]
+        return [
+            lane_place if name == lane else (places[name] if name in done else slice(None))
+            for name in held_names[job]
+        ]
+
+    def slot(reach, side):
+        shared = (depth_z - 2) // 2
+        return reach - 1 if reach <= shared else shared + 2 * (reach - 1 - shared) + side
+
+    def copies(job, step, receiving):
+        kind = kinds[job]
+        lane, reach = lanes_of(kind, depth_z)[step]
+        base = job * (2 * depth_z + 1)
+        if lane == "z":
+            pairs = []
+            for side, depth in enumerate((z, mirrored)):
+                way = 1 - 2 * side
+                aim = depth_z - reach + depth
+                if side:
+                    aim = depth_z - 1 - aim
+                landing = received[job]["z"].at[slot(reach, side)]
+                number = base + 2 * (reach - 1) + side
+                source = landing if receiving else held[job].at[tuple(chosen(job, step, aim))]
+                copy = pltpu.make_async_remote_copy(
+                    src_ref=source,
+                    dst_ref=landing,
+                    send_sem=send_sems.at[number],
+                    recv_sem=receive_sems.at[number],
+                    device_id=beside(way, coordinates),
+                    device_id_type=pl.DeviceIdType.MESH,
+                )
+                condition = (depth >= 1) & (depth <= reach) if receiving else depth <= reach - 1
+                pairs.append((condition, copy))
+            return pairs
+        number = base + 2 * (depth_z - 1) + ("x", "y", "core").index(lane)
+        if step == 0:
+            spot = tuple(
+                1 - places[name] if name == lane else slice(None)
+                for name in BYTE_LANES
+                if name in kind
             )
-    for copy in copies:
-        copy.start()
-    for copy in copies:
-        copy.wait()
-
-
-def place(groups, over_tensor):
-    marks = [(dp_mask, tensor_mask) for dp_mask, tensor_mask, _ in groups]
-    arrays = [group for _, _, group in groups]
-    count = sum(array.shape[0] for array in arrays)
+            source = grads[job].at[spot]
+        else:
+            source = held[job].at[tuple(chosen(job, step, 1 - places[lane]))]
+        copy = pltpu.make_async_remote_copy(
+            src_ref=source,
+            dst_ref=received[job][lane],
+            send_sem=send_sems.at[number],
+            recv_sem=receive_sems.at[number],
+            device_id=partner(lane, 1, coordinates),
+            device_id_type=pl.DeviceIdType.MESH,
+        )
+        return [(None, copy)]
+
+    def add_pieces(job, step, lane_place, buffers, last):
+        steps = lanes_of(kinds[job], depth_z)
+        lane = steps[step][0]
+        done = [name for name, _ in steps[:step] if name != lane]
+        free = [name for name in BYTE_LANES if name in kinds[job] and name not in done + [lane]]
+        sizes = [depth_z if name == "z" else 2 for name in free]
+        pieces = 1
+        for size in sizes:
+            pieces *= size
+
+        def piece(index, carry):
+            spots, remainder = {}, index
+            for name, size in reversed(list(zip(free, sizes))):
+                spots[name] = remainder % size
+                remainder = remainder // size
+            mine = tuple(
+                spots[name] if name in spots else (lane_place if name == lane else places[name])
+                for name in held_names[job]
+            )
+            theirs = tuple(spots[name] for name in free)
+            target = held[job].at[mine] if mine else held[job]
+            arrived = [buffer.at[theirs] if theirs else buffer for buffer in buffers]
+            rows, columns = target.shape[-2:]
+
+            def row_step(number, inner):
+                part = pl.ds(pl.multiple_of(number * 16, 16), 16)
+                value = target[part, :].astype(jnp.float32)
+                for other in arrived:
+                    value = value + other[part, :].astype(jnp.float32)
+                if last:
+                    outputs[job][part, :] = value
+                    square = jnp.zeros((16, 128), jnp.float32)
+                    for first in range(0, columns, 128):
+                        square = square + value[:, first : first + 128] * value[:, first : first + 128]
+                    squares[...] += square
+                else:
+                    target[part, :] = to_low(value)
+                return inner
+
+            lax.fori_loop(0, rows // 16, row_step, 0)
+            return carry
+
+        if pieces == 1:
+            piece(0, 0)
+        else:
+            lax.fori_loop(0, pieces, piece, 0)
+
+    def accumulate(job, step):
+        steps = lanes_of(kinds[job], depth_z)
+        lane, reach = steps[step]
+        last = step == len(steps) - 1
+        if lane != "z":
+            add_pieces(job, step, places[lane], [received[job][lane]], last)
+            return
+        buffers = [received[job]["z"].at[slot(reach, side)] for side in range(2)]
+        if reach < depth_z - 1:
+            for side, depth in enumerate((z, mirrored)):
+                aim = depth_z - reach + depth - 1
+                if side:
+                    aim = depth_z - 1 - aim
+                pl.when((depth >= 1) & (depth <= reach))(
+                    partial(add_pieces, job, step, aim, [buffers[side]], False)
+                )
+            return
+        ends = (z == 0) | (mirrored == 0)
+        pl.when(jnp.logical_not(ends))(partial(add_pieces, job, step, z, buffers, last))
+        pl.when(z == 0)(partial(add_pieces, job, step, z, buffers[1:], last))
+        pl.when(mirrored == 0)(partial(add_pieces, job, step, z, buffers[:1], last))
+
+    def perform(pairs, action):
+        for condition, copy in pairs:
+            if condition is None:
+                getattr(copy, action)()
+            else:
+                pl.when(condition)(getattr(copy, action))
+
+    loaded = set()
+    for action, job, step in plan:
+        lane = lanes_of(kinds[job], depth_z)[step][0]
+        if job not in loaded and (action == "wait" or lane == "z"):
+            loads[job].wait()
+            loaded.add(job)
+        if action == "start":
+            perform(copies(job, step, False), "start")
+        else:
+            perform(copies(job, step, True), "wait_recv")
+            accumulate(job, step)
+    totals[...] = extra[...]
+    totals[0:8, :] += squares[0:8, :] + squares[8:16, :]
+    exchanges = [("core", 1), ("y", 1), ("x", 1)]
+    mask = 1
+    while mask < depth_z:
+        exchanges.append(("z", mask))
+        mask *= 2
+    tiles = []
+    for number, (lane, mask) in enumerate(exchanges):
+        tiles.append(
+            pltpu.make_async_remote_copy(
+                src_ref=arrivals.at[2 * number],
+                dst_ref=arrivals.at[2 * number + 1],
+                send_sem=tile_sems.at[2 * number],
+                recv_sem=tile_sems.at[2 * number + 1],
+                device_id=partner(lane, mask, coordinates),
+                device_id_type=pl.DeviceIdType.MESH,
+            )
+        )
+        arrivals[2 * number] = totals[...]
+        tiles[-1].start()
+        tiles[-1].wait_recv()
+        totals[...] += arrivals[2 * number + 1]
+    for copy in tiles:
+        copy.wait_send()
+    for action, job, step in plan:
+        if action == "start":
+            perform(copies(job, step, False), "wait_send")
+
+
+def names_held(kind):
+    return [name for name in BYTE_LANES if name in kind and (name == "z" or name != kind[0])]
+
+
+def sum_whole(grads, kinds, extra, collective_id):
+    depth_z = lax.axis_size("dp") // 2
+    sizes = {"z": depth_z, "x": 2, "y": 2, "core": 2}
+    jobs, arrays, shapes, scratch = [], [], [], []
+    for grad, kind in zip(grads, kinds):
+        names = [name for name in BYTE_LANES if name in kind]
+        pieces = 1
+        for name in names:
+            pieces *= sizes[name]
+        piece = (grad.shape[0] // pieces, grad.shape[1])
+        arrays.append(grad.reshape(tuple(sizes[name] for name in names) + piece))
+        shapes.append(jax.ShapeDtypeStruct(piece, jnp.float32))
+        steps, left = [], list(names)
+        scratch.append(
+            pltpu.VMEM(tuple(sizes[name] for name in names_held(kind)) + piece, jnp.bfloat16)
+        )
+        for lane in kind:
+            left.remove(lane)
+            rest = tuple(sizes[name] for name in left)
+            extent = piece[0] * piece[1]
+            for size in rest:
+                extent *= size
+            cost = 23.0 if lane != "core" else 3.4
+            steps += [(lane, extent * 2e-6 * cost)] * (depth_z - 1 if lane == "z" else 1)
+            lead = (2 * (depth_z - 1) - (depth_z - 2) // 2,) if lane == "z" else ()
+            scratch.append(pltpu.VMEM(lead + rest + piece, jnp.bfloat16))
+        jobs.append(steps)
+    plan = order_steps(jobs)
+    numbers = len(grads) * (2 * depth_z + 1)
+    tile = jax.ShapeDtypeStruct(extra.shape, jnp.float32)
+    rounds = 3 + len(bit_masks(depth_z))
     return pl.pallas_call(
-        partial(place_kernel, marks, over_tensor),
-        out_shape=jax.ShapeDtypeStruct((count,) + arrays[0].shape[1:], arrays[0].dtype),
-        in_specs=[pl.BlockSpec(memory_space=pl.ANY)] * len(arrays),
-        out_specs=pl.BlockSpec(memory_space=pl.ANY),
-        scratch_shapes=[pltpu.SemaphoreType.DMA((count,))],
-        cost_estimate=pl.CostEstimate(
-            flops=0, transcendentals=0, bytes_accessed=4 * count * arrays[0][0].size
+        partial(sum_kernel, plan, kinds, depth_z),
+        out_shape=tuple(shapes) + (tile,),
+        in_specs=[pl.BlockSpec(memory_space=pl.ANY)] * len(grads)
+        + [pl.BlockSpec(memory_space=pltpu.VMEM)],
+        out_specs=(pl.BlockSpec(memory_space=pltpu.VMEM),) * (len(grads) + 1),
+        scratch_shapes=scratch
+        + [
+            pltpu.VMEM((16, 128), jnp.float32),
+            pltpu.VMEM((2 * rounds, 16, 128), jnp.float32),
+            pltpu.SemaphoreType.DMA((numbers,)),
+            pltpu.SemaphoreType.DMA((numbers,)),
+            pltpu.SemaphoreType.DMA((len(grads),)),
+            pltpu.SemaphoreType.DMA((2 * rounds,)),
+        ],
+        compiler_params=pltpu.CompilerParams(
+            collective_id=collective_id, has_side_effects=True, vmem_limit_bytes=60 * 2**20
         ),
-    )(*arrays)
-
-
-def gather_all(shard):
-    return place(spread_all(shard), True)
-
-
-def gather_dp(shard):
-    return place(spread_dp(shard), False)
+    )(*arrays, extra)
 
 
 def take(value_entries, axis, index):
@@ -324,36 +816,6 @@
     return result
 
 
-def reduce_dp(addends):
-    size = lax.axis_size("dp")
-    place_dp = lax.axis_index("dp")
-    split = [a.reshape((size // 2, 2) + a.shape[1:]) for a in addends]
-    low = place_dp % 2
-    sent = to_low(total([take(a, 1, 1 - low) for a in split]))
-    addends = [take(a, 1, low) for a in split] + [swap(sent, "dp", 1)]
-    high = place_dp // 2
-    received = [
-        swap(to_low(total([take(a, 0, high ^ mask) for a in addends])), "dp", 2 * mask)
-        for mask in range(1, size // 2)
-    ]
-    return total([take(a, 0, high) for a in addends] + received)
-
-
-def reduce_all(grad):
-    tensor_size = lax.axis_size("tensor")
-    place_tensor = lax.axis_index("tensor")
-    grad = grad.reshape((lax.axis_size("dp"), tensor_size) + grad.shape[1:])
-    addends = [grad]
-    for mask in reversed(bit_masks(tensor_size)):
-        split = [
-            a.reshape((a.shape[0], a.shape[1] // 2, 2) + a.shape[2:]) for a in addends
-        ]
-        low = (place_tensor // mask) % 2
-        sent = to_low(total([take(a, 2, 1 - low) for a in split]))
-        addends = [take(a, 2, low) for a in split] + [swap(sent, "tensor", mask)]
-    return reduce_dp([a[:, 0] for a in addends])
-
-
 def add_everywhere(value_entries):
     for axis in ("tensor", "dp"):
         for mask in bit_masks(lax.axis_size(axis)):
@@ -363,7 +825,7 @@
 
 def gather_rows(value_entries):
     pieces = [value_entries]
-    for mask in bit_masks(lax.axis_size("tensor")):
+    for mask in reversed(bit_masks(lax.axis_size("tensor"))):
         pieces = pieces + [swap(piece, "tensor", mask) for piece in pieces]
     return jnp.concatenate(pieces, axis=0)
 
@@ -372,7 +834,7 @@
     size = lax.axis_size("tensor")
     rows = value_entries.shape[0] // size
     pieces = [to_low(value_entries[i * rows : (i + 1) * rows]) for i in range(size)]
-    for mask in reversed(bit_masks(size)):
+    for mask in bit_masks(size):
         half = len(pieces) // 2
         pieces = [
             pieces[i].astype(jnp.float32)
@@ -386,27 +848,566 @@
 sum_grads = total_lines
 
 
+def low_dot(left, right, left_dim, right_dim):
+    return lax.dot_general(
+        left, right, (((left_dim,), (right_dim,)), ((), ())), preferred_element_type=jnp.float32
+    )
+
+
+def three_parts(value_entries):
+    high = to_low(value_entries)
+    rest = value_entries - high.astype(jnp.float32)
+    middle = to_low(rest)
+    tail = to_low(rest - middle.astype(jnp.float32))
+    return jnp.concatenate([high, middle, tail, jnp.zeros_like(high)], axis=1)
+
+
+def sigmoid(value_entries):
+    return 0.5 * jnp.tanh(0.5 * value_entries) + 0.5
+
+
+def fold_rows(value_entries):
+    return jnp.sum(value_entries.reshape(-1, 8, value_entries.shape[1]), axis=0)
+
+
+def lower_ones():
+    rows = lax.broadcasted_iota(jnp.int32, (ssd_block, ssd_block), 0)
+    columns = lax.broadcasted_iota(jnp.int32, (ssd_block, ssd_block), 1)
+    return (rows >= columns).astype(jnp.float32)
+
+
+PROJ_WIDE = 2 * INNER + 2 * STATE + 128
+
+
+def step_terms(raw_steps, decay_refs):
+    shifted = raw_steps + decay_refs[1:2, :]
+    steps = softplus(shifted)
+    rates = -jnp.exp(decay_refs[0:1, :])
+    cumulative = jnp.dot(
+        lower_ones(), steps * rates, precision=deepest_tier, preferred_element_type=jnp.float32
+    )
+    return shifted, steps, rates, cumulative
+
+
+def wide(parts, spread_wide, pair):
+    columns = pl.ds(pl.multiple_of(pair * 2 * ssd_block, 2 * ssd_block), 2 * ssd_block)
+    return low_dot(parts, spread_wide[:, columns], 1, 0)
+
+
+def narrow(parts, spread_narrow, pair):
+    return low_dot(parts, spread_narrow[:, lanes(pair)], 1, 0)
+
+
+def head_tables():
+    part = jnp.arange(ssd_block) % MHEADS
+    valid = jnp.arange(ssd_block) < 3 * MHEADS
+    heads = jnp.arange(MHEADS)
+    hit = (part[:, None] == heads[None, :]) & valid[:, None]
+    spread_wide = to_low(jnp.repeat(hit, ssd_block, axis=1))
+    spread_narrow = to_low(jnp.repeat(hit, HEADDIM, axis=1))
+    chosen = to_low(
+        jnp.arange(INNER)[:, None] // HEADDIM == jnp.arange(ssd_block)[None, :]
+    )
+    later = jnp.where(
+        jnp.arange(ssd_block)[:, None] >= jnp.arange(2 * ssd_block)[None, :] % ssd_block, 0.0, -1e30
+    )
+    return spread_wide, spread_narrow, chosen, later
+
+
+def first_head():
+    return lax.broadcasted_iota(jnp.int32, (ssd_block, ssd_block), 1) < HEADDIM
+
+
+def both_heads(value_entries):
+    mask = first_head()
+    zeros = jnp.zeros_like(value_entries)
+    return jnp.concatenate(
+        [jnp.where(mask, value_entries, zeros), jnp.where(mask, zeros, value_entries)], axis=0
+    )
+
+
+def gap_decay(cumulative_wide, cumulative_rows, later):
+    return jnp.exp((cumulative_wide - cumulative_rows) + later[...])
+
+
+def store_turned(cumulative, turned_ref):
+    blank = jnp.zeros((ssd_block, ssd_block - MHEADS), jnp.float32)
+    turned_ref[...] = jnp.concatenate([cumulative, blank], axis=1).T
+
+
+def turned_rows(turned_ref, pair):
+    return jnp.concatenate(
+        [turned_ref[pl.ds(2 * pair, 1), :], turned_ref[pl.ds(2 * pair + 1, 1), :]], axis=1
+    )
+
+
+def lanes(block):
+    return pl.ds(pl.multiple_of(block * ssd_block, ssd_block), ssd_block)
+
+
+def convolve(padded_ref, taps_ref, block):
+    columns = lanes(block)
+    result = taps_ref[0:1, columns] * padded_ref[5 : 5 + ssd_block, columns]
+    for tap in range(1, 4):
+        result = result + taps_ref[tap : tap + 1, columns] * padded_ref[
+            5 + tap : 5 + tap + ssd_block, columns
+        ]
+    return result
+
+
+def middle_kernel(
+    projected,
+    taps,
+    skip,
+    decay,
+    gain,
+    spread_wide,
+    spread_narrow,
+    later,
+    middle,
+    outcome,
+    starts,
+    padded,
+    turned,
+    state,
+    gated,
+):
+    chunk = pl.program_id(0)
+    streams_extent = INNER + 2 * STATE
+
+    @pl.when(chunk == 0)
+    def _():
+        padded[0:8, :] = jnp.zeros((8, streams_extent), jnp.float32)
+        state[...] = jnp.zeros_like(state)
+
+    @pl.when(chunk > 0)
+    def _():
+        padded[0:8, :] = padded[ssd_block : ssd_block + 8, :]
+
+    padded[8 : 8 + ssd_block, :] = projected[:, INNER : INNER + streams_extent]
+    _, steps, _, cumulative = step_terms(
+        projected[:, INNER + streams_extent : INNER + streams_extent + MHEADS], decay
+    )
+    store_turned(cumulative, turned)
+    step_parts = three_parts(steps)
+    cumulative_parts = three_parts(cumulative)
+
+    def active(block):
+        convolved = convolve(padded, taps, block)
+        return convolved * sigmoid(convolved)
+
+    in_low = to_low(active(INNER // ssd_block))
+    out_low = to_low(active(INNER // ssd_block + 1))
+    affinity = low_dot(out_low, in_low, 1, 1)
+    affinity = jnp.concatenate([affinity, affinity], axis=1)
+    mask = first_head()
+
+    def pair_step(pair, square_sum):
+        columns = lanes(pair)
+        inputs = active(pair)
+        weighted = inputs * narrow(step_parts, spread_narrow, pair)
+        cumulative_wide = wide(cumulative_parts, spread_wide, pair)
+        mixing = to_low(affinity * gap_decay(cumulative_wide, turned_rows(turned, pair), later))
+        within = low_dot(mixing, both_heads(to_low(weighted)), 1, 0)
+        cumulative_here = jnp.where(
+            mask, cumulative_wide[:, :ssd_block], cumulative_wide[:, ssd_block:]
+        )
+        last = cumulative_here[ssd_block - 1 :, :]
+        held = state[:, columns]
+        starts[0, :, columns] = held
+        across = jnp.exp(cumulative_here) * low_dot(out_low, to_low(held), 1, 0)
+        to_end = to_low(weighted * jnp.exp(last - cumulative_here))
+        state[:, columns] = jnp.exp(last) * held + low_dot(in_low, to_end, 0, 0)
+        result = within + across + inputs * skip[:, columns]
+        outcome[:, columns] = result
+        gate = projected[:, columns]
+        product = result * (gate * sigmoid(gate))
+        gated[:, columns] = product
+        return square_sum + product * product
+
+    square_sum = lax.fori_loop(
+        0,
+        INNER // ssd_block,
+        pair_step,
+        jnp.zeros((ssd_block, ssd_block), jnp.float32),
+        unroll=4,
+    )
+    scale = lax.rsqrt(jnp.sum(square_sum, axis=1, keepdims=True) * (1.0 / INNER) + norm_eps)
+
+    def scale_step(pair, carry):
+        columns = lanes(pair)
+        middle[:, columns] = to_low(gated[:, columns] * scale * gain[:, columns])
+        return carry
+
+    lax.fori_loop(0, INNER // ssd_block, scale_step, 0, unroll=4)
+
+
+def middle_slope_kernel(
+    projected,
+    earlier,
+    outcome,
+    starts,
+    slope,
+    taps,
+    skip,
+    decay,
+    gain,
+    spread_wide,
+    spread_narrow,
+    chosen_heads,
+    masked,
+    slope_projected,
+    slope_taps,
+    slope_skip,
+    slope_gain,
+    slope_decay,
+    padded,
+    turned,
+    slope_state,
+    slope_conv,
+    slope_affinity,
+    slope_maps,
+    slope_cumulative,
+    slope_steps,
+):
+    chunk = pl.num_programs(0) - 1 - pl.program_id(0)
+    streams_extent = INNER + 2 * STATE
+    pairs = INNER // ssd_block
+
+    @pl.when(pl.program_id(0) == 0)
+    def _():
+        slope_state[...] = jnp.zeros_like(slope_state)
+        slope_conv[ssd_block : ssd_block + 8, :] = jnp.zeros((8, streams_extent), jnp.float32)
+        slope_taps[...] = jnp.zeros_like(slope_taps)
+        slope_skip[...] = jnp.zeros_like(slope_skip)
+        slope_gain[...] = jnp.zeros_like(slope_gain)
+        slope_decay[...] = jnp.zeros_like(slope_decay)
+
+    @pl.when(pl.program_id(0) > 0)
+    def _():
+        slope_conv[ssd_block : ssd_block + 8, :] = slope_conv[0:8, :]
+
+    @pl.when(chunk == 0)
+    def _():
+        padded[0:8, :] = jnp.zeros((8, streams_extent), jnp.float32)
+
+    @pl.when(chunk > 0)
+    def _():
+        padded[0:8, :] = earlier[:, INNER : INNER + streams_extent]
+
+    padded[8 : 8 + ssd_block, :] = projected[:, INNER : INNER + streams_extent]
+    slope_affinity[...] = jnp.zeros_like(slope_affinity)
+    slope_maps[...] = jnp.zeros_like(slope_maps)
+    slope_cumulative[...] = jnp.zeros_like(slope_cumulative)
+    slope_steps[...] = jnp.zeros_like(slope_steps)
+    shifted, steps, rates, cumulative = step_terms(
+        projected[:, INNER + streams_extent : INNER + streams_extent + MHEADS], decay
+    )
+    store_turned(cumulative, turned)
+    step_parts = three_parts(steps)
+    cumulative_parts = three_parts(cumulative)
+
+    def silu_pair(value_entries):
+        share = sigmoid(value_entries)
+        return value_entries * share, share * (1.0 + value_entries * (1.0 - share))
+
+    def pull_convolved(block, slope_block):
+        columns = lanes(block)
+        slope_conv[0:ssd_block, columns] = slope_block
+        result = taps[3:4, columns] * slope_block
+        for tap in range(3):
+            reach = 3 - tap
+            result = result + taps[tap : tap + 1, columns] * slope_conv[
+                reach : reach + ssd_block, columns
+            ]
+        for tap in range(4):
+            slope_taps[tap, :, columns] += fold_rows(
+                slope_block * padded[5 + tap : 5 + tap + ssd_block, columns]
+            )
+        slope_projected[:, lanes(block + pairs)] = to_low(result)
+
+    in_map, in_pull = silu_pair(convolve(padded, taps, pairs))
+    out_map, out_pull = silu_pair(convolve(padded, taps, pairs + 1))
+    in_low, out_low = to_low(in_map), to_low(out_map)
+    affinity = low_dot(out_low, in_low, 1, 1)
+    affinity = jnp.concatenate([affinity, affinity], axis=1)
+    mask = first_head()
+
+    def sums_step(pair, sums):
+        columns = lanes(pair)
+        gate = projected[:, columns]
+        product = outcome[:, columns] * (gate * sigmoid(gate))
+        return (
+            sums[0] + product * product,
+            sums[1] + product * (slope[:, columns] * gain[:, columns]),
+        )
+
+    blank = jnp.zeros((ssd_block, ssd_block), jnp.float32)
+    squares, crossed = lax.fori_loop(0, pairs, sums_step, (blank, blank), unroll=2)
+    scale = lax.rsqrt(jnp.sum(squares, axis=1, keepdims=True) * (1.0 / INNER) + norm_eps)
+    pulled = scale * scale * scale * (jnp.sum(crossed, axis=1, keepdims=True) * (1.0 / INNER))
+
+    def pair_step(pair, carry):
+        columns = lanes(pair)
+        gate, total_here = projected[:, columns], outcome[:, columns]
+        gate_value, gate_pull = silu_pair(gate)
+        product = total_here * gate_value
+        slope_here = slope[:, columns]
+        slope_gain[:, columns] += fold_rows(slope_here * product * scale)
+        slope_product = scale * (slope_here * gain[:, columns]) - product * pulled
+        slope_out = slope_product * gate_value
+        slope_projected[:, columns] = to_low(slope_product * total_here * gate_pull)
+        inputs, inputs_pull = silu_pair(convolve(padded, taps, pair))
+        slope_skip[:, columns] += fold_rows(slope_out * inputs)
+        skip_here = skip[:, columns]
+        scanned = total_here - inputs * skip_here
+        steps_here = narrow(step_parts, spread_narrow, pair)
+        weighted = inputs * steps_here
+        weighted_low = to_low(weighted)
+        slope_low = to_low(slope_out)
+        cumulative_wide = wide(cumulative_parts, spread_wide, pair)
+        gaps = gap_decay(cumulative_wide, turned_rows(turned, pair), masked)
+        mixing = to_low(affinity * gaps)
+        slope_mixing = low_dot(slope_low, both_heads(weighted_low), 1, 1)
+        slope_gaps = slope_mixing * gaps
+        slope_affinity[...] += slope_gaps[:, :ssd_block] + slope_gaps[:, ssd_block:]
+        turned_back = low_dot(mixing, slope_low, 0, 0)
+        slope_weighted = jnp.where(mask, turned_back[:ssd_block], turned_back[ssd_block:])
+        cumulative_here = jnp.where(
+            mask, cumulative_wide[:, :ssd_block], cumulative_wide[:, ssd_block:]
+        )
+        last = cumulative_here[ssd_block - 1 :, :]
+        decayed = jnp.exp(last)
+        held = starts[0, :, columns]
+        held_low = to_low(held)
+        slope_across = to_low(slope_out * jnp.exp(cumulative_here))
+        slope_maps[1] += low_dot(slope_across, held_low, 1, 1)
+        later = slope_state[:, columns]
+        later_low = to_low(later)
+        to_end = jnp.exp(last - cumulative_here)
+        carried = to_low(weighted * to_end)
+        slope_carried = low_dot(in_low, later_low, 1, 0)
+        slope_maps[0] += low_dot(carried, later_low, 1, 1)
+        slope_state[:, columns] = decayed * later + low_dot(out_low, slope_across, 0, 0)
+        slope_within = slope_weighted
+        slope_weighted = slope_weighted + slope_carried * to_end
+        carried_slope = slope_carried * carried.astype(jnp.float32)
+        ends = jnp.sum(carried_slope, axis=0, keepdims=True) + decayed * jnp.sum(
+            later * held, axis=0, keepdims=True
+        )
+        rows = lax.broadcasted_iota(jnp.int32, (ssd_block, ssd_block), 0)
+        slope_gathered = (
+            slope_low.astype(jnp.float32) * scanned
+            - weighted_low.astype(jnp.float32) * slope_within
+            - carried_slope
+            + jnp.where(rows == ssd_block - 1, ends, 0.0)
+        )
+        chosen = chosen_heads[lanes(pair), :]
+
+        def head_sums(value_entries):
+            high = to_low(value_entries)
+            rest = to_low(value_entries - high.astype(jnp.float32))
+            return low_dot(high, chosen, 1, 0) + low_dot(rest, chosen, 1, 0)
+
+        slope_cumulative[...] += head_sums(slope_gathered)
+        slope_steps[...] += head_sums(slope_weighted * inputs)
+        slope_inputs = slope_out * skip_here + slope_weighted * steps_here
+        pull_convolved(pair, slope_inputs * inputs_pull)
+        return carry
+
+    lax.fori_loop(0, pairs, pair_step, 0, unroll=2)
+    affinity_low = to_low(slope_affinity[...])
+    slope_in = slope_maps[0] + low_dot(affinity_low, out_low, 0, 0)
+    slope_out_map = slope_maps[1] + low_dot(affinity_low, in_low, 1, 0)
+    pull_convolved(pairs, slope_in * in_pull)
+    pull_convolved(pairs + 1, slope_out_map * out_pull)
+    slope_changes = lax.dot_general(
+        lower_ones(),
+        slope_cumulative[...],
+        (((0,), (0,)), ((), ())),
+        precision=deepest_tier,
+        preferred_element_type=jnp.float32,
+    )[:, :MHEADS]
+    slope_step = slope_steps[:, :MHEADS] + slope_changes * rates
+    slope_raw = slope_step * sigmoid(shifted)
+    slope_decay[0] += fold_rows(slope_changes * steps) * rates
+    slope_decay[1] += fold_rows(slope_raw)
+    slope_projected[:, INNER + streams_extent :] = jnp.concatenate(
+        [to_low(slope_raw), jnp.zeros((ssd_block, 128 - MHEADS), jnp.bfloat16)], axis=1
+    )
+
+
+def fixed(shape):
+    return pl.BlockSpec(shape, lambda chunk: (0,) * len(shape))
+
+
+def middle_forward(projected, smalls):
+    conv_taps, skip_gain, a_log, dt_bias, gated_gain = smalls
+    spread_wide, spread_narrow, chosen, later = head_tables()
+    extent, columns = projected.shape
+    chunks = extent // ssd_block
+    streams_extent = INNER + 2 * STATE
+    return pl.pallas_call(
+        middle_kernel,
+        grid=(chunks,),
+        out_shape=(
+            jax.ShapeDtypeStruct((extent, INNER), jnp.bfloat16),
+            jax.ShapeDtypeStruct((extent, INNER), jnp.float32),
+            jax.ShapeDtypeStruct((chunks, STATE, INNER), jnp.float32),
+        ),
+        in_specs=[
+            pl.BlockSpec((ssd_block, columns), lambda chunk: (chunk, 0)),
+            fixed((4, streams_extent)),
+            fixed((1, INNER)),
+            fixed((2, MHEADS)),
+            fixed((1, INNER)),
+            fixed(spread_wide.shape),
+            fixed(spread_narrow.shape),
+            fixed(later.shape),
+        ],
+        out_specs=(
+            pl.BlockSpec((ssd_block, INNER), lambda chunk: (chunk, 0)),
+            pl.BlockSpec((ssd_block, INNER), lambda chunk: (chunk, 0)),
+            pl.BlockSpec((1, STATE, INNER), lambda chunk: (chunk, 0, 0)),
+        ),
+        scratch_shapes=[
+            pltpu.VMEM((ssd_block + 8, streams_extent), jnp.float32),
+            pltpu.VMEM((ssd_block, ssd_block), jnp.float32),
+            pltpu.VMEM((STATE, INNER), jnp.float32),
+            pltpu.VMEM((ssd_block, INNER), jnp.float32),
+        ],
+        compiler_params=pltpu.CompilerParams(vmem_limit_bytes=48 * 2**20),
+        cost_estimate=pl.CostEstimate(
+            flops=2 * 10**10, transcendentals=4 * 10**6, bytes_accessed=20 * 10**6
+        ),
+    )(
+        projected,
+        conv_taps,
+        skip_gain.reshape(1, INNER),
+        jnp.stack([a_log, dt_bias]),
+        gated_gain.reshape(1, INNER),
+        spread_wide,
+        spread_narrow,
+        later,
+    )
+
+
+def middle_backward(projected, outcome, starts, slope, smalls):
+    conv_taps, skip_gain, a_log, dt_bias, gated_gain = smalls
+    spread_wide, spread_narrow, chosen, later = head_tables()
+    extent, columns = projected.shape
+    chunks = extent // ssd_block
+    streams_extent = INNER + 2 * STATE
+
+    def back(chunk):
+        return (chunks - 1 - chunk, 0)
+
+    slope_projected, slope_taps, slope_skip, slope_gain, slope_decay = pl.pallas_call(
+        middle_slope_kernel,
+        grid=(chunks,),
+        out_shape=(
+            jax.ShapeDtypeStruct((extent, columns), jnp.bfloat16),
+            jax.ShapeDtypeStruct((4, 8, streams_extent), jnp.float32),
+            jax.ShapeDtypeStruct((8, INNER), jnp.float32),
+            jax.ShapeDtypeStruct((8, INNER), jnp.float32),
+            jax.ShapeDtypeStruct((2, 8, MHEADS), jnp.float32),
+        ),
+        in_specs=[
+            pl.BlockSpec((ssd_block, columns), back),
+            pl.BlockSpec(
+                (8, columns),
+                lambda chunk: (jnp.maximum((chunks - 1 - chunk) * (ssd_block // 8) - 1, 0), 0),
+            ),
+            pl.BlockSpec((ssd_block, INNER), back),
+            pl.BlockSpec((1, STATE, INNER), lambda chunk: (chunks - 1 - chunk, 0, 0)),
+            pl.BlockSpec((ssd_block, INNER), back),
+            fixed((4, streams_extent)),
+            fixed((1, INNER)),
+            fixed((2, MHEADS)),
+            fixed((1, INNER)),
+            fixed(spread_wide.shape),
+            fixed(spread_narrow.shape),
+            fixed(chosen.shape),
+            fixed(later.shape),
+        ],
+        out_specs=(
+            pl.BlockSpec((ssd_block, columns), back),
+            fixed((4, 8, streams_extent)),
+            fixed((8, INNER)),
+            fixed((8, INNER)),
+            fixed((2, 8, MHEADS)),
+        ),
+        scratch_shapes=[
+            pltpu.VMEM((ssd_block + 8, streams_extent), jnp.float32),
+            pltpu.VMEM((ssd_block, ssd_block), jnp.float32),
+            pltpu.VMEM((STATE, INNER), jnp.float32),
+            pltpu.VMEM((ssd_block + 8, streams_extent), jnp.float32),
+            pltpu.VMEM((ssd_block, ssd_block), jnp.float32),
+            pltpu.VMEM((2, ssd_block, STATE), jnp.float32),
+            pltpu.VMEM((ssd_block, ssd_block), jnp.float32),
+            pltpu.VMEM((ssd_block, ssd_block), jnp.float32),
+        ],
+        compiler_params=pltpu.CompilerParams(vmem_limit_bytes=48 * 2**20),
+        cost_estimate=pl.CostEstimate(
+            flops=5 * 10**10, transcendentals=8 * 10**6, bytes_accessed=30 * 10**6
+        ),
+    )(
+        projected,
+        projected,
+        outcome,
+        starts,
+        slope,
+        conv_taps,
+        skip_gain.reshape(1, INNER),
+        jnp.stack([a_log, dt_bias]),
+        gated_gain.reshape(1, INNER),
+        spread_wide,
+        spread_narrow,
+        chosen,
+        later,
+    )
+    slope_decay = jnp.sum(slope_decay, axis=1)
+    return (
+        slope_projected,
+        (
+            jnp.sum(slope_taps, axis=1),
+            jnp.sum(slope_skip, axis=0),
+            slope_decay[0],
+            slope_decay[1],
+            jnp.sum(slope_gain, axis=0),
+        ),
+    )
+
+
+Y_LANE = (("tensor", 2),)
+
+
 def mixer_forward(value_entries, w_in, exit_matrix, block_gain, smalls):
     rescaled_rows, rescale_grad = jax.vjp(root_mean_rescale, value_entries, block_gain)
     normed_low = to_low(rescaled_rows)
     projected = matmul_apply(normed_low, w_in)
-    middle, middle_pull = jax.vjp(mixer_middle, projected, *smalls)
-    middle_low = to_low(middle)
+    middle_low, outcome, starts = middle_forward(projected, smalls)
     return (
         value_entries + matmul_apply(middle_low, exit_matrix),
-        (rescale_grad, normed_low, middle_pull, middle_low),
-    )
-
-
-def mixer_backward(slope_emitted, kept, w_in, exit_matrix):
-    rescale_grad, normed_low, middle_pull, middle_low = kept
+        (rescale_grad, normed_low, (projected, outcome, starts), middle_low),
+    )
+
+
+def mixer_backward(conductor, last, slope_emitted, kept, w_in, exit_matrix, smalls):
+    rescale_grad, normed_low, middle_kept, middle_low = kept
     grad_low = to_low(slope_emitted)
-    slope_exit_matrix = product_tn(middle_low, grad_low)
-    pulled = middle_pull(product_nt(grad_low, exit_matrix))
-    grad_proj = to_low(pulled[0])
-    grad_w_in = product_tn(normed_low, grad_proj)
+    slope_exit_matrix = to_low(product_tn(middle_low, grad_low))
+    job_out = conductor.add(Summing(slope_exit_matrix, True))
+    slope_middle = product_nt(grad_low, exit_matrix)
+    slope_middle = conductor.tick(after(slope_middle, [slope_exit_matrix]), 7.0)
+    grad_proj, slope_smalls = middle_backward(*middle_kept, slope_middle, smalls)
+    grad_proj = conductor.tick(grad_proj, 48.0, limit=0 if last else 5)
+    grad_w_in = to_low(product_tn(normed_low, grad_proj))
+    job_in = conductor.add(Summing(grad_w_in, True))
+    grad_proj = conductor.tick(after(grad_proj, [grad_w_in]), 7.0, limit=0 if last else 5)
     grad_values, slope_scale = rescale_grad(product_nt(grad_proj, w_in))
-    return (grad_values + slope_emitted, grad_w_in, slope_exit_matrix, slope_scale, pulled[1:])
+    slope_value = conductor.tick(grad_values + slope_emitted, 10.0, Y_LANE, limit=0 if last else 5)
+    return (slope_value, slope_scale, slope_smalls, (job_out, job_in))
 
 
 def causal_scores(queries, key_rows):
@@ -420,11 +1421,9 @@
 def apply_heads(latent_holder, heed_scale, triple_matrix, exit_matrix):
     rescaled_rows, rescale_grad = jax.vjp(root_mean_rescale, latent_holder, heed_scale)
     rows_low = gather_rows(to_low(rescaled_rows))
-    triple = to_low(
-        jnp.einsum("td,dsh->tsh", rows_low, triple_matrix, preferred_element_type=jnp.float32)
-    )
+    triple = to_low(matmul_apply(rows_low, triple_matrix))
     groups = rows_low.shape[0] // MAX_PIECES
-    heads_here = triple_matrix.shape[2] // HD
+    heads_here = triple_matrix.shape[1] // (3 * HD)
     split_heads = triple.reshape(groups, MAX_PIECES, 3, heads_here, HD)
     queries, key_rows, value_rows = (
         split_heads[:, :, 0],
@@ -446,10 +1445,10 @@
     )
 
 
-def apply_heads_grad(slope_emitted, kept, triple_matrix, exit_matrix):
+def apply_heads_grad(conductor, slope_emitted, kept, triple_matrix, exit_matrix):
     rescale_grad, rows_low, queries, key_rows, value_rows, log_total, heads_output = kept
-    grad_rows = gather_grads(to_low(slope_emitted))
-    slope_exit_matrix = product_tn(grad_rows, heads_output)
+    grad_rows = conductor.tick(gather_grads(to_low(slope_emitted)), 12.0, Y_LANE)
+    slope_exit_matrix = to_low(product_tn(grad_rows, heads_output))
     grad_attended = to_low(matmul_apply(grad_rows, exit_matrix)).reshape(queries.shape)
     weights_soft = jnp.exp(causal_scores(queries, key_rows) - log_total)
     grad_values = jnp.einsum(
@@ -468,47 +1467,52 @@
         "ghqk,gqhd->gkhd", grad_scores, queries, preferred_element_type=jnp.float32
     ) * HD ** (-0.5)
     grad_triple = to_low(
-        jnp.stack([grad_queries, grad_keys, grad_values], axis=2).reshape(rows_low.shape[0], 3, -1)
-    )
-    slope_triple_matrix = jnp.einsum(
-        "td,tsh->dsh", rows_low, grad_triple, preferred_element_type=jnp.float32
-    )
-    slope_rescaled = sum_grads(
-        jnp.einsum("tsh,dsh->td", grad_triple, triple_matrix, preferred_element_type=jnp.float32)
+        jnp.stack([grad_queries, grad_keys, grad_values], axis=2).reshape(rows_low.shape[0], -1)
+    )
+    grad_triple = conductor.tick(after(grad_triple, [slope_exit_matrix]), 10.0, Y_LANE)
+    slope_rescaled = sum_grads(product_nt(grad_triple, triple_matrix))
+    slope_triple_matrix = to_low(product_tn(rows_low, grad_triple))
+    job_exit = conductor.add(Summing(slope_exit_matrix, False))
+    job_triple = conductor.add(Summing(slope_triple_matrix, False))
+    slope_rescaled = conductor.tick(
+        after(slope_rescaled, [slope_triple_matrix]), 10.0, Y_LANE
     )
     gradient_holder, slope_scale = rescale_grad(slope_rescaled)
-    return (gradient_holder + slope_emitted, slope_triple_matrix, slope_exit_matrix, slope_scale)
+    return (gradient_holder + slope_emitted, slope_scale, job_triple, job_exit)
 
 
 def swiglu(both):
-    return jax.nn.silu(both[:, 0]) * both[:, 1]
+    half = both.shape[1] // 2
+    return jax.nn.silu(both[:, :half]) * both[:, half:]
 
 
 def perceptron_apply(latent_holder, perceptron_scale, lift_matrix, lower_matrix):
     rescaled_rows, rescale_grad = jax.vjp(root_mean_rescale, latent_holder, perceptron_scale)
     rows_low = gather_rows(to_low(rescaled_rows))
-    latent_state, act_pull = jax.vjp(
-        swiglu, jnp.einsum("td,dsf->tsf", rows_low, lift_matrix, preferred_element_type=jnp.float32)
-    )
+    latent_state, act_pull = jax.vjp(swiglu, matmul_apply(rows_low, lift_matrix))
     latent_merged = to_low(latent_state)
     outcome = latent_holder + total_lines(product_nt(latent_merged, lower_matrix))
     return (outcome, (rescale_grad, rows_low, act_pull, latent_merged))
 
 
-def perceptron_grad(slope_emitted, kept, lift_matrix, lower_matrix):
+def perceptron_grad(conductor, slope_emitted, kept, lift_matrix, lower_matrix):
     rescale_grad, rows_low, act_pull, latent_merged = kept
-    grad_rows = gather_grads(to_low(slope_emitted))
-    slope_lower_matrix = product_tn(grad_rows, latent_merged)
+    grad_rows = conductor.tick(gather_grads(to_low(slope_emitted)), 13.0, Y_LANE)
+    slope_lower_matrix = to_low(product_tn(grad_rows, latent_merged))
+    job_lower = conductor.add(Summing(slope_lower_matrix, False))
+    grad_rows = conductor.tick(after(grad_rows, [slope_lower_matrix]), 2.0, Y_LANE)
     (grad_both,) = act_pull(matmul_apply(grad_rows, lower_matrix))
-    grad_both = to_low(grad_both)
-    slope_lift_matrix = jnp.einsum(
-        "td,tsf->dsf", rows_low, grad_both, preferred_element_type=jnp.float32
-    )
-    slope_rescaled = sum_grads(
-        jnp.einsum("tsf,dsf->td", grad_both, lift_matrix, preferred_element_type=jnp.float32)
-    )
+    grad_both = conductor.tick(to_low(grad_both), 4.0, Y_LANE)
+    slope_rescaled = sum_grads(product_nt(grad_both, lift_matrix))
+    half = grad_both.shape[1] // 2
+    slope_lifts = [
+        to_low(product_tn(rows_low, grad_both[:, :half])),
+        to_low(product_tn(rows_low, grad_both[:, half:])),
+    ]
+    slope_lifts = [conductor.add(Summing(slope, False)) for slope in slope_lifts]
+    slope_rescaled = conductor.tick(slope_rescaled, 14.0, Y_LANE)
     gradient_holder, slope_scale = rescale_grad(slope_rescaled)
-    return (gradient_holder + slope_emitted, slope_lift_matrix, slope_lower_matrix, slope_scale)
+    return (gradient_holder + slope_emitted, slope_scale, job_lower, slope_lifts)
 
 
 def body(
@@ -556,7 +1560,60 @@
             jnp.pad(tail, (0, 16 * BYTE_WIDTH - tail.shape[0])).reshape(16, BYTE_WIDTH),
         ]
     )
-    mixed_whole = gather_all(mixed)
+    mixed_rows = mixed.shape[0]
+
+    def wide_in(layer):
+        low = to_low(mamba_in[layer])
+        return jnp.pad(low, ((0, 0), (0, PROJ_WIDE - low.shape[1])))
+
+    conductor = Conductor()
+    exact_tiles = mamba_in.shape[1] % 16 == 0
+    shards = [
+        mixed,
+        wide_in(0),
+        to_low(mamba_out[0]),
+        to_low(route_proj),
+        to_low(heed_triple_matrix).reshape(heed_triple_matrix.shape[0], -1),
+        to_low(heed_exit_matrix).T,
+        to_low(lifting_matrix).reshape(lifting_matrix.shape[0], -1),
+        to_low(lowering_matrix).T,
+        wide_in(1),
+        to_low(mamba_out[1]),
+    ]
+    kinds = [BYTE_LANES] * 4 + [MAIN_LANES] * 4 + [BYTE_LANES] * 2
+    if exact_tiles:
+        fan, late = MAIN_LANES, MAIN_LANES[::-1]
+        in_first, in_last = 18 * 128, PROJ_WIDE - 18 * 128
+        half_route = route_proj.shape[1] // 2
+        half_lift = shards[6].shape[1] // 2
+        jobs = [
+            (3, BYTE_LANES, half_route, half_route),
+            (9, BYTE_LANES, 0, BYTE_WIDTH),
+            (8, BYTE_LANES, 0, in_first),
+            (0, BYTE_LANES, 0, BYTE_WIDTH),
+            (1, BYTE_LANES, in_first, in_last),
+            (2, BYTE_LANES, 0, BYTE_WIDTH),
+            (8, BYTE_LANES, in_first, in_last),
+            (4, fan, 0, shards[4].shape[1]),
+            (1, BYTE_LANES, 0, in_first),
+            (6, fan, half_lift, half_lift),
+            (3, BYTE_LANES, 0, half_route),
+            (7, fan, 0, shards[7].shape[1]),
+            (5, late, 0, shards[5].shape[1]),
+            (6, late, 0, half_lift),
+        ]
+        wholes = spread_whole(shards, jobs, 0)
+    else:
+        wholes = [
+            lax.all_gather(
+                shard, ("dp", "tensor") if kind == BYTE_LANES else "dp", axis=0, tiled=True
+            )
+            for shard, kind in zip(shards, kinds)
+        ]
+    mixed_whole = wholes[0]
+    full_in, full_out, full_route = [wholes[1], wholes[8]], [wholes[2], wholes[9]], wholes[3]
+    triple_whole, heed_exit_whole, lift_matrix_whole, lower_matrix_whole = wholes[4:8]
+    mixed_whole = mixed_whole.reshape(devices, mixed_rows, BYTE_WIDTH)
     full_tables = (
         mixed_whole[:, : 2 * table_rows]
         .reshape(devices, 2, table_rows, BYTE_WIDTH)
@@ -567,21 +1624,6 @@
     full_small = tails[:, :small_here].reshape(-1)
     pairs = tails[:, small_here : small_here + 2].astype(jnp.float32)
     byte_count = jnp.sum(pairs[:, 0] * 16.0 + pairs[:, 1])
-    full_in = [None, None]
-    full_out = [None, None]
-    full_in[0] = gather_all(to_low(mamba_in[0])).reshape(BYTE_WIDTH, -1)
-    full_out[0] = gather_all(to_low(mamba_out[0])).reshape(INNER, BYTE_WIDTH)
-    full_route = gather_all(to_low(route_proj)).reshape(BYTE_WIDTH, -1)
-    triple_whole = gather_dp(to_low(heed_triple_matrix)).reshape(
-        (CORE_WIDTH,) + heed_triple_matrix.shape[1:]
-    )
-    heed_exit_whole = gather_dp(to_low(heed_exit_matrix).T).reshape(CORE_WIDTH, -1)
-    lift_matrix_whole = gather_dp(to_low(lifting_matrix)).reshape(
-        (CORE_WIDTH,) + lifting_matrix.shape[1:]
-    )
-    lower_matrix_whole = gather_dp(to_low(lowering_matrix).T).reshape(CORE_WIDTH, -1)
-    full_in[1] = gather_all(to_low(mamba_in[1])).reshape(BYTE_WIDTH, -1)
-    full_out[1] = gather_all(to_low(mamba_out[1])).reshape(INNER, BYTE_WIDTH)
     (
         block_gains,
         gated_gains,
@@ -647,24 +1689,32 @@
     grad_logits = to_low((jnp.exp(logits - log_total) - onehot_out) * counted / byte_count)
     grad_table_out = product_tn(grad_logits, head_low)
     grad_final, grad_head_gain = head_pull(matmul_apply(grad_logits, full_tables[1]))
-    slope_unpacked, grad_in_dec, grad_out_dec, grad_block_dec, grad_small_dec = mixer_backward(
-        grad_final, kept_dec, full_in[1], full_out[1]
+    slope_unpacked, grad_block_dec, grad_small_dec, jobs_dec = mixer_backward(
+        conductor, False, grad_final, kept_dec, full_in[1], full_out[1], layer_smalls[1]
     )
     gradient_holder, slope_closing_scale, slope_likelihood, slope_shortcut = link_layers_grad(
         slope_unpacked
     )
-    gradient_holder, slope_lifting, slope_lowering, slope_perceptron_scale = perceptron_grad(
-        gradient_holder, saved_perceptron, lift_matrix_whole, lower_matrix_whole
-    )
-    gradient_holder, slope_triple, slope_heed_exit, slope_heed_scale = apply_heads_grad(
-        gradient_holder, saved_heeding, triple_whole, heed_exit_whole
+    gradient_holder, slope_perceptron_scale, job_lower, slope_lifts = perceptron_grad(
+        conductor, conductor.tick(gradient_holder, 14.0, Y_LANE), saved_perceptron, lift_matrix_whole, lower_matrix_whole
+    )
+    gradient_holder, slope_heed_scale, *jobs_heads = apply_heads_grad(
+        conductor, gradient_holder, saved_heeding, triple_whole, heed_exit_whole
     )
     gradient_merged, gradient_blank = merge_transpose(gradient_holder)
     grad_query, grad_key = prob_pull(slope_likelihood)
     grad_routed = to_low(jnp.concatenate([grad_query, grad_key, slope_shortcut], axis=1))
-    grad_route = product_tn(encoded_low, grad_routed)
-    grad_embedded, grad_in_enc, grad_out_enc, grad_block_enc, grad_small_enc = mixer_backward(
-        gradient_merged + product_nt(grad_routed, full_route), kept_enc, full_in[0], full_out[0]
+    grad_route = to_low(product_tn(encoded_low, grad_routed))
+    job_route = conductor.add(Summing(grad_route, True))
+    grad_routed = conductor.tick(after(grad_routed, [grad_route]), 7.0)
+    grad_embedded, grad_block_enc, grad_small_enc, jobs_enc = mixer_backward(
+        conductor,
+        True,
+        gradient_merged + product_nt(grad_routed, full_route),
+        kept_enc,
+        full_in[0],
+        full_out[0],
+        layer_smalls[0],
     )
     grad_table_in = jnp.dot(onehot_in.astype(jnp.float32).T, grad_embedded, precision=deepest_tier)
     grad_small = jnp.concatenate(
@@ -683,22 +1733,7 @@
             )
         ]
     )
-    def by_device(grad):
-        return to_low(grad).reshape((devices, grad.shape[0] // devices) + grad.shape[1:])
-
-    def by_dp(grad):
-        size = lax.axis_size("dp")
-        return to_low(grad).reshape((size, grad.shape[0] // size) + grad.shape[1:])
-
-    reduced_in_dec = reduce_all(by_device(grad_in_dec))
-    reduced_out_dec = reduce_all(by_device(grad_out_dec))
-    reduced_gate_up = reduce_dp([by_dp(slope_lifting)])
-    reduced_down = reduce_dp([by_dp(slope_lowering)]).T
-    reduced_qkv = reduce_dp([by_dp(slope_triple)])
-    reduced_wo = reduce_dp([by_dp(slope_heed_exit)]).T
-    reduced_route = reduce_all(by_device(grad_route))
-    reduced_in_enc = reduce_all(by_device(grad_in_enc))
-    reduced_out_enc = reduce_all(by_device(grad_out_enc))
+    width = mamba_in.shape[2]
     grad_mixed = jnp.concatenate(
         [
             to_low(grad_table_in).reshape(devices, table_rows, BYTE_WIDTH),
@@ -710,7 +1745,45 @@
         ],
         axis=1,
     )
-    reduced_mixed = reduce_all(grad_mixed)
+    conductor.close()
+    parts = [
+        jobs_heads[1],
+        slope_lifts[0],
+        slope_lifts[1],
+        jobs_heads[0],
+        job_lower,
+        jobs_dec[1],
+        jobs_dec[0],
+        jobs_enc[0],
+        job_route,
+        jobs_enc[1],
+        Summing(grad_mixed.reshape(-1, BYTE_WIDTH), True),
+    ]
+    sums = [None if part.masks else part.result() for part in parts]
+    open_parts = [number for number, part in enumerate(parts) if part.masks]
+    rests = [parts[number].rest() for number in open_parts]
+    grads = [grad for grad, _ in rests]
+    sum_kinds = [
+        kind[::-1] if number == 0 and len(kind) == 2 else kind
+        for number, (_, kind) in enumerate(rests)
+    ]
+    if exact_tiles:
+        early = sum((jnp.sum(part * part) for part in sums if part is not None), jnp.float32(0.0))
+        extra = jnp.zeros((16, 128), jnp.float32).at[0, 0].set(early).at[8, 0].set(loss_local)
+        *ends, totals = sum_whole(grads, sum_kinds, extra, 1)
+        square_total, loss_sum = jnp.sum(totals[:8]), jnp.sum(totals[8:])
+    else:
+        ends = [sum_slowly(parts[number]) for number in open_parts]
+    for number, end in zip(open_parts, ends):
+        sums[number] = end
+    reduced_wo = sums[0].T
+    reduced_gate_up = jnp.stack([sums[1], sums[2]], axis=1)
+    reduced_qkv = sums[3].reshape(heed_triple_matrix.shape)
+    reduced_down = sums[4].T
+    reduced_in_dec = sums[5][:, :width]
+    reduced_out_dec, reduced_out_enc, reduced_route = sums[6:9]
+    reduced_in_enc = sums[9][:, :width]
+    reduced_mixed = sums[10]
     reduced_tables = reduced_mixed[: 2 * table_rows].reshape(2, table_rows, BYTE_WIDTH)
     reduced_small = reduced_mixed[2 * table_rows :].reshape(-1)[:small_here]
     reduced_in = jnp.stack([reduced_in_enc, reduced_in_dec])
@@ -726,9 +1799,10 @@
         reduced_gate_up,
         reduced_down,
     )
-    squares = sum((jnp.sum(grad * grad) for grad in reduced))
-    totals = add_everywhere(jnp.stack([squares, loss_local]).reshape(1, 2))
-    square_total, loss_sum = (totals[0, 0], totals[0, 1])
+    if not exact_tiles:
+        squares = sum((jnp.sum(grad * grad) for grad in reduced))
+        totals = add_everywhere(jnp.stack([squares, loss_local]).reshape(1, 2))
+        square_total, loss_sum = (totals[0, 0], totals[0, 1])
     grad_norm = jnp.sqrt(square_total)
     clip_factor = jnp.minimum(1.0, max_norm / (grad_norm + 1e-06))
     masters = (

time: 3070 us -> 1010 us (0.33)
  Pallas kernels: 1540 us -> 579 us
  waiting for transfers between devices: 513 us -> 63.1 us
  matrix products: 346 us -> 164 us
  other arithmetic: 261 us -> 81.4 us
  starting transfers between devices: 190 us -> 22 us
  local copies, waits for them, and re-layouts: 196 us -> 81.6 us
    pallas_call x10 -> x6, Pallas kernels: 1540 us -> 579 us  [the longest x1 229 us: spread_whole(): pl.pallas_call(partial(spread_kernel, plan, jobs, depth_z), out_shape=tup...]
    ppermute x157 -> x34, waiting for transfers between devices: 513 us -> 63.1 us  [swap(): lax.ppermute(value_entries, axis, [(place, place ^ mask) for place in ran...]
    dot_general x30 -> x0, matrix products: 198 us -> none  [the longest x6 93.5 us: ssd_scan(): jnp.einsum('bij,bijh,bjhp->bihp', affinity, jnp.exp(log_gaps), weighted,...]
    ppermute x157 -> x34, starting transfers between devices: 190 us -> 22 us  [swap(): lax.ppermute(value_entries, axis, [(place, place ^ mask) for place in ran...]
    reduce_sum x20 -> x10, other arithmetic: 67.7 us -> 3.99 us  [the longest x1 1.76 us: body(): jnp.sum(part * part)]
    another operation x27 -> x8, other arithmetic: 40.6 us -> 2.9 us  [the longest x15 24.6 us: spread_dp(): group = jnp.stack(pieces)]
  transfers between devices with their start and end apart: 157 -> 34, of which waited for: 55 -> 13; matrix products, arithmetic and copies ran while one was open for 16% -> 11% of each run, Pallas kernels for 50% -> 10%
where the time goes in v2:
time: 1010 us; the launch traced here: 998 us
  Pallas kernels  579 us (57%)
  matrix products  164 us (16%)
  local copies, waits for them, and re-layouts  81.6 us (8%)
  other arithmetic  81.4 us (8%)
  waiting for transfers between devices  63.1 us (6%)
  starting transfers between devices  22 us (2%)
    pallas_call x1, Pallas kernels, spread_whole(): pl.pallas_call(partial(spread_kernel, plan, jobs, depth_z), out_shape=tup...  229 us
    pallas_call x1, Pallas kernels, sum_whole(): pl.pallas_call(partial(sum_kernel, plan, kinds, depth_z), out_shape=tuple...  206 us
    pallas_call x2, Pallas kernels, middle_backward(): pl.pallas_call(middle_slope_kernel, grid=(chunks,), out_shape=(jax.ShapeD...  97.2 us
    ppermute x34, waiting for transfers between devices, swap(): lax.ppermute(value_entries, axis, [(place, place ^ mask) for place in ran...  63.1 us
    dot_general x11, matrix products, matmul_apply(): return jnp.dot(left, right, preferred_element_type=jnp.float32)  50.4 us
    dot_general x11, matrix products, product_tn(): lax.dot_general(left, right, (((0,), (0,)), ((), ())), preferred_element_...  48.4 us
    unnamed x398, local copies, waits for them, and re-layouts  48 us
    pallas_call x2, Pallas kernels, middle_forward(): pl.pallas_call(middle_kernel, grid=(chunks,), out_shape=(jax.ShapeDtypeSt...  47.2 us
  transfers between devices with their start and end apart: 34, of which 13 were waited for; matrix products, arithmetic and copies ran while one was open for 11% of the time, Pallas kernels for 10%

profile of v2, /device:TPU:0, one launch (start us, length us, event | category | flops | bytes accessed | tf_op | source)
XLA Modules:
  0.0 998.1 jit_solution(14639885860605417448)
XLA Ops:
  9.7 228.7 %shard_map.526 = (bf16[4,2,2,2,32,1024]{5,4,3,2,1,0:T(8,128)(2,1)S(1)}, bf16[4,2,2,2,32,4480]{5,4,3,2,1,0:T(8,128)(2,1)}, bf16[4,2,2,2,64,1024]{5,4,3,2,1,0:T(8,...) custom-call(bf16[32,1024]{1,0:T(8,128)(2,1)S(1)} %pad_maximum_fusion, ...), custom_call_target="tpu_custom_call" | custom-call | tf_op jit(solution)/shard_map/pallas_call | solution.py:529
  238.5 2.6 copy-done.4
  256.6 11.3 %fusion.155.projected.earlier = f32[512,4480]{1,0:T(8,128)} fusion(bf16[1024,4480]{1,0:T(8,128)(2,1)} %bitcast.497, f32[512,1024]{1,0:T(8,128)S(1)} %get-tuple-element.372, f32[1024]{0:T(1024)S(1)} %get-tuple-element.352, f32[512]{0:T(512)S(1)} %fusion.138), kind=kOutput, calls=%fused_computation.395 | convolution fusion | flops 4699193344 | bytes 20453376 | tf_op jit(solution)/shard_map/dot_general | solution.py:172
  267.9 23.8 %shard_map.527 = (bf16[512,2048]{1,0:T(8,128)(2,1)S(1)}, f32[512,2048]{1,0:T(8,128)}, f32[4,128,2048]{2,1,0:T(8,128)}) custom-call(f32[512,4480]{1,0:T(8,128)} %fusion.155.projected.earlier, f32[4,2304]{1,0:T(4,128)S(1)} %squeeze.95.taps, f32[1,2048]{1,0:T(1,128)S(1)} %bitcast.395, f32[2,32]{1,0:T(2,128)S(1)} %get-tuple-element.387.decay, ...), custom_call_target="tpu_custom_call" | custom-call | flops 20000000000 | bytes 20000000 | tf_op jit(solution)/shard_map/pallas_call | solution.py:1250
  291.8 4.7 convolution_add_fusion.2
  300.0 3.5 fusion.76
  304.0 2.1 copy-done.20
  312.3 3.2 convolution_convert_fusion.10
  315.5 4.5 reshape.777
  320.0 2.9 fusion.182
  324.2 2.1 copy.184
  326.3 2.0 copy.186
  336.1 9.5 collective-permute-done.5
  347.9 8.6 collective-permute-done.6
  359.0 5.6 fusion.157
  377.2 9.3 collective-permute-done.11
  389.7 4.3 multiply_reduce_fusion.10
  394.0 11.9 %fusion.156.projected.earlier = f32[512,4480]{1,0:T(8,128)} fusion(bf16[1024,4480]{1,0:T(8,128)(2,1)} %bitcast.501, f32[512,1024]{1,0:T(8,128)S(1)} %get-tuple-element.316, f32[1024]{0:T(1024)S(1)} %get-tuple-element.351, f32[512]{0:T(512)S(1)} %fusion.139), kind=kOutput, calls=%fused_computation.396 | convolution fusion | flops 4699193344 | bytes 20453376 | tf_op jit(solution)/shard_map/dot_general | solution.py:172
  405.9 23.4 %shard_map.528 = (bf16[512,2048]{1,0:T(8,128)(2,1)S(1)}, f32[512,2048]{1,0:T(8,128)}, f32[4,128,2048]{2,1,0:T(8,128)}) custom-call(f32[512,4480]{1,0:T(8,128)} %fusion.156.projected.earlier, f32[4,2304]{1,0:T(4,128)S(1)} %slice.409.taps, f32[1,2048]{1,0:T(1,128)S(1)} %bitcast.399, f32[2,32]{1,0:T(2,128)S(1)} %get-tuple-element.388.decay, ...), custom_call_target="tpu_custom_call" | custom-call | flops 20000000000 | bytes 20000000 | tf_op jit(solution)/shard_map/pallas_call | solution.py:1250
  429.3 2.4 multiply_reduce_fusion.9
  432.5 2.0 multiply_reduce_fusion
  435.1 4.3 fusion.71.slope
  439.4 2.4 convolution_convert_fusion.8
  444.5 48.8 %shard_map.529 = (bf16[512,4480]{1,0:T(8,128)(2,1)}, f32[4,8,2304]{2,1,0:T(8,128)S(1)}, f32[8,2048]{1,0:T(8,128)S(1)}, f32[8,2048]{1,0:T(8,128)S(1)}, f32[2,8,32]{2,1,0:T(8,128)S(1)}) custom-call(f32[512,4480]{1,0:T(8,128)} %fusion.156.projected.earlier, f32[512,4480]{1,0:T(8,128)} %fusion.156.projected.earlier, f32[512,2048]{1,0:T(8,128)} %get-tuple-element.124.outcome, ...), custom_call_target="tpu_custom_call" | custom-call | flops 49999998976 | bytes 30000000 | tf_op jit(solution)/shard_map/pallas_call | solution.py:1305
  497.7 4.4 convolution_convert_fusion.15
  502.1 7.9 convolution_convert_fusion.1
  510.0 11.4 %multiply_reduce_fusion.1 = (bf16[1024]{0:T(1024)(128)(2,1)S(1)}, f32[512]{0:T(512)S(1)}, f32[512,1024]{1,0:T(8,128)S(1)}) fusion(f32[512,1024]{1,0:T(8,128)S(1)} %copy-done.36, f32[512]{0:T(512)S(1)} %fusion.139, f32[1024]{0:T(1024)S(1)} %get-tuple-element.351, bf16[512,4480]{1,0:T(8,128)(2,1)S(1)} %bitcast.506, bf16[1024,4480]{1,0:T(8,128)(2,1)} %bitcast.502), kind=kOutput, calls=%fused_computation.51 | convolution fusion | flops 4700764672 | bytes 17967104 | tf_op jit(solution)/shard_map/dot_general | solution.py:182
  522.3 2.0 fusion.17
  524.5 2.6 copy_bitcast_fusion
  530.8 2.9 fusion.14
  538.3 7.4 convolution_convert_fusion.3
  545.7 2.0 pad_maximum_fusion
  548.9 14.1 %collective-permute-done.16 = bf16[2,2,2,64,1024]{4,3,2,1,0:T(8,128)(2,1)} collective-permute-done((bf16[2,2,2,64,1024]{4,3,2,1,0:T(8,128)(2,1)}, bf16[2,2,2,64,1024]{4,3,2,1,0:T(8,128)(2,1)}, u32[]{:S(2)}, u32[]{:S(2)}) %collective-permute-start.16) | collective-permute-done | bytes 1048608 | tf_op jit(solution)/shard_map/ppermute | solution.py:189
  564.9 2.5 fusion.107
  569.1 7.2 convolution_convert_fusion.11
  576.5 2.0 dynamic-slice_bitcast_fusion
  587.3 7.6 collective-permute-done.20
  598.3 3.6 convolution_convert_fusion.5
  601.9 5.1 collective-permute-done.21
  607.0 2.3 convolution_convert_fusion.6
  610.8 2.4 fusion.66
  616.1 2.2 reshape.778
  618.4 2.0 copy.153
  625.4 2.1 convolution_convert_fusion.14
  627.4 2.2 convolution_convert_fusion.9
  631.2 3.3 fusion.4
  641.9 4.1 convolution_convert_fusion.2
  650.4 2.7 collective-permute-done.31
  656.9 6.1 convolution_add_fusion
  663.0 4.5 fusion.67.slope
  667.5 4.4 convolution_convert_fusion.4
  671.9 48.4 %shard_map.530 = (bf16[512,4480]{1,0:T(8,128)(2,1)}, f32[4,8,2304]{2,1,0:T(8,128)S(1)}, f32[8,2048]{1,0:T(8,128)S(1)}, f32[8,2048]{1,0:T(8,128)S(1)}, f32[2,8,32]{2,1,0:T(8,128)S(1)}) custom-call(f32[512,4480]{1,0:T(8,128)} %fusion.155.projected.earlier, f32[512,4480]{1,0:T(8,128)} %fusion.155.projected.earlier, f32[512,2048]{1,0:T(8,128)} %get-tuple-element.148.outcome, ...), custom_call_target="tpu_custom_call" | custom-call | flops 49999998976 | bytes 30000000 | tf_op jit(solution)/shard_map/pallas_call | solution.py:1305
  721.9 3.7 fusion.5
  725.7 5.4 fusion.3
  731.1 8.1 convolution_convert_fusion
  739.3 6.5 multiply_reduce_fusion.3
  747.8 4.1 fusion.26
  753.5 5.7 fusion
  759.2 206.2 %shard_map.531 = (f32[192,384]{1,0:T(8,128)}, f32[192,1024]{1,0:T(8,128)}, f32[192,1024]{1,0:T(8,128)}, f32[192,1152]{1,0:T(8,128)}, f32[192,1024]{1,0:T(8,128)}...) custom-call(bf16[4,2,192,384]{3,2,1,0:T(8,128)(2,1)} %bitcast.456, ...), custom_call_target="tpu_custom_call" | custom-call | tf_op jit(solution)/shard_map/pallas_call | solution.py:787
  972.3 4.1 multiply_subtract_fusion
  976.4 2.4 copy.175
  978.8 2.4 copy.174
  981.3 2.4 copy.173
  994.4 2.3 multiply_subtract_fusion.1
  (653 shorter events, 145.2 us)
Async XLA Ops:
  248.5 82.9 %copy-start = (bf16[4,2,192,384]{3,2,1,0:T(8,128)(2,1)}, bf16[4,2,192,384]{3,2,1,0:T(8,128)(2,1)S(1)}, u32[]{:S(2)}) copy-start(bf16[4,2,192,384]{3,2,1,0:T(8,128)(2,1)S(1)} %get-tuple-element.119) | copy-start | bytes 3538948
  252.2 45.8 %copy-start.117 = (f32[1536]{0:T(1024)}, f32[1536]{0:T(1024)S(1)}, u32[]{:S(2)}) copy-start(f32[1536]{0:T(1024)S(1)} %get-tuple-element.348) | copy-start | bytes 18436
  252.2 93.8 %copy-start.120 = (f32[1536]{0:T(1024)}, f32[1536]{0:T(1024)S(1)}, u32[]{:S(2)}) copy-start(f32[1536]{0:T(1024)S(1)} %get-tuple-element.347) | copy-start | bytes 18436
  252.2 80.4 %copy-start.132 = (f32[1,512]{1,0:T(1,128)}, f32[1,512]{1,0:T(1,128)S(1)}, u32[]{:S(2)}) copy-start(f32[1,512]{1,0:T(1,128)S(1)} %convert_element_type.515) | copy-start | bytes 6148
  256.0 11.9 %copy-start.33 = (f32[512,1024]{1,0:T(8,128)}, f32[512,1024]{1,0:T(8,128)S(1)}, u32[]{:S(2)}) copy-start(f32[512,1024]{1,0:T(8,128)S(1)} %get-tuple-element.372) | copy-start | bytes 6291460
  256.1 89.5 %copy-start.107 = (f32[1536]{0:T(1024)}, f32[1536]{0:T(1024)S(1)}, u32[]{:S(2)}) copy-start(f32[1536]{0:T(1024)S(1)} %pad.108.clone) | copy-start | bytes 18436
  256.6 43.4 %slice-start = ((s8[6291456]{0:T(1024)(128)(4,1)}), s8[4194304]{0:T(1024)(128)(4,1)S(1)}, s32[]{:S(2)}) async-start(s8[6291456]{0:T(1024)(128)(4,1)} %bitcast.402), calls=%async_computation | async-start | bytes 8388608
  267.9 23.9 %copy-start.6 = (bf16[4,2,2,2,64,1024]{5,4,3,2,1,0:T(8,128)(2,1)S(1)}, bf16[4,2,2,2,64,1024]{5,4,3,2,1,0:T(8,128)(2,1)}, u32[]{:S(2)}) copy-start(bf16[4,2,2,2,64,1024]{5,4,3,2,1,0:T(8,128)(2,1)} %copy-done.5) | copy-start | bytes 12582916
  267.9 32.1 %slice-start.1 = ((s8[6291456]{0:T(1024)(128)(4,1)}), s8[2097152]{0:T(1024)(128)(4,1)S(1)}, s32[]{:S(2)}) async-start(s8[6291456]{0:T(1024)(128)(4,1)} %bitcast.402), calls=%async_computation.1 | async-start | bytes 4194304
  298.2 13.3 %copy-start.100 = (bf16[128,1536]{1,0:T(8,128)(2,1)}, bf16[128,1536]{1,0:T(8,128)(2,1)S(1)}, u32[]{:S(2)}) copy-start(bf16[128,1536]{1,0:T(8,128)(2,1)S(1)} %multiply_convert_fusion.6) | copy-start | bytes 1179652
  298.2 11.7 %collective-permute-start.1 = (bf16[128,1536]{1,0:T(8,128)(2,1)S(1)}, bf16[128,1536]{1,0:T(8,128)(2,1)S(1)}, u32[]{:S(2)}, u32[]{:S(2)}) collective-permute-start(bf16[128,1536]{1,0:T(8,128)(2,1)S(1)} %multiply_convert_fusion.6), channel_id=1, source_target_pairs={{0,1},{1,0},{2,3},{3,2},{4,5},{5,4},{6,7},{7,6},{8,9},{9,8},{10,11... | collective-permute-start | bytes 1179656 | tf_op jit(solution)/shard_map/ppermute | solution.py:189
  298.5 11.3 %collective-permute-start = (bf16[128,1536]{1,0:T(8,128)(2,1)S(1)}, bf16[128,1536]{1,0:T(8,128)(2,1)S(1)}, u32[]{:S(2)}, u32[]{:S(2)}) collective-permute-start(bf16[128,1536]{1,0:T(8,128)(2,1)S(1)} %multiply_convert_fusion.6), channel_id=1, source_target_pairs={{0,2},{1,3},{2,0},{3,1},{4,6},{5,7},{6,4},{7,5},{8,10},{9,11},{10,... | collective-permute-start | bytes 1179656 | tf_op jit(solution)/shard_map/ppermute | solution.py:189
  309.8 1.7 collective-permute-start.2
  332.4 13.2 %copy-start.26 = (f32[128,1024]{1,0:T(8,128)S(1)}, f32[128,1024]{1,0:T(8,128)}, u32[]{:S(2)}) copy-start(f32[128,1024]{1,0:T(8,128)} %copy-done.25) | copy-start | bytes 1572868
  332.5 1.8 collective-permute-start.4
  333.0 3.1 collective-permute-start.3
  334.4 11.2 %collective-permute-start.5 = (bf16[128,1536]{1,0:T(8,128)(2,1)S(1)}, bf16[128,1536]{1,0:T(8,128)(2,1)S(1)}, u32[]{:S(2)}, u32[]{:S(2)}) collective-permute-start(bf16[128,1536]{1,0:T(8,128)(2,1)S(1)} %add_convert_fusion.4), channel_id=1, source_target_pairs={{0,2},{1,3},{2,0},{3,1},{4,6},{5,7},{6,4},{7,5},{8,10},{9,11},{10,... | collective-permute-start | bytes 1179656 | tf_op jit(solution)/shard_map/ppermute | solution.py:189
  345.9 18.7 %copy-start.165 = (f32[128]{0:T(128)}, f32[128]{0:T(128)S(1)}, u32[]{:S(2)}) copy-start(f32[128]{0:T(128)S(1)} %get-tuple-element.319) | copy-start | bytes 1540
  345.9 40.6 %copy-start.23 = (f32[128,1536]{1,0:T(8,128)}, f32[128,1536]{1,0:T(8,128)S(1)}, u32[]{:S(2)}) copy-start(f32[128,1536]{1,0:T(8,128)S(1)} %get-tuple-element.320) | copy-start | bytes 2359300
  345.9 18.7 %copy-start.153 = (f32[128]{0:T(128)}, f32[128]{0:T(128)S(1)}, u32[]{:S(2)}) copy-start(f32[128]{0:T(128)S(1)} %fusion.143) | copy-start | bytes 1540
  346.1 18.5 %copy-start.102 = (bf16[128,1536]{1,0:T(8,128)(2,1)}, bf16[128,1536]{1,0:T(8,128)(2,1)S(1)}, u32[]{:S(2)}) copy-start(bf16[128,1536]{1,0:T(8,128)(2,1)S(1)} %multiply_convert_fusion.5) | copy-start | bytes 1179652
  346.1 10.4 %collective-permute-start.6 = (bf16[128,1536]{1,0:T(8,128)(2,1)S(1)}, bf16[128,1536]{1,0:T(8,128)(2,1)S(1)}, u32[]{:S(2)}, u32[]{:S(2)}) collective-permute-start(bf16[128,1536]{1,0:T(8,128)(2,1)S(1)} %multiply_convert_fusion.5), channel_id=1, source_target_pairs={{0,2},{1,3},{2,0},{3,1},{4,6},{5,7},{6,4},{7,5},{8,10},{9,11},{10,... | collective-permute-start | bytes 1179656 | tf_op jit(solution)/shard_map/ppermute | solution.py:189
  347.8 9.6 collective-permute-start.7
  356.5 1.7 collective-permute-start.8
  372.2 1.9 collective-permute-start.10
  373.1 4.0 collective-permute-start.9
  375.3 11.2 %collective-permute-start.11 = (bf16[128,1536]{1,0:T(8,128)(2,1)S(1)}, bf16[128,1536]{1,0:T(8,128)(2,1)S(1)}, u32[]{:S(2)}, u32[]{:S(2)}) collective-permute-start(bf16[128,1536]{1,0:T(8,128)(2,1)S(1)} %add_convert_fusion.3), channel_id=1, source_target_pairs={{0,2},{1,3},{2,0},{3,1},{4,6},{5,7},{6,4},{7,5},{8,10},{9,11},{10,... | collective-permute-start | bytes 1179656 | tf_op jit(solution)/shard_map/ppermute | solution.py:189
  394.0 35.3 %copy-start.35 = (f32[512,1024]{1,0:T(8,128)}, f32[512,1024]{1,0:T(8,128)S(1)}, u32[]{:S(2)}) copy-start(f32[512,1024]{1,0:T(8,128)S(1)} %get-tuple-element.316) | copy-start | bytes 6291460
  405.9 23.4 %copy-start.9 = (bf16[4,2,2,2,64,1024]{5,4,3,2,1,0:T(8,128)(2,1)S(1)}, bf16[4,2,2,2,64,1024]{5,4,3,2,1,0:T(8,128)(2,1)}, u32[]{:S(2)}) copy-start(bf16[4,2,2,2,64,1024]{5,4,3,2,1,0:T(8,128)(2,1)} %copy-done.8) | copy-start | bytes 12582916
  444.5 57.6 %collective-permute-start.12 = (bf16[2,2,2,2,64,1024]{5,4,3,2,1,0:T(8,128)(2,1)}, bf16[2,2,2,2,64,1024]{5,4,3,2,1,0:T(8,128)(2,1)}, u32[]{:S(2)}, u32[]{:S(2)}) collective-permute-start(bf16[2,2,2,2,64,1024]{5,4,3,2,1,0:T(8,128)(2,1)} %dynamic-slice_bitcast_fusion.1), channel_id=1, source_target_pairs={{0,1},{1,0},{2,3},{3,2},{4,5},{5,4},{6,7},{7,6},{8,9},{9,8},{10,11... | collective-permute-start | bytes 6291464 | tf_op jit(solution)/shard_map/ppermute | solution.py:189
  497.7 12.3 %slice-start.9 = ((s8[4587520]{0:T(1024)(128)(4,1)}), s8[4194304]{0:T(1024)(128)(4,1)S(1)}, s32[]{:S(2)}) async-start(s8[4587520]{0:T(1024)(128)(4,1)} %bitcast.505), calls=%async_computation.9 | async-start | bytes 8388608
  510.0 75.4 %copy-start.32 = (bf16[1024,4480]{1,0:T(8,128)(2,1)}, bf16[1024,4480]{1,0:T(8,128)(2,1)S(1)}, u32[]{:S(2)}) copy-start(bf16[1024,4480]{1,0:T(8,128)(2,1)S(1)} %convolution_convert_fusion.1) | copy-start | bytes 27525124
  527.1 35.9 %collective-permute-start.17 = (bf16[2,2,2,2,32,4480]{5,4,2,1,0,3:T(8,128)(2,1)}, bf16[2,2,2,2,32,4480]{5,4,2,1,0,3:T(8,128)(2,1)S(1)}, u32[]{:S(2)}, u32[]{:S(2)}) collective-permute-start(bf16[2,2,2,2,32,4480]{5,4,2,1,0,3:T(8,128)(2,1)} %copy_bitcast_fusion), channel_id=1, source_target_pairs={{0,1},{1,0},{2,3},{3,2},{4,5},{5,4},{6,7},{7,6},{8,9},{9,8},{10,11... | collective-permute-start | bytes 13762568 | tf_op jit(solution)/shard_map/ppermute | solution.py:189
  528.9 18.8 %collective-permute-start.14 = (bf16[128,1536]{1,0:T(8,128)(2,1)S(1)}, bf16[128,1536]{1,0:T(8,128)(2,1)S(1)}, u32[]{:S(2)}, u32[]{:S(2)}) collective-permute-start(bf16[128,1536]{1,0:T(8,128)(2,1)S(1)} %fusion.125), channel_id=1, source_target_pairs={{0,1},{1,0},{2,3},{3,2},{4,5},{5,4},{6,7},{7,6},{8,9},{9,8},{10,11... | collective-permute-start | bytes 1179656 | tf_op jit(solution)/shard_map/ppermute | solution.py:189
  529.3 16.4 %collective-permute-start.13 = (bf16[128,1536]{1,0:T(8,128)(2,1)S(1)}, bf16[128,1536]{1,0:T(8,128)(2,1)}, u32[]{:S(2)}, u32[]{:S(2)}) collective-permute-start(bf16[128,1536]{1,0:T(8,128)(2,1)S(1)} %fusion.125), channel_id=1, source_target_pairs={{0,2},{1,3},{2,0},{3,1},{4,6},{5,7},{6,4},{7,5},{8,10},{9,11},{10,... | collective-permute-start | bytes 1179656 | tf_op jit(solution)/shard_map/ppermute | solution.py:189
  533.7 29.4 %collective-permute-start.16 = (bf16[2,2,2,64,1024]{4,3,2,1,0:T(8,128)(2,1)}, bf16[2,2,2,64,1024]{4,3,2,1,0:T(8,128)(2,1)}, u32[]{:S(2)}, u32[]{:S(2)}) collective-permute-start(bf16[2,2,2,64,1024]{4,3,2,1,0:T(8,128)(2,1)} %fusion.14), channel_id=1, source_target_pairs={{0,2},{1,3},{2,0},{3,1},{4,6},{5,7},{6,4},{7,5},{8,10},{9,11},{10,... | collective-permute-start | bytes 3145736 | tf_op jit(solution)/shard_map/ppermute | solution.py:189
  545.7 2.0 collective-permute-start.15
  547.7 15.4 %copy-start.89 = (bf16[512,1024]{1,0:T(8,128)(2,1)S(1)}, bf16[512,1024]{1,0:T(8,128)(2,1)}, u32[]{:S(2)}) copy-start(bf16[512,1024]{1,0:T(8,128)(2,1)} %copy-done.88) | copy-start | bytes 3145732
  548.9 16.0 %copy-start.15 = (bf16[4,2,192,1024]{3,2,1,0:T(8,128)(2,1)S(1)}, bf16[4,2,192,1024]{3,2,1,0:T(8,128)(2,1)}, u32[]{:S(2)}) copy-start(bf16[4,2,192,1024]{3,2,1,0:T(8,128)(2,1)} %copy-done.13) | copy-start | bytes 9437188
  548.9 16.0 %copy-start.52 = (f32[512,2048]{1,0:T(8,128)S(1)}, f32[512,2048]{1,0:T(8,128)}, u32[]{:S(2)}) copy-start(f32[512,2048]{1,0:T(8,128)} %copy-done.51) | copy-start | bytes 12582916
  563.1 22.3 %copy-start.46 = (bf16[2,2,2,2,32,4480]{5,4,2,1,0,3:T(8,128)(2,1)}, bf16[2,2,2,2,32,4480]{5,4,2,1,0,3:T(8,128)(2,1)S(1)}, u32[]{:S(2)}) copy-start(bf16[2,2,2,2,32,4480]{5,4,2,1,0,3:T(8,128)(2,1)S(1)} %collective-permute-done.17) | copy-start | bytes 13762564
  564.9 16.9 %copy-start.65 = (bf16[1536,1024]{1,0:T(8,128)(2,1)}, bf16[1536,1024]{1,0:T(8,128)(2,1)S(1)}, u32[]{:S(2)}) copy-start(bf16[1536,1024]{1,0:T(8,128)(2,1)S(1)} %convolution_convert_fusion.7) | copy-start | bytes 9437188
  576.4 7.3 collective-permute-start.19
  580.2 30.6 %collective-permute-start.24 = (bf16[2,2,64,1024]{3,2,1,0:T(8,128)(2,1)S(1)}, bf16[2,2,64,1024]{3,2,1,0:T(8,128)(2,1)S(1)}, u32[]{:S(2)}, u32[]{:S(2)}) collective-permute-start(bf16[2,2,64,1024]{3,2,1,0:T(8,128)(2,1)S(1)} %fusion.38), channel_id=1, source_target_pairs={{0,4},{4,0},{8,12},{12,8},{16,20},{20,16},{24,28},{28,24},{1,5},{5... | collective-permute-start | bytes 1572872 | tf_op jit(solution)/shard_map/ppermute | solution.py:189
  581.7 5.7 collective-permute-start.18
  583.1 48.1 %collective-permute-start.26 = (bf16[2,2,192,1024]{3,2,1,0:T(8,128)(2,1)}, bf16[2,2,192,1024]{3,2,1,0:T(8,128)(2,1)}, u32[]{:S(2)}, u32[]{:S(2)}) collective-permute-start(bf16[2,2,192,1024]{3,2,1,0:T(8,128)(2,1)} %dynamic-slice_bitcast_fusion.2), channel_id=1, source_target_pairs={{0,4},{4,0},{8,12},{12,8},{16,20},{20,16},{24,28},{28,24},{1,5},{5... | collective-permute-start | bytes 4718600 | tf_op jit(solution)/shard_map/ppermute | solution.py:189
  583.9 11.1 %collective-permute-start.20 = (bf16[128,1536]{1,0:T(8,128)(2,1)S(1)}, bf16[128,1536]{1,0:T(8,128)(2,1)S(1)}, u32[]{:S(2)}, u32[]{:S(2)}) collective-permute-start(bf16[128,1536]{1,0:T(8,128)(2,1)S(1)} %add_convert_fusion.2), channel_id=1, source_target_pairs={{0,2},{1,3},{2,0},{3,1},{4,6},{5,7},{6,4},{7,5},{8,10},{9,11},{10,... | collective-permute-start | bytes 1179656 | tf_op jit(solution)/shard_map/ppermute | solution.py:189
  596.8 10.2 %collective-permute-start.21 = (bf16[128,1536]{1,0:T(8,128)(2,1)S(1)}, bf16[128,1536]{1,0:T(8,128)(2,1)S(1)}, u32[]{:S(2)}, u32[]{:S(2)}) collective-permute-start(bf16[128,1536]{1,0:T(8,128)(2,1)S(1)} %get-tuple-element.313), channel_id=1, source_target_pairs={{0,2},{1,3},{2,0},{3,1},{4,6},{5,7},{6,4},{7,5},{8,10},{9,11},{10,... | collective-permute-start | bytes 1179656 | tf_op jit(solution)/shard_map/ppermute | solution.py:189
  601.9 11.3 %collective-permute-start.22 = (bf16[128,1536]{1,0:T(8,128)(2,1)S(1)}, bf16[128,1536]{1,0:T(8,128)(2,1)S(1)}, u32[]{:S(2)}, u32[]{:S(2)}) collective-permute-start(bf16[128,1536]{1,0:T(8,128)(2,1)S(1)} %get-tuple-element.313), channel_id=1, source_target_pairs={{0,1},{1,0},{2,3},{3,2},{4,5},{5,4},{6,7},{7,6},{8,9},{9,8},{10,11... | collective-permute-start | bytes 1179656 | tf_op jit(solution)/shard_map/ppermute | solution.py:189
  607.0 6.1 collective-permute-start.23
  622.4 14.8 %collective-permute-start.27 = (bf16[2,64,1024]{2,1,0:T(8,128)(2,1)S(1)}, bf16[2,64,1024]{2,1,0:T(8,128)(2,1)S(1)}, u32[]{:S(2)}, u32[]{:S(2)}) collective-permute-start(bf16[2,64,1024]{2,1,0:T(8,128)(2,1)S(1)} %copy-done.112), channel_id=1, source_target_pairs={{0,16},{4,20},{8,24},{12,28},{16,0},{20,4},{24,8},{28,12},{1,17},{... | collective-permute-start | bytes 786440 | tf_op jit(solution)/shard_map/ppermute | solution.py:189
  630.6 9.2 collective-permute-start.30
  634.5 15.8 %collective-permute-start.29 = (bf16[128,1536]{1,0:T(8,128)(2,1)}, bf16[128,1536]{1,0:T(8,128)(2,1)}, u32[]{:S(2)}, u32[]{:S(2)}) collective-permute-start(bf16[128,1536]{1,0:T(8,128)(2,1)} %get-tuple-element.329), channel_id=1, source_target_pairs={{0,1},{1,0},{2,3},{3,2},{4,5},{5,4},{6,7},{7,6},{8,9},{9,8},{10,11... | collective-permute-start | bytes 1179656 | tf_op jit(solution)/shard_map/ppermute | solution.py:189
  634.6 87.3 %collective-permute-start.25 = (bf16[2,2,192,1024]{3,2,1,0:T(8,128)(2,1)}, bf16[2,2,192,1024]{3,2,1,0:T(8,128)(2,1)}, u32[]{:S(2)}, u32[]{:S(2)}) collective-permute-start(bf16[2,2,192,1024]{3,2,1,0:T(8,128)(2,1)} %dynamic-slice_bitcast_fusion.3), channel_id=1, source_target_pairs={{0,4},{4,0},{8,12},{12,8},{16,20},{20,16},{24,28},{28,24},{1,5},{5... | collective-permute-start | bytes 4718600 | tf_op jit(solution)/shard_map/ppermute | solution.py:189
  638.4 8.6 collective-permute-start.33
  640.7 12.4 %collective-permute-start.31 = (bf16[128,1536]{1,0:T(8,128)(2,1)}, bf16[128,1536]{1,0:T(8,128)(2,1)}, u32[]{:S(2)}, u32[]{:S(2)}) collective-permute-start(bf16[128,1536]{1,0:T(8,128)(2,1)} %add_convert_fusion.1), channel_id=1, source_target_pairs={{0,2},{1,3},{2,0},{3,1},{4,6},{5,7},{6,4},{7,5},{8,10},{9,11},{10,... | collective-permute-start | bytes 1179656 | tf_op jit(solution)/shard_map/ppermute | solution.py:189
  646.0 79.6 %collective-permute-start.28 = (bf16[2,2,2,32,4480]{4,3,2,1,0:T(8,128)(2,1)}, bf16[2,2,2,32,4480]{4,3,2,1,0:T(8,128)(2,1)}, u32[]{:S(2)}, u32[]{:S(2)}) collective-permute-start(bf16[2,2,2,32,4480]{4,3,2,1,0:T(8,128)(2,1)} %fusion.1), channel_id=1, source_target_pairs={{0,2},{1,3},{2,0},{3,1},{4,6},{5,7},{6,4},{7,5},{8,10},{9,11},{10,... | collective-permute-start | bytes 6881288 | tf_op jit(solution)/shard_map/ppermute | solution.py:189
  647.0 84.1 %collective-permute-start.32 = (bf16[2,2,2,2,32,3072]{5,4,3,2,1,0:T(8,128)(2,1)}, bf16[2,2,2,2,32,3072]{5,4,3,2,1,0:T(8,128)(2,1)}, u32[]{:S(2)}, u32[]{:S(2)}) collective-permute-start(bf16[2,2,2,2,32,3072]{5,4,3,2,1,0:T(8,128)(2,1)} %dynamic-slice_bitcast_fusion), channel_id=1, source_target_pairs={{0,1},{1,0},{2,3},{3,2},{4,5},{5,4},{6,7},{7,6},{8,9},{9,8},{10,11... | collective-permute-start | bytes 9437192 | tf_op jit(solution)/shard_map/ppermute | solution.py:189
  671.9 48.5 %copy-start.164 = (bf16[1,32]{1,0:T(2,128)(2,1)S(1)}, bf16[1,32]{1,0:T(2,128)(2,1)}, u32[]{:S(2)}) copy-start(bf16[1,32]{1,0:T(2,128)(2,1)} %get-tuple-element.369) | copy-start | bytes 196
  671.9 48.6 %copy-start.163 = (bf16[1,32]{1,0:T(2,128)(2,1)S(1)}, bf16[1,32]{1,0:T(2,128)(2,1)}, u32[]{:S(2)}) copy-start(bf16[1,32]{1,0:T(2,128)(2,1)} %get-tuple-element.370) | copy-start | bytes 196
  671.9 48.7 %copy-start.131 = (bf16[1,2048]{1,0:T(2,128)(2,1)S(1)}, bf16[1,2048]{1,0:T(2,128)(2,1)}, u32[]{:S(2)}) copy-start(bf16[1,2048]{1,0:T(2,128)(2,1)} %stack.133) | copy-start | bytes 12292
  671.9 48.9 %copy-start.123 = (bf16[4,2304]{1,0:T(4,128)(2,1)S(1)}, bf16[4,2304]{1,0:T(4,128)(2,1)}, u32[]{:S(2)}) copy-start(bf16[4,2304]{1,0:T(4,128)(2,1)} %reduce_sum.471) | copy-start | bytes 55300
  671.9 49.0 %copy-start.130 = (bf16[1,2048]{1,0:T(2,128)(2,1)S(1)}, bf16[1,2048]{1,0:T(2,128)(2,1)}, u32[]{:S(2)}) copy-start(bf16[1,2048]{1,0:T(2,128)(2,1)} %stack.140) | copy-start | bytes 12292
  725.7 13.6 %slice-start.6 = ((s8[9175040]{0:T(1024)(128)(4,1)}), s8[4194304]{0:T(1024)(128)(4,1)S(1)}, s32[]{:S(2)}) async-start(s8[9175040]{0:T(1024)(128)(4,1)} %bitcast.498), calls=%async_computation.6 | async-start | bytes 8388608
  (161 other events, 647.3 us)

commit v3 on v2

--- a/solution.py
+++ b/solution.py
@@ -241,7 +241,9 @@
         left = [mask for axis, mask in self.masks if axis == "dp" and mask > 1]
         return 0 < len(left) == len(self.masks) < len(bit_masks(lax.axis_size("dp"))) - 1
 
-    def rest(self):
+    def rest(self, token):
+        if len(self.addends) > 1:
+            self.addends = [after(addend, [token]) for addend in self.addends]
         kind = []
         for axis, mask in self.masks:
             name = ("core", "y")[mask - 1] if axis == "tensor" else ("x" if mask == 1 else "z")
@@ -250,7 +252,9 @@
         value_entries = to_low(total(self.addends)) if len(self.addends) > 1 else self.addends[0]
         return value_entries.reshape(-1, value_entries.shape[-1]), tuple(kind)
 
-    def result(self):
+    def result(self, token=None):
+        if token is not None:
+            self.addends = [after(addend, [token]) for addend in self.addends]
         return total(self.addends)
 
 
@@ -277,23 +281,27 @@
         return (axis, mask if axis == "tensor" else min(mask, 2))
 
     def launch(self, limit, banned, value_entries):
+        operands = []
         for job in self.jobs:
             if len(self.flights) >= limit:
-                return
+                break
             if job.pending is not None or not job.masks:
                 continue
             lane = self.lane(job)
-            depth = 2 if lane in (("dp", 1), ("tensor", 1)) else 1
+            depth = {("dp", 1): 3, ("tensor", 1): 2}.get(lane, 1)
             if lane in banned or sum(flight[1] == lane for flight in self.flights) >= depth:
                 continue
             axis, mask = job.masks[0]
             operand = job.operand()
-            rate = 3.4 if (axis, mask) == ("tensor", 1) else 24.0
+            rate = 3.4 if (axis, mask) == ("tensor", 1) else 25.3
             if axis == "dp" and mask > 2:
-                rate = 48.0
-            job.pending = swap(after(operand, [value_entries]), axis, mask)
-            start = max([self.clock] + [flight[0] - 8.0 for flight in self.flights if flight[1] == lane])
-            self.flights.append((start + 8.0 + 1.2 * rate * operand.size * 2e-6, lane, job))
+                rate = 50.0
+            operand = after(operand, [value_entries])
+            operands.append(operand)
+            job.pending = swap(operand, axis, mask)
+            start = max([self.clock] + [flight[0] - 6.0 for flight in self.flights if flight[1] == lane])
+            self.flights.append((start + 6.0 + rate * operand.size * 2e-6, lane, job))
+        return after(value_entries, operands)
 
     def tick(self, value_entries, elapsed, banned=(), limit=5):
         self.clock += elapsed
@@ -303,8 +311,7 @@
             self.flights = [flight for flight in self.flights if flight[0] > self.clock]
             for flight in ended:
                 flight[2].accept()
-        self.launch(limit, banned, value_entries)
-        return value_entries
+        return self.launch(limit, banned, value_entries)
 
     def close(self):
         for _, _, job in sorted(self.flights, key=lambda flight: flight[0]):
@@ -537,7 +544,7 @@
             pltpu.SemaphoreType.DMA((len(jobs),)),
         ],
         compiler_params=pltpu.CompilerParams(
-            collective_id=collective_id, has_side_effects=True, vmem_limit_bytes=24 * 2**20
+            collective_id=collective_id, has_side_effects=True, vmem_limit_bytes=60 * 2**20
         ),
     )(*shards)
     return [whole.reshape(-1, whole.shape[-1]) for whole in wholes]
@@ -854,14 +861,6 @@
     )
 
 
-def three_parts(value_entries):
-    high = to_low(value_entries)
-    rest = value_entries - high.astype(jnp.float32)
-    middle = to_low(rest)
-    tail = to_low(rest - middle.astype(jnp.float32))
-    return jnp.concatenate([high, middle, tail, jnp.zeros_like(high)], axis=1)
-
-
 def sigmoid(value_entries):
     return 0.5 * jnp.tanh(0.5 * value_entries) + 0.5
 
@@ -876,6 +875,8 @@
     return (rows >= columns).astype(jnp.float32)
 
 
+FORWARD_UNROLL = 4
+BACKWARD_UNROLL = 2
 PROJ_WIDE = 2 * INNER + 2 * STATE + 128
 
 
@@ -889,29 +890,12 @@
     return shifted, steps, rates, cumulative
 
 
-def wide(parts, spread_wide, pair):
-    columns = pl.ds(pl.multiple_of(pair * 2 * ssd_block, 2 * ssd_block), 2 * ssd_block)
-    return low_dot(parts, spread_wide[:, columns], 1, 0)
-
-
-def narrow(parts, spread_narrow, pair):
-    return low_dot(parts, spread_narrow[:, lanes(pair)], 1, 0)
-
-
 def head_tables():
-    part = jnp.arange(ssd_block) % MHEADS
-    valid = jnp.arange(ssd_block) < 3 * MHEADS
-    heads = jnp.arange(MHEADS)
-    hit = (part[:, None] == heads[None, :]) & valid[:, None]
-    spread_wide = to_low(jnp.repeat(hit, ssd_block, axis=1))
-    spread_narrow = to_low(jnp.repeat(hit, HEADDIM, axis=1))
-    chosen = to_low(
-        jnp.arange(INNER)[:, None] // HEADDIM == jnp.arange(ssd_block)[None, :]
-    )
+    chosen = to_low(jnp.arange(INNER)[:, None] // HEADDIM == jnp.arange(ssd_block)[None, :])
     later = jnp.where(
-        jnp.arange(ssd_block)[:, None] >= jnp.arange(2 * ssd_block)[None, :] % ssd_block, 0.0, -1e30
-    )
-    return spread_wide, spread_narrow, chosen, later
+        jnp.arange(ssd_block)[:, None] >= jnp.arange(ssd_block)[None, :], 0.0, -1e30
+    )
+    return chosen, later
 
 
 def first_head():
@@ -926,27 +910,46 @@
     )
 
 
-def gap_decay(cumulative_wide, cumulative_rows, later):
-    return jnp.exp((cumulative_wide - cumulative_rows) + later[...])
-
-
-def store_turned(cumulative, turned_ref):
+def spread_heads(steps, cumulative, turned, wide, narrow):
     blank = jnp.zeros((ssd_block, ssd_block - MHEADS), jnp.float32)
-    turned_ref[...] = jnp.concatenate([cumulative, blank], axis=1).T
-
-
-def turned_rows(turned_ref, pair):
+    turned[...] = jnp.concatenate([cumulative, blank], axis=1).T
+    mask = first_head()
+
+    def over_lanes(value_entries, head):
+        return jnp.broadcast_to(value_entries[:, head : head + 1], (ssd_block, ssd_block))
+
+    for head in range(MHEADS):
+        wide[head] = over_lanes(cumulative, head)
+    for pair in range(MHEADS // 2):
+        narrow[:, pair * ssd_block : (pair + 1) * ssd_block] = jnp.where(
+            mask, over_lanes(steps, 2 * pair), over_lanes(steps, 2 * pair + 1)
+        )
+
+
+def gaps_of(wide, turned, later, head):
+    return jnp.exp((wide[head] - turned[pl.ds(head, 1), :]) + later[...])
+
+
+def quad_cumulative(wide, quad):
+    mask = first_head()
     return jnp.concatenate(
-        [turned_ref[pl.ds(2 * pair, 1), :], turned_ref[pl.ds(2 * pair + 1, 1), :]], axis=1
-    )
+        [
+            jnp.where(mask, wide[4 * quad], wide[4 * quad + 1]),
+            jnp.where(mask, wide[4 * quad + 2], wide[4 * quad + 3]),
+        ],
+        axis=1,
+    )
+
+
+def quad_lanes(quad, first=0):
+    return pl.ds(pl.multiple_of(quad * 2 * ssd_block + first, ssd_block), 2 * ssd_block)
 
 
 def lanes(block):
     return pl.ds(pl.multiple_of(block * ssd_block, ssd_block), ssd_block)
 
 
-def convolve(padded_ref, taps_ref, block):
-    columns = lanes(block)
+def convolve(padded_ref, taps_ref, columns):
     result = taps_ref[0:1, columns] * padded_ref[5 : 5 + ssd_block, columns]
     for tap in range(1, 4):
         result = result + taps_ref[tap : tap + 1, columns] * padded_ref[
@@ -961,14 +964,14 @@
     skip,
     decay,
     gain,
-    spread_wide,
-    spread_narrow,
     later,
     middle,
     outcome,
     starts,
     padded,
     turned,
+    wide,
+    narrow,
     state,
     gated,
 ):
@@ -988,36 +991,43 @@
     _, steps, _, cumulative = step_terms(
         projected[:, INNER + streams_extent : INNER + streams_extent + MHEADS], decay
     )
-    store_turned(cumulative, turned)
-    step_parts = three_parts(steps)
-    cumulative_parts = three_parts(cumulative)
-
-    def active(block):
-        convolved = convolve(padded, taps, block)
+    spread_heads(steps, cumulative, turned, wide, narrow)
+
+    def active(columns):
+        convolved = convolve(padded, taps, columns)
         return convolved * sigmoid(convolved)
 
-    in_low = to_low(active(INNER // ssd_block))
-    out_low = to_low(active(INNER // ssd_block + 1))
+    in_map = active(pl.ds(INNER, STATE))
+    in_low = to_low(in_map)
+    in_turned = to_low(in_map.T)
+    out_low = to_low(active(pl.ds(INNER + STATE, STATE)))
     affinity = low_dot(out_low, in_low, 1, 1)
-    affinity = jnp.concatenate([affinity, affinity], axis=1)
-    mask = first_head()
-
-    def pair_step(pair, square_sum):
-        columns = lanes(pair)
-        inputs = active(pair)
-        weighted = inputs * narrow(step_parts, spread_narrow, pair)
-        cumulative_wide = wide(cumulative_parts, spread_wide, pair)
-        mixing = to_low(affinity * gap_decay(cumulative_wide, turned_rows(turned, pair), later))
-        within = low_dot(mixing, both_heads(to_low(weighted)), 1, 0)
-        cumulative_here = jnp.where(
-            mask, cumulative_wide[:, :ssd_block], cumulative_wide[:, ssd_block:]
-        )
+
+    def quad_step(quad, square_sum):
+        columns = quad_lanes(quad)
+        inputs = active(columns)
+        weighted = inputs * narrow[:, columns]
+        weighted_low = to_low(weighted)
+        within = []
+        for pair in range(2):
+            head = 4 * quad + 2 * pair
+            mixing = jnp.concatenate(
+                [
+                    to_low(affinity * gaps_of(wide, turned, later, head)),
+                    to_low(affinity * gaps_of(wide, turned, later, head + 1)),
+                ],
+                axis=1,
+            )
+            part = weighted_low[:, pair * ssd_block : (pair + 1) * ssd_block]
+            within.append(low_dot(mixing, both_heads(part), 1, 0))
+        within = jnp.concatenate(within, axis=1)
+        cumulative_here = quad_cumulative(wide, quad)
         last = cumulative_here[ssd_block - 1 :, :]
         held = state[:, columns]
         starts[0, :, columns] = held
         across = jnp.exp(cumulative_here) * low_dot(out_low, to_low(held), 1, 0)
         to_end = to_low(weighted * jnp.exp(last - cumulative_here))
-        state[:, columns] = jnp.exp(last) * held + low_dot(in_low, to_end, 0, 0)
+        state[:, columns] = jnp.exp(last) * held + low_dot(in_turned, to_end, 1, 0)
         result = within + across + inputs * skip[:, columns]
         outcome[:, columns] = result
         gate = projected[:, columns]
@@ -1027,19 +1037,19 @@
 
     square_sum = lax.fori_loop(
         0,
-        INNER // ssd_block,
-        pair_step,
-        jnp.zeros((ssd_block, ssd_block), jnp.float32),
-        unroll=4,
+        INNER // (2 * ssd_block),
+        quad_step,
+        jnp.zeros((ssd_block, 2 * ssd_block), jnp.float32),
+        unroll=FORWARD_UNROLL,
     )
     scale = lax.rsqrt(jnp.sum(square_sum, axis=1, keepdims=True) * (1.0 / INNER) + norm_eps)
 
-    def scale_step(pair, carry):
-        columns = lanes(pair)
+    def scale_step(quad, carry):
+        columns = quad_lanes(quad)
         middle[:, columns] = to_low(gated[:, columns] * scale * gain[:, columns])
         return carry
 
-    lax.fori_loop(0, INNER // ssd_block, scale_step, 0, unroll=4)
+    lax.fori_loop(0, INNER // (2 * ssd_block), scale_step, 0, unroll=2)
 
 
 def middle_slope_kernel(
@@ -1052,10 +1062,8 @@
     skip,
     decay,
     gain,
-    spread_wide,
-    spread_narrow,
-    chosen_heads,
-    masked,
+    chosen,
+    later,
     slope_projected,
     slope_taps,
     slope_skip,
@@ -1063,6 +1071,8 @@
     slope_decay,
     padded,
     turned,
+    wide,
+    narrow,
     slope_state,
     slope_conv,
     slope_affinity,
@@ -1072,7 +1082,7 @@
 ):
     chunk = pl.num_programs(0) - 1 - pl.program_id(0)
     streams_extent = INNER + 2 * STATE
-    pairs = INNER // ssd_block
+    quads = INNER // (2 * ssd_block)
 
     @pl.when(pl.program_id(0) == 0)
     def _():
@@ -1103,16 +1113,13 @@
     shifted, steps, rates, cumulative = step_terms(
         projected[:, INNER + streams_extent : INNER + streams_extent + MHEADS], decay
     )
-    store_turned(cumulative, turned)
-    step_parts = three_parts(steps)
-    cumulative_parts = three_parts(cumulative)
+    spread_heads(steps, cumulative, turned, wide, narrow)
 
     def silu_pair(value_entries):
         share = sigmoid(value_entries)
         return value_entries * share, share * (1.0 + value_entries * (1.0 - share))
 
-    def pull_convolved(block, slope_block):
-        columns = lanes(block)
+    def pull_convolved(columns, target_columns, slope_block):
         slope_conv[0:ssd_block, columns] = slope_block
         result = taps[3:4, columns] * slope_block
         for tap in range(3):
@@ -1124,17 +1131,17 @@
             slope_taps[tap, :, columns] += fold_rows(
                 slope_block * padded[5 + tap : 5 + tap + ssd_block, columns]
             )
-        slope_projected[:, lanes(block + pairs)] = to_low(result)
-
-    in_map, in_pull = silu_pair(convolve(padded, taps, pairs))
-    out_map, out_pull = silu_pair(convolve(padded, taps, pairs + 1))
-    in_low, out_low = to_low(in_map), to_low(out_map)
+        slope_projected[:, target_columns] = to_low(result)
+
+    maps = (pl.ds(INNER, STATE), pl.ds(INNER + STATE, STATE))
+    in_map, in_pull = silu_pair(convolve(padded, taps, maps[0]))
+    out_map, out_pull = silu_pair(convolve(padded, taps, maps[1]))
+    in_low, out_low, out_turned = to_low(in_map), to_low(out_map), to_low(out_map.T)
     affinity = low_dot(out_low, in_low, 1, 1)
-    affinity = jnp.concatenate([affinity, affinity], axis=1)
     mask = first_head()
 
-    def sums_step(pair, sums):
-        columns = lanes(pair)
+    def sums_step(quad, sums):
+        columns = quad_lanes(quad)
         gate = projected[:, columns]
         product = outcome[:, columns] * (gate * sigmoid(gate))
         return (
@@ -1142,13 +1149,13 @@
             sums[1] + product * (slope[:, columns] * gain[:, columns]),
         )
 
-    blank = jnp.zeros((ssd_block, ssd_block), jnp.float32)
-    squares, crossed = lax.fori_loop(0, pairs, sums_step, (blank, blank), unroll=2)
+    blank = jnp.zeros((ssd_block, 2 * ssd_block), jnp.float32)
+    squares, crossed = lax.fori_loop(0, quads, sums_step, (blank, blank), unroll=2)
     scale = lax.rsqrt(jnp.sum(squares, axis=1, keepdims=True) * (1.0 / INNER) + norm_eps)
     pulled = scale * scale * scale * (jnp.sum(crossed, axis=1, keepdims=True) * (1.0 / INNER))
 
-    def pair_step(pair, carry):
-        columns = lanes(pair)
+    def quad_step(quad, carry):
+        columns = quad_lanes(quad)
         gate, total_here = projected[:, columns], outcome[:, columns]
         gate_value, gate_pull = silu_pair(gate)
         product = total_here * gate_value
@@ -1157,70 +1164,74 @@
         slope_product = scale * (slope_here * gain[:, columns]) - product * pulled
         slope_out = slope_product * gate_value
         slope_projected[:, columns] = to_low(slope_product * total_here * gate_pull)
-        inputs, inputs_pull = silu_pair(convolve(padded, taps, pair))
+        inputs, inputs_pull = silu_pair(convolve(padded, taps, columns))
         slope_skip[:, columns] += fold_rows(slope_out * inputs)
         skip_here = skip[:, columns]
         scanned = total_here - inputs * skip_here
-        steps_here = narrow(step_parts, spread_narrow, pair)
+        steps_here = narrow[:, columns]
         weighted = inputs * steps_here
         weighted_low = to_low(weighted)
         slope_low = to_low(slope_out)
-        cumulative_wide = wide(cumulative_parts, spread_wide, pair)
-        gaps = gap_decay(cumulative_wide, turned_rows(turned, pair), masked)
-        mixing = to_low(affinity * gaps)
-        slope_mixing = low_dot(slope_low, both_heads(weighted_low), 1, 1)
-        slope_gaps = slope_mixing * gaps
-        slope_affinity[...] += slope_gaps[:, :ssd_block] + slope_gaps[:, ssd_block:]
-        turned_back = low_dot(mixing, slope_low, 0, 0)
-        slope_weighted = jnp.where(mask, turned_back[:ssd_block], turned_back[ssd_block:])
-        cumulative_here = jnp.where(
-            mask, cumulative_wide[:, :ssd_block], cumulative_wide[:, ssd_block:]
-        )
+        slope_within = []
+        for pair in range(2):
+            head = 4 * quad + 2 * pair
+            here_low = slope_low[:, pair * ssd_block : (pair + 1) * ssd_block]
+            part = weighted_low[:, pair * ssd_block : (pair + 1) * ssd_block]
+            slope_mixing = low_dot(here_low, both_heads(part), 1, 1)
+            mixing = []
+            for side in range(2):
+                gaps = gaps_of(wide, turned, later, head + side)
+                mixing.append(to_low(affinity * gaps))
+                slope_affinity[...] += (
+                    slope_mixing[:, side * ssd_block : (side + 1) * ssd_block] * gaps
+                )
+            turned_back = low_dot(jnp.concatenate(mixing, axis=1), here_low, 0, 0)
+            slope_within.append(
+                jnp.where(mask, turned_back[:ssd_block], turned_back[ssd_block:])
+            )
+        slope_within = jnp.concatenate(slope_within, axis=1)
+        cumulative_here = quad_cumulative(wide, quad)
         last = cumulative_here[ssd_block - 1 :, :]
         decayed = jnp.exp(last)
         held = starts[0, :, columns]
-        held_low = to_low(held)
         slope_across = to_low(slope_out * jnp.exp(cumulative_here))
-        slope_maps[1] += low_dot(slope_across, held_low, 1, 1)
-        later = slope_state[:, columns]
-        later_low = to_low(later)
+        slope_maps[1] += low_dot(slope_across, to_low(held), 1, 1)
+        carried_state = slope_state[:, columns]
+        carried_low = to_low(carried_state)
         to_end = jnp.exp(last - cumulative_here)
-        carried = to_low(weighted * to_end)
-        slope_carried = low_dot(in_low, later_low, 1, 0)
-        slope_maps[0] += low_dot(carried, later_low, 1, 1)
-        slope_state[:, columns] = decayed * later + low_dot(out_low, slope_across, 0, 0)
-        slope_within = slope_weighted
-        slope_weighted = slope_weighted + slope_carried * to_end
-        carried_slope = slope_carried * carried.astype(jnp.float32)
-        ends = jnp.sum(carried_slope, axis=0, keepdims=True) + decayed * jnp.sum(
-            later * held, axis=0, keepdims=True
+        ending = to_low(weighted * to_end)
+        slope_ending = low_dot(in_low, carried_low, 1, 0)
+        slope_maps[0] += low_dot(ending, carried_low, 1, 1)
+        slope_state[:, columns] = decayed * carried_state + low_dot(out_turned, slope_across, 1, 0)
+        slope_weighted = slope_within + slope_ending * to_end
+        ending_slope = slope_ending * ending.astype(jnp.float32)
+        ends = jnp.sum(ending_slope, axis=0, keepdims=True) + decayed * jnp.sum(
+            carried_state * held, axis=0, keepdims=True
         )
-        rows = lax.broadcasted_iota(jnp.int32, (ssd_block, ssd_block), 0)
+        rows = lax.broadcasted_iota(jnp.int32, (ssd_block, 2 * ssd_block), 0)
         slope_gathered = (
             slope_low.astype(jnp.float32) * scanned
             - weighted_low.astype(jnp.float32) * slope_within
-            - carried_slope
+            - ending_slope
             + jnp.where(rows == ssd_block - 1, ends, 0.0)
         )
-        chosen = chosen_heads[lanes(pair), :]
-
-        def head_sums(value_entries):
+        parts = []
+        for value_entries in (slope_gathered, slope_weighted * inputs):
             high = to_low(value_entries)
-            rest = to_low(value_entries - high.astype(jnp.float32))
-            return low_dot(high, chosen, 1, 0) + low_dot(rest, chosen, 1, 0)
-
-        slope_cumulative[...] += head_sums(slope_gathered)
-        slope_steps[...] += head_sums(slope_weighted * inputs)
+            parts += [high, to_low(value_entries - high.astype(jnp.float32))]
+        sums = low_dot(jnp.concatenate(parts, axis=0), chosen[columns, :], 1, 0)
+        slope_cumulative[...] += sums[:ssd_block] + sums[ssd_block : 2 * ssd_block]
+        slope_steps[...] += sums[2 * ssd_block : 3 * ssd_block] + sums[3 * ssd_block :]
         slope_inputs = slope_out * skip_here + slope_weighted * steps_here
-        pull_convolved(pair, slope_inputs * inputs_pull)
+        pull_convolved(columns, quad_lanes(quad, INNER), slope_inputs * inputs_pull)
         return carry
 
-    lax.fori_loop(0, pairs, pair_step, 0, unroll=2)
+    lax.fori_loop(0, quads, quad_step, 0, unroll=BACKWARD_UNROLL)
     affinity_low = to_low(slope_affinity[...])
     slope_in = slope_maps[0] + low_dot(affinity_low, out_low, 0, 0)
     slope_out_map = slope_maps[1] + low_dot(affinity_low, in_low, 1, 0)
-    pull_convolved(pairs, slope_in * in_pull)
-    pull_convolved(pairs + 1, slope_out_map * out_pull)
+    pull_convolved(maps[0], pl.ds(2 * INNER, STATE), slope_in * in_pull)
+    pull_convolved(maps[1], pl.ds(2 * INNER + STATE, STATE), slope_out_map * out_pull)
     slope_changes = lax.dot_general(
         lower_ones(),
         slope_cumulative[...],
@@ -1243,7 +1254,7 @@
 
 def middle_forward(projected, smalls):
     conv_taps, skip_gain, a_log, dt_bias, gated_gain = smalls
-    spread_wide, spread_narrow, chosen, later = head_tables()
+    chosen, later = head_tables()
     extent, columns = projected.shape
     chunks = extent // ssd_block
     streams_extent = INNER + 2 * STATE
@@ -1261,8 +1272,6 @@
             fixed((1, INNER)),
             fixed((2, MHEADS)),
             fixed((1, INNER)),
-            fixed(spread_wide.shape),
-            fixed(spread_narrow.shape),
             fixed(later.shape),
         ],
         out_specs=(
@@ -1273,6 +1282,8 @@
         scratch_shapes=[
             pltpu.VMEM((ssd_block + 8, streams_extent), jnp.float32),
             pltpu.VMEM((ssd_block, ssd_block), jnp.float32),
+            pltpu.VMEM((MHEADS, ssd_block, ssd_block), jnp.float32),
+            pltpu.VMEM((ssd_block, INNER), jnp.float32),
             pltpu.VMEM((STATE, INNER), jnp.float32),
             pltpu.VMEM((ssd_block, INNER), jnp.float32),
         ],
@@ -1286,15 +1297,13 @@
         skip_gain.reshape(1, INNER),
         jnp.stack([a_log, dt_bias]),
         gated_gain.reshape(1, INNER),
-        spread_wide,
-        spread_narrow,
         later,
     )
 
 
 def middle_backward(projected, outcome, starts, slope, smalls):
     conv_taps, skip_gain, a_log, dt_bias, gated_gain = smalls
-    spread_wide, spread_narrow, chosen, later = head_tables()
+    chosen, later = head_tables()
     extent, columns = projected.shape
     chunks = extent // ssd_block
     streams_extent = INNER + 2 * STATE
@@ -1325,8 +1334,6 @@
             fixed((1, INNER)),
             fixed((2, MHEADS)),
             fixed((1, INNER)),
-            fixed(spread_wide.shape),
-            fixed(spread_narrow.shape),
             fixed(chosen.shape),
             fixed(later.shape),
         ],
@@ -1340,6 +1347,8 @@
         scratch_shapes=[
             pltpu.VMEM((ssd_block + 8, streams_extent), jnp.float32),
             pltpu.VMEM((ssd_block, ssd_block), jnp.float32),
+            pltpu.VMEM((MHEADS, ssd_block, ssd_block), jnp.float32),
+            pltpu.VMEM((ssd_block, INNER), jnp.float32),
             pltpu.VMEM((STATE, INNER), jnp.float32),
             pltpu.VMEM((ssd_block + 8, streams_extent), jnp.float32),
             pltpu.VMEM((ssd_block, ssd_block), jnp.float32),
@@ -1361,8 +1370,6 @@
         skip_gain.reshape(1, INNER),
         jnp.stack([a_log, dt_bias]),
         gated_gain.reshape(1, INNER),
-        spread_wide,
-        spread_narrow,
         chosen,
         later,
     )
@@ -1401,7 +1408,7 @@
     slope_middle = product_nt(grad_low, exit_matrix)
     slope_middle = conductor.tick(after(slope_middle, [slope_exit_matrix]), 7.0)
     grad_proj, slope_smalls = middle_backward(*middle_kept, slope_middle, smalls)
-    grad_proj = conductor.tick(grad_proj, 48.0, limit=0 if last else 5)
+    grad_proj = conductor.tick(grad_proj, 60.0 if last else 44.0, limit=0 if last else 5)
     grad_w_in = to_low(product_tn(normed_low, grad_proj))
     job_in = conductor.add(Summing(grad_w_in, True))
     grad_proj = conductor.tick(after(grad_proj, [grad_w_in]), 7.0, limit=0 if last else 5)
@@ -1704,6 +1711,7 @@
     gradient_merged, gradient_blank = merge_transpose(gradient_holder)
     grad_query, grad_key = prob_pull(slope_likelihood)
     grad_routed = to_low(jnp.concatenate([grad_query, grad_key, slope_shortcut], axis=1))
+    grad_routed = after(grad_routed, [gradient_merged])
     grad_route = to_low(product_tn(encoded_low, grad_routed))
     job_route = conductor.add(Summing(grad_route, True))
     grad_routed = conductor.tick(after(grad_routed, [grad_route]), 7.0)
@@ -1759,14 +1767,11 @@
         jobs_enc[1],
         Summing(grad_mixed.reshape(-1, BYTE_WIDTH), True),
     ]
-    sums = [None if part.masks else part.result() for part in parts]
+    sums = [None if part.masks else part.result(jobs_enc[1].addends[0]) for part in parts]
     open_parts = [number for number, part in enumerate(parts) if part.masks]
-    rests = [parts[number].rest() for number in open_parts]
+    rests = [parts[number].rest(jobs_enc[1].addends[0]) for number in open_parts]
     grads = [grad for grad, _ in rests]
-    sum_kinds = [
-        kind[::-1] if number == 0 and len(kind) == 2 else kind
-        for number, (_, kind) in enumerate(rests)
-    ]
+    sum_kinds = [kind for _, kind in rests]
     if exact_tiles:
         early = sum((jnp.sum(part * part) for part in sums if part is not None), jnp.float32(0.0))
         extra = jnp.zeros((16, 128), jnp.float32).at[0, 0].set(early).at[8, 0].set(loss_local)

time: 1010 us -> 964 us (0.954)
  Pallas kernels: 579 us -> 536 us
  waiting for transfers between devices: 63.1 us -> 77.5 us
  matrix products: 164 us -> 150 us
    pallas_call x1, Pallas kernels: 206 us -> 176 us  [sum_whole(): pl.pallas_call(partial(sum_kernel, plan, kinds, depth_z), out_shape=tuple...]
    squeeze x5 -> x16, local copies, waits for them, and re-layouts: 9.06 us -> 23.6 us  [take(): return lax.dynamic_index_in_dim(value_entries, index, axis, keepdims=False)]
    ppermute x34 -> x37, waiting for transfers between devices: 63.1 us -> 77.5 us  [swap(): lax.ppermute(value_entries, axis, [(place, place ^ mask) for place in ran...]
    pallas_call x2, Pallas kernels: 97.2 us -> 86.4 us  [middle_backward(): pl.pallas_call(middle_slope_kernel, grid=(chunks,), out_shape=(jax.ShapeD...]
    unnamed x398 -> x417, local copies, waits for them, and re-layouts: 48 us -> 39.6 us
    ppermute x34 -> x37, starting transfers between devices: 22 us -> 21 us  [swap(): lax.ppermute(value_entries, axis, [(place, place ^ mask) for place in ran...]
    convert_element_type x25 -> x26, other arithmetic: 37.4 us -> 36.4 us  [to_low(): return value_entries.astype(jnp.bfloat16)]
  transfers between devices with their start and end apart: 34 -> 37, of which waited for: 13 -> 13; matrix products, arithmetic and copies ran while one was open for 11% -> 14% of each run, Pallas kernels for 10% -> 9%
where the time goes in v3:
time: 964 us; the launch traced here: 958 us
  Pallas kernels  536 us (56%)
  matrix products  150 us (16%)
  local copies, waits for them, and re-layouts  83.7 us (9%)
  other arithmetic  82.2 us (9%)
  waiting for transfers between devices  77.5 us (8%)
  starting transfers between devices  21 us (2%)
    pallas_call x1, Pallas kernels, spread_whole(): pl.pallas_call(partial(spread_kernel, plan, jobs, depth_z), out_shape=tup...  230 us
    pallas_call x1, Pallas kernels, sum_whole(): pl.pallas_call(partial(sum_kernel, plan, kinds, depth_z), out_shape=tuple...  176 us
    pallas_call x2, Pallas kernels, middle_backward(): pl.pallas_call(middle_slope_kernel, grid=(chunks,), out_shape=(jax.ShapeD...  86.4 us
    ppermute x37, waiting for transfers between devices, swap(): lax.ppermute(value_entries, axis, [(place, place ^ mask) for place in ran...  77.5 us
    dot_general x11, matrix products, matmul_apply(): return jnp.dot(left, right, preferred_element_type=jnp.float32)  46.4 us
    dot_general x10, matrix products, product_nt(): lax.dot_general(left, right, (((1,), (1,)), ((), ())), preferred_element_...  44 us
    dot_general x11, matrix products, product_tn(): lax.dot_general(left, right, (((0,), (0,)), ((), ())), preferred_element_...  43.4 us
    pallas_call x2, Pallas kernels, middle_forward(): pl.pallas_call(middle_kernel, grid=(chunks,), out_shape=(jax.ShapeDtypeSt...  43.1 us
  transfers between devices with their start and end apart: 37, of which 13 were waited for; matrix products, arithmetic and copies ran while one was open for 14% of the time, Pallas kernels for 9%

profile of v3, /device:TPU:0, one launch (start us, length us, event | category | flops | bytes accessed | tf_op | source)
XLA Modules:
  0.0 957.7 jit_solution(14100042447955229439)
XLA Ops:
  13.9 229.7 %shard_map.526 = (bf16[4,2,2,2,32,1024]{5,4,3,2,1,0:T(8,128)(2,1)}, bf16[4,2,2,2,32,4480]{5,4,3,2,1,0:T(8,128)(2,1)}, bf16[4,2,2,2,64,1024]{5,4,3,2,1,0:T(8,128)...) custom-call(bf16[32,1024]{1,0:T(8,128)(2,1)} %pad_maximum_fusion.12., ...), custom_call_target="tpu_custom_call" | custom-call | tf_op jit(solution)/shard_map/pallas_call | solution.py:536
  249.7 11.4 %fusion.142.projected.earlier = f32[512,4480]{1,0:T(8,128)} fusion(bf16[1024,4480]{1,0:T(8,128)(2,1)} %bitcast.460, f32[512,1024]{1,0:T(8,128)S(1)} %get-tuple-element.446, f32[1024]{0:T(1024)S(1)} %get-tuple-element.426, f32[512]{0:T(512)S(1)} %fusion.122), kind=kOutput, calls=%fused_computation.398 | convolution fusion | flops 4699193344 | bytes 20453376 | tf_op jit(solution)/shard_map/dot_general | solution.py:172
  261.1 21.6 %shard_map.527 = (bf16[512,2048]{1,0:T(8,128)(2,1)S(1)}, f32[512,2048]{1,0:T(8,128)}, f32[4,128,2048]{2,1,0:T(8,128)}) custom-call(f32[512,4480]{1,0:T(8,128)} %fusion.142.projected.earlier, f32[4,2304]{1,0:T(4,128)S(1)} %squeeze.137.taps, f32[1,2048]{1,0:T(1,128)S(1)} %bitcast.375, f32[2,32]{1,0:T(2,128)S(1)} %get-tuple-element.461.decay, ...), custom_call_target="tpu_custom_call" | custom-call | flops 20000000000 | bytes 20000000 | tf_op jit(solution)/shard_map/pallas_call | solution.py:1261
  282.7 2.4 convolution_add_fusion.2
  288.5 5.5 fusion.62
  294.6 2.1 copy-done.14
  302.1 3.3 convolution_convert_fusion.10
  316.4 10.5 %collective-permute-done.5 = bf16[128,1536]{1,0:T(8,128)(2,1)S(1)} collective-permute-done((bf16[128,1536]{1,0:T(8,128)(2,1)S(1)}, bf16[128,1536]{1,0:T(8,128)(2,1)S(1)}, u32[]{:S(2)}, u32[]{:S(2)}) %collective-permute-start.5) | collective-permute-done | bytes 393248 | tf_op jit(solution)/shard_map/ppermute | solution.py:189
  328.2 9.7 %collective-permute-done.6 = bf16[128,1536]{1,0:T(8,128)(2,1)S(1)} collective-permute-done((bf16[128,1536]{1,0:T(8,128)(2,1)S(1)}, bf16[128,1536]{1,0:T(8,128)(2,1)S(1)}, u32[]{:S(2)}, u32[]{:S(2)}) %collective-permute-start.6) | collective-permute-done | bytes 393248 | tf_op jit(solution)/shard_map/ppermute | solution.py:189
  339.6 3.5 fusion.144
  354.2 10.3 %collective-permute-done.11 = bf16[128,1536]{1,0:T(8,128)(2,1)S(1)} collective-permute-done((bf16[128,1536]{1,0:T(8,128)(2,1)S(1)}, bf16[128,1536]{1,0:T(8,128)(2,1)S(1)}, u32[]{:S(2)}, u32[]{:S(2)}) %collective-permute-start.11) | collective-permute-done | bytes 393248 | tf_op jit(solution)/shard_map/ppermute | solution.py:189
  366.6 4.4 multiply_reduce_fusion.10
  371.0 12.0 %fusion.143.projected.earlier = f32[512,4480]{1,0:T(8,128)} fusion(bf16[1024,4480]{1,0:T(8,128)(2,1)} %bitcast.462, f32[512,1024]{1,0:T(8,128)S(1)} %get-tuple-element.382, f32[1024]{0:T(1024)S(1)} %get-tuple-element.425, f32[512]{0:T(512)S(1)} %fusion.123), kind=kOutput, calls=%fused_computation.399 | convolution fusion | flops 4699193344 | bytes 20453376 | tf_op jit(solution)/shard_map/dot_general | solution.py:172
  383.0 21.6 %shard_map.528 = (bf16[512,2048]{1,0:T(8,128)(2,1)S(1)}, f32[512,2048]{1,0:T(8,128)}, f32[4,128,2048]{2,1,0:T(8,128)}) custom-call(f32[512,4480]{1,0:T(8,128)} %fusion.143.projected.earlier, f32[4,2304]{1,0:T(4,128)S(1)} %slice.409.taps, f32[1,2048]{1,0:T(1,128)S(1)} %bitcast.379, f32[2,32]{1,0:T(2,128)S(1)} %get-tuple-element.462.decay, ...), custom_call_target="tpu_custom_call" | custom-call | flops 20000000000 | bytes 20000000 | tf_op jit(solution)/shard_map/pallas_call | solution.py:1261
  404.6 2.4 multiply_reduce_fusion.9
  411.9 4.5 fusion.57.slope
  416.4 2.4 convolution_convert_fusion.8
  420.6 2.6 copy-done.11
  423.1 43.3 %shard_map.529 = (bf16[512,4480]{1,0:T(8,128)(2,1)}, f32[4,8,2304]{2,1,0:T(8,128)S(1)}, f32[8,2048]{1,0:T(8,128)S(1)}, f32[8,2048]{1,0:T(8,128)S(1)}, f32[2,8,32]{2,1,0:T(8,128)S(1)}) custom-call(f32[512,4480]{1,0:T(8,128)} %fusion.143.projected.earlier, f32[512,4480]{1,0:T(8,128)} %fusion.143.projected.earlier, f32[512,2048]{1,0:T(8,128)S(1)} %copy-done.11, ...), custom_call_target="tpu_custom_call" | custom-call | flops 49999998976 | bytes 30000000 | tf_op jit(solution)/shard_map/pallas_call | solution.py:1314
  471.4 4.0 convolution_convert_fusion.15
  475.4 3.1 fusion.7
  479.0 5.5 convolution_convert_fusion.1
  484.5 2.5 copy_bitcast_fusion
  487.0 9.4 multiply_reduce_fusion.1
  497.3 2.0 fusion.8
  508.0 8.4 collective-permute-done.14
  516.4 1.9 pad_maximum_fusion
  528.7 2.4 copy-done.177
  531.0 2.4 fusion.92
  533.8 6.3 convolution_convert_fusion.11
  545.8 2.0 dynamic-slice_bitcast_fusion.5
  547.9 2.0 dynamic-slice_bitcast_fusion.6
  551.4 4.6 collective-permute-done.20
  560.9 7.2 collective-permute-done.22
  571.2 3.1 collective-permute-done.25
  583.2 2.0 convolution_convert_fusion.14
  585.2 2.2 convolution_convert_fusion.9
  591.9 15.3 %collective-permute-done.30 = bf16[2,2,192,1024]{3,2,1,0:T(8,128)(2,1)} collective-permute-done((bf16[2,2,192,1024]{3,2,1,0:T(8,128)(2,1)}, bf16[2,2,192,1024]{3,2,1,0:T(8,128)(2,1)}, u32[]{:S(2)}, u32[]{:S(2)}) %collective-permute-start.30) | collective-permute-done | bytes 1572896 | tf_op jit(solution)/shard_map/ppermute | solution.py:189
  608.2 2.7 fusion.14
  612.7 5.7 convolution_convert_fusion.2
  618.4 4.3 collective-permute-done.28
  625.9 3.7 convolution_convert_fusion.3
  631.3 3.2 dynamic-slice_bitcast_fusion
  634.5 5.7 convolution_add_fusion
  640.3 4.4 fusion.54.slope
  644.7 4.4 convolution_convert_fusion.4
  649.1 2.4 collective-permute-start.34
  651.5 43.1 %shard_map.530 = (bf16[512,4480]{1,0:T(8,128)(2,1)}, f32[4,8,2304]{2,1,0:T(8,128)S(1)}, f32[8,2048]{1,0:T(8,128)S(1)}, f32[8,2048]{1,0:T(8,128)S(1)}, f32[2,8,32]{2,1,0:T(8,128)S(1)}) custom-call(f32[512,4480]{1,0:T(8,128)} %fusion.142.projected.earlier, f32[512,4480]{1,0:T(8,128)} %fusion.142.projected.earlier, f32[512,2048]{1,0:T(8,128)S(1)} %copy-done.10, ...), custom_call_target="tpu_custom_call" | custom-call | flops 49999998976 | bytes 30000000 | tf_op jit(solution)/shard_map/pallas_call | solution.py:1314
  699.1 10.1 %convolution_convert_fusion = bf16[1024,4480]{1,0:T(8,128)(2,1)} fusion(bf16[512,4480]{1,0:T(8,128)(2,1)} %get-tuple-element.212, f32[512,1024]{1,0:T(8,128)S(1)} %copy-done.27, f32[1024]{0:T(1024)S(1)} %copy-done.148, f32[512]{0:T(512)S(1)} %copy-done.151), kind=kOutput, calls=%fused_computation | convolution fusion | flops 4703780864 | bytes 15865856 | tf_op jit(solution)/shard_map/dot_general | solution.py:176
  710.1 8.0 multiply_reduce_fusion.3
  718.9 2.1 convolution_convert_fusion.16
  723.0 2.8 fusion.141
  729.6 4.8 add_convert_fusion
  734.4 3.4 add_convert_fusion.3
  737.8 3.4 add_convert_fusion.4
  741.2 4.0 add_convert_fusion.1
  747.6 176.4 %shard_map.531 = (f32[192,384]{1,0:T(8,128)}, f32[192,1024]{1,0:T(8,128)}, f32[192,1024]{1,0:T(8,128)}, f32[192,1152]{1,0:T(8,128)}, f32[32,4480]{1,0:T(8,128)},...) custom-call(bf16[4,2,192,384]{3,2,1,0:T(8,128)(2,1)} %bitcast.425, ...), custom_call_target="tpu_custom_call" | custom-call | tf_op jit(solution)/shard_map/pallas_call | solution.py:794
  931.4 4.2 multiply_subtract_fusion
  935.6 2.4 copy.152
  937.9 2.4 copy.151
  940.3 2.4 copy.150
  943.5 2.1 multiply_subtract_fusion.3
  949.5 1.9 multiply_subtract_fusion.2
  954.0 2.3 multiply_subtract_fusion.1
  (690 shorter events, 148.3 us)
Async XLA Ops:
  247.8 38.7 %copy-start.118 = (f32[1536]{0:T(1024)}, f32[1536]{0:T(1024)S(1)}, u32[]{:S(2)}) copy-start(f32[1536]{0:T(1024)S(1)} %get-tuple-element.422) | copy-start | bytes 18436
  247.8 79.5 %copy-start.120 = (f32[1536]{0:T(1024)}, f32[1536]{0:T(1024)S(1)}, u32[]{:S(2)}) copy-start(f32[1536]{0:T(1024)S(1)} %get-tuple-element.421) | copy-start | bytes 18436
  247.9 66.1 %copy-start.134 = (f32[1,512]{1,0:T(1,128)}, f32[1,512]{1,0:T(1,128)S(1)}, u32[]{:S(2)}) copy-start(f32[1,512]{1,0:T(1,128)S(1)} %convert_element_type.495) | copy-start | bytes 6148
  249.1 33.6 %copy-start.26 = (f32[512,1024]{1,0:T(8,128)}, f32[512,1024]{1,0:T(8,128)S(1)}, u32[]{:S(2)}) copy-start(f32[512,1024]{1,0:T(8,128)S(1)} %get-tuple-element.446) | copy-start | bytes 6291460
  249.1 77.7 %copy-start.107 = (f32[1536]{0:T(1024)}, f32[1536]{0:T(1024)S(1)}, u32[]{:S(2)}) copy-start(f32[1536]{0:T(1024)S(1)} %pad.108.clone) | copy-start | bytes 18436
  261.1 21.6 %copy-start.170 = (bf16[4,2,2,2,64,1024]{5,4,3,2,1,0:T(8,128)(2,1)S(1)}, bf16[4,2,2,2,64,1024]{5,4,3,2,1,0:T(8,128)(2,1)}, u32[]{:S(2)}) copy-start(bf16[4,2,2,2,64,1024]{5,4,3,2,1,0:T(8,128)(2,1)} %get-tuple-element.151) | copy-start | bytes 12582916
  286.4 40.5 %copy-start.17 = (f32[128,1024]{1,0:T(8,128)}, f32[128,1024]{1,0:T(8,128)S(1)}, u32[]{:S(2)}) copy-start(f32[128,1024]{1,0:T(8,128)S(1)} %fusion.68) | copy-start | bytes 1572868
  286.7 12.9 %collective-permute-start.1 = (bf16[128,1536]{1,0:T(8,128)(2,1)S(1)}, bf16[128,1536]{1,0:T(8,128)(2,1)}, u32[]{:S(2)}, u32[]{:S(2)}) collective-permute-start(bf16[128,1536]{1,0:T(8,128)(2,1)S(1)} %multiply_convert_fusion.6), channel_id=1, source_target_pairs={{0,1},{1,0},{2,3},{3,2},{4,5},{5,4},{6,7},{7,6},{8,9},{9,8},{10,11... | collective-permute-start | bytes 1179656 | tf_op jit(solution)/shard_map/ppermute | solution.py:189
  286.8 12.5 %collective-permute-start = (bf16[128,1536]{1,0:T(8,128)(2,1)S(1)}, bf16[128,1536]{1,0:T(8,128)(2,1)}, u32[]{:S(2)}, u32[]{:S(2)}) collective-permute-start(bf16[128,1536]{1,0:T(8,128)(2,1)S(1)} %multiply_convert_fusion.6), channel_id=1, source_target_pairs={{0,2},{1,3},{2,0},{3,1},{4,6},{5,7},{6,4},{7,5},{8,10},{9,11},{10,... | collective-permute-start | bytes 1179656 | tf_op jit(solution)/shard_map/ppermute | solution.py:189
  299.3 2.0 collective-permute-start.2
  311.9 27.6 %slice-start.2 = ((s8[6291456]{0:T(1024)(128)(4,1)}), s8[4194304]{0:T(1024)(128)(4,1)S(1)}, s32[]{:S(2)}) async-start(s8[6291456]{0:T(1024)(128)(4,1)} %bitcast.467), calls=%async_computation.2 | async-start | bytes 8388608
  313.7 25.9 %slice-start.3 = ((s8[6291456]{0:T(1024)(128)(4,1)}), s8[2097152]{0:T(1024)(128)(4,1)S(1)}, s32[]{:S(2)}) async-start(s8[6291456]{0:T(1024)(128)(4,1)} %bitcast.467), calls=%async_computation.3 | async-start | bytes 4194304
  313.7 1.8 collective-permute-start.4
  314.4 2.0 collective-permute-start.3
  315.6 11.2 %collective-permute-start.5 = (bf16[128,1536]{1,0:T(8,128)(2,1)S(1)}, bf16[128,1536]{1,0:T(8,128)(2,1)S(1)}, u32[]{:S(2)}, u32[]{:S(2)}) collective-permute-start(bf16[128,1536]{1,0:T(8,128)(2,1)S(1)} %add_convert_fusion.8), channel_id=1, source_target_pairs={{0,2},{1,3},{2,0},{3,1},{4,6},{5,7},{6,4},{7,5},{8,10},{9,11},{10,... | collective-permute-start | bytes 1179656 | tf_op jit(solution)/shard_map/ppermute | solution.py:189
  327.2 15.9 %copy-start.168 = (f32[128]{0:T(128)}, f32[128]{0:T(128)S(1)}, u32[]{:S(2)}) copy-start(f32[128]{0:T(128)S(1)} %get-tuple-element.385) | copy-start | bytes 1540
  327.2 37.3 %copy-start.15 = (f32[128,1536]{1,0:T(8,128)}, f32[128,1536]{1,0:T(8,128)S(1)}, u32[]{:S(2)}) copy-start(f32[128,1536]{1,0:T(8,128)S(1)} %get-tuple-element.386) | copy-start | bytes 2359300
  327.4 10.4 %collective-permute-start.6 = (bf16[128,1536]{1,0:T(8,128)(2,1)S(1)}, bf16[128,1536]{1,0:T(8,128)(2,1)S(1)}, u32[]{:S(2)}, u32[]{:S(2)}) collective-permute-start(bf16[128,1536]{1,0:T(8,128)(2,1)S(1)} %multiply_convert_fusion.5), channel_id=1, source_target_pairs={{0,2},{1,3},{2,0},{3,1},{4,6},{5,7},{6,4},{7,5},{8,10},{9,11},{10,... | collective-permute-start | bytes 1179656 | tf_op jit(solution)/shard_map/ppermute | solution.py:189
  328.1 9.8 %collective-permute-start.7 = (bf16[128,1536]{1,0:T(8,128)(2,1)S(1)}, bf16[128,1536]{1,0:T(8,128)(2,1)S(1)}, u32[]{:S(2)}, u32[]{:S(2)}) collective-permute-start(bf16[128,1536]{1,0:T(8,128)(2,1)S(1)} %multiply_convert_fusion.5), channel_id=1, source_target_pairs={{0,1},{1,0},{2,3},{3,2},{4,5},{5,4},{6,7},{7,6},{8,9},{9,8},{10,11... | collective-permute-start | bytes 1179656 | tf_op jit(solution)/shard_map/ppermute | solution.py:189
  337.8 1.7 collective-permute-start.8
  350.0 2.1 collective-permute-start.10
  351.8 2.4 collective-permute-start.9
  353.2 11.3 %collective-permute-start.11 = (bf16[128,1536]{1,0:T(8,128)(2,1)S(1)}, bf16[128,1536]{1,0:T(8,128)(2,1)S(1)}, u32[]{:S(2)}, u32[]{:S(2)}) collective-permute-start(bf16[128,1536]{1,0:T(8,128)(2,1)S(1)} %add_convert_fusion.7), channel_id=1, source_target_pairs={{0,2},{1,3},{2,0},{3,1},{4,6},{5,7},{6,4},{7,5},{8,10},{9,11},{10,... | collective-permute-start | bytes 1179656 | tf_op jit(solution)/shard_map/ppermute | solution.py:189
  371.0 33.6 %copy-start.28 = (f32[512,1024]{1,0:T(8,128)}, f32[512,1024]{1,0:T(8,128)S(1)}, u32[]{:S(2)}) copy-start(f32[512,1024]{1,0:T(8,128)S(1)} %get-tuple-element.382) | copy-start | bytes 6291460
  383.0 21.6 %copy-start.172 = (bf16[4,2,2,2,64,1024]{5,4,3,2,1,0:T(8,128)(2,1)S(1)}, bf16[4,2,2,2,64,1024]{5,4,3,2,1,0:T(8,128)(2,1)}, u32[]{:S(2)}) copy-start(bf16[4,2,2,2,64,1024]{5,4,3,2,1,0:T(8,128)(2,1)} %get-tuple-element.161) | copy-start | bytes 12582916
  418.7 47.7 %copy-start.44 = (bf16[2048,1024]{1,0:T(8,128)(2,1)}, bf16[2048,1024]{1,0:T(8,128)(2,1)S(1)}, u32[]{:S(2)}) copy-start(bf16[2048,1024]{1,0:T(8,128)(2,1)S(1)} %convolution_convert_fusion.8) | copy-start | bytes 12582916
  420.6 54.8 %collective-permute-start.12 = (bf16[2,2,2,2,64,1024]{5,4,1,3,2,0:T(8,128)(2,1)}, bf16[2,2,2,2,64,1024]{5,4,1,3,2,0:T(8,128)(2,1)}, u32[]{:S(2)}, u32[]{:S(2)}) collective-permute-start(bf16[2,2,2,2,64,1024]{5,4,1,3,2,0:T(8,128)(2,1)} %copy.130), channel_id=1, source_target_pairs={{0,1},{1,0},{2,3},{3,2},{4,5},{5,4},{6,7},{7,6},{8,9},{9,8},{10,11... | collective-permute-start | bytes 6291464 | tf_op jit(solution)/shard_map/ppermute | solution.py:189
  478.5 42.1 %collective-permute-start.17 = (bf16[2,2,2,64,1024]{4,3,2,1,0:T(8,128)(2,1)}, bf16[2,2,2,64,1024]{4,3,2,1,0:T(8,128)(2,1)}, u32[]{:S(2)}, u32[]{:S(2)}) collective-permute-start(bf16[2,2,2,64,1024]{4,3,2,1,0:T(8,128)(2,1)} %fusion.7), channel_id=1, source_target_pairs={{0,2},{1,3},{2,0},{3,1},{4,6},{5,7},{6,4},{7,5},{8,10},{9,11},{10,... | collective-permute-start | bytes 3145736 | tf_op jit(solution)/shard_map/ppermute | solution.py:189
  487.0 17.9 %collective-permute-start.13 = (bf16[2,2,2,2,32,4480]{5,4,2,1,0,3:T(8,128)(2,1)}, bf16[2,2,2,2,32,4480]{5,4,2,1,0,3:T(8,128)(2,1)S(1)}, u32[]{:S(2)}, u32[]{:S(2)}) collective-permute-start(bf16[2,2,2,2,32,4480]{5,4,2,1,0,3:T(8,128)(2,1)} %copy_bitcast_fusion), channel_id=1, source_target_pairs={{0,1},{1,0},{2,3},{3,2},{4,5},{5,4},{6,7},{7,6},{8,9},{9,8},{10,11... | collective-permute-start | bytes 13762568 | tf_op jit(solution)/shard_map/ppermute | solution.py:189
  505.0 11.4 %collective-permute-start.14 = (bf16[128,1536]{1,0:T(8,128)(2,1)S(1)}, bf16[128,1536]{1,0:T(8,128)(2,1)S(1)}, u32[]{:S(2)}, u32[]{:S(2)}) collective-permute-start(bf16[128,1536]{1,0:T(8,128)(2,1)S(1)} %convert_element_type.545), channel_id=1, source_target_pairs={{0,2},{1,3},{2,0},{3,1},{4,6},{5,7},{6,4},{7,5},{8,10},{9,11},{10,... | collective-permute-start | bytes 1179656 | tf_op jit(solution)/shard_map/ppermute | solution.py:189
  507.9 15.9 %collective-permute-start.15 = (bf16[128,1536]{1,0:T(8,128)(2,1)S(1)}, bf16[128,1536]{1,0:T(8,128)(2,1)S(1)}, u32[]{:S(2)}, u32[]{:S(2)}) collective-permute-start(bf16[128,1536]{1,0:T(8,128)(2,1)S(1)} %convert_element_type.545), channel_id=1, source_target_pairs={{0,1},{1,0},{2,3},{3,2},{4,5},{5,4},{6,7},{7,6},{8,9},{9,8},{10,11... | collective-permute-start | bytes 1179656 | tf_op jit(solution)/shard_map/ppermute | solution.py:189
  516.4 7.4 collective-permute-start.16
  523.9 25.9 %collective-permute-start.21 = (bf16[2,2,64,1024]{3,2,1,0:T(8,128)(2,1)S(1)}, bf16[2,2,64,1024]{3,2,1,0:T(8,128)(2,1)S(1)}, u32[]{:S(2)}, u32[]{:S(2)}) collective-permute-start(bf16[2,2,64,1024]{3,2,1,0:T(8,128)(2,1)S(1)} %fusion.26), channel_id=1, source_target_pairs={{0,4},{4,0},{8,12},{12,8},{16,20},{20,16},{24,28},{28,24},{1,5},{5... | collective-permute-start | bytes 1572872 | tf_op jit(solution)/shard_map/ppermute | solution.py:189
  527.3 43.9 %copy-start.64 = (bf16[1536,1024]{1,0:T(8,128)(2,1)}, bf16[1536,1024]{1,0:T(8,128)(2,1)S(1)}, u32[]{:S(2)}) copy-start(bf16[1536,1024]{1,0:T(8,128)(2,1)S(1)} %convolution_convert_fusion.7) | copy-start | bytes 9437188
  540.2 11.1 %collective-permute-start.18 = (bf16[128,1536]{1,0:T(8,128)(2,1)S(1)}, bf16[128,1536]{1,0:T(8,128)(2,1)S(1)}, u32[]{:S(2)}, u32[]{:S(2)}) collective-permute-start(bf16[128,1536]{1,0:T(8,128)(2,1)S(1)} %get-tuple-element.403), channel_id=1, source_target_pairs={{0,1},{1,0},{2,3},{3,2},{4,5},{5,4},{6,7},{7,6},{8,9},{9,8},{10,11... | collective-permute-start | bytes 1179656 | tf_op jit(solution)/shard_map/ppermute | solution.py:189
  540.5 4.0 collective-permute-start.19
  544.7 11.3 %collective-permute-start.20 = (bf16[128,1536]{1,0:T(8,128)(2,1)S(1)}, bf16[128,1536]{1,0:T(8,128)(2,1)S(1)}, u32[]{:S(2)}, u32[]{:S(2)}) collective-permute-start(bf16[128,1536]{1,0:T(8,128)(2,1)S(1)} %add_convert_fusion.6), channel_id=1, source_target_pairs={{0,2},{1,3},{2,0},{3,1},{4,6},{5,7},{6,4},{7,5},{8,10},{9,11},{10,... | collective-permute-start | bytes 1179656 | tf_op jit(solution)/shard_map/ppermute | solution.py:189
  549.8 24.5 %copy-start.93 = (bf16[2,2,64,1024]{3,2,1,0:T(8,128)(2,1)}, bf16[2,2,64,1024]{3,2,1,0:T(8,128)(2,1)S(1)}, u32[]{:S(2)}) copy-start(bf16[2,2,64,1024]{3,2,1,0:T(8,128)(2,1)S(1)} %collective-permute-done.21) | copy-start | bytes 1572868
  557.7 17.9 %copy-start.104 = (bf16[128,1536]{1,0:T(8,128)(2,1)}, bf16[128,1536]{1,0:T(8,128)(2,1)S(1)}, u32[]{:S(2)}) copy-start(bf16[128,1536]{1,0:T(8,128)(2,1)S(1)} %get-tuple-element.379) | copy-start | bytes 1179652
  557.7 10.4 %collective-permute-start.22 = (bf16[128,1536]{1,0:T(8,128)(2,1)S(1)}, bf16[128,1536]{1,0:T(8,128)(2,1)S(1)}, u32[]{:S(2)}, u32[]{:S(2)}) collective-permute-start(bf16[128,1536]{1,0:T(8,128)(2,1)S(1)} %get-tuple-element.379), channel_id=1, source_target_pairs={{0,2},{1,3},{2,0},{3,1},{4,6},{5,7},{6,4},{7,5},{8,10},{9,11},{10,... | collective-permute-start | bytes 1179656 | tf_op jit(solution)/shard_map/ppermute | solution.py:189
  560.9 16.1 %copy-start.83 = (bf16[4,2,192,384]{3,2,1,0:T(8,128)(2,1)S(1)}, bf16[4,2,192,384]{3,2,1,0:T(8,128)(2,1)}, u32[]{:S(2)}) copy-start(bf16[4,2,192,384]{3,2,1,0:T(8,128)(2,1)} %get-tuple-element.153) | copy-start | bytes 3538948
  560.9 13.4 %collective-permute-start.25 = (bf16[2,64,1024]{2,1,0:T(8,128)(2,1)S(1)}, bf16[2,64,1024]{2,1,0:T(8,128)(2,1)S(1)}, u32[]{:S(2)}, u32[]{:S(2)}) collective-permute-start(bf16[2,64,1024]{2,1,0:T(8,128)(2,1)S(1)} %fusion.52), channel_id=1, source_target_pairs={{0,16},{4,20},{8,24},{12,28},{16,0},{20,4},{24,8},{28,12},{1,17},{... | collective-permute-start | bytes 786440 | tf_op jit(solution)/shard_map/ppermute | solution.py:189
  560.9 14.6 %collective-permute-start.23 = (bf16[128,1536]{1,0:T(8,128)(2,1)S(1)}, bf16[128,1536]{1,0:T(8,128)(2,1)S(1)}, u32[]{:S(2)}, u32[]{:S(2)}) collective-permute-start(bf16[128,1536]{1,0:T(8,128)(2,1)S(1)} %get-tuple-element.379), channel_id=1, source_target_pairs={{0,1},{1,0},{2,3},{3,2},{4,5},{5,4},{6,7},{7,6},{8,9},{9,8},{10,11... | collective-permute-start | bytes 1179656 | tf_op jit(solution)/shard_map/ppermute | solution.py:189
  568.1 7.5 collective-permute-start.24
  569.7 37.5 %collective-permute-start.30 = (bf16[2,2,192,1024]{3,2,1,0:T(8,128)(2,1)}, bf16[2,2,192,1024]{3,2,1,0:T(8,128)(2,1)}, u32[]{:S(2)}, u32[]{:S(2)}) collective-permute-start(bf16[2,2,192,1024]{3,2,1,0:T(8,128)(2,1)} %dynamic-slice_bitcast_fusion.9), channel_id=1, source_target_pairs={{0,4},{4,0},{8,12},{12,8},{16,20},{20,16},{24,28},{28,24},{1,5},{5... | collective-permute-start | bytes 4718600 | tf_op jit(solution)/shard_map/ppermute | solution.py:189
  587.5 23.4 %collective-permute-start.27 = (bf16[128,1536]{1,0:T(8,128)(2,1)S(1)}, bf16[128,1536]{1,0:T(8,128)(2,1)S(1)}, u32[]{:S(2)}, u32[]{:S(2)}) collective-permute-start(bf16[128,1536]{1,0:T(8,128)(2,1)S(1)} %get-tuple-element.402), channel_id=1, source_target_pairs={{0,1},{1,0},{2,3},{3,2},{4,5},{5,4},{6,7},{7,6},{8,9},{9,8},{10,11... | collective-permute-start | bytes 1179656 | tf_op jit(solution)/shard_map/ppermute | solution.py:189
  589.2 109.9 %collective-permute-start.31 = (bf16[2,2,192,1024]{3,2,1,0:T(8,128)(2,1)}, bf16[2,2,192,1024]{3,2,1,0:T(8,128)(2,1)}, u32[]{:S(2)}, u32[]{:S(2)}) collective-permute-start(bf16[2,2,192,1024]{3,2,1,0:T(8,128)(2,1)} %get-tuple-element.181), channel_id=1, source_target_pairs={{0,4},{4,0},{8,12},{12,8},{16,20},{20,16},{24,28},{28,24},{1,5},{5... | collective-permute-start | bytes 4718600 | tf_op jit(solution)/shard_map/ppermute | solution.py:189
  590.1 119.2 %collective-permute-start.35 = (bf16[2,2,192,1024]{3,2,1,0:T(8,128)(2,1)}, bf16[2,2,192,1024]{3,2,1,0:T(8,128)(2,1)}, u32[]{:S(2)}, u32[]{:S(2)}) collective-permute-start(bf16[2,2,192,1024]{3,2,1,0:T(8,128)(2,1)} %get-tuple-element.182), channel_id=1, source_target_pairs={{0,4},{4,0},{8,12},{12,8},{16,20},{20,16},{24,28},{28,24},{1,5},{5... | collective-permute-start | bytes 4718600 | tf_op jit(solution)/shard_map/ppermute | solution.py:189
  591.9 20.8 %copy-start.99 = (bf16[128,1536]{1,0:T(8,128)(2,1)S(1)}, bf16[128,1536]{1,0:T(8,128)(2,1)}, u32[]{:S(2)}) copy-start(bf16[128,1536]{1,0:T(8,128)(2,1)} %copy-done.97) | copy-start | bytes 1179652
  591.9 20.8 %copy-start.179 = (bf16[128,1536]{1,0:T(8,128)(2,1)S(1)}, bf16[128,1536]{1,0:T(8,128)(2,1)}, u32[]{:S(2)}) copy-start(bf16[128,1536]{1,0:T(8,128)(2,1)} %copy-done.178) | copy-start | bytes 1179652
  608.2 114.0 %copy-start.56 = (bf16[192,1024]{1,0:T(8,128)(2,1)}, bf16[192,1024]{1,0:T(8,128)(2,1)S(1)}, u32[]{:S(2)}) copy-start(bf16[192,1024]{1,0:T(8,128)(2,1)S(1)} %dynamic-slice_bitcast_fusion.11) | copy-start | bytes 1179652
  610.9 11.9 %collective-permute-start.29 = (bf16[64,1024]{1,0:T(8,128)(2,1)S(1)}, bf16[64,1024]{1,0:T(8,128)(2,1)S(1)}, u32[]{:S(2)}, u32[]{:S(2)}) collective-permute-start(bf16[64,1024]{1,0:T(8,128)(2,1)S(1)} %fusion.87), channel_id=1, source_target_pairs={{0,8},{4,12},{8,0},{12,4},{16,24},{20,28},{24,16},{28,20},{1,9},{5... | collective-permute-start | bytes 393224 | tf_op jit(solution)/shard_map/ppermute | solution.py:189
  610.9 7.4 collective-permute-start.26
  611.1 11.6 %collective-permute-start.28 = (bf16[128,1536]{1,0:T(8,128)(2,1)S(1)}, bf16[128,1536]{1,0:T(8,128)(2,1)S(1)}, u32[]{:S(2)}, u32[]{:S(2)}) collective-permute-start(bf16[128,1536]{1,0:T(8,128)(2,1)S(1)} %add_convert_fusion.5), channel_id=1, source_target_pairs={{0,2},{1,3},{2,0},{3,1},{4,6},{5,7},{6,4},{7,5},{8,10},{9,11},{10,... | collective-permute-start | bytes 1179656 | tf_op jit(solution)/shard_map/ppermute | solution.py:189
  629.7 69.4 %collective-permute-start.32 = (bf16[2,2,2,32,4480]{4,3,2,1,0:T(8,128)(2,1)}, bf16[2,2,2,32,4480]{4,3,2,1,0:T(8,128)(2,1)}, u32[]{:S(2)}, u32[]{:S(2)}) collective-permute-start(bf16[2,2,2,32,4480]{4,3,2,1,0:T(8,128)(2,1)} %fusion), channel_id=1, source_target_pairs={{0,2},{1,3},{2,0},{3,1},{4,6},{5,7},{6,4},{7,5},{8,10},{9,11},{10,... | collective-permute-start | bytes 6881288 | tf_op jit(solution)/shard_map/ppermute | solution.py:189
  649.1 47.2 %collective-permute-start.34 = (bf16[2,192,1024]{2,1,0:T(8,128)(2,1)}, bf16[2,192,1024]{2,1,0:T(8,128)(2,1)}, u32[]{:S(2)}, u32[]{:S(2)}) collective-permute-start(bf16[2,192,1024]{2,1,0:T(8,128)(2,1)} %fusion.14), channel_id=1, source_target_pairs={{0,16},{4,20},{8,24},{12,28},{16,0},{20,4},{24,8},{28,12},{1,17},{... | collective-permute-start | bytes 2359304 | tf_op jit(solution)/shard_map/ppermute | solution.py:189
  651.5 47.6 %collective-permute-start.33 = (bf16[2,2,2,2,32,3072]{5,4,3,2,1,0:T(8,128)(2,1)}, bf16[2,2,2,2,32,3072]{5,4,3,2,1,0:T(8,128)(2,1)}, u32[]{:S(2)}, u32[]{:S(2)}) collective-permute-start(bf16[2,2,2,2,32,3072]{5,4,3,2,1,0:T(8,128)(2,1)} %get-tuple-element.195), channel_id=1, source_target_pairs={{0,1},{1,0},{2,3},{3,2},{4,5},{5,4},{6,7},{7,6},{8,9},{9,8},{10,11... | collective-permute-start | bytes 9437192 | tf_op jit(solution)/shard_map/ppermute | solution.py:189
  651.5 43.3 %copy-start.167 = (bf16[1,32]{1,0:T(2,128)(2,1)S(1)}, bf16[1,32]{1,0:T(2,128)(2,1)}, u32[]{:S(2)}) copy-start(bf16[1,32]{1,0:T(2,128)(2,1)} %get-tuple-element.443) | copy-start | bytes 196
  651.5 43.4 %copy-start.166 = (bf16[1,32]{1,0:T(2,128)(2,1)S(1)}, bf16[1,32]{1,0:T(2,128)(2,1)}, u32[]{:S(2)}) copy-start(bf16[1,32]{1,0:T(2,128)(2,1)} %get-tuple-element.444) | copy-start | bytes 196
  651.5 43.5 %copy-start.132 = (bf16[1,2048]{1,0:T(2,128)(2,1)S(1)}, bf16[1,2048]{1,0:T(2,128)(2,1)}, u32[]{:S(2)}) copy-start(bf16[1,2048]{1,0:T(2,128)(2,1)} %stack.133) | copy-start | bytes 12292
  651.5 43.6 %copy-start.131 = (bf16[1,2048]{1,0:T(2,128)(2,1)S(1)}, bf16[1,2048]{1,0:T(2,128)(2,1)}, u32[]{:S(2)}) copy-start(bf16[1,2048]{1,0:T(2,128)(2,1)} %stack.140) | copy-start | bytes 12292
  651.5 43.7 %copy-start.125 = (bf16[4,2304]{1,0:T(4,128)(2,1)S(1)}, bf16[4,2304]{1,0:T(4,128)(2,1)}, u32[]{:S(2)}) copy-start(bf16[4,2304]{1,0:T(4,128)(2,1)} %reduce_sum.480) | copy-start | bytes 55300
  697.8 11.6 %collective-permute-start.36 = (bf16[192,1024]{1,0:T(8,128)(2,1)S(1)}, bf16[192,1024]{1,0:T(8,128)(2,1)S(1)}, u32[]{:S(2)}, u32[]{:S(2)}) collective-permute-start(bf16[192,1024]{1,0:T(8,128)(2,1)S(1)} %fusion.46), channel_id=1, source_target_pairs={{0,8},{4,12},{8,0},{12,4},{16,24},{20,28},{24,16},{28,20},{1,9},{5... | collective-permute-start | bytes 1179656 | tf_op jit(solution)/shard_map/ppermute | solution.py:189
  699.0 23.1 %copy-start.58 = (bf16[192,1024]{1,0:T(8,128)(2,1)}, bf16[192,1024]{1,0:T(8,128)(2,1)S(1)}, u32[]{:S(2)}) copy-start(bf16[192,1024]{1,0:T(8,128)(2,1)S(1)} %dynamic-slice_bitcast_fusion.10) | copy-start | bytes 1179652
  (174 other events, 717.7 us)

commit v4 on v3

--- a/solution.py
+++ b/solution.py
@@ -220,42 +220,61 @@
             names += [("tensor", mask) for mask in reversed(bit_masks(lax.axis_size("tensor")))]
         self.names = names
         rows = grad.shape[0] // 2 ** len(names)
-        self.addends = [grad.reshape((2,) * len(names) + (rows,) + grad.shape[1:])]
+        self.addends = [(grad.reshape((2,) * len(names) + (rows,) + grad.shape[1:]), names)]
         self.pending = None
 
+    def picked(self, other=None, token=None):
+        result = []
+        for array, names in self.addends:
+            if token is not None:
+                array = after(array, [token])
+            for position in reversed(range(len(names))):
+                axis, mask = names[position]
+                own = (lax.axis_index(axis) // mask) % 2
+                if names[position] == other:
+                    array = take(array, position, 1 - own)
+                elif names[position] not in self.names:
+                    array = take(array, position, own)
+            result.append(array)
+        return result
+
     def operand(self):
-        axis, mask = self.masks[0]
-        position = self.names.index((axis, mask))
-        own = (lax.axis_index(axis) // mask) % 2
-        return to_low(total([take(addend, position, 1 - own) for addend in self.addends]))
+        return to_low(total(self.picked(self.masks[0])))
 
     def accept(self):
-        axis, mask = self.masks.pop(0)
-        position = self.names.index((axis, mask))
-        own = (lax.axis_index(axis) // mask) % 2
-        self.addends = [take(addend, position, own) for addend in self.addends] + [self.pending]
+        self.names = [name for name in self.names if name != self.masks[0]]
+        self.masks = self.masks[1:]
+        self.addends.append((self.pending, self.names))
         self.pending = None
-        self.names.pop(position)
 
     def begun_last(self):
         left = [mask for axis, mask in self.masks if axis == "dp" and mask > 1]
         return 0 < len(left) == len(self.masks) < len(bit_masks(lax.axis_size("dp"))) - 1
 
     def rest(self, token):
-        if len(self.addends) > 1:
-            self.addends = [after(addend, [token]) for addend in self.addends]
         kind = []
         for axis, mask in self.masks:
-            name = ("core", "y")[mask - 1] if axis == "tensor" else ("x" if mask == 1 else "z")
-            if name not in kind:
-                kind.append(name)
-        value_entries = to_low(total(self.addends)) if len(self.addends) > 1 else self.addends[0]
-        return value_entries.reshape(-1, value_entries.shape[-1]), tuple(kind)
+            if lane_name(axis, mask) not in kind:
+                kind.append(lane_name(axis, mask))
+        if len(self.addends) == 1 or kind[0] in ("core", "y"):
+            array = self.addends[0][0]
+            if len(self.addends) > 1:
+                array = to_low(total(self.picked(token=token)))
+            return [(array, tuple(name for name in BYTE_LANES if name in kind))], tuple(kind)
+        arrays = []
+        for array, names in self.addends:
+            lanes_here = {lane_name(axis, mask) for axis, mask in names}
+            arrays.append((array, tuple(name for name in BYTE_LANES if name in lanes_here)))
+        return arrays, tuple(kind)
 
     def result(self, token=None):
-        if token is not None:
-            self.addends = [after(addend, [token]) for addend in self.addends]
-        return total(self.addends)
+        return total(self.picked(token=token))
+
+
+def lane_name(axis, mask):
+    if axis == "tensor":
+        return ("core", "y")[mask - 1]
+    return "x" if mask == 1 else "z"
 
 
 def sum_slowly(job):
@@ -554,32 +573,70 @@
 MAIN_LANES = ("z", "x")
 
 
-def sum_kernel(plan, kinds, depth_z, *refs):
+def sum_kernel(plan, kinds, sources, depth_z, *refs):
     count = len(kinds)
-    grads, extra = refs[:count], refs[count]
-    outputs, totals = refs[count + 1 : 2 * count + 1], refs[2 * count + 1]
-    rest = list(refs[2 * count + 2 :])
+    pieces_in = [[refs[number] for number, _ in parts] for parts in sources]
+    total_in = sum(len(parts) for parts in sources)
+    grads, extra = [parts[0] for parts in pieces_in], refs[total_in]
+    outputs = refs[total_in + 1 : total_in + 1 + count]
+    totals = refs[total_in + 1 + count]
+    rest = list(refs[total_in + 2 + count :])
     coordinates = here()
     places = dict(zip(BYTE_LANES, coordinates))
     z = coordinates[0]
     mirrored = depth_z - 1 - z
-    held, received, held_names = [], [], []
-    for kind in kinds:
+    held, received, held_names, temporary = [], [], [], {}
+    for job, kind in enumerate(kinds):
         held.append(rest.pop(0))
         received.append({lane: rest.pop(0) for lane in kind})
-        held_names.append(names_held(kind))
+        held_names.append(names_held(kind, len(sources[job])))
+    for key in temporary_shapes(kinds, sources, [ref.shape for ref in held]):
+        temporary[key] = rest.pop(0)
     squares, arrivals, send_sems, receive_sems, own_sems, tile_sems = rest
+
+    def slice_of(job, part):
+        names = sources[job][part][1]
+        spot = tuple(slice(None) if name in held_names[job] else places[name] for name in names)
+        return pieces_in[job][part].at[spot]
+
     loads = []
-    for job, kind in enumerate(kinds):
-        spot = tuple(
-            slice(None) if name in held_names[job] else places[name]
-            for name in BYTE_LANES
-            if name in kind
-        )
-        loads.append(pltpu.make_async_copy(grads[job].at[spot], held[job], own_sems.at[job]))
+    for job in range(count):
+        loads.append(pltpu.make_async_copy(slice_of(job, 0), held[job], own_sems.at[job]))
         loads[-1].start()
     squares[...] = jnp.zeros_like(squares)
     greet(False, depth_z, coordinates)
+
+    def prepare(job):
+        loads[job].wait()
+        for part in range(1, len(sources[job])):
+            buffer = temporary[held[job].shape]
+            copy = pltpu.make_async_copy(slice_of(job, part), buffer, own_sems.at[job])
+            copy.start()
+            copy.wait()
+            lead, rows = held[job].shape[:-2], held[job].shape[-2]
+            pieces = 1
+            for size in lead:
+                pieces *= size
+
+            def piece(index, carry, buffer=buffer, lead=lead, rows=rows):
+                spot, remainder = [], index
+                for size in reversed(lead):
+                    spot.insert(0, remainder % size)
+                    remainder = remainder // size
+                target, other = held[job].at[tuple(spot)], buffer.at[tuple(spot)]
+
+                def row_step(number, inner):
+                    part_rows = pl.ds(pl.multiple_of(number * 16, 16), 16)
+                    target[part_rows, :] = to_low(
+                        target[part_rows, :].astype(jnp.float32)
+                        + other[part_rows, :].astype(jnp.float32)
+                    )
+                    return inner
+
+                lax.fori_loop(0, rows // 16, row_step, 0)
+                return carry
+
+            lax.fori_loop(0, pieces, piece, 0)
 
     def chosen(job, step, lane_place):
         steps = lanes_of(kinds[job], depth_z)
@@ -620,7 +677,7 @@
                 pairs.append((condition, copy))
             return pairs
         number = base + 2 * (depth_z - 1) + ("x", "y", "core").index(lane)
-        if step == 0:
+        if step == 0 and len(sources[job]) == 1:
             spot = tuple(
                 1 - places[name] if name == lane else slice(None)
                 for name in BYTE_LANES
@@ -718,8 +775,8 @@
     loaded = set()
     for action, job, step in plan:
         lane = lanes_of(kinds[job], depth_z)[step][0]
-        if job not in loaded and (action == "wait" or lane == "z"):
-            loads[job].wait()
+        if job not in loaded and (action == "wait" or lane == "z" or len(sources[job]) > 1):
+            prepare(job)
             loaded.add(job)
         if action == "start":
             perform(copies(job, step, False), "start")
@@ -756,26 +813,42 @@
             perform(copies(job, step, False), "wait_send")
 
 
-def names_held(kind):
-    return [name for name in BYTE_LANES if name in kind and (name == "z" or name != kind[0])]
+def names_held(kind, addends):
+    return [
+        name
+        for name in BYTE_LANES
+        if name in kind and (name == "z" or addends > 1 or name != kind[0])
+    ]
+
+
+def temporary_shapes(kinds, sources, shapes):
+    return list(
+        dict.fromkeys(
+            tuple(shape) for shape, parts in zip(shapes, sources) if len(parts) > 1
+        )
+    )
 
 
 def sum_whole(grads, kinds, extra, collective_id):
     depth_z = lax.axis_size("dp") // 2
     sizes = {"z": depth_z, "x": 2, "y": 2, "core": 2}
-    jobs, arrays, shapes, scratch = [], [], [], []
-    for grad, kind in zip(grads, kinds):
-        names = [name for name in BYTE_LANES if name in kind]
-        pieces = 1
-        for name in names:
-            pieces *= sizes[name]
-        piece = (grad.shape[0] // pieces, grad.shape[1])
-        arrays.append(grad.reshape(tuple(sizes[name] for name in names) + piece))
+    jobs, arrays, shapes, scratch, sources, held_shapes = [], [], [], [], [], []
+    for parts, kind in zip(grads, kinds):
+        sources.append([])
+        for array, names in parts:
+            piece = array.shape[-2:]
+            lead = tuple(sizes[name] for name in names)
+            if array.ndim == 2:
+                pieces = 1
+                for size in lead:
+                    pieces *= size
+                piece = (array.shape[0] // pieces, array.shape[1])
+            sources[-1].append((len(arrays), names))
+            arrays.append(array.reshape(lead + piece))
         shapes.append(jax.ShapeDtypeStruct(piece, jnp.float32))
-        steps, left = [], list(names)
-        scratch.append(
-            pltpu.VMEM(tuple(sizes[name] for name in names_held(kind)) + piece, jnp.bfloat16)
-        )
+        steps, left = [], [name for name in BYTE_LANES if name in kind]
+        held_shapes.append(tuple(sizes[name] for name in names_held(kind, len(parts))) + piece)
+        scratch.append(pltpu.VMEM(held_shapes[-1], jnp.bfloat16))
         for lane in kind:
             left.remove(lane)
             rest = tuple(sizes[name] for name in left)
@@ -787,14 +860,18 @@
             lead = (2 * (depth_z - 1) - (depth_z - 2) // 2,) if lane == "z" else ()
             scratch.append(pltpu.VMEM(lead + rest + piece, jnp.bfloat16))
         jobs.append(steps)
+    scratch += [
+        pltpu.VMEM(shape, jnp.bfloat16)
+        for shape in temporary_shapes(kinds, sources, held_shapes)
+    ]
     plan = order_steps(jobs)
     numbers = len(grads) * (2 * depth_z + 1)
     tile = jax.ShapeDtypeStruct(extra.shape, jnp.float32)
     rounds = 3 + len(bit_masks(depth_z))
     return pl.pallas_call(
-        partial(sum_kernel, plan, kinds, depth_z),
+        partial(sum_kernel, plan, kinds, sources, depth_z),
         out_shape=tuple(shapes) + (tile,),
-        in_specs=[pl.BlockSpec(memory_space=pl.ANY)] * len(grads)
+        in_specs=[pl.BlockSpec(memory_space=pl.ANY)] * len(arrays)
         + [pl.BlockSpec(memory_space=pltpu.VMEM)],
         out_specs=(pl.BlockSpec(memory_space=pltpu.VMEM),) * (len(grads) + 1),
         scratch_shapes=scratch
@@ -1417,65 +1494,88 @@
     return (slope_value, slope_scale, slope_smalls, (job_out, job_in))
 
 
-def causal_scores(queries, key_rows):
-    scores = jnp.einsum(
-        "gqhd,gkhd->ghqk", queries, key_rows, preferred_element_type=jnp.float32
-    ) * HD ** (-0.5)
-    causal = jnp.tril(jnp.ones((MAX_PIECES, MAX_PIECES), dtype=bool))
-    return jnp.where(causal[None, None], scores, -jnp.inf)
+def head_mask(head, extent):
+    columns = lax.broadcasted_iota(jnp.int32, (1, extent), 1)
+    inside = (columns >= head * HD) & (columns < (head + 1) * HD)
+    return jnp.where(inside, 1.0, 0.0).astype(jnp.bfloat16)
+
+
+def head_weights(queries, key_rows):
+    scores = low_dot(queries, key_rows, 1, 1) * HD ** (-0.5)
+    rows = lax.broadcasted_iota(jnp.int32, (MAX_PIECES, MAX_PIECES), 0)
+    columns = lax.broadcasted_iota(jnp.int32, (MAX_PIECES, MAX_PIECES), 1)
+    scores = jnp.where(rows >= columns, scores, -jnp.inf)
+    exponents = jnp.exp(scores - jnp.max(scores, axis=-1, keepdims=True))
+    return exponents / jnp.sum(exponents, axis=-1, keepdims=True)
+
+
+def attend_kernel(triple, output):
+    extent = output.shape[1]
+    queries, key_rows = triple[:, :extent], triple[:, extent : 2 * extent]
+    value_rows = triple[:, 2 * extent :]
+    attended = jnp.zeros(output.shape, jnp.float32)
+    for head in range(extent // HD):
+        mask = head_mask(head, extent)
+        weights = to_low(head_weights(queries * mask, key_rows))
+        attended = attended + low_dot(weights, value_rows * mask, 1, 0)
+    output[...] = to_low(attended)
+
+
+def attend_slope_kernel(triple, slope, output):
+    extent = slope.shape[1]
+    queries, key_rows = triple[:, :extent], triple[:, extent : 2 * extent]
+    value_rows = triple[:, 2 * extent :]
+    slope_here = slope[...]
+    slopes = [jnp.zeros(slope.shape, jnp.float32)] * 3
+    for head in range(extent // HD):
+        mask = head_mask(head, extent)
+        weights = head_weights(queries * mask, key_rows)
+        slope_masked = slope_here * mask
+        slope_weights = low_dot(slope_masked, value_rows, 1, 1)
+        slope_scores = to_low(
+            weights
+            * (slope_weights - jnp.sum(weights * slope_weights, axis=-1, keepdims=True))
+        )
+        slopes[0] = slopes[0] + low_dot(slope_scores, key_rows * mask, 1, 0)
+        slopes[1] = slopes[1] + low_dot(slope_scores, queries * mask, 0, 0)
+        slopes[2] = slopes[2] + low_dot(to_low(weights), slope_masked, 0, 0)
+    output[:, :extent] = to_low(slopes[0] * HD ** (-0.5))
+    output[:, extent : 2 * extent] = to_low(slopes[1] * HD ** (-0.5))
+    output[:, 2 * extent :] = to_low(slopes[2])
+
+
+def by_sequence(kernel, columns, *arrays):
+    rows = arrays[0].shape[0]
+    return pl.pallas_call(
+        kernel,
+        grid=(rows // MAX_PIECES,),
+        out_shape=jax.ShapeDtypeStruct((rows, columns), jnp.bfloat16),
+        in_specs=[
+            pl.BlockSpec((MAX_PIECES, array.shape[1]), lambda group: (group, 0)) for array in arrays
+        ],
+        out_specs=pl.BlockSpec((MAX_PIECES, columns), lambda group: (group, 0)),
+        compiler_params=pltpu.CompilerParams(vmem_limit_bytes=24 * 2**20),
+        cost_estimate=pl.CostEstimate(
+            flops=3 * 10**9, transcendentals=3 * 10**5, bytes_accessed=4 * 10**6
+        ),
+    )(*arrays)
 
 
 def apply_heads(latent_holder, heed_scale, triple_matrix, exit_matrix):
     rescaled_rows, rescale_grad = jax.vjp(root_mean_rescale, latent_holder, heed_scale)
     rows_low = gather_rows(to_low(rescaled_rows))
     triple = to_low(matmul_apply(rows_low, triple_matrix))
-    groups = rows_low.shape[0] // MAX_PIECES
-    heads_here = triple_matrix.shape[1] // (3 * HD)
-    split_heads = triple.reshape(groups, MAX_PIECES, 3, heads_here, HD)
-    queries, key_rows, value_rows = (
-        split_heads[:, :, 0],
-        split_heads[:, :, 1],
-        split_heads[:, :, 2],
-    )
-    scores = causal_scores(queries, key_rows)
-    maxima = jnp.max(scores, axis=-1, keepdims=True)
-    log_total = maxima + jnp.log(jnp.sum(jnp.exp(scores - maxima), axis=-1, keepdims=True))
-    weights_soft = to_low(jnp.exp(scores - log_total))
-    heads_output = to_low(
-        jnp.einsum("ghqk,gkhd->gqhd", weights_soft, value_rows, preferred_element_type=jnp.float32)
-    )
-    heads_output = heads_output.reshape(rows_low.shape[0], heads_here * HD)
+    heads_output = by_sequence(attend_kernel, triple.shape[1] // 3, triple)
     outcome = latent_holder + total_lines(product_nt(heads_output, exit_matrix))
-    return (
-        outcome,
-        (rescale_grad, rows_low, queries, key_rows, value_rows, log_total, heads_output),
-    )
+    return outcome, (rescale_grad, rows_low, triple, heads_output)
 
 
 def apply_heads_grad(conductor, slope_emitted, kept, triple_matrix, exit_matrix):
-    rescale_grad, rows_low, queries, key_rows, value_rows, log_total, heads_output = kept
+    rescale_grad, rows_low, triple, heads_output = kept
     grad_rows = conductor.tick(gather_grads(to_low(slope_emitted)), 12.0, Y_LANE)
     slope_exit_matrix = to_low(product_tn(grad_rows, heads_output))
-    grad_attended = to_low(matmul_apply(grad_rows, exit_matrix)).reshape(queries.shape)
-    weights_soft = jnp.exp(causal_scores(queries, key_rows) - log_total)
-    grad_values = jnp.einsum(
-        "ghqk,gqhd->gkhd", to_low(weights_soft), grad_attended, preferred_element_type=jnp.float32
-    )
-    grad_weights = jnp.einsum(
-        "gqhd,gkhd->ghqk", grad_attended, value_rows, preferred_element_type=jnp.float32
-    )
-    grad_scores = to_low(
-        weights_soft * (grad_weights - jnp.sum(weights_soft * grad_weights, axis=-1, keepdims=True))
-    )
-    grad_queries = jnp.einsum(
-        "ghqk,gkhd->gqhd", grad_scores, key_rows, preferred_element_type=jnp.float32
-    ) * HD ** (-0.5)
-    grad_keys = jnp.einsum(
-        "ghqk,gqhd->gkhd", grad_scores, queries, preferred_element_type=jnp.float32
-    ) * HD ** (-0.5)
-    grad_triple = to_low(
-        jnp.stack([grad_queries, grad_keys, grad_values], axis=2).reshape(rows_low.shape[0], -1)
-    )
+    grad_attended = to_low(matmul_apply(grad_rows, exit_matrix))
+    grad_triple = by_sequence(attend_slope_kernel, triple.shape[1], triple, grad_attended)
     grad_triple = conductor.tick(after(grad_triple, [slope_exit_matrix]), 10.0, Y_LANE)
     slope_rescaled = sum_grads(product_nt(grad_triple, triple_matrix))
     slope_triple_matrix = to_low(product_tn(rows_low, grad_triple))
@@ -1767,9 +1867,9 @@
         jobs_enc[1],
         Summing(grad_mixed.reshape(-1, BYTE_WIDTH), True),
     ]
-    sums = [None if part.masks else part.result(jobs_enc[1].addends[0]) for part in parts]
-    open_parts = [number for number, part in enumerate(parts) if part.masks]
-    rests = [parts[number].rest(jobs_enc[1].addends[0]) for number in open_parts]
+    sums = [None if part.masks else part.result(jobs_enc[1].addends[0][0]) for part in parts]
+    open_parts = [number for number in (8, 9, 7, 10, 3, 0, 1, 2, 4, 5, 6) if parts[number].masks]
+    rests = [parts[number].rest(jobs_enc[1].addends[0][0]) for number in open_parts]
     grads = [grad for grad, _ in rests]
     sum_kinds = [kind for _, kind in rests]
     if exact_tiles:

time: 964 us -> 951 us (0.987)
  local copies, waits for them, and re-layouts: 83.7 us -> 58.8 us
  Pallas kernels: 536 us -> 554 us
  other arithmetic: 82.2 us -> 69.2 us
    pallas_call x1 -> x3, Pallas kernels: 176 us -> 194 us  [the longest x1 181 us: sum_whole(): pl.pallas_call(partial(sum_kernel, plan, kinds, sources, depth_z), out_sh...]
    squeeze x16 -> x6, local copies, waits for them, and re-layouts: 23.6 us -> 8.88 us  [take(): return lax.dynamic_index_in_dim(value_entries, index, axis, keepdims=False)]
    convert_element_type x26 -> x22, other arithmetic: 36.4 us -> 26.7 us  [to_low(): return value_entries.astype(jnp.bfloat16)]
    unnamed x417 -> x363, local copies, waits for them, and re-layouts: 39.6 us -> 31 us
  transfers between devices with their start and end apart: 37 -> 37, of which waited for: 13 -> 15; matrix products, arithmetic and copies ran while one was open for 14% -> 13% of each run, Pallas kernels for 9% -> 10%
where the time goes in v4:
time: 951 us; the launch traced here: 942 us
  Pallas kernels  554 us (58%)
  matrix products  147 us (15%)
  waiting for transfers between devices  79.8 us (8%)
  other arithmetic  69.2 us (7%)
  local copies, waits for them, and re-layouts  58.8 us (6%)
  starting transfers between devices  24.5 us (3%)
    pallas_call x1, Pallas kernels, spread_whole(): pl.pallas_call(partial(spread_kernel, plan, jobs, depth_z), out_shape=tup...  230 us
    pallas_call x1, Pallas kernels, sum_whole(): pl.pallas_call(partial(sum_kernel, plan, kinds, sources, depth_z), out_sh...  181 us
    pallas_call x2, Pallas kernels, middle_backward(): pl.pallas_call(middle_slope_kernel, grid=(chunks,), out_shape=(jax.ShapeD...  86.4 us
    ppermute x37, waiting for transfers between devices, swap(): lax.ppermute(value_entries, axis, [(place, place ^ mask) for place in ran...  79.8 us
    dot_general x11, matrix products, matmul_apply(): return jnp.dot(left, right, preferred_element_type=jnp.float32)  48.8 us
    dot_general x11, matrix products, product_tn(): lax.dot_general(left, right, (((0,), (0,)), ((), ())), preferred_element_...  44.1 us
    pallas_call x2, Pallas kernels, middle_forward(): pl.pallas_call(middle_kernel, grid=(chunks,), out_shape=(jax.ShapeDtypeSt...  43.7 us
    dot_general x10, matrix products, product_nt(): lax.dot_general(left, right, (((1,), (1,)), ((), ())), preferred_element_...  41.8 us
  transfers between devices with their start and end apart: 37, of which 15 were waited for; matrix products, arithmetic and copies ran while one was open for 13% of the time, Pallas kernels for 10%

profile of v4, /device:TPU:0, one launch (start us, length us, event | category | flops | bytes accessed | tf_op | source)
XLA Modules:
  0.0 941.7 jit_solution(5857674043038437795)
XLA Ops:
  13.9 229.7 %shard_map.526 = (bf16[4,2,2,2,32,1024]{5,4,3,2,1,0:T(8,128)(2,1)}, bf16[4,2,2,2,32,4480]{5,4,3,2,1,0:T(8,128)(2,1)}, bf16[4,2,2,2,64,1024]{5,4,3,2,1,0:T(8,128)...) custom-call(bf16[32,1024]{1,0:T(8,128)(2,1)} %pad_maximum_fusion.11., ...), custom_call_target="tpu_custom_call" | custom-call | tf_op jit(solution)/shard_map/pallas_call | solution.py:555
  248.7 11.3 %fusion.123.projected.earlier = f32[512,4480]{1,0:T(8,128)} fusion(bf16[1024,4480]{1,0:T(8,128)(2,1)} %bitcast.411, f32[512,1024]{1,0:T(8,128)S(1)} %get-tuple-element.425, f32[1024]{0:T(1024)S(1)} %get-tuple-element.405, f32[512]{0:T(512)S(1)} %fusion.104), kind=kOutput, calls=%fused_computation.355 | convolution fusion | flops 4699193344 | bytes 20453376 | tf_op jit(solution)/shard_map/dot_general | solution.py:172
  260.1 22.0 %shard_map.527 = (bf16[512,2048]{1,0:T(8,128)(2,1)S(1)}, f32[512,2048]{1,0:T(8,128)}, f32[4,128,2048]{2,1,0:T(8,128)}) custom-call(f32[512,4480]{1,0:T(8,128)} %fusion.123.projected.earlier, f32[4,2304]{1,0:T(4,128)S(1)} %squeeze.124.taps, f32[1,2048]{1,0:T(1,128)S(1)} %bitcast.335, f32[2,32]{1,0:T(2,128)S(1)} %get-tuple-element.436.decay, ...), custom_call_target="tpu_custom_call" | custom-call | flops 20000000000 | bytes 20000000 | tf_op jit(solution)/shard_map/pallas_call | solution.py:1338
  282.1 5.3 convolution_add_fusion.2
  290.8 3.5 fusion.56
  294.8 2.1 copy-done.16
  303.2 2.2 convolution_convert_fusion.10.triple
  305.5 5.3 shard_map.528
  315.5 9.5 %collective-permute-done.5 = bf16[128,1536]{1,0:T(8,128)(2,1)S(1)} collective-permute-done((bf16[128,1536]{1,0:T(8,128)(2,1)S(1)}, bf16[128,1536]{1,0:T(8,128)(2,1)S(1)}, u32[]{:S(2)}, u32[]{:S(2)}) %collective-permute-start.5) | collective-permute-done | bytes 393248 | tf_op jit(solution)/shard_map/ppermute | solution.py:189
  327.2 8.7 collective-permute-done.6
  337.7 3.5 fusion.125
  345.0 1.8 convolution_convert_fusion.12
  352.9 9.3 collective-permute-done.11
  364.3 4.2 multiply_reduce_fusion.10
  368.5 11.9 %fusion.124.projected.earlier = f32[512,4480]{1,0:T(8,128)} fusion(bf16[1024,4480]{1,0:T(8,128)(2,1)} %bitcast.413, f32[512,1024]{1,0:T(8,128)S(1)} %get-tuple-element.372, f32[1024]{0:T(1024)S(1)} %get-tuple-element.404, f32[512]{0:T(512)S(1)} %fusion.105), kind=kOutput, calls=%fused_computation.356 | convolution fusion | flops 4699193344 | bytes 20453376 | tf_op jit(solution)/shard_map/dot_general | solution.py:172
  380.4 21.7 %shard_map.529 = (bf16[512,2048]{1,0:T(8,128)(2,1)S(1)}, f32[512,2048]{1,0:T(8,128)}, f32[4,128,2048]{2,1,0:T(8,128)}) custom-call(f32[512,4480]{1,0:T(8,128)} %fusion.124.projected.earlier, f32[4,2304]{1,0:T(4,128)S(1)} %slice.397.taps, f32[1,2048]{1,0:T(1,128)S(1)} %bitcast.339, f32[2,32]{1,0:T(2,128)S(1)} %get-tuple-element.437.decay, ...), custom_call_target="tpu_custom_call" | custom-call | flops 20000000000 | bytes 20000000 | tf_op jit(solution)/shard_map/pallas_call | solution.py:1338
  402.2 2.4 multiply_reduce_fusion.9
  405.3 1.9 multiply_reduce_fusion
  409.4 4.4 fusion.51.slope
  413.8 2.4 convolution_convert_fusion.8
  420.6 43.3 %shard_map.530 = (bf16[512,4480]{1,0:T(8,128)(2,1)}, f32[4,8,2304]{2,1,0:T(8,128)S(1)}, f32[8,2048]{1,0:T(8,128)S(1)}, f32[8,2048]{1,0:T(8,128)S(1)}, f32[2,8,32]{2,1,0:T(8,128)S(1)}) custom-call(f32[512,4480]{1,0:T(8,128)} %fusion.124.projected.earlier, f32[512,4480]{1,0:T(8,128)} %fusion.124.projected.earlier, f32[512,2048]{1,0:T(8,128)S(1)} %copy-done.15, ...), custom_call_target="tpu_custom_call" | custom-call | flops 49999998976 | bytes 30000000 | tf_op jit(solution)/shard_map/pallas_call | solution.py:1391
  464.0 3.1 fusion.8
  467.1 7.8 convolution_convert_fusion.1
  474.9 2.7 copy_bitcast_fusion
  477.6 2.3 copy-done.17
  483.2 4.0 convolution_convert_fusion.15
  488.7 9.4 %multiply_reduce_fusion.1 = (bf16[1024]{0:T(1024)(128)(2,1)S(1)}, f32[512]{0:T(512)S(1)}, f32[512,1024]{1,0:T(8,128)S(1)}) fusion(f32[512,1024]{1,0:T(8,128)S(1)} %copy-done.30, f32[512]{0:T(512)S(1)} %fusion.105, f32[1024]{0:T(1024)S(1)} %get-tuple-element.404, bf16[512,4480]{1,0:T(8,128)(2,1)} %get-tuple-element.164, bf16[1024,4480]{1,0:T(8,128)(2,1)} %bitcast.414), kind=kOutput, calls=%fused_computation.43 | convolution fusion | flops 4700764672 | bytes 17967104 | tf_op jit(solution)/shard_map/dot_general | solution.py:182
  499.1 2.0 fusion.9
  504.7 16.5 %collective-permute-done.14 = bf16[128,1536]{1,0:T(8,128)(2,1)S(1)} collective-permute-done((bf16[128,1536]{1,0:T(8,128)(2,1)S(1)}, bf16[128,1536]{1,0:T(8,128)(2,1)S(1)}, u32[]{:S(2)}, u32[]{:S(2)}) %collective-permute-start.14) | collective-permute-done | bytes 393248 | tf_op jit(solution)/shard_map/ppermute | solution.py:189
  521.8 1.9 fusion.20
  527.6 5.2 fusion.76
  533.1 6.7 convolution_convert_fusion.11
  549.4 6.1 collective-permute-done.20
  559.7 7.0 collective-permute-done.22
  568.6 4.3 collective-permute-done.25
  575.3 7.9 shard_map.531
  583.2 2.1 convolution_convert_fusion.14
  585.4 2.2 convolution_convert_fusion.9
  587.7 4.3 fusion.1
  592.0 4.9 copy.114
  599.0 5.2 collective-permute-done.30
  607.4 4.0 convolution_convert_fusion.2
  611.4 5.9 collective-permute-done.28
  618.0 1.8 fusion.43
  619.9 4.0 convolution_convert_fusion.3
  626.5 2.0 dynamic-slice_bitcast_fusion
  628.5 3.5 convolution_add_fusion
  632.0 4.4 fusion.48.slope
  636.4 4.4 convolution_convert_fusion.4
  640.8 2.4 collective-permute-start.34
  643.2 43.1 %shard_map.532 = (bf16[512,4480]{1,0:T(8,128)(2,1)}, f32[4,8,2304]{2,1,0:T(8,128)S(1)}, f32[8,2048]{1,0:T(8,128)S(1)}, f32[8,2048]{1,0:T(8,128)S(1)}, f32[2,8,32]{2,1,0:T(8,128)S(1)}) custom-call(f32[512,4480]{1,0:T(8,128)} %fusion.123.projected.earlier, f32[512,4480]{1,0:T(8,128)} %fusion.123.projected.earlier, f32[512,2048]{1,0:T(8,128)S(1)} %copy-done.14, ...), custom_call_target="tpu_custom_call" | custom-call | flops 49999998976 | bytes 30000000 | tf_op jit(solution)/shard_map/pallas_call | solution.py:1391
  691.3 9.9 %convolution_convert_fusion = bf16[1024,4480]{1,0:T(8,128)(2,1)} fusion(bf16[512,4480]{1,0:T(8,128)(2,1)} %get-tuple-element.198, f32[512,1024]{1,0:T(8,128)S(1)} %copy-done.27, f32[1024]{0:T(1024)S(1)} %copy-done.126, f32[512]{0:T(512)} %copy-done.128), kind=kOutput, calls=%fused_computation | convolution fusion | flops 4703780864 | bytes 15865856 | tf_op jit(solution)/shard_map/dot_general | solution.py:176
  702.7 7.9 multiply_reduce_fusion.3
  713.0 2.1 multiply_reduce_fusion.15
  718.9 5.8 fusion
  726.9 181.1 %shard_map.533 = (f32[32,3072]{1,0:T(8,128)}, f32[32,4480]{1,0:T(8,128)}, f32[64,1024]{1,0:T(8,128)}, f32[32,1024]{1,0:T(8,128)}, f32[192,1152]{1,0:T(8,128)}, /...) custom-call(bf16[4,2,2,32,3072]{4,3,2,1,0:T(8,128)(2,1)} %bitcast.34, ...), custom_call_target="tpu_custom_call" | custom-call | tf_op jit(solution)/shard_map/pallas_call | solution.py:871
  912.1 1.9 slice_bitcast_fusion.1
  915.8 4.2 multiply_subtract_fusion
  919.9 2.4 copy.124
  922.3 2.4 copy.123
  924.8 2.4 copy.122
  930.9 1.8 multiply_subtract_fusion.3
  933.4 2.0 multiply_subtract_fusion.2
  937.8 2.3 multiply_subtract_fusion.1
  (609 shorter events, 120.4 us)
Async XLA Ops:
  246.2 13.8 %copy-start.125 = (f32[1024]{0:T(1024)}, f32[1024]{0:T(1024)S(1)}, u32[]{:S(2)}) copy-start(f32[1024]{0:T(1024)S(1)} %get-tuple-element.405) | copy-start | bytes 12292
  246.8 42.1 %copy-start.97 = (f32[1536]{0:T(1024)}, f32[1536]{0:T(1024)S(1)}, u32[]{:S(2)}) copy-start(f32[1536]{0:T(1024)S(1)} %get-tuple-element.401) | copy-start | bytes 18436
  246.8 78.5 %copy-start.99 = (f32[1536]{0:T(1024)}, f32[1536]{0:T(1024)S(1)}, u32[]{:S(2)}) copy-start(f32[1536]{0:T(1024)S(1)} %get-tuple-element.400) | copy-start | bytes 18436
  246.8 13.2 %copy-start.4 = (f32[2048]{0:T(1024)}, f32[2048]{0:T(1024)S(1)}, u32[]{:S(2)}) copy-start(f32[2048]{0:T(1024)S(1)} %get-tuple-element.408) | copy-start | bytes 24580
  246.9 13.2 %copy-start.6 = (f32[2048]{0:T(1024)}, f32[2048]{0:T(1024)S(1)}, u32[]{:S(2)}) copy-start(f32[2048]{0:T(1024)S(1)} %get-tuple-element.409) | copy-start | bytes 24580
  246.9 65.2 %copy-start.112 = (f32[1,512]{1,0:T(1,128)}, f32[1,512]{1,0:T(1,128)S(1)}, u32[]{:S(2)}) copy-start(f32[1,512]{1,0:T(1,128)S(1)} %convert_element_type.490) | copy-start | bytes 6148
  248.1 34.0 %copy-start.26 = (f32[512,1024]{1,0:T(8,128)}, f32[512,1024]{1,0:T(8,128)S(1)}, u32[]{:S(2)}) copy-start(f32[512,1024]{1,0:T(8,128)S(1)} %get-tuple-element.425) | copy-start | bytes 6291460
  248.2 76.8 %copy-start.88 = (f32[1536]{0:T(1024)}, f32[1536]{0:T(1024)S(1)}, u32[]{:S(2)}) copy-start(f32[1536]{0:T(1024)S(1)} %pad.103.clone) | copy-start | bytes 18436
  248.7 42.1 %slice-start.2 = ((s8[6291456]{0:T(1024)(128)(4,1)}), s8[4194304]{0:T(1024)(128)(4,1)S(1)}, s32[]{:S(2)}) async-start(s8[6291456]{0:T(1024)(128)(4,1)} %bitcast.415), calls=%async_computation.2 | async-start | bytes 8388608
  260.1 30.7 %slice-start.3 = ((s8[6291456]{0:T(1024)(128)(4,1)}), s8[2097152]{0:T(1024)(128)(4,1)S(1)}, s32[]{:S(2)}) async-start(s8[6291456]{0:T(1024)(128)(4,1)} %bitcast.415), calls=%async_computation.3 | async-start | bytes 4194304
  288.7 36.3 %copy-start.20 = (f32[128,1024]{1,0:T(8,128)}, f32[128,1024]{1,0:T(8,128)S(1)}, u32[]{:S(2)}) copy-start(f32[128,1024]{1,0:T(8,128)S(1)} %fusion.61) | copy-start | bytes 1572868
  289.1 13.4 %copy-start.81 = (bf16[128,1536]{1,0:T(8,128)(2,1)}, bf16[128,1536]{1,0:T(8,128)(2,1)S(1)}, u32[]{:S(2)}) copy-start(bf16[128,1536]{1,0:T(8,128)(2,1)S(1)} %multiply_convert_fusion.5) | copy-start | bytes 1179652
  289.1 11.7 %collective-permute-start.1 = (bf16[128,1536]{1,0:T(8,128)(2,1)S(1)}, bf16[128,1536]{1,0:T(8,128)(2,1)S(1)}, u32[]{:S(2)}, u32[]{:S(2)}) collective-permute-start(bf16[128,1536]{1,0:T(8,128)(2,1)S(1)} %multiply_convert_fusion.5), channel_id=1, source_target_pairs={{0,1},{1,0},{2,3},{3,2},{4,5},{5,4},{6,7},{7,6},{8,9},{9,8},{10,11... | collective-permute-start | bytes 1179656 | tf_op jit(solution)/shard_map/ppermute | solution.py:189
  289.2 11.5 %collective-permute-start = (bf16[128,1536]{1,0:T(8,128)(2,1)S(1)}, bf16[128,1536]{1,0:T(8,128)(2,1)S(1)}, u32[]{:S(2)}, u32[]{:S(2)}) collective-permute-start(bf16[128,1536]{1,0:T(8,128)(2,1)S(1)} %multiply_convert_fusion.5), channel_id=1, source_target_pairs={{0,2},{1,3},{2,0},{3,1},{4,6},{5,7},{6,4},{7,5},{8,10},{9,11},{10,... | collective-permute-start | bytes 1179656 | tf_op jit(solution)/shard_map/ppermute | solution.py:189
  300.7 1.7 collective-permute-start.2
  305.5 32.2 %slice-start.6 = ((s8[6291456]{0:T(1024)(128)(4,1)}), s8[4194304]{0:T(1024)(128)(4,1)S(1)}, s32[]{:S(2)}) async-start(s8[6291456]{0:T(1024)(128)(4,1)} %bitcast.422), calls=%async_computation.6 | async-start | bytes 8388608
  310.8 26.9 %slice-start.7 = ((s8[6291456]{0:T(1024)(128)(4,1)}), s8[2097152]{0:T(1024)(128)(4,1)S(1)}, s32[]{:S(2)}) async-start(s8[6291456]{0:T(1024)(128)(4,1)} %bitcast.422), calls=%async_computation.7 | async-start | bytes 4194304
  311.9 1.8 collective-permute-start.4
  312.5 3.0 collective-permute-start.3
  313.8 11.2 %collective-permute-start.5 = (bf16[128,1536]{1,0:T(8,128)(2,1)S(1)}, bf16[128,1536]{1,0:T(8,128)(2,1)S(1)}, u32[]{:S(2)}, u32[]{:S(2)}) collective-permute-start(bf16[128,1536]{1,0:T(8,128)(2,1)S(1)} %add_convert_fusion.4), channel_id=1, source_target_pairs={{0,2},{1,3},{2,0},{3,1},{4,6},{5,7},{6,4},{7,5},{8,10},{9,11},{10,... | collective-permute-start | bytes 1179656 | tf_op jit(solution)/shard_map/ppermute | solution.py:189
  325.3 36.8 %copy-start.18 = (f32[128,1536]{1,0:T(8,128)}, f32[128,1536]{1,0:T(8,128)S(1)}, u32[]{:S(2)}) copy-start(f32[128,1536]{1,0:T(8,128)S(1)} %get-tuple-element.376) | copy-start | bytes 2359300
  325.5 15.6 %copy-start.83 = (bf16[128,1536]{1,0:T(8,128)(2,1)}, bf16[128,1536]{1,0:T(8,128)(2,1)S(1)}, u32[]{:S(2)}) copy-start(bf16[128,1536]{1,0:T(8,128)(2,1)S(1)} %multiply_convert_fusion.4) | copy-start | bytes 1179652
  325.5 10.4 %collective-permute-start.6 = (bf16[128,1536]{1,0:T(8,128)(2,1)S(1)}, bf16[128,1536]{1,0:T(8,128)(2,1)S(1)}, u32[]{:S(2)}, u32[]{:S(2)}) collective-permute-start(bf16[128,1536]{1,0:T(8,128)(2,1)S(1)} %multiply_convert_fusion.4), channel_id=1, source_target_pairs={{0,2},{1,3},{2,0},{3,1},{4,6},{5,7},{6,4},{7,5},{8,10},{9,11},{10,... | collective-permute-start | bytes 1179656 | tf_op jit(solution)/shard_map/ppermute | solution.py:189
  327.2 8.9 collective-permute-start.7
  335.9 1.7 collective-permute-start.8
  348.1 1.8 collective-permute-start.10
  349.1 3.7 collective-permute-start.9
  350.9 11.2 %collective-permute-start.11 = (bf16[128,1536]{1,0:T(8,128)(2,1)S(1)}, bf16[128,1536]{1,0:T(8,128)(2,1)S(1)}, u32[]{:S(2)}, u32[]{:S(2)}) collective-permute-start(bf16[128,1536]{1,0:T(8,128)(2,1)S(1)} %add_convert_fusion.3), channel_id=1, source_target_pairs={{0,2},{1,3},{2,0},{3,1},{4,6},{5,7},{6,4},{7,5},{8,10},{9,11},{10,... | collective-permute-start | bytes 1179656 | tf_op jit(solution)/shard_map/ppermute | solution.py:189
  368.5 33.6 %copy-start.28 = (f32[512,1024]{1,0:T(8,128)}, f32[512,1024]{1,0:T(8,128)S(1)}, u32[]{:S(2)}) copy-start(f32[512,1024]{1,0:T(8,128)S(1)} %get-tuple-element.372) | copy-start | bytes 6291460
  380.4 21.7 %copy-start.149 = (bf16[4,2,2,2,64,1024]{5,4,3,2,1,0:T(8,128)(2,1)S(1)}, bf16[4,2,2,2,64,1024]{5,4,3,2,1,0:T(8,128)(2,1)}, u32[]{:S(2)}) copy-start(bf16[4,2,2,2,64,1024]{5,4,3,2,1,0:T(8,128)(2,1)} %get-tuple-element.154) | copy-start | bytes 12582916
  419.3 44.6 %collective-permute-start.12 = (bf16[2,2,2,2,64,1024]{5,4,3,2,1,0:T(8,128)(2,1)}, bf16[2,2,2,2,64,1024]{5,4,3,2,1,0:T(8,128)(2,1)}, u32[]{:S(2)}, u32[]{:S(2)}) collective-permute-start(bf16[2,2,2,2,64,1024]{5,4,3,2,1,0:T(8,128)(2,1)} %dynamic-slice_bitcast_fusion.1), channel_id=1, source_target_pairs={{0,1},{1,0},{2,3},{3,2},{4,5},{5,4},{6,7},{7,6},{8,9},{9,8},{10,11... | collective-permute-start | bytes 6291464 | tf_op jit(solution)/shard_map/ppermute | solution.py:189
  479.9 22.7 %collective-permute-start.13 = (bf16[2,2,2,2,32,4480]{5,4,2,1,0,3:T(8,128)(2,1)}, bf16[2,2,2,2,32,4480]{5,4,2,1,0,3:T(8,128)(2,1)}, u32[]{:S(2)}, u32[]{:S(2)}) collective-permute-start(bf16[2,2,2,2,32,4480]{5,4,2,1,0,3:T(8,128)(2,1)} %copy_bitcast_fusion), channel_id=1, source_target_pairs={{0,1},{1,0},{2,3},{3,2},{4,5},{5,4},{6,7},{7,6},{8,9},{9,8},{10,11... | collective-permute-start | bytes 13762568 | tf_op jit(solution)/shard_map/ppermute | solution.py:189
  487.2 34.7 %collective-permute-start.17 = (bf16[2,2,2,64,1024]{4,3,2,1,0:T(8,128)(2,1)S(1)}, bf16[2,2,2,64,1024]{4,3,2,1,0:T(8,128)(2,1)S(1)}, u32[]{:S(2)}, u32[]{:S(2)}) collective-permute-start(bf16[2,2,2,64,1024]{4,3,2,1,0:T(8,128)(2,1)S(1)} %copy-done.72), channel_id=1, source_target_pairs={{0,2},{1,3},{2,0},{3,1},{4,6},{5,7},{6,4},{7,5},{8,10},{9,11},{10,... | collective-permute-start | bytes 3145736 | tf_op jit(solution)/shard_map/ppermute | solution.py:189
  501.1 20.1 %slice-start = ((s8[6291456]{0:T(1024)(128)(4,1)}), s8[4194304]{0:T(1024)(128)(4,1)S(1)}, s32[]{:S(2)}) async-start(s8[6291456]{0:T(1024)(128)(4,1)} %bitcast.341), calls=%async_computation | async-start | bytes 8388608
  502.7 18.5 %slice-start.1 = ((s8[6291456]{0:T(1024)(128)(4,1)}), s8[2097152]{0:T(1024)(128)(4,1)S(1)}, s32[]{:S(2)}) async-start(s8[6291456]{0:T(1024)(128)(4,1)} %bitcast.341), calls=%async_computation.1 | async-start | bytes 4194304
  502.7 18.5 %collective-permute-start.14 = (bf16[128,1536]{1,0:T(8,128)(2,1)S(1)}, bf16[128,1536]{1,0:T(8,128)(2,1)S(1)}, u32[]{:S(2)}, u32[]{:S(2)}) collective-permute-start(bf16[128,1536]{1,0:T(8,128)(2,1)S(1)} %convert_element_type.522), channel_id=1, source_target_pairs={{0,2},{1,3},{2,0},{3,1},{4,6},{5,7},{6,4},{7,5},{8,10},{9,11},{10,... | collective-permute-start | bytes 1179656 | tf_op jit(solution)/shard_map/ppermute | solution.py:189
  504.4 19.4 %collective-permute-start.15 = (bf16[128,1536]{1,0:T(8,128)(2,1)S(1)}, bf16[128,1536]{1,0:T(8,128)(2,1)S(1)}, u32[]{:S(2)}, u32[]{:S(2)}) collective-permute-start(bf16[128,1536]{1,0:T(8,128)(2,1)S(1)} %convert_element_type.522), channel_id=1, source_target_pairs={{0,1},{1,0},{2,3},{3,2},{4,5},{5,4},{6,7},{7,6},{8,9},{9,8},{10,11... | collective-permute-start | bytes 1179656 | tf_op jit(solution)/shard_map/ppermute | solution.py:189
  521.2 2.6 collective-permute-start.16
  521.8 51.0 %copy-start.71 = (bf16[2,2,2,64,1024]{4,3,2,1,0:T(8,128)(2,1)}, bf16[2,2,2,64,1024]{4,3,2,1,0:T(8,128)(2,1)S(1)}, u32[]{:S(2)}) copy-start(bf16[2,2,2,64,1024]{4,3,2,1,0:T(8,128)(2,1)S(1)} %collective-permute-done.17) | copy-start | bytes 3145732
  523.9 24.1 %collective-permute-start.21 = (bf16[2,2,64,1024]{3,2,1,0:T(8,128)(2,1)S(1)}, bf16[2,2,64,1024]{3,2,1,0:T(8,128)(2,1)S(1)}, u32[]{:S(2)}, u32[]{:S(2)}) collective-permute-start(bf16[2,2,64,1024]{3,2,1,0:T(8,128)(2,1)S(1)} %fusion.20), channel_id=1, source_target_pairs={{0,4},{4,0},{8,12},{12,8},{16,20},{20,16},{24,28},{28,24},{1,5},{5... | collective-permute-start | bytes 1572872 | tf_op jit(solution)/shard_map/ppermute | solution.py:189
  527.2 76.9 %copy-start.51 = (bf16[1536,1024]{1,0:T(8,128)(2,1)}, bf16[1536,1024]{1,0:T(8,128)(2,1)S(1)}, u32[]{:S(2)}) copy-start(bf16[1536,1024]{1,0:T(8,128)(2,1)S(1)} %convolution_convert_fusion.7) | copy-start | bytes 9437188
  539.9 9.6 %collective-permute-start.18 = (bf16[128,1536]{1,0:T(8,128)(2,1)S(1)}, bf16[128,1536]{1,0:T(8,128)(2,1)S(1)}, u32[]{:S(2)}, u32[]{:S(2)}) collective-permute-start(bf16[128,1536]{1,0:T(8,128)(2,1)S(1)} %get-tuple-element.387), channel_id=1, source_target_pairs={{0,1},{1,0},{2,3},{3,2},{4,5},{5,4},{6,7},{7,6},{8,9},{9,8},{10,11... | collective-permute-start | bytes 1179656 | tf_op jit(solution)/shard_map/ppermute | solution.py:189
  540.1 4.0 collective-permute-start.19
  544.3 11.3 %collective-permute-start.20 = (bf16[128,1536]{1,0:T(8,128)(2,1)S(1)}, bf16[128,1536]{1,0:T(8,128)(2,1)S(1)}, u32[]{:S(2)}, u32[]{:S(2)}) collective-permute-start(bf16[128,1536]{1,0:T(8,128)(2,1)S(1)} %add_convert_fusion.2), channel_id=1, source_target_pairs={{0,2},{1,3},{2,0},{3,1},{4,6},{5,7},{6,4},{7,5},{8,10},{9,11},{10,... | collective-permute-start | bytes 1179656 | tf_op jit(solution)/shard_map/ppermute | solution.py:189
  548.0 24.9 %copy-start.77 = (bf16[2,2,64,1024]{3,2,1,0:T(8,128)(2,1)}, bf16[2,2,64,1024]{3,2,1,0:T(8,128)(2,1)S(1)}, u32[]{:S(2)}) copy-start(bf16[2,2,64,1024]{3,2,1,0:T(8,128)(2,1)S(1)} %collective-permute-done.21) | copy-start | bytes 1572868
  556.2 10.5 %collective-permute-start.22 = (bf16[128,1536]{1,0:T(8,128)(2,1)S(1)}, bf16[128,1536]{1,0:T(8,128)(2,1)S(1)}, u32[]{:S(2)}, u32[]{:S(2)}) collective-permute-start(bf16[128,1536]{1,0:T(8,128)(2,1)S(1)} %get-tuple-element.367), channel_id=1, source_target_pairs={{0,2},{1,3},{2,0},{3,1},{4,6},{5,7},{6,4},{7,5},{8,10},{9,11},{10,... | collective-permute-start | bytes 1179656 | tf_op jit(solution)/shard_map/ppermute | solution.py:189
  559.5 13.3 %collective-permute-start.25 = (bf16[2,64,1024]{2,1,0:T(8,128)(2,1)S(1)}, bf16[2,64,1024]{2,1,0:T(8,128)(2,1)S(1)}, u32[]{:S(2)}, u32[]{:S(2)}) collective-permute-start(bf16[2,64,1024]{2,1,0:T(8,128)(2,1)S(1)} %fusion.46), channel_id=1, source_target_pairs={{0,16},{4,20},{8,24},{12,28},{16,0},{20,4},{24,8},{28,12},{1,17},{... | collective-permute-start | bytes 786440 | tf_op jit(solution)/shard_map/ppermute | solution.py:189
  559.6 14.4 %collective-permute-start.23 = (bf16[128,1536]{1,0:T(8,128)(2,1)S(1)}, bf16[128,1536]{1,0:T(8,128)(2,1)S(1)}, u32[]{:S(2)}, u32[]{:S(2)}) collective-permute-start(bf16[128,1536]{1,0:T(8,128)(2,1)S(1)} %get-tuple-element.367), channel_id=1, source_target_pairs={{0,1},{1,0},{2,3},{3,2},{4,5},{5,4},{6,7},{7,6},{8,9},{9,8},{10,11... | collective-permute-start | bytes 1179656 | tf_op jit(solution)/shard_map/ppermute | solution.py:189
  566.7 7.3 collective-permute-start.24
  566.9 37.3 %collective-permute-start.30 = (bf16[2,2,192,1024]{3,2,1,0:T(8,128)(2,1)S(1)}, bf16[2,2,192,1024]{3,2,1,0:T(8,128)(2,1)S(1)}, u32[]{:S(2)}, u32[]{:S(2)}) collective-permute-start(bf16[2,2,192,1024]{3,2,1,0:T(8,128)(2,1)S(1)} %dynamic-slice_bitcast_fusion.4), channel_id=1, source_target_pairs={{0,4},{4,0},{8,12},{12,8},{16,20},{20,16},{24,28},{28,24},{1,5},{5... | collective-permute-start | bytes 4718600 | tf_op jit(solution)/shard_map/ppermute | solution.py:189
  587.7 17.9 %collective-permute-start.27 = (bf16[128,1536]{1,0:T(8,128)(2,1)S(1)}, bf16[128,1536]{1,0:T(8,128)(2,1)S(1)}, u32[]{:S(2)}, u32[]{:S(2)}) collective-permute-start(bf16[128,1536]{1,0:T(8,128)(2,1)S(1)} %get-tuple-element.386), channel_id=1, source_target_pairs={{0,1},{1,0},{2,3},{3,2},{4,5},{5,4},{6,7},{7,6},{8,9},{9,8},{10,11... | collective-permute-start | bytes 1179656 | tf_op jit(solution)/shard_map/ppermute | solution.py:189
  596.9 94.3 %collective-permute-start.31 = (bf16[2,2,192,1024]{3,2,1,0:T(8,128)(2,1)}, bf16[2,2,192,1024]{3,2,1,0:T(8,128)(2,1)}, u32[]{:S(2)}, u32[]{:S(2)}) collective-permute-start(bf16[2,2,192,1024]{3,2,1,0:T(8,128)(2,1)} %dynamic-slice_bitcast_fusion.3), channel_id=1, source_target_pairs={{0,4},{4,0},{8,12},{12,8},{16,20},{20,16},{24,28},{28,24},{1,5},{5... | collective-permute-start | bytes 4718600 | tf_op jit(solution)/shard_map/ppermute | solution.py:189
  597.9 113.3 %collective-permute-start.35 = (bf16[2,2,192,1024]{3,2,1,0:T(8,128)(2,1)}, bf16[2,2,192,1024]{3,2,1,0:T(8,128)(2,1)}, u32[]{:S(2)}, u32[]{:S(2)}) collective-permute-start(bf16[2,2,192,1024]{3,2,1,0:T(8,128)(2,1)} %dynamic-slice_bitcast_fusion.2), channel_id=1, source_target_pairs={{0,4},{4,0},{8,12},{12,8},{16,20},{20,16},{24,28},{28,24},{1,5},{5... | collective-permute-start | bytes 4718600 | tf_op jit(solution)/shard_map/ppermute | solution.py:189
  605.6 11.9 %collective-permute-start.29 = (bf16[64,1024]{1,0:T(8,128)(2,1)S(1)}, bf16[64,1024]{1,0:T(8,128)(2,1)S(1)}, u32[]{:S(2)}, u32[]{:S(2)}) collective-permute-start(bf16[64,1024]{1,0:T(8,128)(2,1)S(1)} %fusion.71), channel_id=1, source_target_pairs={{0,8},{4,12},{8,0},{12,4},{16,24},{20,28},{24,16},{28,20},{1,9},{5... | collective-permute-start | bytes 393224 | tf_op jit(solution)/shard_map/ppermute | solution.py:189
  605.6 5.8 collective-permute-start.26
  605.7 11.6 %collective-permute-start.28 = (bf16[128,1536]{1,0:T(8,128)(2,1)S(1)}, bf16[128,1536]{1,0:T(8,128)(2,1)S(1)}, u32[]{:S(2)}, u32[]{:S(2)}) collective-permute-start(bf16[128,1536]{1,0:T(8,128)(2,1)S(1)} %add_convert_fusion.1), channel_id=1, source_target_pairs={{0,2},{1,3},{2,0},{3,1},{4,6},{5,7},{6,4},{7,5},{8,10},{9,11},{10,... | collective-permute-start | bytes 1179656 | tf_op jit(solution)/shard_map/ppermute | solution.py:189
  623.9 67.3 %collective-permute-start.32 = (bf16[2,2,2,32,4480]{4,3,2,1,0:T(8,128)(2,1)}, bf16[2,2,2,32,4480]{4,3,2,1,0:T(8,128)(2,1)}, u32[]{:S(2)}, u32[]{:S(2)}) collective-permute-start(bf16[2,2,2,32,4480]{4,3,2,1,0:T(8,128)(2,1)} %fusion.1), channel_id=1, source_target_pairs={{0,2},{1,3},{2,0},{3,1},{4,6},{5,7},{6,4},{7,5},{8,10},{9,11},{10,... | collective-permute-start | bytes 6881288 | tf_op jit(solution)/shard_map/ppermute | solution.py:189
  640.8 48.7 %collective-permute-start.34 = (bf16[2,192,1024]{2,1,0:T(8,128)(2,1)}, bf16[2,192,1024]{2,1,0:T(8,128)(2,1)}, u32[]{:S(2)}, u32[]{:S(2)}) collective-permute-start(bf16[2,192,1024]{2,1,0:T(8,128)(2,1)} %fusion.15), channel_id=1, source_target_pairs={{0,16},{4,20},{8,24},{12,28},{16,0},{20,4},{24,8},{28,12},{1,17},{... | collective-permute-start | bytes 2359304 | tf_op jit(solution)/shard_map/ppermute | solution.py:189
  643.1 48.1 %collective-permute-start.33 = (bf16[2,2,2,2,32,3072]{5,4,3,2,1,0:T(8,128)(2,1)}, bf16[2,2,2,2,32,3072]{5,4,3,2,1,0:T(8,128)(2,1)}, u32[]{:S(2)}, u32[]{:S(2)}) collective-permute-start(bf16[2,2,2,2,32,3072]{5,4,3,2,1,0:T(8,128)(2,1)} %dynamic-slice_bitcast_fusion), channel_id=1, source_target_pairs={{0,1},{1,0},{2,3},{3,2},{4,5},{5,4},{6,7},{7,6},{8,9},{9,8},{10,11... | collective-permute-start | bytes 9437192 | tf_op jit(solution)/shard_map/ppermute | solution.py:189
  643.2 45.9 %copy-start.111 = (bf16[1,2048]{1,0:T(2,128)(2,1)S(1)}, bf16[1,2048]{1,0:T(2,128)(2,1)}, u32[]{:S(2)}) copy-start(bf16[1,2048]{1,0:T(2,128)(2,1)} %stack.113) | copy-start | bytes 12292
  643.2 46.0 %copy-start.110 = (bf16[1,2048]{1,0:T(2,128)(2,1)S(1)}, bf16[1,2048]{1,0:T(2,128)(2,1)}, u32[]{:S(2)}) copy-start(bf16[1,2048]{1,0:T(2,128)(2,1)} %stack.120) | copy-start | bytes 12292
  643.2 46.2 %copy-start.103 = (bf16[4,2304]{1,0:T(4,128)(2,1)S(1)}, bf16[4,2304]{1,0:T(4,128)(2,1)}, u32[]{:S(2)}) copy-start(bf16[4,2304]{1,0:T(4,128)(2,1)} %reduce_sum.460) | copy-start | bytes 55300
  689.5 13.2 %slice-start.8 = ((s8[4587520]{0:T(1024)(128)(4,1)}), s8[4194304]{0:T(1024)(128)(4,1)S(1)}, s32[]{:S(2)}) async-start(s8[4587520]{0:T(1024)(128)(4,1)} %bitcast.433), calls=%async_computation.8 | async-start | bytes 8388608
  691.1 11.6 %collective-permute-start.36 = (bf16[192,1024]{1,0:T(8,128)(2,1)S(1)}, bf16[192,1024]{1,0:T(8,128)(2,1)S(1)}, u32[]{:S(2)}, u32[]{:S(2)}) collective-permute-start(bf16[192,1024]{1,0:T(8,128)(2,1)S(1)} %fusion.39), channel_id=1, source_target_pairs={{0,8},{4,12},{8,0},{12,4},{16,24},{20,28},{24,16},{28,20},{1,9},{5... | collective-permute-start | bytes 1179656 | tf_op jit(solution)/shard_map/ppermute | solution.py:189
  (149 other events, 670.7 us)

commit v5 on v4

--- a/solution.py
+++ b/solution.py
@@ -164,6 +164,35 @@
     return (first_new, second_new, weight - rate * (ratio + decay * weight))
 
 
+def lift_kernel(clip, gate, up, weight, first, second, *outputs):
+    for side, grad in enumerate((gate, up)):
+        updated = adam_step(
+            weight[:, side, :],
+            clip[0, 0] * grad[...],
+            first[:, side, :],
+            second[:, side, :],
+            rate_main,
+            weight_decay,
+        )
+        for output, value_entries in zip(outputs, updated):
+            output[:, side, :] = value_entries
+
+
+def lift_step(clip_factor, gate, up, weight, first, second):
+    rows, columns = gate.shape
+    block = 48 if rows % 48 == 0 else rows
+    flat = pl.BlockSpec((block, columns), lambda part: (part, 0))
+    paired = pl.BlockSpec((block, 2, columns), lambda part: (part, 0, 0))
+    return pl.pallas_call(
+        lift_kernel,
+        grid=(rows // block,),
+        out_shape=(jax.ShapeDtypeStruct(weight.shape, jnp.float32),) * 3,
+        in_specs=[pl.BlockSpec(memory_space=pltpu.SMEM), flat, flat, paired, paired, paired],
+        out_specs=(paired,) * 3,
+        compiler_params=pltpu.CompilerParams(vmem_limit_bytes=32 * 2**20),
+    )(clip_factor.reshape(1, 1), gate, up, weight, first, second)
+
+
 def to_low(value_entries):
     return value_entries.astype(jnp.bfloat16)
 
@@ -411,13 +440,15 @@
             barrier, inc=1, device_id=device, device_id_type=pl.DeviceIdType.MESH
         )
 
+    if not line:
+        others = peers("tensor", 4) + peers("dp", 2 * depth_z)
+        for device in others:
+            tell(device)
+        pl.semaphore_wait(barrier, len(others))
+        return
+
     for lane in ("x", "y", "core"):
         tell(partner(lane, 1, coordinates))
-    if not line:
-        for mask in range(1, depth_z):
-            tell(partner("z", mask, coordinates))
-        pl.semaphore_wait(barrier, depth_z + 2)
-        return
 
     @pl.when(z > 0)
     def _():
@@ -429,6 +460,13 @@
 
     ends = (z == 0).astype(jnp.int32) + (z == depth_z - 1).astype(jnp.int32)
     pl.semaphore_wait(barrier, 5 - ends)
+
+
+def peers(axis, size):
+    dp_place, tensor_place = lax.axis_index("dp"), lax.axis_index("tensor")
+    if axis == "dp":
+        return [(flip(dp_place, mask), tensor_place) for mask in range(1, size)]
+    return [(dp_place, flip(tensor_place, mask)) for mask in range(1, size)]
 
 
 def beside(way, coordinates):
@@ -785,27 +823,28 @@
             accumulate(job, step)
     totals[...] = extra[...]
     totals[0:8, :] += squares[0:8, :] + squares[8:16, :]
-    exchanges = [("core", 1), ("y", 1), ("x", 1)]
-    mask = 1
-    while mask < depth_z:
-        exchanges.append(("z", mask))
-        mask *= 2
     tiles = []
-    for number, (lane, mask) in enumerate(exchanges):
-        tiles.append(
-            pltpu.make_async_remote_copy(
-                src_ref=arrivals.at[2 * number],
-                dst_ref=arrivals.at[2 * number + 1],
-                send_sem=tile_sems.at[2 * number],
-                recv_sem=tile_sems.at[2 * number + 1],
-                device_id=partner(lane, mask, coordinates),
-                device_id_type=pl.DeviceIdType.MESH,
+    for axis, size, first in (("tensor", 4, 0), ("dp", 2 * depth_z, 4)):
+        spot = first + lax.axis_index(axis)
+        arrivals[spot] = totals[...]
+        for mask, device in enumerate(peers(axis, size), 1):
+            tiles.append(
+                pltpu.make_async_remote_copy(
+                    src_ref=arrivals.at[spot],
+                    dst_ref=arrivals.at[spot],
+                    send_sem=tile_sems.at[2 * (first + mask)],
+                    recv_sem=tile_sems.at[2 * (first + mask) + 1],
+                    device_id=device,
+                    device_id_type=pl.DeviceIdType.MESH,
+                )
             )
-        )
-        arrivals[2 * number] = totals[...]
-        tiles[-1].start()
-        tiles[-1].wait_recv()
-        totals[...] += arrivals[2 * number + 1]
+            tiles[-1].start()
+        for copy in tiles[1 - size :]:
+            copy.wait_recv()
+        result = arrivals[first]
+        for place in range(1, size):
+            result = result + arrivals[first + place]
+        totals[...] = result
     for copy in tiles:
         copy.wait_send()
     for action, job, step in plan:
@@ -867,7 +906,7 @@
     plan = order_steps(jobs)
     numbers = len(grads) * (2 * depth_z + 1)
     tile = jax.ShapeDtypeStruct(extra.shape, jnp.float32)
-    rounds = 3 + len(bit_masks(depth_z))
+    places = 4 + 2 * depth_z
     return pl.pallas_call(
         partial(sum_kernel, plan, kinds, sources, depth_z),
         out_shape=tuple(shapes) + (tile,),
@@ -877,11 +916,11 @@
         scratch_shapes=scratch
         + [
             pltpu.VMEM((16, 128), jnp.float32),
-            pltpu.VMEM((2 * rounds, 16, 128), jnp.float32),
+            pltpu.VMEM((places, 16, 128), jnp.float32),
             pltpu.SemaphoreType.DMA((numbers,)),
             pltpu.SemaphoreType.DMA((numbers,)),
             pltpu.SemaphoreType.DMA((len(grads),)),
-            pltpu.SemaphoreType.DMA((2 * rounds,)),
+            pltpu.SemaphoreType.DMA((2 * places,)),
         ],
         compiler_params=pltpu.CompilerParams(
             collective_id=collective_id, has_side_effects=True, vmem_limit_bytes=60 * 2**20
@@ -1292,13 +1331,12 @@
             - ending_slope
             + jnp.where(rows == ssd_block - 1, ends, 0.0)
         )
-        parts = []
-        for value_entries in (slope_gathered, slope_weighted * inputs):
-            high = to_low(value_entries)
-            parts += [high, to_low(value_entries - high.astype(jnp.float32))]
+        high = to_low(slope_gathered)
+        rest = to_low(slope_gathered - high.astype(jnp.float32))
+        parts = [high, rest, to_low(slope_weighted * inputs)]
         sums = low_dot(jnp.concatenate(parts, axis=0), chosen[columns, :], 1, 0)
         slope_cumulative[...] += sums[:ssd_block] + sums[ssd_block : 2 * ssd_block]
-        slope_steps[...] += sums[2 * ssd_block : 3 * ssd_block] + sums[3 * ssd_block :]
+        slope_steps[...] += sums[2 * ssd_block :]
         slope_inputs = slope_out * skip_here + slope_weighted * steps_here
         pull_convolved(columns, quad_lanes(quad, INNER), slope_inputs * inputs_pull)
         return carry
@@ -1658,16 +1696,16 @@
     devices = lax.axis_size("dp") * lax.axis_size("tensor")
     table_rows = tables.shape[1]
     small_here = small_params.shape[0]
-    mixed_rows = 2 * table_rows + 16
+    mixed_rows = 2 * table_rows
     length_pair = jnp.stack([lengths[0] // 16, lengths[0] % 16]).astype(jnp.bfloat16)
     tail = jnp.concatenate([to_low(small_params), length_pair])
     mixed = jnp.concatenate(
         [
-            to_low(tables).reshape(2 * table_rows, BYTE_WIDTH),
-            jnp.pad(tail, (0, 16 * BYTE_WIDTH - tail.shape[0])).reshape(16, BYTE_WIDTH),
-        ]
-    )
-    mixed_rows = mixed.shape[0]
+            to_low(tables).reshape(mixed_rows, BYTE_WIDTH),
+            jnp.pad(tail, (0, mixed_rows * 128 - tail.shape[0])).reshape(mixed_rows, 128),
+        ],
+        axis=1,
+    )
 
     def wide_in(layer):
         low = to_low(mamba_in[layer])
@@ -1697,7 +1735,7 @@
             (3, BYTE_LANES, half_route, half_route),
             (9, BYTE_LANES, 0, BYTE_WIDTH),
             (8, BYTE_LANES, 0, in_first),
-            (0, BYTE_LANES, 0, BYTE_WIDTH),
+            (0, BYTE_LANES, 0, BYTE_WIDTH + 128),
             (1, BYTE_LANES, in_first, in_last),
             (2, BYTE_LANES, 0, BYTE_WIDTH),
             (8, BYTE_LANES, in_first, in_last),
@@ -1720,14 +1758,14 @@
     mixed_whole = wholes[0]
     full_in, full_out, full_route = [wholes[1], wholes[8]], [wholes[2], wholes[9]], wholes[3]
     triple_whole, heed_exit_whole, lift_matrix_whole, lower_matrix_whole = wholes[4:8]
-    mixed_whole = mixed_whole.reshape(devices, mixed_rows, BYTE_WIDTH)
+    mixed_whole = mixed_whole.reshape(devices, mixed_rows, BYTE_WIDTH + 128)
     full_tables = (
-        mixed_whole[:, : 2 * table_rows]
+        mixed_whole[:, :, :BYTE_WIDTH]
         .reshape(devices, 2, table_rows, BYTE_WIDTH)
         .transpose(1, 0, 2, 3)
         .reshape(2, VOCAB, BYTE_WIDTH)
     )
-    tails = mixed_whole[:, 2 * table_rows :].reshape(devices, -1)
+    tails = mixed_whole[:, :, BYTE_WIDTH:].reshape(devices, -1)
     full_small = tails[:, :small_here].reshape(-1)
     pairs = tails[:, small_here : small_here + 2].astype(jnp.float32)
     byte_count = jnp.sum(pairs[:, 0] * 16.0 + pairs[:, 1])
@@ -1844,14 +1882,19 @@
     width = mamba_in.shape[2]
     grad_mixed = jnp.concatenate(
         [
-            to_low(grad_table_in).reshape(devices, table_rows, BYTE_WIDTH),
-            to_low(grad_table_out).reshape(devices, table_rows, BYTE_WIDTH),
+            jnp.concatenate(
+                [
+                    to_low(grad_table_in).reshape(devices, table_rows, BYTE_WIDTH),
+                    to_low(grad_table_out).reshape(devices, table_rows, BYTE_WIDTH),
+                ],
+                axis=1,
+            ),
             jnp.pad(
                 to_low(grad_small).reshape(devices, small_here),
-                ((0, 0), (0, 16 * BYTE_WIDTH - small_here)),
-            ).reshape(devices, 16, BYTE_WIDTH),
+                ((0, 0), (0, mixed_rows * 128 - small_here)),
+            ).reshape(devices, mixed_rows, 128),
         ],
-        axis=1,
+        axis=2,
     )
     conductor.close()
     parts = [
@@ -1865,7 +1908,7 @@
         jobs_enc[0],
         job_route,
         jobs_enc[1],
-        Summing(grad_mixed.reshape(-1, BYTE_WIDTH), True),
+        Summing(grad_mixed.reshape(-1, BYTE_WIDTH + 128), True),
     ]
     sums = [None if part.masks else part.result(jobs_enc[1].addends[0][0]) for part in parts]
     open_parts = [number for number in (8, 9, 7, 10, 3, 0, 1, 2, 4, 5, 6) if parts[number].masks]
@@ -1889,8 +1932,8 @@
     reduced_out_dec, reduced_out_enc, reduced_route = sums[6:9]
     reduced_in_enc = sums[9][:, :width]
     reduced_mixed = sums[10]
-    reduced_tables = reduced_mixed[: 2 * table_rows].reshape(2, table_rows, BYTE_WIDTH)
-    reduced_small = reduced_mixed[2 * table_rows :].reshape(-1)[:small_here]
+    reduced_tables = reduced_mixed[:, :BYTE_WIDTH].reshape(2, table_rows, BYTE_WIDTH)
+    reduced_small = reduced_mixed[:, BYTE_WIDTH:].reshape(-1)[:small_here]
     reduced_in = jnp.stack([reduced_in_enc, reduced_in_dec])
     reduced_out = jnp.stack([reduced_out_enc, reduced_out_dec])
     reduced = (
@@ -1976,6 +2019,9 @@
         )
         for position in range(9)
     ]
+    updated[7] = lift_step(
+        clip_factor, sums[1], sums[2], lifting_matrix, mlp_gate_up_first, mlp_gate_up_second
+    )
     return (loss_sum, byte_count, grad_norm) + tuple(
         (member for triple_out in updated for member in triple_out)
     )

time: 951 us -> 935 us (0.983)
    unnamed x363 -> x355, local copies, waits for them, and re-layouts: 31 us -> 22.3 us
where the time goes in v5:
time: 935 us; the launch traced here: 926 us
  Pallas kernels  547 us (59%)
  matrix products  151 us (16%)
  waiting for transfers between devices  80.5 us (9%)
  other arithmetic  65 us (7%)
  local copies, waits for them, and re-layouts  50.4 us (5%)
  starting transfers between devices  24.5 us (3%)
    pallas_call x1, Pallas kernels, spread_whole(): pl.pallas_call(partial(spread_kernel, plan, jobs, depth_z), out_shape=tup...  228 us
    pallas_call x1, Pallas kernels, sum_whole(): pl.pallas_call(partial(sum_kernel, plan, kinds, sources, depth_z), out_sh...  175 us
    pallas_call x2, Pallas kernels, middle_backward(): pl.pallas_call(middle_slope_kernel, grid=(chunks,), out_shape=(jax.ShapeD...  83.6 us
    ppermute x37, waiting for transfers between devices, swap(): lax.ppermute(value_entries, axis, [(place, place ^ mask) for place in ran...  80.5 us
    dot_general x11, matrix products, matmul_apply(): return jnp.dot(left, right, preferred_element_type=jnp.float32)  48.8 us
    dot_general x10, matrix products, product_nt(): lax.dot_general(left, right, (((1,), (1,)), ((), ())), preferred_element_...  45.3 us
    dot_general x11, matrix products, product_tn(): lax.dot_general(left, right, (((0,), (0,)), ((), ())), preferred_element_...  44 us
    pallas_call x2, Pallas kernels, middle_forward(): pl.pallas_call(middle_kernel, grid=(chunks,), out_shape=(jax.ShapeDtypeSt...  43.7 us
  transfers between devices with their start and end apart: 37, of which 15 were waited for; matrix products, arithmetic and copies ran while one was open for 13% of the time, Pallas kernels for 10%

profile of v5, /device:TPU:0, one launch (start us, length us, event | category | flops | bytes accessed | tf_op | source)
XLA Modules:
  0.0 926.0 jit_solution(16951243384173542966)
XLA Ops:
  13.8 227.9 %shard_map.526 = (bf16[4,2,2,2,16,1152]{5,4,3,2,1,0:T(8,128)(2,1)}, bf16[4,2,2,2,32,4480]{5,4,3,2,1,0:T(8,128)(2,1)}, bf16[4,2,2,2,64,1024]{5,4,3,2,1,0:T(8,128)...) custom-call(bf16[16,1152]{1,0:T(8,128)(2,1)} %pad_maximum_fusion.11., ...), custom_call_target="tpu_custom_call" | custom-call | tf_op jit(solution)/shard_map/pallas_call | solution.py:593
  246.8 11.3 %fusion.121.projected.earlier = f32[512,4480]{1,0:T(8,128)} fusion(bf16[1024,4480]{1,0:T(8,128)(2,1)} %bitcast.411, f32[512,1024]{1,0:T(8,128)S(1)} %get-tuple-element.366, f32[1024]{0:T(1024)S(1)} %get-tuple-element.346, f32[512]{0:T(512)S(1)} %fusion.102), kind=kOutput, calls=%fused_computation.351 | convolution fusion | flops 4699193344 | bytes 20453376 | tf_op jit(solution)/shard_map/dot_general | solution.py:201
  258.2 21.7 %shard_map.527 = (bf16[512,2048]{1,0:T(8,128)(2,1)S(1)}, f32[512,2048]{1,0:T(8,128)}, f32[4,128,2048]{2,1,0:T(8,128)}) custom-call(f32[512,4480]{1,0:T(8,128)} %fusion.121.projected.earlier, f32[4,2304]{1,0:T(4,128)S(1)} %squeeze.124.taps, f32[1,2048]{1,0:T(1,128)S(1)} %bitcast.338, f32[2,32]{1,0:T(2,128)S(1)} %get-tuple-element.377.decay, ...), custom_call_target="tpu_custom_call" | custom-call | flops 20000000000 | bytes 20000000 | tf_op jit(solution)/shard_map/pallas_call | solution.py:1376
  279.9 5.3 convolution_add_fusion.2
  288.5 3.5 fusion.54
  292.6 2.1 copy-done.22
  296.7 1.8 collective-permute-done
  300.2 2.2 convolution_convert_fusion.10.triple
  302.5 5.3 shard_map.528
  312.6 9.5 %collective-permute-done.5 = bf16[128,1536]{1,0:T(8,128)(2,1)S(1)} collective-permute-done((bf16[128,1536]{1,0:T(8,128)(2,1)S(1)}, bf16[128,1536]{1,0:T(8,128)(2,1)S(1)}, u32[]{:S(2)}, u32[]{:S(2)}) %collective-permute-start.5) | collective-permute-done | bytes 393248 | tf_op jit(solution)/shard_map/ppermute | solution.py:218
  324.3 8.7 collective-permute-done.6
  334.8 3.5 fusion.123
  342.1 1.8 convolution_convert_fusion.12
  350.0 9.3 %collective-permute-done.11 = bf16[128,1536]{1,0:T(8,128)(2,1)S(1)} collective-permute-done((bf16[128,1536]{1,0:T(8,128)(2,1)S(1)}, bf16[128,1536]{1,0:T(8,128)(2,1)S(1)}, u32[]{:S(2)}, u32[]{:S(2)}) %collective-permute-start.11) | collective-permute-done | bytes 393248 | tf_op jit(solution)/shard_map/ppermute | solution.py:218
  361.4 4.2 multiply_reduce_fusion.10
  365.6 11.9 %fusion.122.projected.earlier = f32[512,4480]{1,0:T(8,128)} fusion(bf16[1024,4480]{1,0:T(8,128)(2,1)} %bitcast.413, f32[512,1024]{1,0:T(8,128)S(1)} %get-tuple-element.315, f32[1024]{0:T(1024)S(1)} %get-tuple-element.345, f32[512]{0:T(512)S(1)} %fusion.103), kind=kOutput, calls=%fused_computation.352 | convolution fusion | flops 4699193344 | bytes 20453376 | tf_op jit(solution)/shard_map/dot_general | solution.py:201
  377.5 22.0 %shard_map.529 = (bf16[512,2048]{1,0:T(8,128)(2,1)S(1)}, f32[512,2048]{1,0:T(8,128)}, f32[4,128,2048]{2,1,0:T(8,128)}) custom-call(f32[512,4480]{1,0:T(8,128)} %fusion.122.projected.earlier, f32[4,2304]{1,0:T(4,128)S(1)} %slice.397.taps, f32[1,2048]{1,0:T(1,128)S(1)} %bitcast.342, f32[2,32]{1,0:T(2,128)S(1)} %get-tuple-element.378.decay, ...), custom_call_target="tpu_custom_call" | custom-call | flops 20000000000 | bytes 20000000 | tf_op jit(solution)/shard_map/pallas_call | solution.py:1376
  399.5 2.4 multiply_reduce_fusion.9
  402.7 1.9 multiply_reduce_fusion
  406.8 4.4 fusion.49.slope
  411.2 2.4 convolution_convert_fusion.8
  418.0 41.9 %shard_map.530 = (bf16[512,4480]{1,0:T(8,128)(2,1)}, f32[4,8,2304]{2,1,0:T(8,128)S(1)}, f32[8,2048]{1,0:T(8,128)S(1)}, f32[8,2048]{1,0:T(8,128)S(1)}, f32[2,8,32]{2,1,0:T(8,128)S(1)}) custom-call(f32[512,4480]{1,0:T(8,128)} %fusion.122.projected.earlier, f32[512,4480]{1,0:T(8,128)} %fusion.122.projected.earlier, f32[512,2048]{1,0:T(8,128)S(1)} %copy-done.21, ...), custom_call_target="tpu_custom_call" | custom-call | flops 49999998976 | bytes 30000000 | tf_op jit(solution)/shard_map/pallas_call | solution.py:1429
  459.9 3.1 fusion.8
  463.0 7.8 convolution_convert_fusion.1
  470.8 2.7 copy_bitcast_fusion
  473.6 2.3 copy-done.23
  479.1 4.0 convolution_convert_fusion.15
  484.6 9.5 %multiply_reduce_fusion.1 = (bf16[1024]{0:T(1024)(128)(2,1)S(1)}, f32[512]{0:T(512)S(1)}, f32[512,1024]{1,0:T(8,128)S(1)}) fusion(f32[512,1024]{1,0:T(8,128)S(1)} %copy-done.36, f32[512]{0:T(512)S(1)} %fusion.103, f32[1024]{0:T(1024)S(1)} %get-tuple-element.345, bf16[512,4480]{1,0:T(8,128)(2,1)} %get-tuple-element.167, bf16[1024,4480]{1,0:T(8,128)(2,1)} %bitcast.414), kind=kOutput, calls=%fused_computation.41 | convolution fusion | flops 4700764672 | bytes 17967104 | tf_op jit(solution)/shard_map/dot_general | solution.py:211
  495.0 2.0 fusion.9
  500.6 16.5 %collective-permute-done.14 = bf16[128,1536]{1,0:T(8,128)(2,1)S(1)} collective-permute-done((bf16[128,1536]{1,0:T(8,128)(2,1)S(1)}, bf16[128,1536]{1,0:T(8,128)(2,1)S(1)}, u32[]{:S(2)}, u32[]{:S(2)}) %collective-permute-start.14) | collective-permute-done | bytes 393248 | tf_op jit(solution)/shard_map/ppermute | solution.py:218
  517.8 1.9 fusion.18
  521.3 1.8 convolution_convert_fusion.7
  523.5 5.2 fusion.74
  529.0 6.9 convolution_convert_fusion.11
  536.5 1.8 convolution_convert_fusion.5
  538.4 1.8 convolution_convert_fusion.6
  545.5 6.1 collective-permute-done.20
  555.8 7.0 collective-permute-done.22
  564.7 4.2 collective-permute-done.25
  571.4 7.7 shard_map.531
  579.1 2.1 convolution_convert_fusion.14
  581.2 2.2 convolution_convert_fusion.9
  583.6 4.3 fusion.1
  587.9 4.9 copy.100
  594.9 5.4 collective-permute-done.30
  603.5 4.0 convolution_convert_fusion.2
  607.5 5.9 collective-permute-done.28
  614.1 1.8 fusion.41
  616.0 3.8 convolution_convert_fusion.3
  622.4 2.0 dynamic-slice_bitcast_fusion
  624.4 6.3 convolution_add_fusion
  630.7 4.4 fusion.46.slope
  635.1 4.4 convolution_convert_fusion.4
  639.5 2.4 collective-permute-start.34
  642.0 41.7 %shard_map.532 = (bf16[512,4480]{1,0:T(8,128)(2,1)}, f32[4,8,2304]{2,1,0:T(8,128)S(1)}, f32[8,2048]{1,0:T(8,128)S(1)}, f32[8,2048]{1,0:T(8,128)S(1)}, f32[2,8,32]{2,1,0:T(8,128)S(1)}) custom-call(f32[512,4480]{1,0:T(8,128)} %fusion.121.projected.earlier, f32[512,4480]{1,0:T(8,128)} %fusion.121.projected.earlier, f32[512,2048]{1,0:T(8,128)S(1)} %copy-done.20, ...), custom_call_target="tpu_custom_call" | custom-call | flops 49999998976 | bytes 30000000 | tf_op jit(solution)/shard_map/pallas_call | solution.py:1429
  689.2 9.9 %convolution_convert_fusion = bf16[1024,4480]{1,0:T(8,128)(2,1)} fusion(bf16[512,4480]{1,0:T(8,128)(2,1)} %get-tuple-element.201, f32[512,1024]{1,0:T(8,128)S(1)} %copy-done.33, f32[1024]{0:T(1024)} %copy-done.125, f32[512]{0:T(512)} %copy-done.128), kind=kOutput, calls=%fused_computation | convolution fusion | flops 4703780864 | bytes 15865856 | tf_op jit(solution)/shard_map/dot_general | solution.py:205
  700.7 8.3 multiply_reduce_fusion.3
  711.4 2.1 multiply_reduce_fusion.15
  716.7 5.8 fusion
  724.3 175.1 %shard_map.533 = (f32[32,3072]{1,0:T(8,128)}, f32[32,4480]{1,0:T(8,128)}, f32[64,1024]{1,0:T(8,128)}, f32[16,1152]{1,0:T(8,128)}, f32[192,1152]{1,0:T(8,128)}, /...) custom-call(bf16[4,2,2,32,3072]{4,3,2,1,0:T(8,128)(2,1)} %bitcast.35, ...), custom_call_target="tpu_custom_call" | custom-call | tf_op jit(solution)/shard_map/pallas_call | solution.py:910
  909.4 1.8 multiply_subtract_fusion.2
  911.9 1.9 multiply_subtract_fusion.1
  916.4 2.3 multiply_subtract_fusion
  920.4 4.2 shard_map.534
  (600 shorter events, 114.0 us)
Async XLA Ops:
  244.0 14.1 %copy-start.51 = (bf16[2,32,8,1024]{3,2,0,1:T(8,128)(2,1)}, bf16[2,32,8,1024]{3,2,0,1:T(8,128)(2,1)S(1)}, u32[]{:S(2)}) copy-start(bf16[2,32,8,1024]{3,2,0,1:T(8,128)(2,1)S(1)} %slice_bitcast_fusion) | copy-start | bytes 3145732
  244.3 13.8 %copy-start.125 = (f32[1024]{0:T(1024)}, f32[1024]{0:T(1024)S(1)}, u32[]{:S(2)}) copy-start(f32[1024]{0:T(1024)S(1)} %get-tuple-element.346) | copy-start | bytes 12292
  244.9 41.8 %copy-start.100 = (f32[1536]{0:T(1024)}, f32[1536]{0:T(1024)S(1)}, u32[]{:S(2)}) copy-start(f32[1536]{0:T(1024)S(1)} %get-tuple-element.342) | copy-start | bytes 18436
  244.9 77.5 %copy-start.102 = (f32[1536]{0:T(1024)}, f32[1536]{0:T(1024)S(1)}, u32[]{:S(2)}) copy-start(f32[1536]{0:T(1024)S(1)} %get-tuple-element.341) | copy-start | bytes 18436
  245.0 64.2 %copy-start.112 = (f32[1,512]{1,0:T(1,128)}, f32[1,512]{1,0:T(1,128)S(1)}, u32[]{:S(2)}) copy-start(f32[1,512]{1,0:T(1,128)S(1)} %convert_element_type.490) | copy-start | bytes 6148
  246.2 33.7 %copy-start.32 = (f32[512,1024]{1,0:T(8,128)}, f32[512,1024]{1,0:T(8,128)S(1)}, u32[]{:S(2)}) copy-start(f32[512,1024]{1,0:T(8,128)S(1)} %get-tuple-element.366) | copy-start | bytes 6291460
  246.3 75.8 %copy-start.91 = (f32[1536]{0:T(1024)}, f32[1536]{0:T(1024)S(1)}, u32[]{:S(2)}) copy-start(f32[1536]{0:T(1024)S(1)} %pad.101.clone) | copy-start | bytes 18436
  246.8 41.7 %slice-start.2 = ((s8[6291456]{0:T(1024)(128)(4,1)}), s8[4194304]{0:T(1024)(128)(4,1)S(1)}, s32[]{:S(2)}) async-start(s8[6291456]{0:T(1024)(128)(4,1)} %bitcast.416), calls=%async_computation.2 | async-start | bytes 8388608
  258.2 30.4 %slice-start.3 = ((s8[6291456]{0:T(1024)(128)(4,1)}), s8[2097152]{0:T(1024)(128)(4,1)S(1)}, s32[]{:S(2)}) async-start(s8[6291456]{0:T(1024)(128)(4,1)} %bitcast.416), calls=%async_computation.3 | async-start | bytes 4194304
  286.5 35.5 %copy-start.26 = (f32[128,1024]{1,0:T(8,128)}, f32[128,1024]{1,0:T(8,128)S(1)}, u32[]{:S(2)}) copy-start(f32[128,1024]{1,0:T(8,128)S(1)} %fusion.59) | copy-start | bytes 1572868
  286.9 13.4 %copy-start.84 = (bf16[128,1536]{1,0:T(8,128)(2,1)}, bf16[128,1536]{1,0:T(8,128)(2,1)S(1)}, u32[]{:S(2)}) copy-start(bf16[128,1536]{1,0:T(8,128)(2,1)S(1)} %multiply_convert_fusion.5) | copy-start | bytes 1179652
  286.9 11.7 %collective-permute-start.1 = (bf16[128,1536]{1,0:T(8,128)(2,1)S(1)}, bf16[128,1536]{1,0:T(8,128)(2,1)S(1)}, u32[]{:S(2)}, u32[]{:S(2)}) collective-permute-start(bf16[128,1536]{1,0:T(8,128)(2,1)S(1)} %multiply_convert_fusion.5), channel_id=1, source_target_pairs={{0,1},{1,0},{2,3},{3,2},{4,5},{5,4},{6,7},{7,6},{8,9},{9,8},{10,11... | collective-permute-start | bytes 1179656 | tf_op jit(solution)/shard_map/ppermute | solution.py:218
  287.0 11.5 %collective-permute-start = (bf16[128,1536]{1,0:T(8,128)(2,1)S(1)}, bf16[128,1536]{1,0:T(8,128)(2,1)S(1)}, u32[]{:S(2)}, u32[]{:S(2)}) collective-permute-start(bf16[128,1536]{1,0:T(8,128)(2,1)S(1)} %multiply_convert_fusion.5), channel_id=1, source_target_pairs={{0,2},{1,3},{2,0},{3,1},{4,6},{5,7},{6,4},{7,5},{8,10},{9,11},{10,... | collective-permute-start | bytes 1179656 | tf_op jit(solution)/shard_map/ppermute | solution.py:218
  298.5 1.7 collective-permute-start.2
  302.5 32.2 %slice-start.4 = ((s8[6291456]{0:T(1024)(128)(4,1)}), s8[4194304]{0:T(1024)(128)(4,1)S(1)}, s32[]{:S(2)}) async-start(s8[6291456]{0:T(1024)(128)(4,1)} %bitcast.420), calls=%async_computation.4 | async-start | bytes 8388608
  307.9 26.9 %slice-start.5 = ((s8[6291456]{0:T(1024)(128)(4,1)}), s8[2097152]{0:T(1024)(128)(4,1)S(1)}, s32[]{:S(2)}) async-start(s8[6291456]{0:T(1024)(128)(4,1)} %bitcast.420), calls=%async_computation.5 | async-start | bytes 4194304
  309.0 1.8 collective-permute-start.4
  309.6 3.0 collective-permute-start.3
  310.9 11.2 %collective-permute-start.5 = (bf16[128,1536]{1,0:T(8,128)(2,1)S(1)}, bf16[128,1536]{1,0:T(8,128)(2,1)S(1)}, u32[]{:S(2)}, u32[]{:S(2)}) collective-permute-start(bf16[128,1536]{1,0:T(8,128)(2,1)S(1)} %add_convert_fusion.4), channel_id=1, source_target_pairs={{0,2},{1,3},{2,0},{3,1},{4,6},{5,7},{6,4},{7,5},{8,10},{9,11},{10,... | collective-permute-start | bytes 1179656 | tf_op jit(solution)/shard_map/ppermute | solution.py:218
  322.4 15.9 %copy-start.146 = (f32[128]{0:T(128)}, f32[128]{0:T(128)S(1)}, u32[]{:S(2)}) copy-start(f32[128]{0:T(128)S(1)} %get-tuple-element.318) | copy-start | bytes 1540
  322.4 36.9 %copy-start.24 = (f32[128,1536]{1,0:T(8,128)}, f32[128,1536]{1,0:T(8,128)S(1)}, u32[]{:S(2)}) copy-start(f32[128,1536]{1,0:T(8,128)S(1)} %get-tuple-element.319) | copy-start | bytes 2359300
  322.4 15.8 %copy-start.134 = (f32[128]{0:T(128)}, f32[128]{0:T(128)S(1)}, u32[]{:S(2)}) copy-start(f32[128]{0:T(128)S(1)} %fusion.107) | copy-start | bytes 1540
  322.6 15.7 %copy-start.86 = (bf16[128,1536]{1,0:T(8,128)(2,1)}, bf16[128,1536]{1,0:T(8,128)(2,1)S(1)}, u32[]{:S(2)}) copy-start(bf16[128,1536]{1,0:T(8,128)(2,1)S(1)} %multiply_convert_fusion.4) | copy-start | bytes 1179652
  322.6 10.4 %collective-permute-start.6 = (bf16[128,1536]{1,0:T(8,128)(2,1)S(1)}, bf16[128,1536]{1,0:T(8,128)(2,1)S(1)}, u32[]{:S(2)}, u32[]{:S(2)}) collective-permute-start(bf16[128,1536]{1,0:T(8,128)(2,1)S(1)} %multiply_convert_fusion.4), channel_id=1, source_target_pairs={{0,2},{1,3},{2,0},{3,1},{4,6},{5,7},{6,4},{7,5},{8,10},{9,11},{10,... | collective-permute-start | bytes 1179656 | tf_op jit(solution)/shard_map/ppermute | solution.py:218
  324.2 8.8 collective-permute-start.7
  333.0 1.7 collective-permute-start.8
  345.2 1.8 collective-permute-start.10
  346.2 3.7 collective-permute-start.9
  348.1 11.2 %collective-permute-start.11 = (bf16[128,1536]{1,0:T(8,128)(2,1)S(1)}, bf16[128,1536]{1,0:T(8,128)(2,1)S(1)}, u32[]{:S(2)}, u32[]{:S(2)}) collective-permute-start(bf16[128,1536]{1,0:T(8,128)(2,1)S(1)} %add_convert_fusion.3), channel_id=1, source_target_pairs={{0,2},{1,3},{2,0},{3,1},{4,6},{5,7},{6,4},{7,5},{8,10},{9,11},{10,... | collective-permute-start | bytes 1179656 | tf_op jit(solution)/shard_map/ppermute | solution.py:218
  365.6 33.9 %copy-start.34 = (f32[512,1024]{1,0:T(8,128)}, f32[512,1024]{1,0:T(8,128)S(1)}, u32[]{:S(2)}) copy-start(f32[512,1024]{1,0:T(8,128)S(1)} %get-tuple-element.315) | copy-start | bytes 6291460
  377.5 22.0 %copy-start.149 = (bf16[4,2,2,2,64,1024]{5,4,3,2,1,0:T(8,128)(2,1)S(1)}, bf16[4,2,2,2,64,1024]{5,4,3,2,1,0:T(8,128)(2,1)}, u32[]{:S(2)}) copy-start(bf16[4,2,2,2,64,1024]{5,4,3,2,1,0:T(8,128)(2,1)} %get-tuple-element.157) | copy-start | bytes 12582916
  416.7 43.2 %collective-permute-start.12 = (bf16[2,2,2,2,64,1024]{5,4,3,2,1,0:T(8,128)(2,1)}, bf16[2,2,2,2,64,1024]{5,4,3,2,1,0:T(8,128)(2,1)}, u32[]{:S(2)}, u32[]{:S(2)}) collective-permute-start(bf16[2,2,2,2,64,1024]{5,4,3,2,1,0:T(8,128)(2,1)} %dynamic-slice_bitcast_fusion.1), channel_id=1, source_target_pairs={{0,1},{1,0},{2,3},{3,2},{4,5},{5,4},{6,7},{7,6},{8,9},{9,8},{10,11... | collective-permute-start | bytes 6291464 | tf_op jit(solution)/shard_map/ppermute | solution.py:218
  475.8 22.7 %collective-permute-start.13 = (bf16[2,2,2,2,32,4480]{5,4,2,1,0,3:T(8,128)(2,1)}, bf16[2,2,2,2,32,4480]{5,4,2,1,0,3:T(8,128)(2,1)}, u32[]{:S(2)}, u32[]{:S(2)}) collective-permute-start(bf16[2,2,2,2,32,4480]{5,4,2,1,0,3:T(8,128)(2,1)} %copy_bitcast_fusion), channel_id=1, source_target_pairs={{0,1},{1,0},{2,3},{3,2},{4,5},{5,4},{6,7},{7,6},{8,9},{9,8},{10,11... | collective-permute-start | bytes 13762568 | tf_op jit(solution)/shard_map/ppermute | solution.py:218
  483.1 34.7 %collective-permute-start.17 = (bf16[2,2,2,64,1024]{4,3,2,1,0:T(8,128)(2,1)S(1)}, bf16[2,2,2,64,1024]{4,3,2,1,0:T(8,128)(2,1)S(1)}, u32[]{:S(2)}, u32[]{:S(2)}) collective-permute-start(bf16[2,2,2,64,1024]{4,3,2,1,0:T(8,128)(2,1)S(1)} %copy-done.74), channel_id=1, source_target_pairs={{0,2},{1,3},{2,0},{3,1},{4,6},{5,7},{6,4},{7,5},{8,10},{9,11},{10,... | collective-permute-start | bytes 3145736 | tf_op jit(solution)/shard_map/ppermute | solution.py:218
  497.0 20.1 %slice-start = ((s8[6291456]{0:T(1024)(128)(4,1)}), s8[4194304]{0:T(1024)(128)(4,1)S(1)}, s32[]{:S(2)}) async-start(s8[6291456]{0:T(1024)(128)(4,1)} %bitcast.344), calls=%async_computation | async-start | bytes 8388608
  498.6 18.5 %slice-start.1 = ((s8[6291456]{0:T(1024)(128)(4,1)}), s8[2097152]{0:T(1024)(128)(4,1)S(1)}, s32[]{:S(2)}) async-start(s8[6291456]{0:T(1024)(128)(4,1)} %bitcast.344), calls=%async_computation.1 | async-start | bytes 4194304
  498.6 18.5 %collective-permute-start.14 = (bf16[128,1536]{1,0:T(8,128)(2,1)S(1)}, bf16[128,1536]{1,0:T(8,128)(2,1)S(1)}, u32[]{:S(2)}, u32[]{:S(2)}) collective-permute-start(bf16[128,1536]{1,0:T(8,128)(2,1)S(1)} %convert_element_type.522), channel_id=1, source_target_pairs={{0,2},{1,3},{2,0},{3,1},{4,6},{5,7},{6,4},{7,5},{8,10},{9,11},{10,... | collective-permute-start | bytes 1179656 | tf_op jit(solution)/shard_map/ppermute | solution.py:218
  500.3 19.3 %collective-permute-start.15 = (bf16[128,1536]{1,0:T(8,128)(2,1)S(1)}, bf16[128,1536]{1,0:T(8,128)(2,1)S(1)}, u32[]{:S(2)}, u32[]{:S(2)}) collective-permute-start(bf16[128,1536]{1,0:T(8,128)(2,1)S(1)} %convert_element_type.522), channel_id=1, source_target_pairs={{0,1},{1,0},{2,3},{3,2},{4,5},{5,4},{6,7},{7,6},{8,9},{9,8},{10,11... | collective-permute-start | bytes 1179656 | tf_op jit(solution)/shard_map/ppermute | solution.py:218
  517.1 2.6 collective-permute-start.16
  517.7 51.2 %copy-start.73 = (bf16[2,2,2,64,1024]{4,3,2,1,0:T(8,128)(2,1)}, bf16[2,2,2,64,1024]{4,3,2,1,0:T(8,128)(2,1)S(1)}, u32[]{:S(2)}) copy-start(bf16[2,2,2,64,1024]{4,3,2,1,0:T(8,128)(2,1)S(1)} %collective-permute-done.17) | copy-start | bytes 3145732
  519.8 24.3 %collective-permute-start.21 = (bf16[2,2,64,1024]{3,2,1,0:T(8,128)(2,1)S(1)}, bf16[2,2,64,1024]{3,2,1,0:T(8,128)(2,1)S(1)}, u32[]{:S(2)}, u32[]{:S(2)}) collective-permute-start(bf16[2,2,64,1024]{3,2,1,0:T(8,128)(2,1)S(1)} %fusion.18), channel_id=1, source_target_pairs={{0,4},{4,0},{8,12},{12,8},{16,20},{20,16},{24,28},{28,24},{1,5},{5... | collective-permute-start | bytes 1572872 | tf_op jit(solution)/shard_map/ppermute | solution.py:218
  523.2 77.1 %copy-start.55 = (bf16[1536,1024]{1,0:T(8,128)(2,1)}, bf16[1536,1024]{1,0:T(8,128)(2,1)S(1)}, u32[]{:S(2)}) copy-start(bf16[1536,1024]{1,0:T(8,128)(2,1)S(1)} %convolution_convert_fusion.7) | copy-start | bytes 9437188
  536.0 9.5 %collective-permute-start.18 = (bf16[128,1536]{1,0:T(8,128)(2,1)S(1)}, bf16[128,1536]{1,0:T(8,128)(2,1)S(1)}, u32[]{:S(2)}, u32[]{:S(2)}) collective-permute-start(bf16[128,1536]{1,0:T(8,128)(2,1)S(1)} %get-tuple-element.328), channel_id=1, source_target_pairs={{0,1},{1,0},{2,3},{3,2},{4,5},{5,4},{6,7},{7,6},{8,9},{9,8},{10,11... | collective-permute-start | bytes 1179656 | tf_op jit(solution)/shard_map/ppermute | solution.py:218
  536.2 4.0 collective-permute-start.19
  540.4 11.3 %collective-permute-start.20 = (bf16[128,1536]{1,0:T(8,128)(2,1)S(1)}, bf16[128,1536]{1,0:T(8,128)(2,1)S(1)}, u32[]{:S(2)}, u32[]{:S(2)}) collective-permute-start(bf16[128,1536]{1,0:T(8,128)(2,1)S(1)} %add_convert_fusion.2), channel_id=1, source_target_pairs={{0,2},{1,3},{2,0},{3,1},{4,6},{5,7},{6,4},{7,5},{8,10},{9,11},{10,... | collective-permute-start | bytes 1179656 | tf_op jit(solution)/shard_map/ppermute | solution.py:218
  544.1 24.9 %copy-start.80 = (bf16[2,2,64,1024]{3,2,1,0:T(8,128)(2,1)}, bf16[2,2,64,1024]{3,2,1,0:T(8,128)(2,1)S(1)}, u32[]{:S(2)}) copy-start(bf16[2,2,64,1024]{3,2,1,0:T(8,128)(2,1)S(1)} %collective-permute-done.21) | copy-start | bytes 1572868
  552.3 10.5 %collective-permute-start.22 = (bf16[128,1536]{1,0:T(8,128)(2,1)S(1)}, bf16[128,1536]{1,0:T(8,128)(2,1)S(1)}, u32[]{:S(2)}, u32[]{:S(2)}) collective-permute-start(bf16[128,1536]{1,0:T(8,128)(2,1)S(1)} %get-tuple-element.310), channel_id=1, source_target_pairs={{0,2},{1,3},{2,0},{3,1},{4,6},{5,7},{6,4},{7,5},{8,10},{9,11},{10,... | collective-permute-start | bytes 1179656 | tf_op jit(solution)/shard_map/ppermute | solution.py:218
  555.6 13.3 %collective-permute-start.25 = (bf16[2,64,1024]{2,1,0:T(8,128)(2,1)S(1)}, bf16[2,64,1024]{2,1,0:T(8,128)(2,1)S(1)}, u32[]{:S(2)}, u32[]{:S(2)}) collective-permute-start(bf16[2,64,1024]{2,1,0:T(8,128)(2,1)S(1)} %fusion.44), channel_id=1, source_target_pairs={{0,16},{4,20},{8,24},{12,28},{16,0},{20,4},{24,8},{28,12},{1,17},{... | collective-permute-start | bytes 786440 | tf_op jit(solution)/shard_map/ppermute | solution.py:218
  555.7 14.4 %collective-permute-start.23 = (bf16[128,1536]{1,0:T(8,128)(2,1)S(1)}, bf16[128,1536]{1,0:T(8,128)(2,1)S(1)}, u32[]{:S(2)}, u32[]{:S(2)}) collective-permute-start(bf16[128,1536]{1,0:T(8,128)(2,1)S(1)} %get-tuple-element.310), channel_id=1, source_target_pairs={{0,1},{1,0},{2,3},{3,2},{4,5},{5,4},{6,7},{7,6},{8,9},{9,8},{10,11... | collective-permute-start | bytes 1179656 | tf_op jit(solution)/shard_map/ppermute | solution.py:218
  562.8 7.3 collective-permute-start.24
  563.0 37.3 %collective-permute-start.30 = (bf16[2,2,192,1024]{3,2,1,0:T(8,128)(2,1)S(1)}, bf16[2,2,192,1024]{3,2,1,0:T(8,128)(2,1)S(1)}, u32[]{:S(2)}, u32[]{:S(2)}) collective-permute-start(bf16[2,2,192,1024]{3,2,1,0:T(8,128)(2,1)S(1)} %dynamic-slice_bitcast_fusion.4), channel_id=1, source_target_pairs={{0,4},{4,0},{8,12},{12,8},{16,20},{20,16},{24,28},{28,24},{1,5},{5... | collective-permute-start | bytes 4718600 | tf_op jit(solution)/shard_map/ppermute | solution.py:218
  583.5 18.2 %collective-permute-start.27 = (bf16[128,1536]{1,0:T(8,128)(2,1)S(1)}, bf16[128,1536]{1,0:T(8,128)(2,1)S(1)}, u32[]{:S(2)}, u32[]{:S(2)}) collective-permute-start(bf16[128,1536]{1,0:T(8,128)(2,1)S(1)} %get-tuple-element.327), channel_id=1, source_target_pairs={{0,1},{1,0},{2,3},{3,2},{4,5},{5,4},{6,7},{7,6},{8,9},{9,8},{10,11... | collective-permute-start | bytes 1179656 | tf_op jit(solution)/shard_map/ppermute | solution.py:218
  592.8 96.4 %collective-permute-start.31 = (bf16[2,2,192,1024]{3,2,1,0:T(8,128)(2,1)}, bf16[2,2,192,1024]{3,2,1,0:T(8,128)(2,1)}, u32[]{:S(2)}, u32[]{:S(2)}) collective-permute-start(bf16[2,2,192,1024]{3,2,1,0:T(8,128)(2,1)} %dynamic-slice_bitcast_fusion.3), channel_id=1, source_target_pairs={{0,4},{4,0},{8,12},{12,8},{16,20},{20,16},{24,28},{28,24},{1,5},{5... | collective-permute-start | bytes 4718600 | tf_op jit(solution)/shard_map/ppermute | solution.py:218
  593.8 115.8 %collective-permute-start.35 = (bf16[2,2,192,1024]{3,2,1,0:T(8,128)(2,1)}, bf16[2,2,192,1024]{3,2,1,0:T(8,128)(2,1)}, u32[]{:S(2)}, u32[]{:S(2)}) collective-permute-start(bf16[2,2,192,1024]{3,2,1,0:T(8,128)(2,1)} %dynamic-slice_bitcast_fusion.2), channel_id=1, source_target_pairs={{0,4},{4,0},{8,12},{12,8},{16,20},{20,16},{24,28},{28,24},{1,5},{5... | collective-permute-start | bytes 4718600 | tf_op jit(solution)/shard_map/ppermute | solution.py:218
  601.7 11.9 %collective-permute-start.29 = (bf16[64,1024]{1,0:T(8,128)(2,1)S(1)}, bf16[64,1024]{1,0:T(8,128)(2,1)S(1)}, u32[]{:S(2)}, u32[]{:S(2)}) collective-permute-start(bf16[64,1024]{1,0:T(8,128)(2,1)S(1)} %fusion.69), channel_id=1, source_target_pairs={{0,8},{4,12},{8,0},{12,4},{16,24},{20,28},{24,16},{28,20},{1,9},{5... | collective-permute-start | bytes 393224 | tf_op jit(solution)/shard_map/ppermute | solution.py:218
  601.7 5.8 collective-permute-start.26
  601.8 11.6 %collective-permute-start.28 = (bf16[128,1536]{1,0:T(8,128)(2,1)S(1)}, bf16[128,1536]{1,0:T(8,128)(2,1)S(1)}, u32[]{:S(2)}, u32[]{:S(2)}) collective-permute-start(bf16[128,1536]{1,0:T(8,128)(2,1)S(1)} %add_convert_fusion.1), channel_id=1, source_target_pairs={{0,2},{1,3},{2,0},{3,1},{4,6},{5,7},{6,4},{7,5},{8,10},{9,11},{10,... | collective-permute-start | bytes 1179656 | tf_op jit(solution)/shard_map/ppermute | solution.py:218
  619.8 69.4 %collective-permute-start.32 = (bf16[2,2,2,32,4480]{4,3,2,1,0:T(8,128)(2,1)}, bf16[2,2,2,32,4480]{4,3,2,1,0:T(8,128)(2,1)}, u32[]{:S(2)}, u32[]{:S(2)}) collective-permute-start(bf16[2,2,2,32,4480]{4,3,2,1,0:T(8,128)(2,1)} %fusion.1), channel_id=1, source_target_pairs={{0,2},{1,3},{2,0},{3,1},{4,6},{5,7},{6,4},{7,5},{8,10},{9,11},{10,... | collective-permute-start | bytes 6881288 | tf_op jit(solution)/shard_map/ppermute | solution.py:218
  639.5 47.9 %collective-permute-start.34 = (bf16[2,192,1024]{2,1,0:T(8,128)(2,1)}, bf16[2,192,1024]{2,1,0:T(8,128)(2,1)}, u32[]{:S(2)}, u32[]{:S(2)}) collective-permute-start(bf16[2,192,1024]{2,1,0:T(8,128)(2,1)} %fusion.14), channel_id=1, source_target_pairs={{0,16},{4,20},{8,24},{12,28},{16,0},{20,4},{24,8},{28,12},{1,17},{... | collective-permute-start | bytes 2359304 | tf_op jit(solution)/shard_map/ppermute | solution.py:218
  641.9 47.3 %collective-permute-start.33 = (bf16[2,2,2,2,32,3072]{5,4,3,2,1,0:T(8,128)(2,1)}, bf16[2,2,2,2,32,3072]{5,4,3,2,1,0:T(8,128)(2,1)}, u32[]{:S(2)}, u32[]{:S(2)}) collective-permute-start(bf16[2,2,2,2,32,3072]{5,4,3,2,1,0:T(8,128)(2,1)} %dynamic-slice_bitcast_fusion), channel_id=1, source_target_pairs={{0,1},{1,0},{2,3},{3,2},{4,5},{5,4},{6,7},{7,6},{8,9},{9,8},{10,11... | collective-permute-start | bytes 9437192 | tf_op jit(solution)/shard_map/ppermute | solution.py:218
  641.9 45.3 %copy-start.111 = (bf16[1,2048]{1,0:T(2,128)(2,1)S(1)}, bf16[1,2048]{1,0:T(2,128)(2,1)}, u32[]{:S(2)}) copy-start(bf16[1,2048]{1,0:T(2,128)(2,1)} %stack.111) | copy-start | bytes 12292
  641.9 45.4 %copy-start.105 = (bf16[4,2304]{1,0:T(4,128)(2,1)S(1)}, bf16[4,2304]{1,0:T(4,128)(2,1)}, u32[]{:S(2)}) copy-start(bf16[4,2304]{1,0:T(4,128)(2,1)} %reduce_sum.460) | copy-start | bytes 55300
  687.5 13.2 %slice-start.6 = ((s8[4587520]{0:T(1024)(128)(4,1)}), s8[4194304]{0:T(1024)(128)(4,1)S(1)}, s32[]{:S(2)}) async-start(s8[4587520]{0:T(1024)(128)(4,1)} %bitcast.431), calls=%async_computation.6 | async-start | bytes 8388608
  689.1 11.6 %collective-permute-start.36 = (bf16[192,1024]{1,0:T(8,128)(2,1)S(1)}, bf16[192,1024]{1,0:T(8,128)(2,1)S(1)}, u32[]{:S(2)}, u32[]{:S(2)}) collective-permute-start(bf16[192,1024]{1,0:T(8,128)(2,1)S(1)} %fusion.37), channel_id=1, source_target_pairs={{0,8},{4,12},{8,0},{12,4},{16,24},{20,28},{24,16},{28,20},{1,9},{5... | collective-permute-start | bytes 1179656 | tf_op jit(solution)/shard_map/ppermute | solution.py:218
  (147 other events, 678.4 us)

commit v6 on v5

--- a/solution.py
+++ b/solution.py
@@ -992,7 +992,7 @@
 
 
 FORWARD_UNROLL = 4
-BACKWARD_UNROLL = 2
+BACKWARD_UNROLL = 4
 PROJ_WIDE = 2 * INNER + 2 * STATE + 128
 
 
@@ -1851,7 +1851,7 @@
     grad_routed = to_low(jnp.concatenate([grad_query, grad_key, slope_shortcut], axis=1))
     grad_routed = after(grad_routed, [gradient_merged])
     grad_route = to_low(product_tn(encoded_low, grad_routed))
-    job_route = conductor.add(Summing(grad_route, True))
+    job_route = Summing(grad_route, True)
     grad_routed = conductor.tick(after(grad_routed, [grad_route]), 7.0)
     grad_embedded, grad_block_enc, grad_small_enc, jobs_enc = mixer_backward(
         conductor,
@@ -1862,7 +1862,9 @@
         full_out[0],
         layer_smalls[0],
     )
-    grad_table_in = jnp.dot(onehot_in.astype(jnp.float32).T, grad_embedded, precision=deepest_tier)
+    embedded_high = to_low(grad_embedded)
+    embedded_rest = to_low(grad_embedded - embedded_high.astype(jnp.float32))
+    grad_table_in = product_tn(onehot_in, embedded_high) + product_tn(onehot_in, embedded_rest)
     grad_small = jnp.concatenate(
         [
             piece.reshape(-1)

time: 935 us -> 929 us (level)
    convert_element_type x22 -> x21, other arithmetic: 26.7 us -> 21 us  [to_low(): return value_entries.astype(jnp.bfloat16)]
    dot_general x11 -> x13, matrix products: 44 us -> 46 us  [product_tn(): lax.dot_general(left, right, (((0,), (0,)), ((), ())), preferred_element_...]
    unnamed x355 -> x361, local copies, waits for them, and re-layouts: 22.3 us -> 23.5 us
  transfers between devices with their start and end apart: 37 -> 37, of which waited for: 15 -> 15; matrix products, arithmetic and copies ran while one was open for 13% -> 14% of each run, Pallas kernels for 10% -> 10%
where the time goes in v6:
time: 929 us; the launch traced here: 921 us
  Pallas kernels  543 us (58%)
  matrix products  148 us (16%)
  waiting for transfers between devices  86.7 us (9%)
  other arithmetic  60.3 us (6%)
  local copies, waits for them, and re-layouts  49.2 us (5%)
  starting transfers between devices  25.3 us (3%)
    pallas_call x1, Pallas kernels, spread_whole(): pl.pallas_call(partial(spread_kernel, plan, jobs, depth_z), out_shape=tup...  228 us
    pallas_call x1, Pallas kernels, sum_whole(): pl.pallas_call(partial(sum_kernel, plan, kinds, sources, depth_z), out_sh...  173 us
    ppermute x37, waiting for transfers between devices, swap(): lax.ppermute(value_entries, axis, [(place, place ^ mask) for place in ran...  86.7 us
    pallas_call x2, Pallas kernels, middle_backward(): pl.pallas_call(middle_slope_kernel, grid=(chunks,), out_shape=(jax.ShapeD...  81.4 us
    dot_general x11, matrix products, matmul_apply(): return jnp.dot(left, right, preferred_element_type=jnp.float32)  48.9 us
    dot_general x13, matrix products, product_tn(): lax.dot_general(left, right, (((0,), (0,)), ((), ())), preferred_element_...  46 us
    pallas_call x2, Pallas kernels, middle_forward(): pl.pallas_call(middle_kernel, grid=(chunks,), out_shape=(jax.ShapeDtypeSt...  43.7 us
    dot_general x10, matrix products, product_nt(): lax.dot_general(left, right, (((1,), (1,)), ((), ())), preferred_element_...  42.1 us
  transfers between devices with their start and end apart: 37, of which 15 were waited for; matrix products, arithmetic and copies ran while one was open for 14% of the time, Pallas kernels for 10%

profile of v6, /device:TPU:0, one launch (start us, length us, event | category | flops | bytes accessed | tf_op | source)
XLA Modules:
  0.0 920.5 jit_solution(15599350810154725307)
XLA Ops:
  13.8 227.9 %shard_map.526 = (bf16[4,2,2,2,16,1152]{5,4,3,2,1,0:T(8,128)(2,1)}, bf16[4,2,2,2,32,4480]{5,4,3,2,1,0:T(8,128)(2,1)}, bf16[4,2,2,2,64,1024]{5,4,3,2,1,0:T(8,128)...) custom-call(bf16[16,1152]{1,0:T(8,128)(2,1)} %pad_maximum_fusion.11., ...), custom_call_target="tpu_custom_call" | custom-call | tf_op jit(solution)/shard_map/pallas_call | solution.py:593
  246.8 11.4 %fusion.125.projected.earlier = f32[512,4480]{1,0:T(8,128)} fusion(bf16[1024,4480]{1,0:T(8,128)(2,1)} %bitcast.408, f32[512,1024]{1,0:T(8,128)S(1)} %get-tuple-element.362, f32[1024]{0:T(1024)S(1)} %get-tuple-element.342, f32[512]{0:T(512)S(1)} %fusion.106), kind=kOutput, calls=%fused_computation.355 | convolution fusion | flops 4699193344 | bytes 20453376 | tf_op jit(solution)/shard_map/dot_general | solution.py:201
  258.2 22.0 %shard_map.527 = (bf16[512,2048]{1,0:T(8,128)(2,1)S(1)}, f32[512,2048]{1,0:T(8,128)}, f32[4,128,2048]{2,1,0:T(8,128)}) custom-call(f32[512,4480]{1,0:T(8,128)} %fusion.125.projected.earlier, f32[4,2304]{1,0:T(4,128)S(1)} %squeeze.123.taps, f32[1,2048]{1,0:T(1,128)S(1)} %bitcast.335, f32[2,32]{1,0:T(2,128)S(1)} %get-tuple-element.373.decay, ...), custom_call_target="tpu_custom_call" | custom-call | flops 20000000000 | bytes 20000000 | tf_op jit(solution)/shard_map/pallas_call | solution.py:1376
  280.3 5.3 convolution_add_fusion.2
  288.9 3.5 fusion.57
  292.9 2.2 copy-done.22
  300.6 2.2 convolution_convert_fusion.10.triple
  302.9 5.2 shard_map.528
  312.9 9.5 %collective-permute-done.5 = bf16[128,1536]{1,0:T(8,128)(2,1)S(1)} collective-permute-done((bf16[128,1536]{1,0:T(8,128)(2,1)S(1)}, bf16[128,1536]{1,0:T(8,128)(2,1)S(1)}, u32[]{:S(2)}, u32[]{:S(2)}) %collective-permute-start.5) | collective-permute-done | bytes 393248 | tf_op jit(solution)/shard_map/ppermute | solution.py:218
  324.6 8.7 collective-permute-done.6
  335.1 3.5 fusion.127
  342.4 1.8 convolution_convert_fusion.12
  350.3 9.3 %collective-permute-done.11 = bf16[128,1536]{1,0:T(8,128)(2,1)S(1)} collective-permute-done((bf16[128,1536]{1,0:T(8,128)(2,1)S(1)}, bf16[128,1536]{1,0:T(8,128)(2,1)S(1)}, u32[]{:S(2)}, u32[]{:S(2)}) %collective-permute-start.11) | collective-permute-done | bytes 393248 | tf_op jit(solution)/shard_map/ppermute | solution.py:218
  361.8 4.2 multiply_reduce_fusion.10
  365.9 11.9 %fusion.126.projected.earlier = f32[512,4480]{1,0:T(8,128)} fusion(bf16[1024,4480]{1,0:T(8,128)(2,1)} %bitcast.410, f32[512,1024]{1,0:T(8,128)S(1)} %get-tuple-element.311, f32[1024]{0:T(1024)S(1)} %get-tuple-element.341, f32[512]{0:T(512)S(1)} %fusion.107), kind=kOutput, calls=%fused_computation.356 | convolution fusion | flops 4699193344 | bytes 20453376 | tf_op jit(solution)/shard_map/dot_general | solution.py:201
  377.8 21.7 %shard_map.529 = (bf16[512,2048]{1,0:T(8,128)(2,1)S(1)}, f32[512,2048]{1,0:T(8,128)}, f32[4,128,2048]{2,1,0:T(8,128)}) custom-call(f32[512,4480]{1,0:T(8,128)} %fusion.126.projected.earlier, f32[4,2304]{1,0:T(4,128)S(1)} %slice.397.taps, f32[1,2048]{1,0:T(1,128)S(1)} %bitcast.339, f32[2,32]{1,0:T(2,128)S(1)} %get-tuple-element.374.decay, ...), custom_call_target="tpu_custom_call" | custom-call | flops 20000000000 | bytes 20000000 | tf_op jit(solution)/shard_map/pallas_call | solution.py:1376
  399.6 2.4 multiply_reduce_fusion.9
  402.7 2.0 multiply_reduce_fusion
  406.9 4.3 fusion.52.slope
  411.2 2.4 convolution_convert_fusion.8
  418.0 40.7 %shard_map.530 = (bf16[512,4480]{1,0:T(8,128)(2,1)}, f32[4,8,2304]{2,1,0:T(8,128)S(1)}, f32[8,2048]{1,0:T(8,128)S(1)}, f32[8,2048]{1,0:T(8,128)S(1)}, f32[2,8,32]{2,1,0:T(8,128)S(1)}) custom-call(f32[512,4480]{1,0:T(8,128)} %fusion.126.projected.earlier, f32[512,4480]{1,0:T(8,128)} %fusion.126.projected.earlier, f32[512,2048]{1,0:T(8,128)S(1)} %copy-done.21, ...), custom_call_target="tpu_custom_call" | custom-call | flops 49999998976 | bytes 30000000 | tf_op jit(solution)/shard_map/pallas_call | solution.py:1429
  458.8 3.1 fusion.7
  461.9 7.8 convolution_convert_fusion.1
  469.8 2.7 copy_bitcast_fusion
  472.4 2.2 copy-done.23
  478.0 4.0 convolution_convert_fusion.15
  483.4 9.4 %multiply_reduce_fusion.1 = (bf16[1024]{0:T(1024)(128)(2,1)S(1)}, f32[512]{0:T(512)S(1)}, f32[512,1024]{1,0:T(8,128)S(1)}) fusion(f32[512,1024]{1,0:T(8,128)S(1)} %copy-done.37, f32[512]{0:T(512)S(1)} %fusion.107, f32[1024]{0:T(1024)S(1)} %get-tuple-element.341, bf16[512,4480]{1,0:T(8,128)(2,1)} %get-tuple-element.165, bf16[1024,4480]{1,0:T(8,128)(2,1)} %bitcast.411), kind=kOutput, calls=%fused_computation.38 | convolution fusion | flops 4700764672 | bytes 17967104 | tf_op jit(solution)/shard_map/dot_general | solution.py:211
  493.8 2.0 fusion.8
  499.4 16.5 %collective-permute-done.14 = bf16[128,1536]{1,0:T(8,128)(2,1)S(1)} collective-permute-done((bf16[128,1536]{1,0:T(8,128)(2,1)S(1)}, bf16[128,1536]{1,0:T(8,128)(2,1)S(1)}, u32[]{:S(2)}, u32[]{:S(2)}) %collective-permute-start.14) | collective-permute-done | bytes 393248 | tf_op jit(solution)/shard_map/ppermute | solution.py:218
  516.7 1.9 fusion.19
  520.2 1.8 convolution_convert_fusion.7
  522.4 5.2 fusion.78
  528.0 6.7 convolution_convert_fusion.11
  535.3 1.8 convolution_convert_fusion.5
  537.1 1.8 convolution_convert_fusion.6
  544.2 6.2 collective-permute-done.20
  553.9 7.6 collective-permute-done.22
  563.4 3.7 collective-permute-done.25
  569.5 7.9 shard_map.531
  579.5 2.2 convolution_convert_fusion.9
  581.8 4.3 fusion
  586.2 5.0 copy.97
  593.2 5.8 collective-permute-done.30
  603.1 4.0 convolution_convert_fusion.2
  607.1 5.9 collective-permute-done.28
  613.9 1.8 fusion.42
  615.8 5.6 convolution_convert_fusion.3
  621.4 3.5 convolution_add_fusion
  624.9 4.5 fusion.49.slope
  629.5 4.5 convolution_convert_fusion.4
  635.6 2.4 collective-permute-start.33
  638.9 40.6 %shard_map.532 = (bf16[512,4480]{1,0:T(8,128)(2,1)}, f32[4,8,2304]{2,1,0:T(8,128)S(1)}, f32[8,2048]{1,0:T(8,128)S(1)}, f32[8,2048]{1,0:T(8,128)S(1)}, f32[2,8,32]{2,1,0:T(8,128)S(1)}) custom-call(f32[512,4480]{1,0:T(8,128)} %fusion.125.projected.earlier, f32[512,4480]{1,0:T(8,128)} %fusion.125.projected.earlier, f32[512,2048]{1,0:T(8,128)S(1)} %copy-done.20, ...), custom_call_target="tpu_custom_call" | custom-call | flops 49999998976 | bytes 30000000 | tf_op jit(solution)/shard_map/pallas_call | solution.py:1429
  681.9 7.3 collective-permute-done.32
  689.3 10.0 %convolution_convert_fusion = bf16[1024,4480]{1,0:T(8,128)(2,1)} fusion(bf16[512,4480]{1,0:T(8,128)(2,1)} %get-tuple-element.197, f32[512,1024]{1,0:T(8,128)S(1)} %copy-done.33, f32[1024]{0:T(1024)S(1)} %copy-done.130, f32[512]{0:T(512)S(1)} %copy-done.132), kind=kOutput, calls=%fused_computation | convolution fusion | flops 4703780864 | bytes 15865856 | tf_op jit(solution)/shard_map/dot_general | solution.py:205
  699.3 8.0 multiply_reduce_fusion.3
  708.3 3.0 multiply_reduce_fusion.15
  711.3 1.8 multiply_reduce_fusion.23
  717.7 2.0 pad_maximum_fusion.5.refs_3_
  719.8 172.7 %shard_map.533 = (f32[32,3072]{1,0:T(8,128)}, f32[32,4480]{1,0:T(8,128)}, f32[64,1024]{1,0:T(8,128)}, f32[16,1152]{1,0:T(8,128)}, f32[192,1152]{1,0:T(8,128)}, /...) custom-call(bf16[4,2,2,2,32,3072]{5,4,3,2,1,0:T(8,128)(2,1)} %bitcas, ...), custom_call_target="tpu_custom_call" | custom-call | tf_op jit(solution)/shard_map/pallas_call | solution.py:910
  900.1 2.3 multiply_subtract_fusion.5
  903.7 1.8 multiply_subtract_fusion.2
  906.2 1.9 multiply_subtract_fusion.1
  910.7 2.3 multiply_subtract_fusion
  914.7 4.2 shard_map.534
  (607 shorter events, 110.7 us)
Async XLA Ops:
  244.9 42.1 %copy-start.99 = (f32[1536]{0:T(1024)}, f32[1536]{0:T(1024)S(1)}, u32[]{:S(2)}) copy-start(f32[1536]{0:T(1024)S(1)} %get-tuple-element.338) | copy-start | bytes 18436
  244.9 77.8 %copy-start.101 = (f32[1536]{0:T(1024)}, f32[1536]{0:T(1024)S(1)}, u32[]{:S(2)}) copy-start(f32[1536]{0:T(1024)S(1)} %get-tuple-element.337) | copy-start | bytes 18436
  245.0 64.5 %copy-start.114 = (f32[1,512]{1,0:T(1,128)}, f32[1,512]{1,0:T(1,128)S(1)}, u32[]{:S(2)}) copy-start(f32[1,512]{1,0:T(1,128)S(1)} %convert_element_type.486) | copy-start | bytes 6148
  246.2 34.0 %copy-start.32 = (f32[512,1024]{1,0:T(8,128)}, f32[512,1024]{1,0:T(8,128)S(1)}, u32[]{:S(2)}) copy-start(f32[512,1024]{1,0:T(8,128)S(1)} %get-tuple-element.362) | copy-start | bytes 6291460
  246.3 76.1 %copy-start.93 = (f32[1536]{0:T(1024)}, f32[1536]{0:T(1024)S(1)}, u32[]{:S(2)}) copy-start(f32[1536]{0:T(1024)S(1)} %pad.101.clone) | copy-start | bytes 18436
  246.8 42.1 %slice-start.2 = ((s8[6291456]{0:T(1024)(128)(4,1)}), s8[4194304]{0:T(1024)(128)(4,1)S(1)}, s32[]{:S(2)}) async-start(s8[6291456]{0:T(1024)(128)(4,1)} %bitcast.412), calls=%async_computation.2 | async-start | bytes 8388608
  258.2 30.7 %slice-start.3 = ((s8[6291456]{0:T(1024)(128)(4,1)}), s8[2097152]{0:T(1024)(128)(4,1)S(1)}, s32[]{:S(2)}) async-start(s8[6291456]{0:T(1024)(128)(4,1)} %bitcast.412), calls=%async_computation.3 | async-start | bytes 4194304
  286.9 35.5 %copy-start.26 = (f32[128,1024]{1,0:T(8,128)}, f32[128,1024]{1,0:T(8,128)S(1)}, u32[]{:S(2)}) copy-start(f32[128,1024]{1,0:T(8,128)S(1)} %fusion.62) | copy-start | bytes 1572868
  287.3 11.7 %collective-permute-start.1 = (bf16[128,1536]{1,0:T(8,128)(2,1)S(1)}, bf16[128,1536]{1,0:T(8,128)(2,1)S(1)}, u32[]{:S(2)}, u32[]{:S(2)}) collective-permute-start(bf16[128,1536]{1,0:T(8,128)(2,1)S(1)} %multiply_convert_fusion.5), channel_id=1, source_target_pairs={{0,1},{1,0},{2,3},{3,2},{4,5},{5,4},{6,7},{7,6},{8,9},{9,8},{10,11... | collective-permute-start | bytes 1179656 | tf_op jit(solution)/shard_map/ppermute | solution.py:218
  287.3 11.5 %collective-permute-start = (bf16[128,1536]{1,0:T(8,128)(2,1)S(1)}, bf16[128,1536]{1,0:T(8,128)(2,1)S(1)}, u32[]{:S(2)}, u32[]{:S(2)}) collective-permute-start(bf16[128,1536]{1,0:T(8,128)(2,1)S(1)} %multiply_convert_fusion.5), channel_id=1, source_target_pairs={{0,2},{1,3},{2,0},{3,1},{4,6},{5,7},{6,4},{7,5},{8,10},{9,11},{10,... | collective-permute-start | bytes 1179656 | tf_op jit(solution)/shard_map/ppermute | solution.py:218
  298.9 1.7 collective-permute-start.2
  302.9 32.2 %slice-start.6 = ((s8[6291456]{0:T(1024)(128)(4,1)}), s8[4194304]{0:T(1024)(128)(4,1)S(1)}, s32[]{:S(2)}) async-start(s8[6291456]{0:T(1024)(128)(4,1)} %bitcast.419), calls=%async_computation.6 | async-start | bytes 8388608
  308.2 26.9 %slice-start.7 = ((s8[6291456]{0:T(1024)(128)(4,1)}), s8[2097152]{0:T(1024)(128)(4,1)S(1)}, s32[]{:S(2)}) async-start(s8[6291456]{0:T(1024)(128)(4,1)} %bitcast.419), calls=%async_computation.7 | async-start | bytes 4194304
  309.3 1.8 collective-permute-start.4
  309.9 3.0 collective-permute-start.3
  311.2 11.2 %collective-permute-start.5 = (bf16[128,1536]{1,0:T(8,128)(2,1)S(1)}, bf16[128,1536]{1,0:T(8,128)(2,1)S(1)}, u32[]{:S(2)}, u32[]{:S(2)}) collective-permute-start(bf16[128,1536]{1,0:T(8,128)(2,1)S(1)} %add_convert_fusion.4), channel_id=1, source_target_pairs={{0,2},{1,3},{2,0},{3,1},{4,6},{5,7},{6,4},{7,5},{8,10},{9,11},{10,... | collective-permute-start | bytes 1179656 | tf_op jit(solution)/shard_map/ppermute | solution.py:218
  322.7 15.9 %copy-start.147 = (f32[128]{0:T(128)}, f32[128]{0:T(128)S(1)}, u32[]{:S(2)}) copy-start(f32[128]{0:T(128)S(1)} %get-tuple-element.314) | copy-start | bytes 1540
  322.7 36.9 %copy-start.24 = (f32[128,1536]{1,0:T(8,128)}, f32[128,1536]{1,0:T(8,128)S(1)}, u32[]{:S(2)}) copy-start(f32[128,1536]{1,0:T(8,128)S(1)} %get-tuple-element.315) | copy-start | bytes 2359300
  322.8 15.8 %copy-start.135 = (f32[128]{0:T(128)}, f32[128]{0:T(128)S(1)}, u32[]{:S(2)}) copy-start(f32[128]{0:T(128)S(1)} %fusion.111) | copy-start | bytes 1540
  322.9 10.4 %collective-permute-start.6 = (bf16[128,1536]{1,0:T(8,128)(2,1)S(1)}, bf16[128,1536]{1,0:T(8,128)(2,1)S(1)}, u32[]{:S(2)}, u32[]{:S(2)}) collective-permute-start(bf16[128,1536]{1,0:T(8,128)(2,1)S(1)} %multiply_convert_fusion.4), channel_id=1, source_target_pairs={{0,2},{1,3},{2,0},{3,1},{4,6},{5,7},{6,4},{7,5},{8,10},{9,11},{10,... | collective-permute-start | bytes 1179656 | tf_op jit(solution)/shard_map/ppermute | solution.py:218
  324.6 8.8 collective-permute-start.7
  333.3 1.7 collective-permute-start.8
  345.5 1.8 collective-permute-start.10
  346.6 3.7 collective-permute-start.9
  348.4 11.2 %collective-permute-start.11 = (bf16[128,1536]{1,0:T(8,128)(2,1)S(1)}, bf16[128,1536]{1,0:T(8,128)(2,1)S(1)}, u32[]{:S(2)}, u32[]{:S(2)}) collective-permute-start(bf16[128,1536]{1,0:T(8,128)(2,1)S(1)} %add_convert_fusion.3), channel_id=1, source_target_pairs={{0,2},{1,3},{2,0},{3,1},{4,6},{5,7},{6,4},{7,5},{8,10},{9,11},{10,... | collective-permute-start | bytes 1179656 | tf_op jit(solution)/shard_map/ppermute | solution.py:218
  365.9 33.6 %copy-start.35 = (f32[512,1024]{1,0:T(8,128)}, f32[512,1024]{1,0:T(8,128)S(1)}, u32[]{:S(2)}) copy-start(f32[512,1024]{1,0:T(8,128)S(1)} %get-tuple-element.311) | copy-start | bytes 6291460
  377.8 21.7 %copy-start.150 = (bf16[4,2,2,2,64,1024]{5,4,3,2,1,0:T(8,128)(2,1)S(1)}, bf16[4,2,2,2,64,1024]{5,4,3,2,1,0:T(8,128)(2,1)}, u32[]{:S(2)}) copy-start(bf16[4,2,2,2,64,1024]{5,4,3,2,1,0:T(8,128)(2,1)} %get-tuple-element.155) | copy-start | bytes 12582916
  416.8 42.0 %collective-permute-start.12 = (bf16[2,2,2,2,64,1024]{5,4,3,2,1,0:T(8,128)(2,1)}, bf16[2,2,2,2,64,1024]{5,4,3,2,1,0:T(8,128)(2,1)}, u32[]{:S(2)}, u32[]{:S(2)}) collective-permute-start(bf16[2,2,2,2,64,1024]{5,4,3,2,1,0:T(8,128)(2,1)} %dynamic-slice_bitcast_fusion), channel_id=1, source_target_pairs={{0,1},{1,0},{2,3},{3,2},{4,5},{5,4},{6,7},{7,6},{8,9},{9,8},{10,11... | collective-permute-start | bytes 6291464 | tf_op jit(solution)/shard_map/ppermute | solution.py:218
  474.6 22.8 %collective-permute-start.13 = (bf16[2,2,2,2,32,4480]{5,4,2,1,0,3:T(8,128)(2,1)}, bf16[2,2,2,2,32,4480]{5,4,2,1,0,3:T(8,128)(2,1)}, u32[]{:S(2)}, u32[]{:S(2)}) collective-permute-start(bf16[2,2,2,2,32,4480]{5,4,2,1,0,3:T(8,128)(2,1)} %copy_bitcast_fusion), channel_id=1, source_target_pairs={{0,1},{1,0},{2,3},{3,2},{4,5},{5,4},{6,7},{7,6},{8,9},{9,8},{10,11... | collective-permute-start | bytes 13762568 | tf_op jit(solution)/shard_map/ppermute | solution.py:218
  481.9 34.7 %collective-permute-start.17 = (bf16[2,2,2,64,1024]{4,3,2,1,0:T(8,128)(2,1)S(1)}, bf16[2,2,2,64,1024]{4,3,2,1,0:T(8,128)(2,1)S(1)}, u32[]{:S(2)}, u32[]{:S(2)}) collective-permute-start(bf16[2,2,2,64,1024]{4,3,2,1,0:T(8,128)(2,1)S(1)} %copy-done.76), channel_id=1, source_target_pairs={{0,2},{1,3},{2,0},{3,1},{4,6},{5,7},{6,4},{7,5},{8,10},{9,11},{10,... | collective-permute-start | bytes 3145736 | tf_op jit(solution)/shard_map/ppermute | solution.py:218
  495.8 20.1 %slice-start = ((s8[6291456]{0:T(1024)(128)(4,1)}), s8[4194304]{0:T(1024)(128)(4,1)S(1)}, s32[]{:S(2)}) async-start(s8[6291456]{0:T(1024)(128)(4,1)} %bitcast.341), calls=%async_computation | async-start | bytes 8388608
  497.5 18.5 %slice-start.1 = ((s8[6291456]{0:T(1024)(128)(4,1)}), s8[2097152]{0:T(1024)(128)(4,1)S(1)}, s32[]{:S(2)}) async-start(s8[6291456]{0:T(1024)(128)(4,1)} %bitcast.341), calls=%async_computation.1 | async-start | bytes 4194304
  497.5 18.5 %collective-permute-start.14 = (bf16[128,1536]{1,0:T(8,128)(2,1)S(1)}, bf16[128,1536]{1,0:T(8,128)(2,1)S(1)}, u32[]{:S(2)}, u32[]{:S(2)}) collective-permute-start(bf16[128,1536]{1,0:T(8,128)(2,1)S(1)} %convert_element_type.518), channel_id=1, source_target_pairs={{0,2},{1,3},{2,0},{3,1},{4,6},{5,7},{6,4},{7,5},{8,10},{9,11},{10,... | collective-permute-start | bytes 1179656 | tf_op jit(solution)/shard_map/ppermute | solution.py:218
  499.1 19.4 %collective-permute-start.15 = (bf16[128,1536]{1,0:T(8,128)(2,1)S(1)}, bf16[128,1536]{1,0:T(8,128)(2,1)S(1)}, u32[]{:S(2)}, u32[]{:S(2)}) collective-permute-start(bf16[128,1536]{1,0:T(8,128)(2,1)S(1)} %convert_element_type.518), channel_id=1, source_target_pairs={{0,1},{1,0},{2,3},{3,2},{4,5},{5,4},{6,7},{7,6},{8,9},{9,8},{10,11... | collective-permute-start | bytes 1179656 | tf_op jit(solution)/shard_map/ppermute | solution.py:218
  515.9 2.6 collective-permute-start.16
  516.7 50.4 %copy-start.75 = (bf16[2,2,2,64,1024]{4,3,2,1,0:T(8,128)(2,1)}, bf16[2,2,2,64,1024]{4,3,2,1,0:T(8,128)(2,1)S(1)}, u32[]{:S(2)}) copy-start(bf16[2,2,2,64,1024]{4,3,2,1,0:T(8,128)(2,1)S(1)} %collective-permute-done.17) | copy-start | bytes 3145732
  518.7 24.1 %collective-permute-start.21 = (bf16[2,2,64,1024]{3,2,1,0:T(8,128)(2,1)S(1)}, bf16[2,2,64,1024]{3,2,1,0:T(8,128)(2,1)S(1)}, u32[]{:S(2)}, u32[]{:S(2)}) collective-permute-start(bf16[2,2,64,1024]{3,2,1,0:T(8,128)(2,1)S(1)} %fusion.19), channel_id=1, source_target_pairs={{0,4},{4,0},{8,12},{12,8},{16,20},{20,16},{24,28},{28,24},{1,5},{5... | collective-permute-start | bytes 1572872 | tf_op jit(solution)/shard_map/ppermute | solution.py:218
  522.1 76.9 %copy-start.55 = (bf16[1536,1024]{1,0:T(8,128)(2,1)}, bf16[1536,1024]{1,0:T(8,128)(2,1)S(1)}, u32[]{:S(2)}) copy-start(bf16[1536,1024]{1,0:T(8,128)(2,1)S(1)} %convolution_convert_fusion.7) | copy-start | bytes 9437188
  534.7 9.5 %collective-permute-start.18 = (bf16[128,1536]{1,0:T(8,128)(2,1)S(1)}, bf16[128,1536]{1,0:T(8,128)(2,1)S(1)}, u32[]{:S(2)}, u32[]{:S(2)}) collective-permute-start(bf16[128,1536]{1,0:T(8,128)(2,1)S(1)} %get-tuple-element.324), channel_id=1, source_target_pairs={{0,1},{1,0},{2,3},{3,2},{4,5},{5,4},{6,7},{7,6},{8,9},{9,8},{10,11... | collective-permute-start | bytes 1179656 | tf_op jit(solution)/shard_map/ppermute | solution.py:218
  535.0 4.0 collective-permute-start.19
  539.1 11.3 %collective-permute-start.20 = (bf16[128,1536]{1,0:T(8,128)(2,1)S(1)}, bf16[128,1536]{1,0:T(8,128)(2,1)S(1)}, u32[]{:S(2)}, u32[]{:S(2)}) collective-permute-start(bf16[128,1536]{1,0:T(8,128)(2,1)S(1)} %add_convert_fusion.2), channel_id=1, source_target_pairs={{0,2},{1,3},{2,0},{3,1},{4,6},{5,7},{6,4},{7,5},{8,10},{9,11},{10,... | collective-permute-start | bytes 1179656 | tf_op jit(solution)/shard_map/ppermute | solution.py:218
  542.8 24.3 %copy-start.82 = (bf16[2,2,64,1024]{3,2,1,0:T(8,128)(2,1)}, bf16[2,2,64,1024]{3,2,1,0:T(8,128)(2,1)S(1)}, u32[]{:S(2)}) copy-start(bf16[2,2,64,1024]{3,2,1,0:T(8,128)(2,1)S(1)} %collective-permute-done.21) | copy-start | bytes 1572868
  551.0 10.5 %collective-permute-start.22 = (bf16[128,1536]{1,0:T(8,128)(2,1)S(1)}, bf16[128,1536]{1,0:T(8,128)(2,1)S(1)}, u32[]{:S(2)}, u32[]{:S(2)}) collective-permute-start(bf16[128,1536]{1,0:T(8,128)(2,1)S(1)} %get-tuple-element.306), channel_id=1, source_target_pairs={{0,2},{1,3},{2,0},{3,1},{4,6},{5,7},{6,4},{7,5},{8,10},{9,11},{10,... | collective-permute-start | bytes 1179656 | tf_op jit(solution)/shard_map/ppermute | solution.py:218
  553.7 13.3 %collective-permute-start.25 = (bf16[2,64,1024]{2,1,0:T(8,128)(2,1)S(1)}, bf16[2,64,1024]{2,1,0:T(8,128)(2,1)S(1)}, u32[]{:S(2)}, u32[]{:S(2)}) collective-permute-start(bf16[2,64,1024]{2,1,0:T(8,128)(2,1)S(1)} %fusion.45), channel_id=1, source_target_pairs={{0,16},{4,20},{8,24},{12,28},{16,0},{20,4},{24,8},{28,12},{1,17},{... | collective-permute-start | bytes 786440 | tf_op jit(solution)/shard_map/ppermute | solution.py:218
  553.8 14.4 %collective-permute-start.23 = (bf16[128,1536]{1,0:T(8,128)(2,1)S(1)}, bf16[128,1536]{1,0:T(8,128)(2,1)S(1)}, u32[]{:S(2)}, u32[]{:S(2)}) collective-permute-start(bf16[128,1536]{1,0:T(8,128)(2,1)S(1)} %get-tuple-element.306), channel_id=1, source_target_pairs={{0,1},{1,0},{2,3},{3,2},{4,5},{5,4},{6,7},{7,6},{8,9},{9,8},{10,11... | collective-permute-start | bytes 1179656 | tf_op jit(solution)/shard_map/ppermute | solution.py:218
  561.5 6.8 collective-permute-start.24
  561.8 37.3 %collective-permute-start.30 = (bf16[2,2,192,1024]{3,2,1,0:T(8,128)(2,1)S(1)}, bf16[2,2,192,1024]{3,2,1,0:T(8,128)(2,1)S(1)}, u32[]{:S(2)}, u32[]{:S(2)}) collective-permute-start(bf16[2,2,192,1024]{3,2,1,0:T(8,128)(2,1)S(1)} %dynamic-slice_bitcast_fusion.3), channel_id=1, source_target_pairs={{0,4},{4,0},{8,12},{12,8},{16,20},{20,16},{24,28},{28,24},{1,5},{5... | collective-permute-start | bytes 4718600 | tf_op jit(solution)/shard_map/ppermute | solution.py:218
  579.5 21.0 %copy-start.59 = (bf16[1536,384]{1,0:T(8,128)(2,1)}, bf16[1536,384]{1,0:T(8,128)(2,1)S(1)}, u32[]{:S(2)}) copy-start(bf16[1536,384]{1,0:T(8,128)(2,1)S(1)} %convolution_convert_fusion.14) | copy-start | bytes 3538948
  581.8 19.6 %collective-permute-start.27 = (bf16[128,1536]{1,0:T(8,128)(2,1)S(1)}, bf16[128,1536]{1,0:T(8,128)(2,1)S(1)}, u32[]{:S(2)}, u32[]{:S(2)}) collective-permute-start(bf16[128,1536]{1,0:T(8,128)(2,1)S(1)} %get-tuple-element.323), channel_id=1, source_target_pairs={{0,1},{1,0},{2,3},{3,2},{4,5},{5,4},{6,7},{7,6},{8,9},{9,8},{10,11... | collective-permute-start | bytes 1179656 | tf_op jit(solution)/shard_map/ppermute | solution.py:218
  591.1 90.8 %collective-permute-start.31 = (bf16[2,2,192,1024]{3,2,1,0:T(8,128)(2,1)}, bf16[2,2,192,1024]{3,2,1,0:T(8,128)(2,1)}, u32[]{:S(2)}, u32[]{:S(2)}) collective-permute-start(bf16[2,2,192,1024]{3,2,1,0:T(8,128)(2,1)} %dynamic-slice_bitcast_fusion.2), channel_id=1, source_target_pairs={{0,4},{4,0},{8,12},{12,8},{16,20},{20,16},{24,28},{28,24},{1,5},{5... | collective-permute-start | bytes 4718600 | tf_op jit(solution)/shard_map/ppermute | solution.py:218
  592.0 115.9 %collective-permute-start.34 = (bf16[2,2,192,1024]{3,2,1,0:T(8,128)(2,1)}, bf16[2,2,192,1024]{3,2,1,0:T(8,128)(2,1)}, u32[]{:S(2)}, u32[]{:S(2)}) collective-permute-start(bf16[2,2,192,1024]{3,2,1,0:T(8,128)(2,1)} %dynamic-slice_bitcast_fusion.1), channel_id=1, source_target_pairs={{0,4},{4,0},{8,12},{12,8},{16,20},{20,16},{24,28},{28,24},{1,5},{5... | collective-permute-start | bytes 4718600 | tf_op jit(solution)/shard_map/ppermute | solution.py:218
  600.4 12.8 %collective-permute-start.29 = (bf16[64,1024]{1,0:T(8,128)(2,1)S(1)}, bf16[64,1024]{1,0:T(8,128)(2,1)S(1)}, u32[]{:S(2)}, u32[]{:S(2)}) collective-permute-start(bf16[64,1024]{1,0:T(8,128)(2,1)S(1)} %fusion.72), channel_id=1, source_target_pairs={{0,8},{4,12},{8,0},{12,4},{16,24},{20,28},{24,16},{28,20},{1,9},{5... | collective-permute-start | bytes 393224 | tf_op jit(solution)/shard_map/ppermute | solution.py:218
  600.4 6.7 collective-permute-start.26
  601.5 11.6 %collective-permute-start.28 = (bf16[128,1536]{1,0:T(8,128)(2,1)S(1)}, bf16[128,1536]{1,0:T(8,128)(2,1)S(1)}, u32[]{:S(2)}, u32[]{:S(2)}) collective-permute-start(bf16[128,1536]{1,0:T(8,128)(2,1)S(1)} %add_convert_fusion.1), channel_id=1, source_target_pairs={{0,2},{1,3},{2,0},{3,1},{4,6},{5,7},{6,4},{7,5},{8,10},{9,11},{10,... | collective-permute-start | bytes 1179656 | tf_op jit(solution)/shard_map/ppermute | solution.py:218
  634.0 85.8 %collective-permute-start.35 = (bf16[2,2,192,384]{3,2,1,0:T(8,128)(2,1)}, bf16[2,2,192,384]{3,2,1,0:T(8,128)(2,1)}, u32[]{:S(2)}, u32[]{:S(2)}) collective-permute-start(bf16[2,2,192,384]{3,2,1,0:T(8,128)(2,1)} %dynamic-slice_bitcast_fusion.4), channel_id=1, source_target_pairs={{0,4},{4,0},{8,12},{12,8},{16,20},{20,16},{24,28},{28,24},{1,5},{5... | collective-permute-start | bytes 1769480 | tf_op jit(solution)/shard_map/ppermute | solution.py:218
  635.6 44.7 %collective-permute-start.33 = (bf16[2,192,1024]{2,1,0:T(8,128)(2,1)}, bf16[2,192,1024]{2,1,0:T(8,128)(2,1)}, u32[]{:S(2)}, u32[]{:S(2)}) collective-permute-start(bf16[2,192,1024]{2,1,0:T(8,128)(2,1)} %fusion.13), channel_id=1, source_target_pairs={{0,16},{4,20},{8,24},{12,28},{16,0},{20,4},{24,8},{28,12},{1,17},{... | collective-permute-start | bytes 2359304 | tf_op jit(solution)/shard_map/ppermute | solution.py:218
  637.9 51.3 %collective-permute-start.32 = (bf16[2,2,2,32,4480]{4,3,2,1,0:T(8,128)(2,1)}, bf16[2,2,2,32,4480]{4,3,2,1,0:T(8,128)(2,1)}, u32[]{:S(2)}, u32[]{:S(2)}) collective-permute-start(bf16[2,2,2,32,4480]{4,3,2,1,0:T(8,128)(2,1)} %fusion), channel_id=1, source_target_pairs={{0,2},{1,3},{2,0},{3,1},{4,6},{5,7},{6,4},{7,5},{8,10},{9,11},{10,... | collective-permute-start | bytes 6881288 | tf_op jit(solution)/shard_map/ppermute | solution.py:218
  638.8 40.8 %copy-start.146 = (bf16[1,32]{1,0:T(2,128)(2,1)S(1)}, bf16[1,32]{1,0:T(2,128)(2,1)}, u32[]{:S(2)}) copy-start(bf16[1,32]{1,0:T(2,128)(2,1)} %get-tuple-element.359) | copy-start | bytes 196
  638.9 40.9 %copy-start.145 = (bf16[1,32]{1,0:T(2,128)(2,1)S(1)}, bf16[1,32]{1,0:T(2,128)(2,1)}, u32[]{:S(2)}) copy-start(bf16[1,32]{1,0:T(2,128)(2,1)} %get-tuple-element.360) | copy-start | bytes 196
  638.9 41.0 %copy-start.112 = (bf16[1,2048]{1,0:T(2,128)(2,1)S(1)}, bf16[1,2048]{1,0:T(2,128)(2,1)}, u32[]{:S(2)}) copy-start(bf16[1,2048]{1,0:T(2,128)(2,1)} %stack.104) | copy-start | bytes 12292
  638.9 41.1 %copy-start.111 = (bf16[1,2048]{1,0:T(2,128)(2,1)S(1)}, bf16[1,2048]{1,0:T(2,128)(2,1)}, u32[]{:S(2)}) copy-start(bf16[1,2048]{1,0:T(2,128)(2,1)} %stack.111) | copy-start | bytes 12292
  638.9 41.2 %copy-start.106 = (bf16[4,2304]{1,0:T(4,128)(2,1)S(1)}, bf16[4,2304]{1,0:T(4,128)(2,1)}, u32[]{:S(2)}) copy-start(bf16[4,2304]{1,0:T(4,128)(2,1)} %reduce_sum.460) | copy-start | bytes 55300
  680.2 19.0 %slice-start.8 = ((s8[4587520]{0:T(1024)(128)(4,1)}), s8[4194304]{0:T(1024)(128)(4,1)S(1)}, s32[]{:S(2)}) async-start(s8[4587520]{0:T(1024)(128)(4,1)} %bitcast.430), calls=%async_computation.8 | async-start | bytes 8388608
  681.9 17.4 %collective-permute-start.36 = (bf16[192,1024]{1,0:T(8,128)(2,1)S(1)}, bf16[192,1024]{1,0:T(8,128)(2,1)S(1)}, u32[]{:S(2)}, u32[]{:S(2)}) collective-permute-start(bf16[192,1024]{1,0:T(8,128)(2,1)S(1)} %fusion.38), channel_id=1, source_target_pairs={{0,8},{4,12},{8,0},{12,4},{16,24},{20,28},{24,16},{28,20},{1,9},{5... | collective-permute-start | bytes 1179656 | tf_op jit(solution)/shard_map/ppermute | solution.py:218
  (150 other events, 756.1 us)

commit v7 on v6

--- a/solution.py
+++ b/solution.py
@@ -903,7 +903,7 @@
         pltpu.VMEM(shape, jnp.bfloat16)
         for shape in temporary_shapes(kinds, sources, held_shapes)
     ]
-    plan = order_steps(jobs)
+    plan = order_steps(jobs, 3)
     numbers = len(grads) * (2 * depth_z + 1)
     tile = jax.ShapeDtypeStruct(extra.shape, jnp.float32)
     places = 4 + 2 * depth_z
@@ -991,7 +991,7 @@
     return (rows >= columns).astype(jnp.float32)
 
 
-FORWARD_UNROLL = 4
+FORWARD_UNROLL = 8
 BACKWARD_UNROLL = 4
 PROJ_WIDE = 2 * INNER + 2 * STATE + 128
 

time: 929 us -> 919 us (0.989)
  Pallas kernels: 543 us -> 533 us
where the time goes in v7:
time: 919 us; the launch traced here: 910 us
  Pallas kernels  533 us (58%)
  matrix products  148 us (16%)
  waiting for transfers between devices  86.7 us (9%)
  other arithmetic  60.3 us (7%)
  local copies, waits for them, and re-layouts  49.1 us (5%)
  starting transfers between devices  25.3 us (3%)
    pallas_call x1, Pallas kernels, spread_whole(): pl.pallas_call(partial(spread_kernel, plan, jobs, depth_z), out_shape=tup...  228 us
    pallas_call x1, Pallas kernels, sum_whole(): pl.pallas_call(partial(sum_kernel, plan, kinds, sources, depth_z), out_sh...  171 us
    ppermute x37, waiting for transfers between devices, swap(): lax.ppermute(value_entries, axis, [(place, place ^ mask) for place in ran...  86.7 us
    pallas_call x2, Pallas kernels, middle_backward(): pl.pallas_call(middle_slope_kernel, grid=(chunks,), out_shape=(jax.ShapeD...  81.4 us
    dot_general x11, matrix products, matmul_apply(): return jnp.dot(left, right, preferred_element_type=jnp.float32)  48.9 us
    dot_general x13, matrix products, product_tn(): lax.dot_general(left, right, (((0,), (0,)), ((), ())), preferred_element_...  46 us
    dot_general x10, matrix products, product_nt(): lax.dot_general(left, right, (((1,), (1,)), ((), ())), preferred_element_...  42.1 us
    pallas_call x2, Pallas kernels, middle_forward(): pl.pallas_call(middle_kernel, grid=(chunks,), out_shape=(jax.ShapeDtypeSt...  35.7 us
  transfers between devices with their start and end apart: 37, of which 15 were waited for; matrix products, arithmetic and copies ran while one was open for 14% of the time, Pallas kernels for 10%

profile of v7, /device:TPU:0, one launch (start us, length us, event | category | flops | bytes accessed | tf_op | source)
XLA Modules:
  0.0 910.4 jit_solution(2244492481126453459)
XLA Ops:
  13.8 227.9 %shard_map.526 = (bf16[4,2,2,2,16,1152]{5,4,3,2,1,0:T(8,128)(2,1)}, bf16[4,2,2,2,32,4480]{5,4,3,2,1,0:T(8,128)(2,1)}, bf16[4,2,2,2,64,1024]{5,4,3,2,1,0:T(8,128)...) custom-call(bf16[16,1152]{1,0:T(8,128)(2,1)} %pad_maximum_fusion.11., ...), custom_call_target="tpu_custom_call" | custom-call | tf_op jit(solution)/shard_map/pallas_call | solution.py:593
  246.8 11.4 %fusion.125.projected.earlier = f32[512,4480]{1,0:T(8,128)} fusion(bf16[1024,4480]{1,0:T(8,128)(2,1)} %bitcast.408, f32[512,1024]{1,0:T(8,128)S(1)} %get-tuple-element.362, f32[1024]{0:T(1024)S(1)} %get-tuple-element.342, f32[512]{0:T(512)S(1)} %fusion.106), kind=kOutput, calls=%fused_computation.355 | convolution fusion | flops 4699193344 | bytes 20453376 | tf_op jit(solution)/shard_map/dot_general | solution.py:201
  258.2 18.0 %shard_map.527 = (bf16[512,2048]{1,0:T(8,128)(2,1)S(1)}, f32[512,2048]{1,0:T(8,128)}, f32[4,128,2048]{2,1,0:T(8,128)}) custom-call(f32[512,4480]{1,0:T(8,128)} %fusion.125.projected.earlier, f32[4,2304]{1,0:T(4,128)S(1)} %squeeze.123.taps, f32[1,2048]{1,0:T(1,128)S(1)} %bitcast.335, f32[2,32]{1,0:T(2,128)S(1)} %get-tuple-element.373.decay, ...), custom_call_target="tpu_custom_call" | custom-call | flops 20000000000 | bytes 20000000 | tf_op jit(solution)/shard_map/pallas_call | solution.py:1376
  276.3 5.3 convolution_add_fusion.2
  284.9 3.5 fusion.57
  288.9 2.2 copy-done.22
  296.6 2.2 convolution_convert_fusion.10.triple
  298.9 5.3 shard_map.528
  308.9 9.5 %collective-permute-done.5 = bf16[128,1536]{1,0:T(8,128)(2,1)S(1)} collective-permute-done((bf16[128,1536]{1,0:T(8,128)(2,1)S(1)}, bf16[128,1536]{1,0:T(8,128)(2,1)S(1)}, u32[]{:S(2)}, u32[]{:S(2)}) %collective-permute-start.5) | collective-permute-done | bytes 393248 | tf_op jit(solution)/shard_map/ppermute | solution.py:218
  320.6 8.7 collective-permute-done.6
  331.1 3.5 fusion.127
  338.5 1.8 convolution_convert_fusion.12
  346.3 9.3 %collective-permute-done.11 = bf16[128,1536]{1,0:T(8,128)(2,1)S(1)} collective-permute-done((bf16[128,1536]{1,0:T(8,128)(2,1)S(1)}, bf16[128,1536]{1,0:T(8,128)(2,1)S(1)}, u32[]{:S(2)}, u32[]{:S(2)}) %collective-permute-start.11) | collective-permute-done | bytes 393248 | tf_op jit(solution)/shard_map/ppermute | solution.py:218
  357.8 4.2 multiply_reduce_fusion.10
  361.9 11.9 %fusion.126.projected.earlier = f32[512,4480]{1,0:T(8,128)} fusion(bf16[1024,4480]{1,0:T(8,128)(2,1)} %bitcast.410, f32[512,1024]{1,0:T(8,128)S(1)} %get-tuple-element.311, f32[1024]{0:T(1024)S(1)} %get-tuple-element.341, f32[512]{0:T(512)S(1)} %fusion.107), kind=kOutput, calls=%fused_computation.356 | convolution fusion | flops 4699193344 | bytes 20453376 | tf_op jit(solution)/shard_map/dot_general | solution.py:201
  373.8 17.7 %shard_map.529 = (bf16[512,2048]{1,0:T(8,128)(2,1)S(1)}, f32[512,2048]{1,0:T(8,128)}, f32[4,128,2048]{2,1,0:T(8,128)}) custom-call(f32[512,4480]{1,0:T(8,128)} %fusion.126.projected.earlier, f32[4,2304]{1,0:T(4,128)S(1)} %slice.397.taps, f32[1,2048]{1,0:T(1,128)S(1)} %bitcast.339, f32[2,32]{1,0:T(2,128)S(1)} %get-tuple-element.374.decay, ...), custom_call_target="tpu_custom_call" | custom-call | flops 20000000000 | bytes 20000000 | tf_op jit(solution)/shard_map/pallas_call | solution.py:1376
  391.6 2.4 multiply_reduce_fusion.9
  394.8 2.0 multiply_reduce_fusion
  398.9 4.3 fusion.52.slope
  403.3 2.4 convolution_convert_fusion.8
  410.1 40.7 %shard_map.530 = (bf16[512,4480]{1,0:T(8,128)(2,1)}, f32[4,8,2304]{2,1,0:T(8,128)S(1)}, f32[8,2048]{1,0:T(8,128)S(1)}, f32[8,2048]{1,0:T(8,128)S(1)}, f32[2,8,32]{2,1,0:T(8,128)S(1)}) custom-call(f32[512,4480]{1,0:T(8,128)} %fusion.126.projected.earlier, f32[512,4480]{1,0:T(8,128)} %fusion.126.projected.earlier, f32[512,2048]{1,0:T(8,128)S(1)} %copy-done.21, ...), custom_call_target="tpu_custom_call" | custom-call | flops 49999998976 | bytes 30000000 | tf_op jit(solution)/shard_map/pallas_call | solution.py:1429
  450.8 3.1 fusion.7
  454.0 7.8 convolution_convert_fusion.1
  461.8 2.7 copy_bitcast_fusion
  464.5 2.2 copy-done.23
  470.0 4.0 convolution_convert_fusion.15
  475.5 9.4 %multiply_reduce_fusion.1 = (bf16[1024]{0:T(1024)(128)(2,1)S(1)}, f32[512]{0:T(512)S(1)}, f32[512,1024]{1,0:T(8,128)S(1)}) fusion(f32[512,1024]{1,0:T(8,128)S(1)} %copy-done.37, f32[512]{0:T(512)S(1)} %fusion.107, f32[1024]{0:T(1024)S(1)} %get-tuple-element.341, bf16[512,4480]{1,0:T(8,128)(2,1)} %get-tuple-element.165, bf16[1024,4480]{1,0:T(8,128)(2,1)} %bitcast.411), kind=kOutput, calls=%fused_computation.38 | convolution fusion | flops 4700764672 | bytes 17967104 | tf_op jit(solution)/shard_map/dot_general | solution.py:211
  485.8 2.0 fusion.8
  491.5 16.5 %collective-permute-done.14 = bf16[128,1536]{1,0:T(8,128)(2,1)S(1)} collective-permute-done((bf16[128,1536]{1,0:T(8,128)(2,1)S(1)}, bf16[128,1536]{1,0:T(8,128)(2,1)S(1)}, u32[]{:S(2)}, u32[]{:S(2)}) %collective-permute-start.14) | collective-permute-done | bytes 393248 | tf_op jit(solution)/shard_map/ppermute | solution.py:218
  508.7 1.9 fusion.19
  512.3 1.8 convolution_convert_fusion.7
  514.5 5.2 fusion.78
  520.0 6.7 convolution_convert_fusion.11
  527.3 1.8 convolution_convert_fusion.5
  529.1 1.8 convolution_convert_fusion.6
  536.3 6.2 collective-permute-done.20
  545.9 7.6 collective-permute-done.22
  555.4 3.7 collective-permute-done.25
  561.5 7.9 shard_map.531
  571.5 2.2 convolution_convert_fusion.9
  573.9 4.3 fusion
  578.2 5.0 copy.97
  585.2 5.8 collective-permute-done.30
  595.1 4.0 convolution_convert_fusion.2
  599.2 5.9 collective-permute-done.28
  605.9 1.8 fusion.42
  607.8 5.6 convolution_convert_fusion.3
  613.4 3.5 convolution_add_fusion
  617.0 4.5 fusion.49.slope
  621.5 4.5 convolution_convert_fusion.4
  627.6 2.4 collective-permute-start.33
  630.9 40.6 %shard_map.532 = (bf16[512,4480]{1,0:T(8,128)(2,1)}, f32[4,8,2304]{2,1,0:T(8,128)S(1)}, f32[8,2048]{1,0:T(8,128)S(1)}, f32[8,2048]{1,0:T(8,128)S(1)}, f32[2,8,32]{2,1,0:T(8,128)S(1)}) custom-call(f32[512,4480]{1,0:T(8,128)} %fusion.125.projected.earlier, f32[512,4480]{1,0:T(8,128)} %fusion.125.projected.earlier, f32[512,2048]{1,0:T(8,128)S(1)} %copy-done.20, ...), custom_call_target="tpu_custom_call" | custom-call | flops 49999998976 | bytes 30000000 | tf_op jit(solution)/shard_map/pallas_call | solution.py:1429
  674.0 7.3 collective-permute-done.32
  681.3 10.0 %convolution_convert_fusion = bf16[1024,4480]{1,0:T(8,128)(2,1)} fusion(bf16[512,4480]{1,0:T(8,128)(2,1)} %get-tuple-element.197, f32[512,1024]{1,0:T(8,128)S(1)} %copy-done.33, f32[1024]{0:T(1024)S(1)} %copy-done.130, f32[512]{0:T(512)S(1)} %copy-done.132), kind=kOutput, calls=%fused_computation | convolution fusion | flops 4703780864 | bytes 15865856 | tf_op jit(solution)/shard_map/dot_general | solution.py:205
  691.3 8.0 multiply_reduce_fusion.3
  700.4 3.0 multiply_reduce_fusion.15
  703.3 1.8 multiply_reduce_fusion.23
  709.8 2.0 pad_maximum_fusion.5.refs_3_
  711.8 170.6 %shard_map.533 = (f32[32,3072]{1,0:T(8,128)}, f32[32,4480]{1,0:T(8,128)}, f32[64,1024]{1,0:T(8,128)}, f32[16,1152]{1,0:T(8,128)}, f32[192,1152]{1,0:T(8,128)}, /...) custom-call(bf16[4,2,2,2,32,3072]{5,4,3,2,1,0:T(8,128)(2,1)} %bitcas, ...), custom_call_target="tpu_custom_call" | custom-call | tf_op jit(solution)/shard_map/pallas_call | solution.py:910
  889.9 2.3 multiply_subtract_fusion.5
  893.6 1.8 multiply_subtract_fusion.2
  896.1 1.9 multiply_subtract_fusion.1
  900.6 2.3 multiply_subtract_fusion
  904.6 4.2 shard_map.534
  (607 shorter events, 110.6 us)
Async XLA Ops:
  244.9 38.2 %copy-start.99 = (f32[1536]{0:T(1024)}, f32[1536]{0:T(1024)S(1)}, u32[]{:S(2)}) copy-start(f32[1536]{0:T(1024)S(1)} %get-tuple-element.338) | copy-start | bytes 18436
  244.9 73.8 %copy-start.101 = (f32[1536]{0:T(1024)}, f32[1536]{0:T(1024)S(1)}, u32[]{:S(2)}) copy-start(f32[1536]{0:T(1024)S(1)} %get-tuple-element.337) | copy-start | bytes 18436
  245.0 60.5 %copy-start.114 = (f32[1,512]{1,0:T(1,128)}, f32[1,512]{1,0:T(1,128)S(1)}, u32[]{:S(2)}) copy-start(f32[1,512]{1,0:T(1,128)S(1)} %convert_element_type.486) | copy-start | bytes 6148
  246.2 30.0 %copy-start.32 = (f32[512,1024]{1,0:T(8,128)}, f32[512,1024]{1,0:T(8,128)S(1)}, u32[]{:S(2)}) copy-start(f32[512,1024]{1,0:T(8,128)S(1)} %get-tuple-element.362) | copy-start | bytes 6291460
  246.3 72.1 %copy-start.93 = (f32[1536]{0:T(1024)}, f32[1536]{0:T(1024)S(1)}, u32[]{:S(2)}) copy-start(f32[1536]{0:T(1024)S(1)} %pad.101.clone) | copy-start | bytes 18436
  246.8 38.1 %slice-start.2 = ((s8[6291456]{0:T(1024)(128)(4,1)}), s8[4194304]{0:T(1024)(128)(4,1)S(1)}, s32[]{:S(2)}) async-start(s8[6291456]{0:T(1024)(128)(4,1)} %bitcast.412), calls=%async_computation.2 | async-start | bytes 8388608
  258.2 26.7 %slice-start.3 = ((s8[6291456]{0:T(1024)(128)(4,1)}), s8[2097152]{0:T(1024)(128)(4,1)S(1)}, s32[]{:S(2)}) async-start(s8[6291456]{0:T(1024)(128)(4,1)} %bitcast.412), calls=%async_computation.3 | async-start | bytes 4194304
  282.9 35.5 %copy-start.26 = (f32[128,1024]{1,0:T(8,128)}, f32[128,1024]{1,0:T(8,128)S(1)}, u32[]{:S(2)}) copy-start(f32[128,1024]{1,0:T(8,128)S(1)} %fusion.62) | copy-start | bytes 1572868
  283.3 11.7 %collective-permute-start.1 = (bf16[128,1536]{1,0:T(8,128)(2,1)S(1)}, bf16[128,1536]{1,0:T(8,128)(2,1)S(1)}, u32[]{:S(2)}, u32[]{:S(2)}) collective-permute-start(bf16[128,1536]{1,0:T(8,128)(2,1)S(1)} %multiply_convert_fusion.5), channel_id=1, source_target_pairs={{0,1},{1,0},{2,3},{3,2},{4,5},{5,4},{6,7},{7,6},{8,9},{9,8},{10,11... | collective-permute-start | bytes 1179656 | tf_op jit(solution)/shard_map/ppermute | solution.py:218
  283.3 11.5 %collective-permute-start = (bf16[128,1536]{1,0:T(8,128)(2,1)S(1)}, bf16[128,1536]{1,0:T(8,128)(2,1)S(1)}, u32[]{:S(2)}, u32[]{:S(2)}) collective-permute-start(bf16[128,1536]{1,0:T(8,128)(2,1)S(1)} %multiply_convert_fusion.5), channel_id=1, source_target_pairs={{0,2},{1,3},{2,0},{3,1},{4,6},{5,7},{6,4},{7,5},{8,10},{9,11},{10,... | collective-permute-start | bytes 1179656 | tf_op jit(solution)/shard_map/ppermute | solution.py:218
  294.9 1.7 collective-permute-start.2
  298.9 32.2 %slice-start.6 = ((s8[6291456]{0:T(1024)(128)(4,1)}), s8[4194304]{0:T(1024)(128)(4,1)S(1)}, s32[]{:S(2)}) async-start(s8[6291456]{0:T(1024)(128)(4,1)} %bitcast.419), calls=%async_computation.6 | async-start | bytes 8388608
  304.2 26.9 %slice-start.7 = ((s8[6291456]{0:T(1024)(128)(4,1)}), s8[2097152]{0:T(1024)(128)(4,1)S(1)}, s32[]{:S(2)}) async-start(s8[6291456]{0:T(1024)(128)(4,1)} %bitcast.419), calls=%async_computation.7 | async-start | bytes 4194304
  305.3 1.8 collective-permute-start.4
  305.9 3.0 collective-permute-start.3
  307.2 11.2 %collective-permute-start.5 = (bf16[128,1536]{1,0:T(8,128)(2,1)S(1)}, bf16[128,1536]{1,0:T(8,128)(2,1)S(1)}, u32[]{:S(2)}, u32[]{:S(2)}) collective-permute-start(bf16[128,1536]{1,0:T(8,128)(2,1)S(1)} %add_convert_fusion.4), channel_id=1, source_target_pairs={{0,2},{1,3},{2,0},{3,1},{4,6},{5,7},{6,4},{7,5},{8,10},{9,11},{10,... | collective-permute-start | bytes 1179656 | tf_op jit(solution)/shard_map/ppermute | solution.py:218
  318.7 15.9 %copy-start.147 = (f32[128]{0:T(128)}, f32[128]{0:T(128)S(1)}, u32[]{:S(2)}) copy-start(f32[128]{0:T(128)S(1)} %get-tuple-element.314) | copy-start | bytes 1540
  318.8 36.9 %copy-start.24 = (f32[128,1536]{1,0:T(8,128)}, f32[128,1536]{1,0:T(8,128)S(1)}, u32[]{:S(2)}) copy-start(f32[128,1536]{1,0:T(8,128)S(1)} %get-tuple-element.315) | copy-start | bytes 2359300
  318.8 15.8 %copy-start.135 = (f32[128]{0:T(128)}, f32[128]{0:T(128)S(1)}, u32[]{:S(2)}) copy-start(f32[128]{0:T(128)S(1)} %fusion.111) | copy-start | bytes 1540
  319.0 10.4 %collective-permute-start.6 = (bf16[128,1536]{1,0:T(8,128)(2,1)S(1)}, bf16[128,1536]{1,0:T(8,128)(2,1)S(1)}, u32[]{:S(2)}, u32[]{:S(2)}) collective-permute-start(bf16[128,1536]{1,0:T(8,128)(2,1)S(1)} %multiply_convert_fusion.4), channel_id=1, source_target_pairs={{0,2},{1,3},{2,0},{3,1},{4,6},{5,7},{6,4},{7,5},{8,10},{9,11},{10,... | collective-permute-start | bytes 1179656 | tf_op jit(solution)/shard_map/ppermute | solution.py:218
  320.6 8.8 collective-permute-start.7
  329.3 1.7 collective-permute-start.8
  341.5 1.8 collective-permute-start.10
  342.6 3.7 collective-permute-start.9
  344.4 11.2 %collective-permute-start.11 = (bf16[128,1536]{1,0:T(8,128)(2,1)S(1)}, bf16[128,1536]{1,0:T(8,128)(2,1)S(1)}, u32[]{:S(2)}, u32[]{:S(2)}) collective-permute-start(bf16[128,1536]{1,0:T(8,128)(2,1)S(1)} %add_convert_fusion.3), channel_id=1, source_target_pairs={{0,2},{1,3},{2,0},{3,1},{4,6},{5,7},{6,4},{7,5},{8,10},{9,11},{10,... | collective-permute-start | bytes 1179656 | tf_op jit(solution)/shard_map/ppermute | solution.py:218
  361.9 29.6 %copy-start.35 = (f32[512,1024]{1,0:T(8,128)}, f32[512,1024]{1,0:T(8,128)S(1)}, u32[]{:S(2)}) copy-start(f32[512,1024]{1,0:T(8,128)S(1)} %get-tuple-element.311) | copy-start | bytes 6291460
  373.8 17.8 %copy-start.150 = (bf16[4,2,2,2,64,1024]{5,4,3,2,1,0:T(8,128)(2,1)S(1)}, bf16[4,2,2,2,64,1024]{5,4,3,2,1,0:T(8,128)(2,1)}, u32[]{:S(2)}) copy-start(bf16[4,2,2,2,64,1024]{5,4,3,2,1,0:T(8,128)(2,1)} %get-tuple-element.155) | copy-start | bytes 12582916
  408.8 42.0 %collective-permute-start.12 = (bf16[2,2,2,2,64,1024]{5,4,3,2,1,0:T(8,128)(2,1)}, bf16[2,2,2,2,64,1024]{5,4,3,2,1,0:T(8,128)(2,1)}, u32[]{:S(2)}, u32[]{:S(2)}) collective-permute-start(bf16[2,2,2,2,64,1024]{5,4,3,2,1,0:T(8,128)(2,1)} %dynamic-slice_bitcast_fusion), channel_id=1, source_target_pairs={{0,1},{1,0},{2,3},{3,2},{4,5},{5,4},{6,7},{7,6},{8,9},{9,8},{10,11... | collective-permute-start | bytes 6291464 | tf_op jit(solution)/shard_map/ppermute | solution.py:218
  466.6 22.8 %collective-permute-start.13 = (bf16[2,2,2,2,32,4480]{5,4,2,1,0,3:T(8,128)(2,1)}, bf16[2,2,2,2,32,4480]{5,4,2,1,0,3:T(8,128)(2,1)}, u32[]{:S(2)}, u32[]{:S(2)}) collective-permute-start(bf16[2,2,2,2,32,4480]{5,4,2,1,0,3:T(8,128)(2,1)} %copy_bitcast_fusion), channel_id=1, source_target_pairs={{0,1},{1,0},{2,3},{3,2},{4,5},{5,4},{6,7},{7,6},{8,9},{9,8},{10,11... | collective-permute-start | bytes 13762568 | tf_op jit(solution)/shard_map/ppermute | solution.py:218
  474.0 34.7 %collective-permute-start.17 = (bf16[2,2,2,64,1024]{4,3,2,1,0:T(8,128)(2,1)S(1)}, bf16[2,2,2,64,1024]{4,3,2,1,0:T(8,128)(2,1)S(1)}, u32[]{:S(2)}, u32[]{:S(2)}) collective-permute-start(bf16[2,2,2,64,1024]{4,3,2,1,0:T(8,128)(2,1)S(1)} %copy-done.76), channel_id=1, source_target_pairs={{0,2},{1,3},{2,0},{3,1},{4,6},{5,7},{6,4},{7,5},{8,10},{9,11},{10,... | collective-permute-start | bytes 3145736 | tf_op jit(solution)/shard_map/ppermute | solution.py:218
  487.9 20.1 %slice-start = ((s8[6291456]{0:T(1024)(128)(4,1)}), s8[4194304]{0:T(1024)(128)(4,1)S(1)}, s32[]{:S(2)}) async-start(s8[6291456]{0:T(1024)(128)(4,1)} %bitcast.341), calls=%async_computation | async-start | bytes 8388608
  489.5 18.5 %slice-start.1 = ((s8[6291456]{0:T(1024)(128)(4,1)}), s8[2097152]{0:T(1024)(128)(4,1)S(1)}, s32[]{:S(2)}) async-start(s8[6291456]{0:T(1024)(128)(4,1)} %bitcast.341), calls=%async_computation.1 | async-start | bytes 4194304
  489.5 18.5 %collective-permute-start.14 = (bf16[128,1536]{1,0:T(8,128)(2,1)S(1)}, bf16[128,1536]{1,0:T(8,128)(2,1)S(1)}, u32[]{:S(2)}, u32[]{:S(2)}) collective-permute-start(bf16[128,1536]{1,0:T(8,128)(2,1)S(1)} %convert_element_type.518), channel_id=1, source_target_pairs={{0,2},{1,3},{2,0},{3,1},{4,6},{5,7},{6,4},{7,5},{8,10},{9,11},{10,... | collective-permute-start | bytes 1179656 | tf_op jit(solution)/shard_map/ppermute | solution.py:218
  491.1 19.4 %collective-permute-start.15 = (bf16[128,1536]{1,0:T(8,128)(2,1)S(1)}, bf16[128,1536]{1,0:T(8,128)(2,1)S(1)}, u32[]{:S(2)}, u32[]{:S(2)}) collective-permute-start(bf16[128,1536]{1,0:T(8,128)(2,1)S(1)} %convert_element_type.518), channel_id=1, source_target_pairs={{0,1},{1,0},{2,3},{3,2},{4,5},{5,4},{6,7},{7,6},{8,9},{9,8},{10,11... | collective-permute-start | bytes 1179656 | tf_op jit(solution)/shard_map/ppermute | solution.py:218
  508.0 2.6 collective-permute-start.16
  508.7 50.4 %copy-start.75 = (bf16[2,2,2,64,1024]{4,3,2,1,0:T(8,128)(2,1)}, bf16[2,2,2,64,1024]{4,3,2,1,0:T(8,128)(2,1)S(1)}, u32[]{:S(2)}) copy-start(bf16[2,2,2,64,1024]{4,3,2,1,0:T(8,128)(2,1)S(1)} %collective-permute-done.17) | copy-start | bytes 3145732
  510.7 24.1 %collective-permute-start.21 = (bf16[2,2,64,1024]{3,2,1,0:T(8,128)(2,1)S(1)}, bf16[2,2,64,1024]{3,2,1,0:T(8,128)(2,1)S(1)}, u32[]{:S(2)}, u32[]{:S(2)}) collective-permute-start(bf16[2,2,64,1024]{3,2,1,0:T(8,128)(2,1)S(1)} %fusion.19), channel_id=1, source_target_pairs={{0,4},{4,0},{8,12},{12,8},{16,20},{20,16},{24,28},{28,24},{1,5},{5... | collective-permute-start | bytes 1572872 | tf_op jit(solution)/shard_map/ppermute | solution.py:218
  514.1 76.9 %copy-start.55 = (bf16[1536,1024]{1,0:T(8,128)(2,1)}, bf16[1536,1024]{1,0:T(8,128)(2,1)S(1)}, u32[]{:S(2)}) copy-start(bf16[1536,1024]{1,0:T(8,128)(2,1)S(1)} %convolution_convert_fusion.7) | copy-start | bytes 9437188
  526.7 9.5 %collective-permute-start.18 = (bf16[128,1536]{1,0:T(8,128)(2,1)S(1)}, bf16[128,1536]{1,0:T(8,128)(2,1)S(1)}, u32[]{:S(2)}, u32[]{:S(2)}) collective-permute-start(bf16[128,1536]{1,0:T(8,128)(2,1)S(1)} %get-tuple-element.324), channel_id=1, source_target_pairs={{0,1},{1,0},{2,3},{3,2},{4,5},{5,4},{6,7},{7,6},{8,9},{9,8},{10,11... | collective-permute-start | bytes 1179656 | tf_op jit(solution)/shard_map/ppermute | solution.py:218
  527.0 4.0 collective-permute-start.19
  531.1 11.3 %collective-permute-start.20 = (bf16[128,1536]{1,0:T(8,128)(2,1)S(1)}, bf16[128,1536]{1,0:T(8,128)(2,1)S(1)}, u32[]{:S(2)}, u32[]{:S(2)}) collective-permute-start(bf16[128,1536]{1,0:T(8,128)(2,1)S(1)} %add_convert_fusion.2), channel_id=1, source_target_pairs={{0,2},{1,3},{2,0},{3,1},{4,6},{5,7},{6,4},{7,5},{8,10},{9,11},{10,... | collective-permute-start | bytes 1179656 | tf_op jit(solution)/shard_map/ppermute | solution.py:218
  534.8 24.3 %copy-start.82 = (bf16[2,2,64,1024]{3,2,1,0:T(8,128)(2,1)}, bf16[2,2,64,1024]{3,2,1,0:T(8,128)(2,1)S(1)}, u32[]{:S(2)}) copy-start(bf16[2,2,64,1024]{3,2,1,0:T(8,128)(2,1)S(1)} %collective-permute-done.21) | copy-start | bytes 1572868
  543.1 10.5 %collective-permute-start.22 = (bf16[128,1536]{1,0:T(8,128)(2,1)S(1)}, bf16[128,1536]{1,0:T(8,128)(2,1)S(1)}, u32[]{:S(2)}, u32[]{:S(2)}) collective-permute-start(bf16[128,1536]{1,0:T(8,128)(2,1)S(1)} %get-tuple-element.306), channel_id=1, source_target_pairs={{0,2},{1,3},{2,0},{3,1},{4,6},{5,7},{6,4},{7,5},{8,10},{9,11},{10,... | collective-permute-start | bytes 1179656 | tf_op jit(solution)/shard_map/ppermute | solution.py:218
  545.8 13.3 %collective-permute-start.25 = (bf16[2,64,1024]{2,1,0:T(8,128)(2,1)S(1)}, bf16[2,64,1024]{2,1,0:T(8,128)(2,1)S(1)}, u32[]{:S(2)}, u32[]{:S(2)}) collective-permute-start(bf16[2,64,1024]{2,1,0:T(8,128)(2,1)S(1)} %fusion.45), channel_id=1, source_target_pairs={{0,16},{4,20},{8,24},{12,28},{16,0},{20,4},{24,8},{28,12},{1,17},{... | collective-permute-start | bytes 786440 | tf_op jit(solution)/shard_map/ppermute | solution.py:218
  545.8 14.4 %collective-permute-start.23 = (bf16[128,1536]{1,0:T(8,128)(2,1)S(1)}, bf16[128,1536]{1,0:T(8,128)(2,1)S(1)}, u32[]{:S(2)}, u32[]{:S(2)}) collective-permute-start(bf16[128,1536]{1,0:T(8,128)(2,1)S(1)} %get-tuple-element.306), channel_id=1, source_target_pairs={{0,1},{1,0},{2,3},{3,2},{4,5},{5,4},{6,7},{7,6},{8,9},{9,8},{10,11... | collective-permute-start | bytes 1179656 | tf_op jit(solution)/shard_map/ppermute | solution.py:218
  553.5 6.8 collective-permute-start.24
  553.8 37.3 %collective-permute-start.30 = (bf16[2,2,192,1024]{3,2,1,0:T(8,128)(2,1)S(1)}, bf16[2,2,192,1024]{3,2,1,0:T(8,128)(2,1)S(1)}, u32[]{:S(2)}, u32[]{:S(2)}) collective-permute-start(bf16[2,2,192,1024]{3,2,1,0:T(8,128)(2,1)S(1)} %dynamic-slice_bitcast_fusion.3), channel_id=1, source_target_pairs={{0,4},{4,0},{8,12},{12,8},{16,20},{20,16},{24,28},{28,24},{1,5},{5... | collective-permute-start | bytes 4718600 | tf_op jit(solution)/shard_map/ppermute | solution.py:218
  571.5 21.0 %copy-start.59 = (bf16[1536,384]{1,0:T(8,128)(2,1)}, bf16[1536,384]{1,0:T(8,128)(2,1)S(1)}, u32[]{:S(2)}) copy-start(bf16[1536,384]{1,0:T(8,128)(2,1)S(1)} %convolution_convert_fusion.14) | copy-start | bytes 3538948
  573.8 19.6 %collective-permute-start.27 = (bf16[128,1536]{1,0:T(8,128)(2,1)S(1)}, bf16[128,1536]{1,0:T(8,128)(2,1)S(1)}, u32[]{:S(2)}, u32[]{:S(2)}) collective-permute-start(bf16[128,1536]{1,0:T(8,128)(2,1)S(1)} %get-tuple-element.323), channel_id=1, source_target_pairs={{0,1},{1,0},{2,3},{3,2},{4,5},{5,4},{6,7},{7,6},{8,9},{9,8},{10,11... | collective-permute-start | bytes 1179656 | tf_op jit(solution)/shard_map/ppermute | solution.py:218
  583.1 90.8 %collective-permute-start.31 = (bf16[2,2,192,1024]{3,2,1,0:T(8,128)(2,1)}, bf16[2,2,192,1024]{3,2,1,0:T(8,128)(2,1)}, u32[]{:S(2)}, u32[]{:S(2)}) collective-permute-start(bf16[2,2,192,1024]{3,2,1,0:T(8,128)(2,1)} %dynamic-slice_bitcast_fusion.2), channel_id=1, source_target_pairs={{0,4},{4,0},{8,12},{12,8},{16,20},{20,16},{24,28},{28,24},{1,5},{5... | collective-permute-start | bytes 4718600 | tf_op jit(solution)/shard_map/ppermute | solution.py:218
  584.0 115.9 %collective-permute-start.34 = (bf16[2,2,192,1024]{3,2,1,0:T(8,128)(2,1)}, bf16[2,2,192,1024]{3,2,1,0:T(8,128)(2,1)}, u32[]{:S(2)}, u32[]{:S(2)}) collective-permute-start(bf16[2,2,192,1024]{3,2,1,0:T(8,128)(2,1)} %dynamic-slice_bitcast_fusion.1), channel_id=1, source_target_pairs={{0,4},{4,0},{8,12},{12,8},{16,20},{20,16},{24,28},{28,24},{1,5},{5... | collective-permute-start | bytes 4718600 | tf_op jit(solution)/shard_map/ppermute | solution.py:218
  592.4 12.8 %collective-permute-start.29 = (bf16[64,1024]{1,0:T(8,128)(2,1)S(1)}, bf16[64,1024]{1,0:T(8,128)(2,1)S(1)}, u32[]{:S(2)}, u32[]{:S(2)}) collective-permute-start(bf16[64,1024]{1,0:T(8,128)(2,1)S(1)} %fusion.72), channel_id=1, source_target_pairs={{0,8},{4,12},{8,0},{12,4},{16,24},{20,28},{24,16},{28,20},{1,9},{5... | collective-permute-start | bytes 393224 | tf_op jit(solution)/shard_map/ppermute | solution.py:218
  592.4 6.7 collective-permute-start.26
  593.5 11.6 %collective-permute-start.28 = (bf16[128,1536]{1,0:T(8,128)(2,1)S(1)}, bf16[128,1536]{1,0:T(8,128)(2,1)S(1)}, u32[]{:S(2)}, u32[]{:S(2)}) collective-permute-start(bf16[128,1536]{1,0:T(8,128)(2,1)S(1)} %add_convert_fusion.1), channel_id=1, source_target_pairs={{0,2},{1,3},{2,0},{3,1},{4,6},{5,7},{6,4},{7,5},{8,10},{9,11},{10,... | collective-permute-start | bytes 1179656 | tf_op jit(solution)/shard_map/ppermute | solution.py:218
  626.0 85.8 %collective-permute-start.35 = (bf16[2,2,192,384]{3,2,1,0:T(8,128)(2,1)}, bf16[2,2,192,384]{3,2,1,0:T(8,128)(2,1)}, u32[]{:S(2)}, u32[]{:S(2)}) collective-permute-start(bf16[2,2,192,384]{3,2,1,0:T(8,128)(2,1)} %dynamic-slice_bitcast_fusion.4), channel_id=1, source_target_pairs={{0,4},{4,0},{8,12},{12,8},{16,20},{20,16},{24,28},{28,24},{1,5},{5... | collective-permute-start | bytes 1769480 | tf_op jit(solution)/shard_map/ppermute | solution.py:218
  627.6 44.7 %collective-permute-start.33 = (bf16[2,192,1024]{2,1,0:T(8,128)(2,1)}, bf16[2,192,1024]{2,1,0:T(8,128)(2,1)}, u32[]{:S(2)}, u32[]{:S(2)}) collective-permute-start(bf16[2,192,1024]{2,1,0:T(8,128)(2,1)} %fusion.13), channel_id=1, source_target_pairs={{0,16},{4,20},{8,24},{12,28},{16,0},{20,4},{24,8},{28,12},{1,17},{... | collective-permute-start | bytes 2359304 | tf_op jit(solution)/shard_map/ppermute | solution.py:218
  629.9 51.3 %collective-permute-start.32 = (bf16[2,2,2,32,4480]{4,3,2,1,0:T(8,128)(2,1)}, bf16[2,2,2,32,4480]{4,3,2,1,0:T(8,128)(2,1)}, u32[]{:S(2)}, u32[]{:S(2)}) collective-permute-start(bf16[2,2,2,32,4480]{4,3,2,1,0:T(8,128)(2,1)} %fusion), channel_id=1, source_target_pairs={{0,2},{1,3},{2,0},{3,1},{4,6},{5,7},{6,4},{7,5},{8,10},{9,11},{10,... | collective-permute-start | bytes 6881288 | tf_op jit(solution)/shard_map/ppermute | solution.py:218
  630.9 40.8 %copy-start.146 = (bf16[1,32]{1,0:T(2,128)(2,1)S(1)}, bf16[1,32]{1,0:T(2,128)(2,1)}, u32[]{:S(2)}) copy-start(bf16[1,32]{1,0:T(2,128)(2,1)} %get-tuple-element.359) | copy-start | bytes 196
  630.9 40.9 %copy-start.145 = (bf16[1,32]{1,0:T(2,128)(2,1)S(1)}, bf16[1,32]{1,0:T(2,128)(2,1)}, u32[]{:S(2)}) copy-start(bf16[1,32]{1,0:T(2,128)(2,1)} %get-tuple-element.360) | copy-start | bytes 196
  630.9 41.0 %copy-start.112 = (bf16[1,2048]{1,0:T(2,128)(2,1)S(1)}, bf16[1,2048]{1,0:T(2,128)(2,1)}, u32[]{:S(2)}) copy-start(bf16[1,2048]{1,0:T(2,128)(2,1)} %stack.104) | copy-start | bytes 12292
  630.9 41.1 %copy-start.111 = (bf16[1,2048]{1,0:T(2,128)(2,1)S(1)}, bf16[1,2048]{1,0:T(2,128)(2,1)}, u32[]{:S(2)}) copy-start(bf16[1,2048]{1,0:T(2,128)(2,1)} %stack.111) | copy-start | bytes 12292
  630.9 41.2 %copy-start.106 = (bf16[4,2304]{1,0:T(4,128)(2,1)S(1)}, bf16[4,2304]{1,0:T(4,128)(2,1)}, u32[]{:S(2)}) copy-start(bf16[4,2304]{1,0:T(4,128)(2,1)} %reduce_sum.460) | copy-start | bytes 55300
  672.3 19.0 %slice-start.8 = ((s8[4587520]{0:T(1024)(128)(4,1)}), s8[4194304]{0:T(1024)(128)(4,1)S(1)}, s32[]{:S(2)}) async-start(s8[4587520]{0:T(1024)(128)(4,1)} %bitcast.430), calls=%async_computation.8 | async-start | bytes 8388608
  673.9 17.4 %collective-permute-start.36 = (bf16[192,1024]{1,0:T(8,128)(2,1)S(1)}, bf16[192,1024]{1,0:T(8,128)(2,1)S(1)}, u32[]{:S(2)}, u32[]{:S(2)}) collective-permute-start(bf16[192,1024]{1,0:T(8,128)(2,1)S(1)} %fusion.38), channel_id=1, source_target_pairs={{0,8},{4,12},{8,0},{12,4},{16,24},{20,28},{24,16},{28,20},{1,9},{5... | collective-permute-start | bytes 1179656 | tf_op jit(solution)/shard_map/ppermute | solution.py:218
  (150 other events, 756.1 us)
